TPU v7x, 32 devices: a whole 2x2x4 slice. The times are simulated.
32 devices in a mesh: ctx: 2 (over y), tp: 16 (over z, x, core).
Axes of the slice: x: 2, y: 2, z: 4, core: 2. Of those that a mesh axis runs over, the one named last changes fastest.
Arguments:
- hidden: bfloat16 [512, 2048], P(('ctx', 'tp')), may hold values from -6 to 6
- w_in: bfloat16 [2048, 2048], P(None, 'tp'), may hold values from -0.125 to 0.125
- w_bc: bfloat16 [2048, 32], replicated, may hold values from -0.125 to 0.125
- w_dt: bfloat16 [16, 2048], P('tp'), may hold values from -0.125 to 0.125
- dt_bias: float32 [16], P('tp'), may hold values from -5 to -3
- a_log: float32 [16], P('tp'), may hold values from -4.6 to 0
- d_skip: float32 [16], P('tp'), may hold values from 0.5 to 1.5
- conv_w: float32 [4, 1024], P(None, 'tp'), may hold values from -3 to 3
- w_out: bfloat16 [1024, 2048], P('tp'), may hold values from -0.1875 to 0.1875
- d_out: bfloat16 [512, 2048], P(('ctx', 'tp')), may hold values from -6 to 6
Outputs:
- d_hidden: bfloat16 [512, 2048], P(('ctx', 'tp'))
- d_w_in: float32 [2048, 2048], P(None, 'tp')
- d_w_out: float32 [1024, 2048], P('tp')
- d_w_bc: float32 [2048, 32], replicated
All inputs are finite; a program needn't handle non-finite values.
Results may differ from a plain program's by a relative error of at most 0.017.
Values may be sent and summed in bfloat16 or wider, within the bound.
No kernel may reach another device: no remote copies, remote signals or barrier semaphores. Data moves between devices by JAX's collectives and lax.ppermute only.
A program may use at most 64 MiB of HBM per device.

v0:
```python
import math

import jax
import jax.numpy as jnp
from jax import lax
from jax.sharding import PartitionSpec as P

STATE = 16
CONV = 4


precise = lax.Precision.HIGHEST


def padded(array, sides, width):
    for axis, dim in sides:
        size, length = (lax.axis_size(axis), array.shape[dim])
        up = [(i, (i + 1) % size) for i in range(size - 1)]
        down = [(j, i) for i, j in up]
        last = lax.slice_in_dim(array, length - width, length, axis=dim)
        leading = lax.slice_in_dim(array, 0, width, axis=dim)
        before = lax.ppermute(last, axis, up)
        after = lax.ppermute(leading, axis, down)
        array = jnp.concatenate([before, array, after], axis=dim)
    return array


def entering(array, axis, combine, identity, reverse):
    length, index = (lax.axis_size(axis), lax.axis_index(axis))
    everything = jax.tree.map(lambda part: lax.all_gather(part, axis), array)
    start = jax.tree.map(
        lambda part, zero: jnp.broadcast_to(jnp.asarray(zero, part.dtype), part.shape),
        array,
        identity,
    )

    def step(k, before):
        at = length - 1 - k if reverse else k
        reached = at > index if reverse else at < index
        new = combine(before, jax.tree.map(lambda part: part[at], everything))
        return jax.tree.map(lambda a, b: jnp.where(reached, a, b), new, before)

    return lax.fori_loop(0, length, step, start)


def times_rows(operand_a, operand_b):
    return lax.dot_general(
        operand_a, operand_b, (((1,), (1,)), ((), ())), preferred_element_type=jnp.float32
    )


def across_rows(operand_a, operand_b):
    return lax.dot_general(
        operand_a, operand_b, (((0,), (0,)), ((), ())), preferred_element_type=jnp.float32
    )


def conv_silu(x_ext, conv_w):
    length = x_ext.shape[0] - CONV + 1
    summed = conv_w[0] * x_ext[0:length]
    for shift_k in range(1, CONV):
        summed = summed + conv_w[shift_k] * x_ext[shift_k : shift_k + length]
    return jax.nn.silu(summed)


def block_ssd(conv_out, steps_dt, b_rows, c_rows, decay_rate, state_in):
    positions = conv_out.shape[0]
    log_keep = jnp.cumsum(steps_dt * decay_rate)
    causal = lax.broadcasted_iota(jnp.int32, (positions, positions), 0) >= lax.broadcasted_iota(
        jnp.int32, (positions, positions), 1
    )
    decays = jnp.exp(jnp.where(causal, log_keep[:, None] - log_keep[None, :], -jnp.inf))
    scores = jnp.einsum("in,jn->ij", c_rows, b_rows, precision=precise) * decays
    weighted = steps_dt[:, None] * conv_out
    outputs = jnp.einsum("ij,jp->ip", scores, weighted, precision=precise)
    outputs = outputs + jnp.exp(log_keep)[:, None] * jnp.einsum(
        "in,pn->ip", c_rows, state_in, precision=precise
    )
    remains = jnp.exp(log_keep[-1] - log_keep)
    state_out = jnp.exp(log_keep[-1]) * state_in + jnp.einsum(
        "j,jp,jn->pn", remains, weighted, b_rows, precision=precise
    )
    return (outputs, state_out)


def strand_core(x_ext, gate_in, b_c, dt_raw, state_in, params):
    dt_bias_h, decay_rate, skip_h, conv_w = params
    conv_out = conv_silu(x_ext, conv_w)
    steps_dt = jax.nn.softplus(dt_raw + dt_bias_h)
    outputs, state_out = block_ssd(
        conv_out, steps_dt, b_c[:, :STATE], b_c[:, STATE:], decay_rate, state_in
    )
    gated = (outputs + skip_h * conv_out) * jax.nn.silu(gate_in)
    return (gated, state_out)


def strand_summary(x_ext, b_c, dt_raw, params):
    dt_bias_h, decay_rate, skip_h, conv_w = params
    conv_out = conv_silu(x_ext, conv_w)
    steps_dt = jax.nn.softplus(dt_raw + dt_bias_h)
    log_keep = jnp.cumsum(steps_dt * decay_rate)
    remains = jnp.exp(log_keep[-1] - log_keep) * steps_dt
    local_state = jnp.einsum("j,jp,jn->pn", remains, conv_out, b_c[:, :STATE], precision=precise)
    return (jnp.exp(log_keep[-1]), local_state)


def chain_step(earlier, following):
    return (earlier[0] * following[0], following[0] * earlier[1] + following[1])


def local(hidden, w_in, w_bc, w_dt, dt_bias, a_log, d_skip, conv_w, w_out, d_out):
    own_rows = hidden.shape[0]
    seq_rows = own_rows * lax.axis_size("tp")
    length_all = seq_rows * lax.axis_size("ctx")
    head_dim = w_out.shape[0]
    rim_rows = CONV - 1
    w_pair = jnp.concatenate([w_in, w_in[::-1]], axis=1)
    bc_pair = jnp.concatenate([w_bc, w_bc[::-1]], axis=1)
    dt_pair = jnp.concatenate([w_dt, w_dt[:, ::-1]], axis=0)
    out_pair = jnp.concatenate([w_out, w_out[:, ::-1]], axis=0)
    params = (dt_bias[0], -jnp.exp(a_log[0]), d_skip[0], conv_w)
    gathered = lax.all_gather(hidden, "tp", axis=0, tiled=True)
    projected = jnp.dot(gathered, w_pair, preferred_element_type=jnp.float32).astype(jnp.bfloat16)
    dt_raw = times_rows(gathered, dt_pair)
    b_c_all = jnp.dot(gathered, bc_pair, preferred_element_type=jnp.float32)
    x_both = jnp.concatenate(
        [projected[:, :head_dim], projected[:, 2 * head_dim : 3 * head_dim]], axis=1
    )
    x_halo = padded(x_both, (("ctx", 0),), rim_rows).astype(jnp.float32)
    x_ext = jnp.stack(
        [x_halo[: seq_rows + rim_rows, :head_dim], x_halo[rim_rows:, head_dim:][::-1]]
    )
    gate_in = jnp.stack(
        [projected[:, head_dim : 2 * head_dim], projected[::-1, 3 * head_dim :]]
    ).astype(jnp.float32)
    b_c = jnp.stack([b_c_all[:, : 2 * STATE], b_c_all[::-1, 2 * STATE :]])
    dt_both = jnp.stack([dt_raw[:, 0], dt_raw[::-1, 1]])
    decays, local_states = jax.vmap(strand_summary, in_axes=(0, 0, 0, None))(
        x_ext, b_c, dt_both, params
    )
    identity = (jnp.ones((), jnp.float32), jnp.zeros((head_dim, STATE), jnp.float32))
    fwd_in = entering((decays[0], local_states[0]), "ctx", chain_step, identity, False)[1]
    rev_in = entering((decays[1], local_states[1]), "ctx", chain_step, identity, True)[1]
    states_in = jnp.stack([fwd_in, rev_in])

    def core_both(x_part, gate_part, bc_part, dt_part, state_part):
        return jax.vmap(strand_core, in_axes=(0, 0, 0, 0, 0, None))(
            x_part, gate_part, bc_part, dt_part, state_part, params
        )

    (gated, states_out), pullback = jax.vjp(core_both, x_ext, gate_in, b_c, dt_both, states_in)
    gated_nat = jnp.concatenate([gated[0], gated[1][::-1]], axis=1).astype(jnp.bfloat16)
    portion = lax.all_gather(d_out, "tp", axis=0, tiled=True)
    grads_g = times_rows(portion, out_pair)
    grad_wout = across_rows(gated_nat, portion)
    grad_stack = jnp.stack([grads_g[:, :head_dim], grads_g[::-1, head_dim:]])
    direct = pullback((grad_stack, jnp.zeros_like(states_out)))
    direct_state = direct[4]
    fwd_adj = entering((decays[0], direct_state[0]), "ctx", chain_step, identity, True)[1]
    rev_adj = entering((decays[1], direct_state[1]), "ctx", chain_step, identity, False)[1]
    carried_grads = pullback((jnp.zeros_like(gated), jnp.stack([fwd_adj, rev_adj])))
    grad_x = direct[0] + carried_grads[0]
    grad_gates = direct[1] + carried_grads[1]
    grad_bcs = direct[2] + carried_grads[2]
    grad_dts = direct[3] + carried_grads[3]
    grad_x_rev = grad_x[1][::-1]
    grad_x_local = jnp.concatenate([grad_x[0][rim_rows:], grad_x_rev[:seq_rows]], axis=1)
    outgoing = jnp.concatenate([grad_x[0][:rim_rows], grad_x_rev[seq_rows:]], axis=0)
    incoming = padded(outgoing, (("ctx", 0),), rim_rows)
    grad_x_local = grad_x_local.at[:rim_rows, head_dim:].add(incoming[:rim_rows])
    grad_x_local = grad_x_local.at[seq_rows - rim_rows :, :head_dim].add(incoming[3 * rim_rows :])
    grad_proj = jnp.concatenate(
        [
            grad_x_local[:, :head_dim],
            grad_gates[0],
            grad_x_local[:, head_dim:],
            grad_gates[1][::-1],
        ],
        axis=1,
    ).astype(jnp.bfloat16)
    grad_bc = jnp.concatenate([grad_bcs[0], grad_bcs[1][::-1]], axis=1).astype(jnp.bfloat16)
    grad_dt = jnp.stack([grad_dts[0], grad_dts[1][::-1]], axis=1).astype(jnp.bfloat16)

    def strand_term(which):
        proj_cols = grad_proj[:, which * 2 * head_dim : (which + 1) * 2 * head_dim]
        wide_cols = w_pair[:, which * 2 * head_dim : (which + 1) * 2 * head_dim]
        bc_cols = grad_bc[:, which * 2 * STATE : (which + 1) * 2 * STATE]
        shared_cols = bc_pair[:, which * 2 * STATE : (which + 1) * 2 * STATE]
        dt_cols = grad_dt[:, which : which + 1]
        dt_rows = dt_pair[which : which + 1]
        summed = times_rows(proj_cols, wide_cols) + times_rows(bc_cols, shared_cols)
        return summed + jnp.dot(dt_cols, dt_rows, preferred_element_type=jnp.float32)

    forward_part = lax.psum_scatter(strand_term(0), "tp", scatter_dimension=0, tiled=True)
    reverse_part = lax.psum_scatter(strand_term(1), "tp", scatter_dimension=0, tiled=True)
    d_hidden = (forward_part + reverse_part).astype(jnp.bfloat16)
    scaling = 1.0 / math.sqrt(length_all)
    grad_pair = across_rows(gathered, grad_proj)
    d_w_in = (grad_pair[:, : 2 * head_dim] + grad_pair[::-1, 2 * head_dim :]) * scaling
    d_w_out = (grad_wout[:head_dim] + grad_wout[head_dim:, ::-1]) * scaling
    d_w_in, d_w_out = (
        lax.psum(d_w_in.astype(jnp.bfloat16), "ctx").astype(jnp.float32),
        lax.psum(d_w_out.astype(jnp.bfloat16), "ctx").astype(jnp.float32),
    )
    grad_bpair = across_rows(gathered, grad_bc)
    d_w_bc = lax.psum(
        (grad_bpair[:, : 2 * STATE] + grad_bpair[::-1, 2 * STATE :]) * scaling, ("ctx", "tp")
    )
    return (d_hidden, d_w_in, d_w_out, d_w_bc)


def solution(mesh):
    in_specs = (
        P(("ctx", "tp"), None),
        P(None, "tp"),
        P(),
        P("tp", None),
        P("tp"),
        P("tp"),
        P("tp"),
        P(None, "tp"),
        P("tp", None),
        P(("ctx", "tp"), None),
    )
    out_specs = (P(("ctx", "tp"), None), P(None, "tp"), P("tp", None), P())
    return jax.shard_map(local, mesh=mesh, in_specs=in_specs, out_specs=out_specs, check_vma=False)
```

profile of v0, /device:TPU:0, one launch (start us, length us, event | category | flops | bytes accessed | tf_op | source)
XLA Modules:
  0.0 427.6 jit_solution(6540800176572279359)
XLA Ops:
  8.7 6.0 %rev.53 = bf16[1,2048]{1,0:T(2,128)(2,1)S(1)} reverse(bf16[1,2048]{1,0:T(2,128)(2,1)} %param.25), dimensions={1} | reverse | bytes 8192 | tf_op jit(solution)/shard_map/rev | solution.py:119
  21.5 6.3 %rev.55 = bf16[2048,32]{0,1:T(8,128)(2,1)S(1)} reverse(bf16[2048,32]{0,1:T(8,128)(2,1)} %param.24), dimensions={0} | reverse | bytes 262144 | tf_op jit(solution)/shard_map/rev | solution.py:118
  27.9 6.6 %rev.49 = bf16[64,2048]{1,0:T(8,128)(2,1)S(1)} reverse(bf16[64,2048]{1,0:T(8,128)(2,1)} %param.30), dimensions={1} | reverse | bytes 524288 | tf_op jit(solution)/shard_map/rev | solution.py:120
  34.4 6.3 %rev.51 = bf16[2048,128]{1,0:T(8,128)(2,1)S(1)} reverse(bf16[2048,128]{1,0:T(8,128)(2,1)} %param.23), dimensions={0} | reverse | bytes 1048576 | tf_op jit(solution)/shard_map/rev | solution.py:117
  41.5 9.5 %all-gather.5.cloned.1.call-done = bf16[256,2048]{1,0:T(8,128)(2,1)} async-done(((bf16[16,2048]{1,0:T(8,128)(2,1)}), bf16[256,2048]{1,0:T(8,128)(2,1)}) %all-gather.5.cloned.1.call-update) | async-done | bytes 1048592 | tf_op jit(solution)/shard_map/all_gather | solution.py:122
  57.4 32.6 %all-gather.3.cloned.1.call-done = bf16[256,2048]{1,0:T(8,128)(2,1)} async-done(((bf16[16,2048]{1,0:T(8,128)(2,1)}), bf16[256,2048]{1,0:T(8,128)(2,1)}) %all-gather.3.cloned.1.call-update) | async-done | bytes 1048592 | tf_op jit(solution)/shard_map/all_gather | solution.py:153
  90.0 1.7 convolution_bitcast_fusion.2
  92.7 3.4 collective-permute-start
  97.7 5.0 %all_gather.29 = f32[2,64,16]{1,2,0:T(8,128)S(1)} all-gather(f32[1,64,16]{1,2,0:T(8,128)S(1)} %get-tuple-element.678), channel_id=1, replica_groups=mesh['ctx'=2,'tp'=16] {'ctx'}, dimensions={0}, use_global_device_ids=true | all-gather | bytes 12288 | tf_op jit(solution)/shard_map/all_gather | solution.py:30
  102.7 4.9 %all-reduce.18 = (f32[2]{0:T(128)S(1)}, f32[2]{0:T(128)S(1)}) all-reduce(f32[2]{0:T(128)S(1)} %slice_dynamic-update-slice_fusion, f32[2]{0:T(128)S(1)} %slice_dynamic-update-slice_fusion.1), channel_id=1, replica_groups=mesh['ctx'=2,'tp'=16] {'ctx'}, use_global_device_ids=true, to_apply=%add.17 | all-reduce | flops 4 | bytes 32
  107.6 2.8 while.62
  110.4 4.4 %all_gather.31 = f32[2,64,16]{1,2,0:T(8,128)S(1)} all-gather(f32[1,64,16]{1,2,0:T(8,128)S(1)} %get-tuple-element.679), channel_id=1, replica_groups=mesh['ctx'=2,'tp'=16] {'ctx'}, dimensions={0}, use_global_device_ids=true | all-gather | bytes 12288 | tf_op jit(solution)/shard_map/all_gather | solution.py:30
  114.7 2.8 while.63
  119.6 4.4 %all_gather.32 = f32[2,64,16]{1,2,0:T(8,128)S(1)} all-gather(f32[1,64,16]{1,2,0:T(8,128)S(1)} %get-tuple-element.676), channel_id=1, replica_groups=mesh['ctx'=2,'tp'=16] {'ctx'}, dimensions={0}, use_global_device_ids=true | all-gather | bytes 12288 | tf_op jit(solution)/shard_map/all_gather | solution.py:30
  124.0 2.5 while.64
  126.5 4.5 %all_gather.33 = f32[2,64,16]{1,2,0:T(8,128)S(1)} all-gather(f32[1,64,16]{1,2,0:T(8,128)S(1)} %get-tuple-element.677), channel_id=1, replica_groups=mesh['ctx'=2,'tp'=16] {'ctx'}, dimensions={0}, use_global_device_ids=true | all-gather | bytes 12288 | tf_op jit(solution)/shard_map/all_gather | solution.py:30
  131.1 2.6 while.65
  142.6 1.8 multiply_reduce_fusion.3
  145.1 2.5 reduce-window.24
  147.9 2.5 reduce-window.26
  155.0 1.8 fusion.188
  162.9 3.9 collective-permute-start.2
  168.4 1.9 add_select_fusion
  170.3 2.0 scatter-add.6
  178.4 9.4 %rev.61 = f32[2048,128]{0,1:T(8,128)} reverse(f32[2048,128]{0,1:T(8,128)} %slice.386), dimensions={0} | reverse | bytes 2097152 | tf_op jit(solution)/shard_map/rev | solution.py:199
  187.8 2.5 fusion.10
  192.5 1.9 fusion.6
  196.8 27.7 %all-reduce.25.cloned.1.call-done = (bf16[2048,128]{0,1:T(8,128)(2,1)}, bf16[64,2048]{1,0:T(8,128)(2,1)}) async-done(((bf16[2048,128]{0,1:T(8,128)(2,1)}, bf16[64,2048]{1,0:T(8,128)(2,1)}), (bf16[2048,128]{0,1:T(8,128)(2,1)}, bf16[64,2048]{1,0:T(8,128)(2,1)})) %all-reduce.25.cloned.1.call-update) | async-done | bytes 786448 | tf_op jit(solution)/shard_map/psum | solution.py:202
  224.5 2.2 copy.41
  226.7 1.8 convert_element_type.39
  228.4 61.6 %reduce-scatter.2.cloned.1.call-done = f32[16,2048]{1,0:T(8,128)} async-done(((f32[256,2048]{1,0:T(8,128)}), f32[16,2048]{1,0:T(8,128)}) %reduce-scatter.2.cloned.1.call-update) | async-done | bytes 131088 | tf_op jit(solution)/shard_map/reduce_scatter | solution.py:194
  291.6 127.8 %all-reduce.23.cloned.1.call-done = f32[2048,32]{0,1:T(8,128)} async-done(((f32[2048,32]{0,1:T(8,128)}), f32[2048,32]{0,1:T(8,128)}) %all-reduce.23.cloned.1.call-update) | async-done | bytes 262160 | tf_op jit(solution)/shard_map/psum | solution.py:206
  (213 shorter events, 64.0 us)
Async XLA Ops:
  7.2 33.6 %copy-start.28 = (u32[32]{0:T(128)S(1)}, u32[32]{0:T(128)}, u32[]{:S(2)}) copy-start(u32[32]{0:T(128)} %constant.245) | copy-start | bytes 388
  7.2 43.8 %copy-start.16 = (bf16[1,2048]{1,0:T(2,128)(2,1)S(1)}, bf16[1,2048]{1,0:T(2,128)(2,1)}, u32[]{:S(2)}) copy-start(bf16[1,2048]{1,0:T(2,128)(2,1)} %param.25) | copy-start | bytes 12292
  7.2 46.6 %copy-start.4 = (bf16[2048,32]{0,1:T(8,128)(2,1)S(1)}, bf16[2048,32]{0,1:T(8,128)(2,1)}, u32[]{:S(2)}) copy-start(bf16[2048,32]{0,1:T(8,128)(2,1)} %param.24) | copy-start | bytes 393220
  7.2 43.7 %all-gather.5.cloned.1.call-start = ((), (), s32[]{:S(2)}) async-start(), calls=%async_computation.2 | async-start | bytes 1114112 | tf_op jit(solution)/shard_map/all_gather | solution.py:122
  7.9 82.1 %all-gather.3.cloned.1.call-start = ((), (), s32[]{:S(2)}) async-start(), calls=%async_computation.1 | async-start | bytes 1114112 | tf_op jit(solution)/shard_map/all_gather | solution.py:153
  8.7 215.8 %all-reduce.25.cloned.1.call-start = ((), (), s32[]{:S(2)}) async-start(), calls=%async_computation.5 | async-start | bytes 1572864 | tf_op jit(solution)/shard_map/psum | solution.py:202
  16.1 138.0 %copy-start.17 = (pred[256,256]{1,0:T(8,128)(4,1)}, pred[256,256]{1,0:T(8,128)(4,1)S(1)}, u32[]{:S(2)}) copy-start(pred[256,256]{1,0:T(8,128)(4,1)S(1)} %iota_compare_fusion) | copy-start | bytes 196612
  27.9 62.1 %copy-start.6 = (bf16[64,2048]{1,0:T(8,128)(2,1)S(1)}, bf16[64,2048]{1,0:T(8,128)(2,1)}, u32[]{:S(2)}) copy-start(bf16[64,2048]{1,0:T(8,128)(2,1)} %param.30) | copy-start | bytes 786436
  40.7 51.2 %copy-start.3 = (bf16[2048,128]{1,0:T(8,128)(2,1)}, bf16[2048,128]{1,0:T(8,128)(2,1)S(1)}, u32[]{:S(2)}) copy-start(bf16[2048,128]{1,0:T(8,128)(2,1)S(1)} %rev.51) | copy-start | bytes 1572868
  52.5 39.4 %copy-start = (bf16[256,2048]{1,0:T(8,128)(2,1)S(1)}, bf16[256,2048]{1,0:T(8,128)(2,1)}, u32[]{:S(2)}) copy-start(bf16[256,2048]{1,0:T(8,128)(2,1)} %all-gather.5.cloned.1.call-done) | copy-start | bytes 3145732
  52.5 39.4 %copy-start.2 = (bf16[2048,128]{1,0:T(8,128)(2,1)S(1)}, bf16[2048,128]{1,0:T(8,128)(2,1)}, u32[]{:S(2)}) copy-start(bf16[2048,128]{1,0:T(8,128)(2,1)} %param.23) | copy-start | bytes 1572868
  53.8 100.2 %copy-start.24 = (f32[1,2,2,128]{3,1,2,0:T(2,128)}, f32[1,2,2,128]{3,1,2,0:T(2,128)S(1)}, u32[]{:S(2)}) copy-start(f32[1,2,2,128]{3,1,2,0:T(2,128)S(1)} %copy.67) | copy-start | bytes 6148
  57.4 97.3 %copy-start.21 = (f32[2,256]{1,0:T(2,128)}, f32[2,256]{1,0:T(2,128)S(1)}, u32[]{:S(2)}) copy-start(f32[2,256]{1,0:T(2,128)S(1)} %fusion.187) | copy-start | bytes 6148
  92.4 50.2 %copy-start.13 = (bf16[1,256,64]{1,2,0:T(8,128)(2,1)}, bf16[1,256,64]{1,2,0:T(8,128)(2,1)S(1)}, u32[]{:S(2)}) copy-start(bf16[1,256,64]{1,2,0:T(8,128)(2,1)S(1)} %get-tuple-element.658) | copy-start | bytes 98308
  92.6 50.0 %copy-start.7 = (bf16[256,64]{0,1:T(8,128)(2,1)}, bf16[256,64]{0,1:T(8,128)(2,1)S(1)}, u32[]{:S(2)}) copy-start(bf16[256,64]{0,1:T(8,128)(2,1)S(1)} %rev.52) | copy-start | bytes 98308
  92.7 24.8 %collective-permute-start = (bf16[3,128]{0,1:T(8,128)(2,1)S(1)}, bf16[3,128]{0,1:T(8,128)(2,1)S(1)}, u32[]{:S(2)}, u32[]{:S(2)}) collective-permute-start(bf16[3,128]{0,1:T(8,128)(2,1)S(1)} %get-tuple-element.670), channel_id=1, source_target_pairs={{0,16},{1,17},{2,18},{3,19},{4,20},{5,21},{6,22},{7,23},{8,24},{9,... | collective-permute-start | bytes 2312 | tf_op jit(solution)/shard_map/ppermute | solution.py:22
  96.1 21.4 %collective-permute-start.1 = (bf16[3,128]{0,1:T(8,128)(2,1)S(1)}, bf16[3,128]{0,1:T(8,128)(2,1)S(1)}, u32[]{:S(2)}, u32[]{:S(2)}) collective-permute-start(bf16[3,128]{0,1:T(8,128)(2,1)S(1)} %get-tuple-element.671), channel_id=1, source_target_pairs={{16,0},{17,1},{18,2},{19,3},{20,4},{21,5},{22,6},{23,7},{24,8},{25... | collective-permute-start | bytes 2312 | tf_op jit(solution)/shard_map/ppermute | solution.py:23
  117.5 25.1 %copy-start.22 = (f32[2,256]{1,0:T(2,128)}, f32[2,256]{1,0:T(2,128)S(1)}, u32[]{:S(2)}) copy-start(f32[2,256]{1,0:T(2,128)S(1)} %compare_select_fusion.3) | copy-start | bytes 6148
  134.1 8.6 %copy-start.11 = (f32[2,256,64]{1,2,0:T(8,128)}, f32[2,256,64]{1,2,0:T(8,128)S(1)}, u32[]{:S(2)}) copy-start(f32[2,256,64]{1,2,0:T(8,128)S(1)} %fusion.153) | copy-start | bytes 393220
  152.1 2.8 copy-start.29
  154.6 2.9 copy-start.9
  154.7 2.9 copy-start.15
  154.7 2.9 copy-start.26
  154.7 2.9 copy-start.30
  154.9 2.9 copy-start.20
  154.9 3.1 copy-start.27
  155.0 3.4 copy-start.5
  159.4 3.3 copy-start.10
  162.9 5.5 %collective-permute-start.2 = (f32[3,64]{0,1:T(8,128)S(1)}, f32[3,64]{0,1:T(8,128)S(1)}, u32[]{:S(2)}, u32[]{:S(2)}) collective-permute-start(f32[3,64]{0,1:T(8,128)S(1)} %slice.317), channel_id=1, source_target_pairs={{0,16},{1,17},{2,18},{3,19},{4,20},{5,21},{6,22},{7,23},{8,24},{9,... | collective-permute-start | bytes 2312 | tf_op jit(solution)/shard_map/ppermute | solution.py:22
  166.8 6.0 %collective-permute-start.3 = (f32[3,64]{0,1:T(8,128)}, f32[3,64]{0,1:T(8,128)S(1)}, u32[]{:S(2)}, u32[]{:S(2)}) collective-permute-start(f32[3,64]{0,1:T(8,128)} %get-tuple-element.638), channel_id=1, source_target_pairs={{16,0},{17,1},{18,2},{19,3},{20,4},{21,5},{22,6},{23,7},{24,8},{25... | collective-permute-start | bytes 2312 | tf_op jit(solution)/shard_map/ppermute | solution.py:23
  190.3 99.8 %reduce-scatter.2.cloned.1.call-start = ((), (), s32[]{:S(2)}) async-start(), calls=%async_computation.4 | async-start | bytes 2228224 | tf_op jit(solution)/shard_map/reduce_scatter | solution.py:194
  194.4 225.0 %all-reduce.23.cloned.1.call-start = ((), (), s32[]{:S(2)}) async-start(), calls=%async_computation.3 | async-start | bytes 524288 | tf_op jit(solution)/shard_map/psum | solution.py:206
  (8 other events, 15.5 us)
Sparse Core Ops, SparseCore 0:
  10.2 40.6 all-gather.4
  53.1 36.8 all-gather.2
  190.4 34.0 all-reduce.24
  228.5 61.5 reduce-scatter.1
  295.4 123.9 all-reduce.22
where the time goes:
time: 431 us; the launch traced here: 428 us
  waiting for transfers between devices  261 us (61%)
  local copies, waits for them, and re-layouts  61 us (14%)
  other arithmetic  28.3 us (7%)
  matrix products  26.8 us (6%)
  blocking collectives  23.2 us (5%)
  between operations  16.6 us (4%)
  starting transfers between devices  10.3 us (2%)
    psum x1, waiting for transfers between devices, local(): lax.psum((grad_bpair[:, :2 * STATE] + grad_bpair[::-1, 2 * STATE:]) * sca...  128 us
    reduce_scatter x1, waiting for transfers between devices, local(): lax.psum_scatter(strand_term(0), 'tp', scatter_dimension=0, tiled=True)  61.6 us
    all_gather x1, waiting for transfers between devices, local(): portion = lax.all_gather(d_out, 'tp', axis=0, tiled=True)  32.6 us
    psum x1, waiting for transfers between devices, local(): lax.psum(d_w_in.astype(jnp.bfloat16), 'ctx').astype(jnp.float32)  27.7 us
    all_gather x4, blocking collectives, entering(): everything = jax.tree.map(lambda part: lax.all_gather(part, axis), array)  18.2 us
    another operation x14, other arithmetic  12 us
    all_gather x1, waiting for transfers between devices, local(): gathered = lax.all_gather(hidden, 'tp', axis=0, tiled=True)  9.48 us
    rev x1, local copies, waits for them, and re-layouts, local(): grad_pair[::-1, 2 * head_dim:]  9.41 us
  transfers between devices with their start and end apart: 9, of which 6 were waited for; matrix products, arithmetic and copies ran while one was open for 14% of the time, Pallas kernels for 0%

commit v1 on v0

v1 whole, which is shorter than its diff:
```python
import functools
import math

import jax
import jax.numpy as jnp
from jax import lax
from jax.experimental import pallas as pl
from jax.experimental.pallas import tpu as pltpu
from jax.sharding import PartitionSpec as P

STATE = 16
CONV = 4
LANES = 128
BLOCK = 256
TILE_ROWS = 16
VMEM_LIMIT = 60 * 1024 * 1024
f32 = jnp.float32
bf16 = jnp.bfloat16


def dot(a, b):
    return jnp.dot(a, b, preferred_element_type=f32)


def dot_nt(a, b):
    return lax.dot_general(a, b, (((1,), (1,)), ((), ())), preferred_element_type=f32)


def dot_tn(a, b):
    return lax.dot_general(a, b, (((0,), (0,)), ((), ())), preferred_element_type=f32)


def iota(shape, dim):
    return lax.broadcasted_iota(jnp.int32, shape, dim)


def mirror(size):
    return jnp.where(iota((size, size), 0) + iota((size, size), 1) == size - 1, 1.0, 0.0).astype(
        bf16
    )


def split(value, terms):
    parts = []
    for _ in range(terms):
        part = value.astype(bf16)
        parts.append(part)
        value = value - part.astype(f32)
    return parts


def flip_rows(value, flip):
    count = value.shape[0] // BLOCK
    return jnp.concatenate(
        [dot(flip, value[(count - 1 - i) * BLOCK : (count - i) * BLOCK]) for i in range(count)],
        axis=0,
    )


def assemble(ids_ref, pieces, h_ref, d_ref, layout):
    tp_size, own_rows, coords = layout
    nz = tp_size // 4
    z, x, core, ctx = (ids_ref[i] for i in range(4))
    ctx_size = max(c[0] for c in coords) + 1
    for piece, (dc, dx, dcore) in zip(pieces, coords):
        from_ctx = lax.rem(ctx + dc, ctx_size)
        for j in range(nz):
            owner = ((z ^ j) * 2 + (x ^ dx)) * 2 + (core ^ dcore)
            at = pl.multiple_of((from_ctx * tp_size + owner) * own_rows, own_rows)
            base = 2 * j * own_rows
            if h_ref is not None:
                h_ref[pl.ds(at, own_rows), :] = piece[base : base + own_rows, :]
            if d_ref is not None:
                d_ref[pl.ds(at, own_rows), :] = piece[base + own_rows : base + 2 * own_rows, :]


def prep_kernel(wcat_ref, wrev_ref):
    flip = mirror(BLOCK)
    count = wcat_ref.shape[0] // BLOCK
    for i in range(count):
        wrev_ref[i * BLOCK : (i + 1) * BLOCK, :] = dot(
            flip, wcat_ref[(count - 1 - i) * BLOCK : (count - i) * BLOCK, :]
        ).astype(bf16)


def own_source(shape, dim, ids_ref, tp_size, own_rows):
    z, x, core, ctx = (ids_ref[i] for i in range(4))
    nz = tp_size // 4
    row = iota(shape, dim)
    block = row // own_rows
    j = block % nz
    dx = 1 - (block // nz) % 2
    dcore = 1 - block // (2 * nz)
    owner = ((z ^ j) * 2 + (x ^ dx)) * 2 + (core ^ dcore)
    return (ctx * tp_size + owner) * own_rows + row % own_rows


def core_kernel(n_pieces, layout, *refs):
    ids_ref, par_ref = refs[:2]
    pieces = refs[2 : 2 + n_pieces]
    wcat_ref, wrev_ref, wout_ref, cw_ref = refs[2 + n_pieces : 6 + n_pieces]
    send_ref, keep_ref, gcat_ref, gated_ref = refs[6 + n_pieces : 10 + n_pieces]
    tp_size, own_rows, coords = layout
    if coords is None:
        h_ref, d_ref = pieces
    else:
        h_ref, d_ref = refs[10 + n_pieces :]
        assemble(ids_ref, pieces, h_ref, d_ref, layout)
    length, width = h_ref.shape
    chunks = length // BLOCK
    columns = width // BLOCK
    flip = mirror(BLOCK)
    bias, rate, skip = par_ref[0], par_ref[1], par_ref[2]
    lane = iota((1, LANES), 1)
    low = lane < LANES // 2
    tri = jnp.where(iota((BLOCK, BLOCK), 0) >= iota((BLOCK, BLOCK), 1), 1.0, 0.0).astype(bf16)
    causal = iota((BLOCK, BLOCK), 0) >= iota((BLOCK, BLOCK), 1)
    row_at = iota((length, LANES), 0)

    proj_f = dot(h_ref[...], wcat_ref[...])
    grad_f = dot_nt(d_ref[...], wout_ref[...])
    proj_r = jnp.zeros_like(proj_f)
    grad_r = jnp.zeros_like(grad_f)
    for i in range(columns):
        cols = slice(i * BLOCK, (i + 1) * BLOCK)
        back = slice((columns - 1 - i) * BLOCK, (columns - i) * BLOCK)
        proj_r += dot(h_ref[:, cols], wrev_ref[cols, :])
        turned = dot(wout_ref[:, back], flip).astype(bf16)
        grad_r += dot_nt(d_ref[:, cols], turned)
    xz_r = flip_rows(proj_r[:, :LANES].astype(bf16), flip)
    rest_r = sum(flip_rows(part, flip) for part in split(proj_r[:, LANES:], 3))
    grad_r = sum(flip_rows(part, flip) for part in split(grad_r, 2))
    strands = (
        (proj_f[:, :LANES].astype(bf16).astype(f32), proj_f[:, LANES:], grad_f),
        (xz_r, rest_r, grad_r),
    )
    small = []
    for which, (xz, rest, grad_g) in enumerate(strands):
        pre = cw_ref[CONV - 1 : CONV, :] * xz
        for shift in range(1, CONV):
            moved = jnp.where(row_at >= shift, pltpu.roll(xz, shift, 0), 0.0)
            pre += cw_ref[CONV - 1 - shift : CONV - shift, :] * moved
        sig = jax.nn.sigmoid(pre)
        u = pre * sig
        slope = sig * (1.0 + pre * (1.0 - sig))
        u_other = pltpu.roll(u, LANES // 2, 1)
        raw = jnp.broadcast_to(rest[:, 2 * STATE : 2 * STATE + 1], (length, LANES)) + bias
        dt = jnp.maximum(raw, 0.0) + jnp.log1p(jnp.exp(-jnp.abs(raw)))
        dt_slope = jax.nn.sigmoid(raw)
        b_all = jnp.where(lane < STATE, rest, 0.0)
        c_all = jnp.where(lane < STATE, pltpu.roll(rest, LANES - STATE, 1), 0.0)
        w_all = dt * u
        g_y = jnp.where(low, grad_g * u_other, 0.0)
        saved = []
        state = jnp.zeros((LANES, LANES), f32)
        outs = []
        for c in range(chunks):
            rows = slice(c * BLOCK, (c + 1) * BLOCK)
            log_keep = sum(dot(tri, part) for part in split(dt[rows] * rate, 3))
            across = jnp.transpose(log_keep)[0:1, :]
            gap = jnp.concatenate([log_keep] * (BLOCK // LANES), axis=1) - across
            decay = jnp.exp(jnp.where(causal, gap, -jnp.inf))
            b_rows, c_rows = b_all[rows], c_all[rows]
            b_low, c_low = b_rows.astype(bf16), c_rows.astype(bf16)
            mixed = (dot_nt(c_low, b_low) * decay).astype(bf16)
            w_low = w_all[rows].astype(bf16)
            last = log_keep[BLOCK - 1 : BLOCK, :]
            enter = jnp.exp(log_keep)
            leave = jnp.exp(last - log_keep)
            total = jnp.exp(last)
            b_left = (leave * b_rows).astype(bf16)
            out = dot(mixed, w_low) + enter * dot(c_low, state.astype(bf16))
            saved.append((decay, mixed, b_low, c_low, w_low, b_left, enter, leave, total, state))
            state = total * state + dot_tn(b_left, w_low)
            saved[-1] += (state,)
            outs.append(out)
        y = jnp.concatenate(outs, axis=0) + skip * u
        gated = jnp.where(low, y * u_other, 0.0).astype(bf16)
        g_gate = jnp.where(low, grad_g * y, 0.0)
        d_state = jnp.zeros((LANES, LANES), f32)
        d_w, g_b, g_c, g_a = [None] * chunks, [None] * chunks, [None] * chunks, [None] * chunks
        for c in reversed(range(chunks)):
            rows = slice(c * BLOCK, (c + 1) * BLOCK)
            decay, mixed, b_low, c_low, w_low, b_left, enter, leave, total, state, after = saved[c]
            gy = g_y[rows]
            gy_low = gy.astype(bf16)
            ds_low = d_state.astype(bf16)
            dw = dot_tn(mixed, gy_low) + dot(b_left, ds_low)
            d_scores = (dot_nt(gy_low, w_low) * decay).astype(bf16)
            g_c[c] = dot(d_scores, b_low) + enter * dot_nt(gy_low, state.astype(bf16))
            g_b[c] = dot_tn(d_scores, c_low) + leave * dot_nt(w_low, ds_low)
            d_log = jnp.sum(
                jnp.where(low, gy * outs[c] - w_all[rows] * dw, 0.0), axis=1, keepdims=True
            )
            at_end = jnp.sum(jnp.where(low, after * d_state, 0.0))
            d_log = jnp.broadcast_to(d_log, (BLOCK, LANES))
            d_sum = sum(dot_tn(tri, part) for part in split(d_log, 2)) + at_end
            d_dt = rate * d_sum + jnp.sum(
                jnp.where(low, u[rows] * dw, 0.0), axis=1, keepdims=True
            )
            g_a[c] = d_dt
            d_w[c] = dw
            carried = (enter * c_all[rows]).astype(bf16)
            d_state = total * d_state + dot_tn(carried, gy_low)
        d_w = jnp.concatenate(d_w, axis=0)
        g_b = jnp.concatenate(g_b, axis=0)
        g_c = jnp.concatenate(g_c, axis=0)
        g_raw = jnp.concatenate(g_a, axis=0) * dt_slope
        d_u = jnp.where(low, skip * g_y + dt * d_w, pltpu.roll(g_gate, LANES // 2, 1))
        d_pre = d_u * slope
        g_xz = cw_ref[CONV - 1 : CONV, :] * d_pre
        for shift in range(1, CONV):
            moved = jnp.where(
                row_at < length - shift, pltpu.roll(d_pre, length - shift, 0), 0.0
            )
            g_xz += cw_ref[CONV - 1 - shift : CONV - shift, :] * moved
        shared = jnp.where(lane < STATE, g_b, 0.0) + jnp.where(
            (lane >= STATE) & (lane < 2 * STATE), pltpu.roll(g_c, STATE, 1), 0.0
        )
        g_rest = shared + jnp.where(lane == 2 * STATE, g_raw, 0.0)
        g_cat = jnp.concatenate([g_xz, g_rest], axis=1).astype(bf16)
        small.append(shared)
        if which == 0:
            gcat_ref[:, 0 : 2 * LANES] = g_cat
            gated_ref[:, 0:LANES] = gated
        else:
            gcat_ref[:, 2 * LANES :] = flip_rows(g_cat, flip).astype(bf16)
            gated_ref[:, LANES:] = flip_rows(gated, flip).astype(bf16)

    pair = small[0] + pltpu.roll(small[1], 2 * STATE, 1)
    shared_t = jnp.transpose(pair)[: 4 * STATE].astype(bf16)
    groups = width // length
    step = 4 * STATE // groups
    for i in range(groups):
        part = shared_t[i * step : (i + 1) * step, :]
        send_ref[0:step, i * length : (i + 1) * length] = part
        keep_ref[0:step, i * length : (i + 1) * length] = part.astype(f32)
    own = tp_size * own_rows
    source = own_source((own, length), 0, ids_ref, tp_size, own_rows)
    pick = jnp.where(source == iota((own, length), 1), 1.0, 0.0).astype(bf16)
    picked = dot(pick, gcat_ref[...]).astype(bf16)
    half = own // 2
    for i in range(columns):
        cols = slice(i * BLOCK, (i + 1) * BLOCK)
        part = dot_nt(picked[:, : 2 * LANES], wcat_ref[cols, :]) + dot_nt(
            picked[:, 2 * LANES :], wrev_ref[cols, :]
        )
        send_ref[step:, cols] = part[:half].astype(bf16)
        keep_ref[step:, cols] = part[half:]


def weight_kernel(n_pieces, layout, scaling, *refs):
    ids_ref = refs[0]
    pieces = refs[1 : 1 + n_pieces]
    gcat_ref, gated_ref, dwin_ref, dwout_ref = refs[1 + n_pieces : 5 + n_pieces]
    if layout[2] is None:
        h_ref, d_ref = pieces
    else:
        h_ref, d_ref = refs[5 + n_pieces :]
        assemble(ids_ref, pieces, h_ref, d_ref, layout)
    flip = mirror(BLOCK)
    columns = h_ref.shape[1] // BLOCK
    head = dwout_ref.shape[0]
    g_f = gcat_ref[:, 0:LANES]
    g_r = gcat_ref[:, 2 * LANES : 3 * LANES]
    y_f = gated_ref[:, 0:LANES]
    y_r = gated_ref[:, LANES:]
    for i in range(columns):
        cols = slice(i * BLOCK, (i + 1) * BLOCK)
        back = slice((columns - 1 - i) * BLOCK, (columns - i) * BLOCK)
        turned = dot(h_ref[:, back], flip).astype(bf16)
        grad = dot_tn(g_f, h_ref[:, cols]) + dot_tn(g_r, turned)
        dwin_ref[cols, :] = jnp.transpose(grad * scaling)
        turned = dot(d_ref[:, back], flip).astype(bf16)
        grad = dot_tn(y_f, d_ref[:, cols]) + dot_tn(y_r, turned)
        dwout_ref[:, cols] = grad[:head] * scaling


def last_kernel(n_pieces, layout, scaling, *refs):
    ids_ref, shared_ref = refs[:2]
    pieces = refs[2 : 2 + n_pieces]
    dwbc_ref = refs[2 + n_pieces]
    if layout[2] is None:
        h_ref = pieces[0]
    else:
        h_ref = refs[3 + n_pieces]
        assemble(ids_ref, pieces, h_ref, None, layout)
    flip = mirror(BLOCK)
    length, width = h_ref.shape
    columns = width // BLOCK
    groups = width // length
    shared = jnp.concatenate(
        [shared_ref[:, i * length : (i + 1) * length] for i in range(groups)], axis=0
    ).astype(bf16)
    fwd = shared[: 2 * STATE]
    rev = shared[2 * STATE :]
    count = length // BLOCK
    rev = jnp.concatenate(
        [
            dot(rev[:, (count - 1 - i) * BLOCK : (count - i) * BLOCK], flip).astype(bf16)
            for i in range(count)
        ],
        axis=1,
    )
    pad = jnp.zeros((LANES - 2 * STATE, length), bf16)
    fwd = jnp.concatenate([fwd, pad], axis=0)
    rev = jnp.concatenate([rev, pad], axis=0)
    for i in range(columns):
        cols = slice(i * BLOCK, (i + 1) * BLOCK)
        back = slice((columns - 1 - i) * BLOCK, (columns - i) * BLOCK)
        turned = dot(h_ref[:, back], flip).astype(bf16)
        grad = (dot(fwd, h_ref[:, cols]) + dot(rev, turned)) * scaling
        dwbc_ref[cols, :] = jnp.transpose(grad)[:, : 2 * STATE]


def spec(memory=pltpu.VMEM):
    return pl.BlockSpec(memory_space=memory)


def call(kernel, inputs, n_smem, outs, scratch, flops, moved):
    return pl.pallas_call(
        kernel,
        out_shape=outs,
        in_specs=[spec(pltpu.SMEM)] * n_smem + [spec()] * (len(inputs) - n_smem),
        out_specs=jax.tree.map(lambda _: spec(), outs),
        scratch_shapes=scratch,
        compiler_params=pltpu.CompilerParams(vmem_limit_bytes=VMEM_LIMIT),
        cost_estimate=pl.CostEstimate(flops=flops, bytes_accessed=moved, transcendentals=0),
    )(*inputs)


def local(ctx_size, tp_size, hidden, w_in, w_bc, w_dt, dt_bias, a_log, d_skip, conv_w, w_out, d_out):
    own_rows, width = hidden.shape
    length = own_rows * tp_size * ctx_size
    head = w_out.shape[0]
    nz = tp_size // 4
    t = lax.axis_index("tp")
    ids = jnp.stack([t >> 2, (t >> 1) & 1, t & 1, lax.axis_index("ctx")]).astype(jnp.int32)
    params = jnp.stack([dt_bias[0], -jnp.exp(a_log[0]), d_skip[0]])
    wcat = jnp.concatenate(
        [w_in, w_bc, w_dt.T, jnp.zeros((width, 2 * LANES - 2 * head - 2 * STATE - 1), bf16)], axis=1
    )
    keep_z = jnp.zeros((CONV, LANES - head), f32).at[CONV - 1].set(1.0)
    taps = jnp.concatenate([conv_w, keep_z], axis=1)
    wout = jnp.concatenate([w_out, jnp.zeros((LANES - head, width), bf16)], axis=0)
    wrev = call(
        prep_kernel,
        [wcat],
        0,
        jax.ShapeDtypeStruct(wcat.shape, bf16),
        [],
        2 * width * BLOCK * BLOCK,
        2 * wcat.size * 2,
    )

    def across(value, flip_bits):
        return lax.ppermute(value, "tp", [(i, i ^ flip_bits) for i in range(tp_size)])

    def along(value, offset):
        return lax.ppermute(
            value, "ctx", [((i + offset) % ctx_size, i) for i in range(ctx_size)]
        )

    def along_x(value, offset):
        pairs = []
        for c in range(ctx_size):
            for i in range(tp_size):
                source = ((c + offset) % ctx_size) * tp_size + (i ^ 2)
                pairs.append((source, c * tp_size + i))
        return lax.ppermute(value, ("ctx", "tp"), pairs)

    if own_rows % TILE_ROWS == 0:
        both = jnp.concatenate([hidden, d_out], axis=0)
        column = jnp.concatenate([both] + [across(both, 4 * j) for j in range(1, nz)], axis=0)
        plane = []
        for dc in range(ctx_size):
            plane.append(((dc, 0), along(column, dc) if dc else column))
            plane.append(((dc, 1), along_x(column, dc) if dc else across(column, 2)))
        coords, pieces = [], []
        for (dc, dx), piece in plane:
            coords += [(dc, dx, 0), (dc, dx, 1)]
            pieces += [piece, across(piece, 1)]
        coords = tuple(coords)
        rows = [pltpu.VMEM((length, width), bf16)]
        h_pieces = pieces
    else:
        pieces = [lax.all_gather(a, ("ctx", "tp"), axis=0, tiled=True) for a in (hidden, d_out)]
        h_pieces = pieces[:1]
        coords, rows = None, []
    layout = (tp_size, own_rows, coords)
    extra = 4 * STATE * length // width
    half = tp_size * own_rows // 2
    send, keep, gcat, gated = call(
        functools.partial(core_kernel, len(pieces), layout),
        [ids, params, *pieces, wcat, wrev, wout, taps],
        2,
        (
            jax.ShapeDtypeStruct((extra + half, width), bf16),
            jax.ShapeDtypeStruct((extra + half, width), f32),
            jax.ShapeDtypeStruct((length, 4 * LANES), bf16),
            jax.ShapeDtypeStruct((length, 2 * LANES), bf16),
        ),
        rows * 2,
        8 * length * width * BLOCK,
        8 * length * width,
    )
    scaling = 1.0 / math.sqrt(length)
    got = across(send, 1)
    d_w_in, d_w_out = call(
        functools.partial(weight_kernel, len(pieces), layout, scaling),
        [ids, *pieces, gcat, gated],
        1,
        (
            jax.ShapeDtypeStruct((width, LANES), f32),
            jax.ShapeDtypeStruct((head, width), f32),
        ),
        rows * 2,
        8 * length * width * BLOCK,
        8 * length * width,
    )
    quarter = half // 2
    summed = keep + got.astype(f32)
    send = summed[: extra + quarter].astype(bf16)
    keep = jnp.concatenate(
        [summed[:extra].astype(bf16).astype(f32), summed[extra + quarter :]], axis=0
    )
    summed = keep + across(send, 2).astype(f32)
    shared = [summed[:extra].astype(bf16)]
    total = summed[extra : extra + own_rows]
    for j in range(1, nz):
        at = extra + j * own_rows
        piece = jnp.concatenate([summed[:extra], summed[at : at + own_rows]], axis=0)
        got = across(piece.astype(bf16), 4 * j)
        shared.append(got[:extra])
        total = total + got[extra:].astype(f32)
    while len(shared) > 1:
        shared = [
            a.astype(f32) + b.astype(f32) for a, b in zip(shared[0::2], shared[1::2])
        ]
    d_w_bc = call(
        functools.partial(last_kernel, len(h_pieces), layout, scaling),
        [ids, shared[0], *h_pieces],
        1,
        jax.ShapeDtypeStruct((width, 2 * STATE), f32),
        rows,
        4 * length * width * BLOCK,
        4 * length * width,
    )
    return (total.astype(bf16), d_w_in, d_w_out, d_w_bc)


def solution(mesh):
    in_specs = (
        P(("ctx", "tp"), None),
        P(None, "tp"),
        P(),
        P("tp", None),
        P("tp"),
        P("tp"),
        P("tp"),
        P(None, "tp"),
        P("tp", None),
        P(("ctx", "tp"), None),
    )
    out_specs = (P(("ctx", "tp"), None), P(None, "tp"), P("tp", None), P())
    body = functools.partial(local, mesh.shape["ctx"], mesh.shape["tp"])
    return jax.shard_map(body, mesh=mesh, in_specs=in_specs, out_specs=out_specs, check_vma=False)
```

time: 431 us -> 102 us (0.24)
  waiting for transfers between devices: 261 us -> 45.1 us
  local copies, waits for them, and re-layouts: 61 us -> 5.65 us
  matrix products: 26.8 us -> 0 us
  Pallas kernels: 0 us -> 26.8 us
  blocking collectives: 23.2 us -> 0 us
  other arithmetic: 28.3 us -> 5.57 us
  between operations: 16.6 us -> 2.82 us
  starting transfers between devices: 10.3 us -> 15.9 us
    psum x2 -> x0, waiting for transfers between devices: 155 us -> none  [the longest x1 128 us: local(): lax.psum((grad_bpair[:, :2 * STATE] + grad_bpair[::-1, 2 * STATE:]) * sca...]
    reduce_scatter x1 -> x0, waiting for transfers between devices: 61.6 us -> none  [local(): lax.psum_scatter(strand_term(0), 'tp', scatter_dimension=0, tiled=True)]
    ppermute x4 -> x15, waiting for transfers between devices: 0.61 us -> 45.1 us  [the longest x13 24.1 us: across(): lax.ppermute(value, 'tp', [(i, i ^ flip_bits) for i in range(tp_size)])]
    all_gather x2 -> x0, waiting for transfers between devices: 42.1 us -> none  [the longest x1 32.6 us: local(): portion = lax.all_gather(d_out, 'tp', axis=0, tiled=True)]
    rev x15 -> x0, local copies, waits for them, and re-layouts: 38.5 us -> none  [the longest x1 9.41 us: local(): grad_pair[::-1, 2 * head_dim:]]
    dot_general x30 -> x0, matrix products: 26.8 us -> none  [the longest x6 8.63 us: times_rows(): lax.dot_general(operand_a, operand_b, (((1,), (1,)), ((), ())), preferred...]
    pallas_call x0 -> x4, Pallas kernels: none -> 26.8 us  [call(): pl.pallas_call(kernel, out_shape=outs, in_specs=[spec(pltpu.SMEM)] * n_sm...]
    all_gather x4 -> x0, blocking collectives: 18.2 us -> none  [entering(): everything = jax.tree.map(lambda part: lax.all_gather(part, axis), array)]
  transfers between devices with their start and end apart: 9 -> 15, of which waited for: 6 -> 8; matrix products, arithmetic and copies ran while one was open for 14% -> 5% of each run, Pallas kernels for 0% -> 9%
where the time goes in v1:
time: 102 us
  waiting for transfers between devices  45.1 us (44%)
  Pallas kernels  26.8 us (26%)
  starting transfers between devices  15.9 us (16%)
  local copies, waits for them, and re-layouts  5.65 us (6%)
  other arithmetic  5.57 us (5%)
  between operations  2.82 us (3%)
    pallas_call x4, Pallas kernels, call(): pl.pallas_call(kernel, out_shape=outs, in_specs=[spec(pltpu.SMEM)] * n_sm...  26.8 us
    ppermute x13, waiting for transfers between devices, across(): lax.ppermute(value, 'tp', [(i, i ^ flip_bits) for i in range(tp_size)])  24.1 us
    ppermute x13, starting transfers between devices, across(): lax.ppermute(value, 'tp', [(i, i ^ flip_bits) for i in range(tp_size)])  12.8 us
    ppermute x1, waiting for transfers between devices, along_x(): return lax.ppermute(value, ('ctx', 'tp'), pairs)  11.6 us
    ppermute x1, waiting for transfers between devices, along(): lax.ppermute(value, 'ctx', [((i + offset) % ctx_size, i) for i in range(c...  9.36 us
    unnamed x23, local copies, waits for them, and re-layouts  3.48 us
    ppermute x1, starting transfers between devices, along_x(): return lax.ppermute(value, ('ctx', 'tp'), pairs)  2.51 us
  transfers between devices with their start and end apart: 15, of which 8 were waited for; matrix products, arithmetic and copies ran while one was open for 5% of the time, Pallas kernels for 9%

profile of v1, /device:TPU:0, one launch (start us, length us, event | category | flops | bytes accessed | tf_op | source)
XLA Modules:
  0.0 101.7 jit_solution(8627605025010694591)
XLA Ops:
  0.7 0.9 constant_dynamic-update-slice_fusion.1
  1.6 0.9 constant_dynamic-update-slice_fusion
  2.4 3.1 %collective-permute-start = (bf16[32,2048]{1,0:T(8,128)(2,1)S(1)}, bf16[32,2048]{1,0:T(8,128)(2,1)S(1)}, u32[]{:S(2)}, u32[]{:S(2)}) collective-permute-start(bf16[32,2048]{1,0:T(8,128)(2,1)S(1)} %get-tuple-element.48), channel_id=1, source_target_pairs={{0,4},{1,5},{2,6},{3,7},{4,0},{5,1},{6,2},{7,3},{8,12},{9,13},{10,... | collective-permute-start | bytes 393224 | tf_op jit(solution)/shard_map/ppermute | solution.py:357
  5.5 2.5 %collective-permute-start.2 = (bf16[32,2048]{1,0:T(8,128)(2,1)S(1)}, bf16[32,2048]{1,0:T(8,128)(2,1)S(1)}, u32[]{:S(2)}, u32[]{:S(2)}) collective-permute-start(bf16[32,2048]{1,0:T(8,128)(2,1)S(1)} %get-tuple-element.48), channel_id=1, source_target_pairs={{0,12},{1,13},{2,14},{3,15},{4,8},{5,9},{6,10},{7,11},{8,4},{9,5},... | collective-permute-start | bytes 393224 | tf_op jit(solution)/shard_map/ppermute | solution.py:357
  8.1 0.9 collective-permute-done
  9.0 10.7 %collective-permute-done.1 = bf16[32,2048]{1,0:T(8,128)(2,1)S(1)} collective-permute-done((bf16[32,2048]{1,0:T(8,128)(2,1)S(1)}, bf16[32,2048]{1,0:T(8,128)(2,1)S(1)}, u32[]{:S(2)}, u32[]{:S(2)}) %collective-permute-start.1) | collective-permute-done | bytes 131104 | tf_op jit(solution)/shard_map/ppermute | solution.py:357
  19.8 2.5 %collective-permute-start.8 = (bf16[128,2048]{1,0:T(8,128)(2,1)S(1)}, bf16[128,2048]{1,0:T(8,128)(2,1)S(1)}, u32[]{:S(2)}, u32[]{:S(2)}) collective-permute-start(bf16[128,2048]{1,0:T(8,128)(2,1)S(1)} %constant_dynamic-update-slice_fusion.2.refs_2_.refs_1_), channel_id=1, source_target_pairs={{18,0},{19,1},{16,2},{17,3},{22,4},{23,5},{20,6},{21,7},{26,8},{27... | collective-permute-start | bytes 1572872 | tf_op jit(solution)/shard_map/ppermute | solution.py:370
  22.3 0.5 collective-permute-start.6
  22.8 0.5 collective-permute-start.4
  23.4 0.3 copy.16
  23.6 0.3 copy.17
  24.1 11.6 %collective-permute-done.8.refs_8_.refs_7_ = bf16[128,2048]{1,0:T(8,128)(2,1)S(1)} collective-permute-done((bf16[128,2048]{1,0:T(8,128)(2,1)S(1)}, bf16[128,2048]{1,0:T(8,128)(2,1)S(1)}, u32[]{:S(2)}, u32[]{:S(2)}) %collective-permute-start.8) | collective-permute-done | bytes 524320 | tf_op jit(solution)/shard_map/ppermute | solution.py:370
  35.7 9.4 %collective-permute-done.6.refs_6_.refs_5_ = bf16[128,2048]{1,0:T(8,128)(2,1)S(1)} collective-permute-done((bf16[128,2048]{1,0:T(8,128)(2,1)S(1)}, bf16[128,2048]{1,0:T(8,128)(2,1)S(1)}, u32[]{:S(2)}, u32[]{:S(2)}) %collective-permute-start.6) | collective-permute-done | bytes 524320 | tf_op jit(solution)/shard_map/ppermute | solution.py:360
  45.2 0.3 collective-permute-start.5
  45.6 1.4 %maximum_maximum_fusion.wcat_ref.refs_10_ = bf16[2048,256]{1,0:T(8,128)(2,1)} fusion(bf16[2048,1]{1,0:T(8,128)(2,1)S(1)} %copy.17, bf16[2048,32]{1,0:T(8,128)(2,1)S(1)} %copy.16, bf16[2048,128]{1,0:T(8,128)(2,1)S(1)} %copy-done.1, bf16[256]{0:T(256)(128)(2,1)S(1)} %pad.16.clone), kind=kLoop, calls=%fused_computation.1 | loop fusion | flops 4194304 | bytes 1708544 | tf_op jit(solution)/shard_map/concatenate | solution.py:340
  48.9 0.8 concatenate.36.refs_12_
  49.8 2.7 %shard_map.129.refs_11_ = bf16[2048,256]{1,0:T(8,128)(2,1)} custom-call(bf16[2048,256]{1,0:T(8,128)(2,1)} %maximum_maximum_fusion.wcat_ref.refs_10_), custom_call_target="tpu_custom_call" | custom-call | flops 268435456 | bytes 2097152 | tf_op jit(solution)/shard_map/pallas_call | solution.py:321
  52.4 0.6 pad_maximum_fusion.4.refs_1_
  53.0 0.7 pad_add_fusion.refs_0_
  53.7 0.7 pad_maximum_fusion.3.refs_13_
  54.4 12.9 %shard_map.130 = (bf16[144,2048]{1,0:T(8,128)(2,1)}, f32[144,2048]{1,0:T(8,128)}, bf16[512,512]{1,0:T(8,128)(2,1)}, bf16[512,256]{1,0:T(8,128)(2,1)}) custom-call(s32[4]{0:T(128)} %pad_add_fusion.refs_0_, f32[3]{0:T(128)} %pad_maximum_fusion.4.refs_1_, bf16[128,2048]{1,0:T(8,128)(2,1)} %copy-done, bf16[128,2048]{1,0:T(8,128)(2,1)} %collective-permute-done.3.refs_3_.refs_2_, ...), custom_call_target="tpu_custom_call" | custom-call | flops 2147483648 | bytes 8388608 | tf_op jit(solution)/shard_map/pallas_call | solution.py:321
  67.5 2.0 %collective-permute-done.10 = bf16[144,2048]{1,0:T(8,128)(2,1)S(1)} collective-permute-done((bf16[144,2048]{1,0:T(8,128)(2,1)}, bf16[144,2048]{1,0:T(8,128)(2,1)S(1)}, u32[]{:S(2)}, u32[]{:S(2)}) %collective-permute-start.10) | collective-permute-done | bytes 589856 | tf_op jit(solution)/shard_map/ppermute | solution.py:357
  69.5 1.4 %fusion.4 = (bf16[144,2048]{1,0:T(8,128)(2,1)S(1)}, f32[144,2048]{1,0:T(8,128)S(1)}) fusion(f32[144,2048]{1,0:T(8,128)} %get-tuple-element.22, bf16[144,2048]{1,0:T(8,128)(2,1)S(1)} %collective-permute-done.10), kind=kLoop, calls=%fused_computation.24 | loop fusion | flops 884736 | bytes 3538944 | tf_op jit(solution)/shard_map/convert.10
  71.1 1.5 %collective-permute-start.11 = (bf16[80,2048]{1,0:T(8,128)(2,1)S(1)}, bf16[80,2048]{1,0:T(8,128)(2,1)S(1)}, u32[]{:S(2)}, u32[]{:S(2)}) collective-permute-start(bf16[80,2048]{1,0:T(8,128)(2,1)S(1)} %slice.80), channel_id=1, source_target_pairs={{0,2},{1,3},{2,0},{3,1},{4,6},{5,7},{6,4},{7,5},{8,10},{9,11},{10,... | collective-permute-start | bytes 983048 | tf_op jit(solution)/shard_map/ppermute | solution.py:357
  72.6 8.3 %collective-permute-done.11 = bf16[80,2048]{1,0:T(8,128)(2,1)S(1)} collective-permute-done((bf16[80,2048]{1,0:T(8,128)(2,1)S(1)}, bf16[80,2048]{1,0:T(8,128)(2,1)S(1)}, u32[]{:S(2)}, u32[]{:S(2)}) %collective-permute-start.11) | collective-permute-done | bytes 327712 | tf_op jit(solution)/shard_map/ppermute | solution.py:357
  81.2 2.9 %collective-permute-start.13 = (bf16[32,2048]{1,0:T(8,128)(2,1)S(1)}, bf16[32,2048]{1,0:T(8,128)(2,1)S(1)}, u32[]{:S(2)}, u32[]{:S(2)}) collective-permute-start(bf16[32,2048]{1,0:T(8,128)(2,1)S(1)} %get-tuple-element.46), channel_id=1, source_target_pairs={{0,8},{1,9},{2,10},{3,11},{4,12},{5,13},{6,14},{7,15},{8,0},{9,1},... | collective-permute-start | bytes 393224 | tf_op jit(solution)/shard_map/ppermute | solution.py:357
  84.1 1.4 %collective-permute-start.14 = (bf16[32,2048]{1,0:T(8,128)(2,1)S(1)}, bf16[32,2048]{1,0:T(8,128)(2,1)S(1)}, u32[]{:S(2)}, u32[]{:S(2)}) collective-permute-start(bf16[32,2048]{1,0:T(8,128)(2,1)S(1)} %get-tuple-element.47), channel_id=1, source_target_pairs={{0,12},{1,13},{2,14},{3,15},{4,8},{5,9},{6,10},{7,11},{8,4},{9,5},... | collective-permute-start | bytes 393224 | tf_op jit(solution)/shard_map/ppermute | solution.py:357
  85.5 6.4 %shard_map.131 = (f32[2048,128]{1,0:T(8,128)}, f32[64,2048]{1,0:T(8,128)}) custom-call(s32[4]{0:T(128)} %pad_add_fusion.refs_0_, bf16[128,2048]{1,0:T(8,128)(2,1)} %copy-done, bf16[128,2048]{1,0:T(8,128)(2,1)} %collective-permute-done.3.refs_3_.refs_2_, bf16[128,2048]{1,0:T(8,128)(2,1)} %collective-permute-done.4.refs_4_.refs_3_, ...), custom_call_target="tpu_custom_call" | custom-call | flops 2147483648 | bytes 8388608 | tf_op jit(solution)/shard_map/pallas_call | solution.py:321
  91.9 2.0 %collective-permute-done.13 = bf16[32,2048]{1,0:T(8,128)(2,1)S(1)} collective-permute-done((bf16[32,2048]{1,0:T(8,128)(2,1)S(1)}, bf16[32,2048]{1,0:T(8,128)(2,1)S(1)}, u32[]{:S(2)}, u32[]{:S(2)}) %collective-permute-start.13) | collective-permute-done | bytes 131104 | tf_op jit(solution)/shard_map/ppermute | solution.py:357
  94.0 0.7 add_add_fusion
  94.7 4.8 %shard_map.132 = f32[2048,32]{1,0:T(8,128)} custom-call(s32[4]{0:T(128)} %pad_add_fusion.refs_0_, f32[16,2048]{1,0:T(8,128)} %get-tuple-element.40.refs_1_, bf16[128,2048]{1,0:T(8,128)(2,1)} %copy-done, bf16[128,2048]{1,0:T(8,128)(2,1)} %collective-permute-done.3.refs_3_.refs_2_, bf16[128,2048]{1,0:T(8,128)(2,1)} %collective-permute-done.4.refs_4_.refs_3_, ...), custom_call_target="tpu_custom_call" | custom-call | flops 1073741824 | bytes 4194304 | tf_op jit(solution)/shard_map/pallas_call | solution.py:321
  99.5 2.2 %copy.18 = f32[2048,32]{0,1:T(8,128)} copy(f32[2048,32]{1,0:T(8,128)} %shard_map.132) | data formatting | bytes 524288
  (44 shorter events, 1.0 us)
Async XLA Ops:
  0.6 22.7 %copy-start.5 = (bf16[2048,32]{0,1:T(8,128)(2,1)S(1)}, bf16[2048,32]{0,1:T(8,128)(2,1)}, u32[]{:S(2)}) copy-start(bf16[2048,32]{0,1:T(8,128)(2,1)} %param.14) | copy-start | bytes 393220
  0.6 23.0 %copy-start.6 = (bf16[1,2048]{1,0:T(2,128)(2,1)S(1)}, bf16[1,2048]{1,0:T(2,128)(2,1)}, u32[]{:S(2)}) copy-start(bf16[1,2048]{1,0:T(2,128)(2,1)} %param.15) | copy-start | bytes 12292
  0.7 44.9 %copy-start.1 = (bf16[2048,128]{1,0:T(8,128)(2,1)S(1)}, bf16[2048,128]{1,0:T(8,128)(2,1)}, u32[]{:S(2)}) copy-start(bf16[2048,128]{1,0:T(8,128)(2,1)} %param.13) | copy-start | bytes 1572868
  2.4 6.6 %collective-permute-start = (bf16[32,2048]{1,0:T(8,128)(2,1)S(1)}, bf16[32,2048]{1,0:T(8,128)(2,1)S(1)}, u32[]{:S(2)}, u32[]{:S(2)}) collective-permute-start(bf16[32,2048]{1,0:T(8,128)(2,1)S(1)} %get-tuple-element.48), channel_id=1, source_target_pairs={{0,4},{1,5},{2,6},{3,7},{4,0},{5,1},{6,2},{7,3},{8,12},{9,13},{10,... | collective-permute-start | bytes 393224 | tf_op jit(solution)/shard_map/ppermute | solution.py:357
  5.5 14.2 %collective-permute-start.2 = (bf16[32,2048]{1,0:T(8,128)(2,1)S(1)}, bf16[32,2048]{1,0:T(8,128)(2,1)S(1)}, u32[]{:S(2)}, u32[]{:S(2)}) collective-permute-start(bf16[32,2048]{1,0:T(8,128)(2,1)S(1)} %get-tuple-element.48), channel_id=1, source_target_pairs={{0,12},{1,13},{2,14},{3,15},{4,8},{5,9},{6,10},{7,11},{8,4},{9,5},... | collective-permute-start | bytes 393224 | tf_op jit(solution)/shard_map/ppermute | solution.py:357
  8.0 11.8 %collective-permute-start.1 = (bf16[32,2048]{1,0:T(8,128)(2,1)S(1)}, bf16[32,2048]{1,0:T(8,128)(2,1)S(1)}, u32[]{:S(2)}, u32[]{:S(2)}) collective-permute-start(bf16[32,2048]{1,0:T(8,128)(2,1)S(1)} %get-tuple-element.48), channel_id=1, source_target_pairs={{0,8},{1,9},{2,10},{3,11},{4,12},{5,13},{6,14},{7,15},{8,0},{9,1},... | collective-permute-start | bytes 393224 | tf_op jit(solution)/shard_map/ppermute | solution.py:357
  19.8 27.1 %copy-start = (bf16[128,2048]{1,0:T(8,128)(2,1)}, bf16[128,2048]{1,0:T(8,128)(2,1)S(1)}, u32[]{:S(2)}) copy-start(bf16[128,2048]{1,0:T(8,128)(2,1)S(1)} %constant_dynamic-update-slice_fusion.2.refs_2_.refs_1_) | copy-start | bytes 1572868
  19.8 15.9 %collective-permute-start.8 = (bf16[128,2048]{1,0:T(8,128)(2,1)S(1)}, bf16[128,2048]{1,0:T(8,128)(2,1)S(1)}, u32[]{:S(2)}, u32[]{:S(2)}) collective-permute-start(bf16[128,2048]{1,0:T(8,128)(2,1)S(1)} %constant_dynamic-update-slice_fusion.2.refs_2_.refs_1_), channel_id=1, source_target_pairs={{18,0},{19,1},{16,2},{17,3},{22,4},{23,5},{20,6},{21,7},{26,8},{27... | collective-permute-start | bytes 1572872 | tf_op jit(solution)/shard_map/ppermute | solution.py:370
  22.3 22.7 %collective-permute-start.6 = (bf16[128,2048]{1,0:T(8,128)(2,1)S(1)}, bf16[128,2048]{1,0:T(8,128)(2,1)S(1)}, u32[]{:S(2)}, u32[]{:S(2)}) collective-permute-start(bf16[128,2048]{1,0:T(8,128)(2,1)S(1)} %constant_dynamic-update-slice_fusion.2.refs_2_.refs_1_), channel_id=1, source_target_pairs={{16,0},{0,16},{17,1},{1,17},{18,2},{2,18},{19,3},{3,19},{20,4},{4,... | collective-permute-start | bytes 1572872 | tf_op jit(solution)/shard_map/ppermute | solution.py:360
  22.8 22.4 %collective-permute-start.4 = (bf16[128,2048]{1,0:T(8,128)(2,1)S(1)}, bf16[128,2048]{1,0:T(8,128)(2,1)}, u32[]{:S(2)}, u32[]{:S(2)}) collective-permute-start(bf16[128,2048]{1,0:T(8,128)(2,1)S(1)} %constant_dynamic-update-slice_fusion.2.refs_2_.refs_1_), channel_id=1, source_target_pairs={{0,2},{1,3},{2,0},{3,1},{4,6},{5,7},{6,4},{7,5},{8,10},{9,11},{10,... | collective-permute-start | bytes 1572872 | tf_op jit(solution)/shard_map/ppermute | solution.py:357
  24.1 24.9 %copy-start.4 = (bf16[64,2048]{1,0:T(8,128)(2,1)S(1)}, bf16[64,2048]{1,0:T(8,128)(2,1)}, u32[]{:S(2)}) copy-start(bf16[64,2048]{1,0:T(8,128)(2,1)} %param.20) | copy-start | bytes 786436
  24.1 30.3 %collective-permute-start.3 = (bf16[128,2048]{1,0:T(8,128)(2,1)S(1)}, bf16[128,2048]{1,0:T(8,128)(2,1)}, u32[]{:S(2)}, u32[]{:S(2)}) collective-permute-start(bf16[128,2048]{1,0:T(8,128)(2,1)S(1)} %constant_dynamic-update-slice_fusion.2.refs_2_.refs_1_), channel_id=1, source_target_pairs={{0,1},{1,0},{2,3},{3,2},{4,5},{5,4},{6,7},{7,6},{8,9},{9,8},{10,11... | collective-permute-start | bytes 1572872 | tf_op jit(solution)/shard_map/ppermute | solution.py:357
  35.7 11.3 %copy-start.2 = (bf16[128,2048]{1,0:T(8,128)(2,1)}, bf16[128,2048]{1,0:T(8,128)(2,1)S(1)}, u32[]{:S(2)}) copy-start(bf16[128,2048]{1,0:T(8,128)(2,1)S(1)} %collective-permute-done.8.refs_8_.refs_7_) | copy-start | bytes 1572868
  35.7 18.7 %collective-permute-start.9 = (bf16[128,2048]{1,0:T(8,128)(2,1)S(1)}, bf16[128,2048]{1,0:T(8,128)(2,1)}, u32[]{:S(2)}, u32[]{:S(2)}) collective-permute-start(bf16[128,2048]{1,0:T(8,128)(2,1)S(1)} %collective-permute-done.8.refs_8_.refs_7_), channel_id=1, source_target_pairs={{0,1},{1,0},{2,3},{3,2},{4,5},{5,4},{6,7},{7,6},{8,9},{9,8},{10,11... | collective-permute-start | bytes 1572872 | tf_op jit(solution)/shard_map/ppermute | solution.py:357
  45.0 1.9 %copy-start.3 = (bf16[128,2048]{1,0:T(8,128)(2,1)}, bf16[128,2048]{1,0:T(8,128)(2,1)S(1)}, u32[]{:S(2)}) copy-start(bf16[128,2048]{1,0:T(8,128)(2,1)S(1)} %collective-permute-done.6.refs_6_.refs_5_) | copy-start | bytes 1572868
  45.0 9.3 %collective-permute-start.7 = (bf16[128,2048]{1,0:T(8,128)(2,1)S(1)}, bf16[128,2048]{1,0:T(8,128)(2,1)}, u32[]{:S(2)}, u32[]{:S(2)}) collective-permute-start(bf16[128,2048]{1,0:T(8,128)(2,1)S(1)} %collective-permute-done.6.refs_6_.refs_5_), channel_id=1, source_target_pairs={{0,1},{1,0},{2,3},{3,2},{4,5},{5,4},{6,7},{7,6},{8,9},{9,8},{10,11... | collective-permute-start | bytes 1572872 | tf_op jit(solution)/shard_map/ppermute | solution.py:357
  45.2 9.1 %collective-permute-start.5 = (bf16[128,2048]{1,0:T(8,128)(2,1)}, bf16[128,2048]{1,0:T(8,128)(2,1)}, u32[]{:S(2)}, u32[]{:S(2)}) collective-permute-start(bf16[128,2048]{1,0:T(8,128)(2,1)} %collective-permute-done.4.refs_4_.refs_3_), channel_id=1, source_target_pairs={{0,1},{1,0},{2,3},{3,2},{4,5},{5,4},{6,7},{7,6},{8,9},{9,8},{10,11... | collective-permute-start | bytes 1572872 | tf_op jit(solution)/shard_map/ppermute | solution.py:357
  49.8 3.9 %copy-start.7 = (f32[4,64]{1,0:T(4,128)S(1)}, f32[4,64]{1,0:T(4,128)}, u32[]{:S(2)}) copy-start(f32[4,64]{1,0:T(4,128)} %param.19) | copy-start | bytes 3076
  49.8 3.9 %copy-start.8 = (f32[4,64]{1,0:T(4,128)S(1)}, f32[4,64]{1,0:T(4,128)}, u32[]{:S(2)}) copy-start(f32[4,64]{1,0:T(4,128)} %constant.46.clone.1) | copy-start | bytes 3076
  67.3 2.2 %collective-permute-start.10 = (bf16[144,2048]{1,0:T(8,128)(2,1)}, bf16[144,2048]{1,0:T(8,128)(2,1)S(1)}, u32[]{:S(2)}, u32[]{:S(2)}) collective-permute-start(bf16[144,2048]{1,0:T(8,128)(2,1)} %get-tuple-element.23), channel_id=1, source_target_pairs={{0,1},{1,0},{2,3},{3,2},{4,5},{5,4},{6,7},{7,6},{8,9},{9,8},{10,11... | collective-permute-start | bytes 1769480 | tf_op jit(solution)/shard_map/ppermute | solution.py:357
  71.1 9.9 %collective-permute-start.11 = (bf16[80,2048]{1,0:T(8,128)(2,1)S(1)}, bf16[80,2048]{1,0:T(8,128)(2,1)S(1)}, u32[]{:S(2)}, u32[]{:S(2)}) collective-permute-start(bf16[80,2048]{1,0:T(8,128)(2,1)S(1)} %slice.80), channel_id=1, source_target_pairs={{0,2},{1,3},{2,0},{3,1},{4,6},{5,7},{6,4},{7,5},{8,10},{9,11},{10,... | collective-permute-start | bytes 983048 | tf_op jit(solution)/shard_map/ppermute | solution.py:357
  81.1 10.8 %collective-permute-start.12 = (bf16[32,2048]{1,0:T(8,128)(2,1)S(1)}, bf16[32,2048]{1,0:T(8,128)(2,1)S(1)}, u32[]{:S(2)}, u32[]{:S(2)}) collective-permute-start(bf16[32,2048]{1,0:T(8,128)(2,1)S(1)} %get-tuple-element.45), channel_id=1, source_target_pairs={{0,4},{1,5},{2,6},{3,7},{4,0},{5,1},{6,2},{7,3},{8,12},{9,13},{10,... | collective-permute-start | bytes 393224 | tf_op jit(solution)/shard_map/ppermute | solution.py:357
  81.2 12.8 %collective-permute-start.13 = (bf16[32,2048]{1,0:T(8,128)(2,1)S(1)}, bf16[32,2048]{1,0:T(8,128)(2,1)S(1)}, u32[]{:S(2)}, u32[]{:S(2)}) collective-permute-start(bf16[32,2048]{1,0:T(8,128)(2,1)S(1)} %get-tuple-element.46), channel_id=1, source_target_pairs={{0,8},{1,9},{2,10},{3,11},{4,12},{5,13},{6,14},{7,15},{8,0},{9,1},... | collective-permute-start | bytes 393224 | tf_op jit(solution)/shard_map/ppermute | solution.py:357
  84.1 9.8 %collective-permute-start.14 = (bf16[32,2048]{1,0:T(8,128)(2,1)S(1)}, bf16[32,2048]{1,0:T(8,128)(2,1)S(1)}, u32[]{:S(2)}, u32[]{:S(2)}) collective-permute-start(bf16[32,2048]{1,0:T(8,128)(2,1)S(1)} %get-tuple-element.47), channel_id=1, source_target_pairs={{0,12},{1,13},{2,14},{3,15},{4,8},{5,9},{6,10},{7,11},{8,4},{9,5},... | collective-permute-start | bytes 393224 | tf_op jit(solution)/shard_map/ppermute | solution.py:357

commit v2 on v1

v2 whole, which is shorter than its diff:
```python
import functools
import math

import jax
import jax.numpy as jnp
from jax import lax
from jax.experimental import pallas as pl
from jax.experimental.pallas import tpu as pltpu
from jax.sharding import PartitionSpec as P

STATE = 16
CONV = 4
LANES = 128
BLOCK = 256
TILE_ROWS = 16
VMEM_LIMIT = 60 * 1024 * 1024
f32 = jnp.float32
bf16 = jnp.bfloat16


def dot(a, b):
    return jnp.dot(a, b, preferred_element_type=f32)


def dot_nt(a, b):
    return lax.dot_general(a, b, (((1,), (1,)), ((), ())), preferred_element_type=f32)


def dot_tn(a, b):
    return lax.dot_general(a, b, (((0,), (0,)), ((), ())), preferred_element_type=f32)


def iota(shape, dim):
    return lax.broadcasted_iota(jnp.int32, shape, dim)


def mirror(size):
    return jnp.where(iota((size, size), 0) + iota((size, size), 1) == size - 1, 1.0, 0.0).astype(
        bf16
    )


def split(value, terms):
    parts = []
    for _ in range(terms):
        part = value.astype(bf16)
        parts.append(part)
        value = value - part.astype(f32)
    return parts


def flip_rows(value, flip):
    count = value.shape[0] // BLOCK
    return jnp.concatenate(
        [dot(flip, value[(count - 1 - i) * BLOCK : (count - i) * BLOCK]) for i in range(count)],
        axis=0,
    )


def assemble(ids_ref, pieces, out_ref, layout):
    tp_size, own_rows, coords = layout
    z, x, core, ctx = (ids_ref[i] for i in range(4))
    ctx_size = max(c[0] for c in coords) + 1
    for piece, (dc, dx, dcore, blocks) in zip(pieces, coords):
        from_ctx = lax.rem(ctx + dc, ctx_size)
        for k, j in enumerate(blocks):
            owner = ((z ^ j) * 2 + (x ^ dx)) * 2 + (core ^ dcore)
            at = pl.multiple_of((from_ctx * tp_size + owner) * own_rows, own_rows)
            out_ref[pl.ds(at, own_rows), :] = piece[k * own_rows : (k + 1) * own_rows, :]


def turn_columns(value, flip):
    count = value.shape[1] // BLOCK
    return jnp.concatenate(
        [dot(value[:, (count - 1 - i) * BLOCK : (count - i) * BLOCK], flip) for i in range(count)],
        axis=1,
    )


def prep_kernel(win_ref, wbct_ref, wdt_ref, wout_ref, conv_ref, late_ref, *outs):
    wcat_ref, wrev_ref, wpad_ref, wturn_ref, taps_ref, copy_ref = outs
    copy_ref[...] = late_ref[...]
    flip = mirror(BLOCK)
    width = win_ref.shape[0]
    head = wout_ref.shape[0]
    count = width // BLOCK
    for i in range(count):
        cols = slice(i * BLOCK, (i + 1) * BLOCK)
        rows = jnp.concatenate(
            [
                wbct_ref[:, cols].astype(f32),
                wdt_ref[:, cols].astype(f32),
                jnp.zeros((LANES - 2 * STATE - 1, BLOCK), f32),
            ],
            axis=0,
        )
        wcat_ref[cols, :LANES] = win_ref[cols, :]
        wcat_ref[cols, LANES:] = jnp.transpose(rows).astype(bf16)
    for i in range(count):
        wrev_ref[i * BLOCK : (i + 1) * BLOCK, :] = dot(
            flip, wcat_ref[(count - 1 - i) * BLOCK : (count - i) * BLOCK, :]
        ).astype(bf16)
    zeros = jnp.zeros((LANES - head, width), bf16)
    wpad_ref[:head, :] = wout_ref[...]
    wpad_ref[head:, :] = zeros
    wturn_ref[...] = turn_columns(wpad_ref[...], flip).astype(bf16)
    tap = iota((CONV, LANES - head), 0)
    taps_ref[:, :head] = conv_ref[...]
    taps_ref[:, head:] = jnp.where(tap == CONV - 1, 1.0, 0.0)


def own_source(shape, dim, ids_ref, tp_size, own_rows):
    z, x, core, ctx = (ids_ref[i] for i in range(4))
    nz = tp_size // 4
    row = iota(shape, dim)
    block = row // own_rows
    j = block % nz
    dx = 1 - (block // nz) % 2
    dcore = 1 - block // (2 * nz)
    owner = ((z ^ j) * 2 + (x ^ dx)) * 2 + (core ^ dcore)
    return (ctx * tp_size + owner) * own_rows + row % own_rows


def exact(parts, apply):
    return sum(apply(part) for part in parts)


def decay_rate(par_refs):
    return -jnp.exp(jnp.full((1, LANES), par_refs[1][0], f32))


def forward_kernel(n_pieces, layout, *refs):
    ids_ref, par_refs = refs[0], refs[1:4]
    pieces = refs[4 : 4 + n_pieces]
    wcat_ref, wrev_ref, taps_ref = refs[4 + n_pieces : 7 + n_pieces]
    full_ref, low_ref, state_ref, gated_ref = refs[7 + n_pieces : 11 + n_pieces]
    if layout[2] is None:
        h_ref = pieces[0]
    else:
        h_ref = refs[11 + n_pieces]
        assemble(ids_ref, pieces, h_ref, layout)
    length, width = h_ref.shape
    chunks = length // BLOCK
    columns = width // BLOCK
    flip = mirror(BLOCK)
    bias, rate, skip = par_refs[0][0], decay_rate(par_refs), par_refs[2][0]
    lane = iota((1, LANES), 1)
    low = lane < LANES // 2
    causal = iota((BLOCK, BLOCK), 0) >= iota((BLOCK, BLOCK), 1)
    tri = jnp.where(causal, 1.0, 0.0).astype(bf16)
    row_at = iota((length, LANES), 0)

    proj_f = dot(h_ref[...], wcat_ref[...])
    proj_r = dot(h_ref[...], wrev_ref[...])
    xz_r = flip_rows(proj_r[:, :LANES].astype(bf16), flip)
    rest_r = exact(split(proj_r[:, LANES:], 3), lambda part: flip_rows(part, flip))
    strands = (
        (proj_f[:, :LANES].astype(bf16).astype(f32), proj_f[:, LANES:]),
        (xz_r, rest_r),
    )
    for s, (xz, rest) in enumerate(strands):
        pre = taps_ref[CONV - 1 : CONV, :] * xz
        for shift in range(1, CONV):
            moved = jnp.where(row_at >= shift, pltpu.roll(xz, shift, 0), 0.0)
            pre += taps_ref[CONV - 1 - shift : CONV - shift, :] * moved
        sig = jax.nn.sigmoid(pre)
        u = pre * sig
        raw = jnp.broadcast_to(rest[:, 2 * STATE : 2 * STATE + 1], (length, LANES)) + bias
        dt = jnp.maximum(raw, 0.0) + jnp.log1p(jnp.exp(-jnp.abs(raw)))
        b_all = jnp.where(lane < STATE, rest, 0.0)
        c_all = jnp.where(lane < STATE, pltpu.roll(rest, LANES - STATE, 1), 0.0)
        w_all = dt * u
        full_ref[s, :, 0:LANES] = u
        full_ref[s, :, LANES : 2 * LANES] = sig * (1.0 + pre * (1.0 - sig))
        full_ref[s, :, 2 * LANES : 3 * LANES] = dt
        full_ref[s, :, 3 * LANES : 4 * LANES] = jax.nn.sigmoid(raw)
        low_ref[s, :, 0:LANES] = b_all.astype(bf16)
        low_ref[s, :, LANES : 2 * LANES] = c_all.astype(bf16)
        low_ref[s, :, 2 * LANES : 3 * LANES] = w_all.astype(bf16)
        state = jnp.zeros((LANES, LANES), f32)
        state_ref[s, 0] = state
        for c in range(chunks):
            rows = slice(c * BLOCK, (c + 1) * BLOCK)
            log_keep = exact(split(dt[rows] * rate, 3), lambda part: dot(tri, part))
            across = jnp.transpose(log_keep)[0:1, :]
            gap = jnp.concatenate([log_keep] * (BLOCK // LANES), axis=1) - across
            decay = jnp.exp(jnp.where(causal, gap, -jnp.inf))
            b_low, c_low = b_all[rows].astype(bf16), c_all[rows].astype(bf16)
            w_low = w_all[rows].astype(bf16)
            mixed = (dot_nt(c_low, b_low) * decay).astype(bf16)
            last = log_keep[BLOCK - 1 : BLOCK, :]
            b_left = (jnp.exp(last - log_keep) * b_all[rows]).astype(bf16)
            out = dot(mixed, w_low) + jnp.exp(log_keep) * dot(c_low, state.astype(bf16))
            state = jnp.exp(last) * state + dot_tn(b_left, w_low)
            full_ref[s, rows, 4 * LANES : 5 * LANES] = out
            full_ref[s, rows, 5 * LANES : 6 * LANES] = log_keep
            full_ref[s, rows, 6 * LANES :] = decay
            low_ref[s, rows, 3 * LANES : 4 * LANES] = b_left
            low_ref[s, rows, 4 * LANES :] = mixed
            state_ref[s, c + 1] = state
        y = full_ref[s, :, 4 * LANES : 5 * LANES] + skip * u
        gated = jnp.where(low, y * pltpu.roll(u, LANES // 2, 1), 0.0).astype(bf16)
        if s == 1:
            gated = flip_rows(gated, flip).astype(bf16)
        gated_ref[:, s * LANES : (s + 1) * LANES] = gated


def backward_kernel(n_pieces, layout, *refs):
    ids_ref, par_refs = refs[0], refs[1:4]
    pieces = refs[4 : 4 + n_pieces]
    full_ref, low_ref, state_ref = refs[4 + n_pieces : 7 + n_pieces]
    wcat_ref, wrev_ref, wpad_ref, wturn_ref, taps_ref = refs[7 + n_pieces : 12 + n_pieces]
    send_ref, keep_ref, gcat_ref = refs[12 + n_pieces : 15 + n_pieces]
    tp_size, own_rows, coords = layout
    if coords is None:
        d_ref = pieces[0]
    else:
        d_ref = refs[15 + n_pieces]
        assemble(ids_ref, pieces, d_ref, layout)
    length, width = d_ref.shape
    chunks = length // BLOCK
    columns = width // BLOCK
    flip = mirror(BLOCK)
    rate, skip = decay_rate(par_refs), par_refs[2][0]
    lane = iota((1, LANES), 1)
    low = lane < LANES // 2
    tri = jnp.where(iota((BLOCK, BLOCK), 0) >= iota((BLOCK, BLOCK), 1), 1.0, 0.0).astype(bf16)
    row_at = iota((length, LANES), 0)
    grad_f = dot_nt(d_ref[...], wpad_ref[...])
    grad_r = exact(
        split(dot_nt(d_ref[...], wturn_ref[...]), 2), lambda part: flip_rows(part, flip)
    )
    small = []
    for s, grad_g in enumerate((grad_f, grad_r)):
        u = full_ref[s, :, 0:LANES]
        slope = full_ref[s, :, LANES : 2 * LANES]
        dt = full_ref[s, :, 2 * LANES : 3 * LANES]
        dt_slope = full_ref[s, :, 3 * LANES : 4 * LANES]
        out = full_ref[s, :, 4 * LANES : 5 * LANES]
        u_other = pltpu.roll(u, LANES // 2, 1)
        g_y = jnp.where(low, grad_g * u_other, 0.0)
        g_gate = jnp.where(low, grad_g * (out + skip * u), 0.0)
        d_state = jnp.zeros((LANES, LANES), f32)
        d_w, g_b, g_c, g_a = [None] * chunks, [None] * chunks, [None] * chunks, [None] * chunks
        for c in reversed(range(chunks)):
            rows = slice(c * BLOCK, (c + 1) * BLOCK)
            log_keep = full_ref[s, rows, 5 * LANES : 6 * LANES]
            decay = full_ref[s, rows, 6 * LANES :]
            b_low = low_ref[s, rows, 0:LANES]
            c_low = low_ref[s, rows, LANES : 2 * LANES]
            w_low = low_ref[s, rows, 2 * LANES : 3 * LANES]
            b_left = low_ref[s, rows, 3 * LANES : 4 * LANES]
            mixed = low_ref[s, rows, 4 * LANES :]
            last = log_keep[BLOCK - 1 : BLOCK, :]
            enter = jnp.exp(log_keep)
            leave = jnp.exp(last - log_keep)
            gy = g_y[rows]
            gy_low = gy.astype(bf16)
            ds_low = d_state.astype(bf16)
            dw = dot_tn(mixed, gy_low) + dot(b_left, ds_low)
            d_scores = (dot_nt(gy_low, w_low) * decay).astype(bf16)
            g_c[c] = dot(d_scores, b_low) + enter * dot_nt(
                gy_low, state_ref[s, c].astype(bf16)
            )
            g_b[c] = dot_tn(d_scores, c_low) + leave * dot_nt(w_low, ds_low)
            d_log = jnp.sum(
                jnp.where(low, gy * out[rows] - dt[rows] * u[rows] * dw, 0.0),
                axis=1,
                keepdims=True,
            )
            at_end = jnp.sum(jnp.where(low, state_ref[s, c + 1] * d_state, 0.0))
            d_log = jnp.broadcast_to(d_log, (BLOCK, LANES))
            d_sum = exact(split(d_log, 2), lambda part: dot_tn(tri, part)) + at_end
            g_a[c] = rate * d_sum + jnp.sum(
                jnp.where(low, u[rows] * dw, 0.0), axis=1, keepdims=True
            )
            d_w[c] = dw
            carried = (enter * c_low).astype(bf16)
            d_state = jnp.exp(last) * d_state + dot_tn(carried, gy_low)
        d_w = jnp.concatenate(d_w, axis=0)
        g_b = jnp.concatenate(g_b, axis=0)
        g_c = jnp.concatenate(g_c, axis=0)
        g_raw = jnp.concatenate(g_a, axis=0) * dt_slope
        d_u = jnp.where(low, skip * g_y + dt * d_w, pltpu.roll(g_gate, LANES // 2, 1))
        d_pre = d_u * slope
        g_xz = taps_ref[CONV - 1 : CONV, :] * d_pre
        for shift in range(1, CONV):
            moved = jnp.where(
                row_at < length - shift, pltpu.roll(d_pre, length - shift, 0), 0.0
            )
            g_xz += taps_ref[CONV - 1 - shift : CONV - shift, :] * moved
        shared = jnp.where(lane < STATE, g_b, 0.0) + jnp.where(
            (lane >= STATE) & (lane < 2 * STATE), pltpu.roll(g_c, STATE, 1), 0.0
        )
        g_rest = shared + jnp.where(lane == 2 * STATE, g_raw, 0.0)
        g_cat = jnp.concatenate([g_xz, g_rest], axis=1).astype(bf16)
        small.append(shared)
        if s == 0:
            gcat_ref[:, : 2 * LANES] = g_cat
        else:
            gcat_ref[:, 2 * LANES :] = flip_rows(g_cat, flip).astype(bf16)

    pair = small[0] + pltpu.roll(small[1], 2 * STATE, 1)
    shared_t = jnp.transpose(pair)[: 4 * STATE].astype(bf16)
    groups = width // length
    step = 4 * STATE // groups
    for i in range(groups):
        part = shared_t[i * step : (i + 1) * step, :]
        send_ref[0:step, i * length : (i + 1) * length] = part
        keep_ref[0:step, i * length : (i + 1) * length] = part.astype(f32)
    own = tp_size * own_rows
    source = own_source((own, length), 0, ids_ref, tp_size, own_rows)
    pick = jnp.where(source == iota((own, length), 1), 1.0, 0.0).astype(bf16)
    picked = dot(pick, gcat_ref[...]).astype(bf16)
    half = own // 2
    for i in range(columns):
        cols = slice(i * BLOCK, (i + 1) * BLOCK)
        part = dot_nt(picked[:, : 2 * LANES], wcat_ref[cols, :]) + dot_nt(
            picked[:, 2 * LANES :], wrev_ref[cols, :]
        )
        send_ref[step:, cols] = part[:half].astype(bf16)
        keep_ref[step:, cols] = part[half:]


def weight_kernel(n_h, n_d, h_layout, d_layout, scaling, *refs):
    ids_ref = refs[0]
    h_pieces = refs[1 : 1 + n_h]
    d_pieces = refs[1 + n_h : 1 + n_h + n_d]
    refs = refs[1 + n_h + n_d :]
    gcat_ref, gated_ref, dwin_ref, dwout_ref = refs[:4]
    if h_layout[2] is None:
        h_ref, d_ref = h_pieces[0], d_pieces[0]
    else:
        h_ref, d_ref = refs[4:]
        assemble(ids_ref, h_pieces, h_ref, h_layout)
        assemble(ids_ref, d_pieces, d_ref, d_layout)
    flip = mirror(BLOCK)
    columns = h_ref.shape[1] // BLOCK
    head = dwout_ref.shape[0]
    g_f = gcat_ref[:, 0:LANES]
    g_r = gcat_ref[:, 2 * LANES : 3 * LANES]
    y_f = gated_ref[:, 0:LANES]
    y_r = gated_ref[:, LANES:]
    for i in range(columns):
        cols = slice(i * BLOCK, (i + 1) * BLOCK)
        back = slice((columns - 1 - i) * BLOCK, (columns - i) * BLOCK)
        turned = dot(h_ref[:, back], flip).astype(bf16)
        grad = dot_tn(g_f, h_ref[:, cols]) + dot_tn(g_r, turned)
        dwin_ref[cols, :] = jnp.transpose(grad * scaling)
        turned = dot(d_ref[:, back], flip).astype(bf16)
        grad = dot_tn(y_f, d_ref[:, cols]) + dot_tn(y_r, turned)
        dwout_ref[:, cols] = grad[:head] * scaling


def last_kernel(n_got, n_pieces, layout, scaling, *refs):
    ids_ref, own_ref = refs[:2]
    got_refs = refs[2 : 2 + n_got]
    pieces = refs[2 + n_got : 2 + n_got + n_pieces]
    refs = refs[2 + n_got + n_pieces :]
    dhid_ref, dwbct_ref = refs[:2]
    if layout[2] is None:
        h_ref = pieces[0]
    else:
        h_ref = refs[2]
        assemble(ids_ref, pieces, h_ref, layout)
    flip = mirror(BLOCK)
    length, width = h_ref.shape
    own_rows = layout[1]
    groups = width // length
    extra = 4 * STATE // groups
    total = own_ref[extra : extra + own_rows, :]
    for got in got_refs:
        total += got[extra : extra + own_rows, :].astype(f32)
    dhid_ref[...] = total.astype(bf16)
    sums = [own_ref[:extra, :].astype(bf16).astype(f32)]
    sums += [got[:extra, :].astype(f32) for got in got_refs]
    while len(sums) > 1:
        sums = [a + b for a, b in zip(sums[0::2], sums[1::2])]
    shared = sums[0].astype(bf16)
    shared = jnp.concatenate(
        [shared[:, i * length : (i + 1) * length] for i in range(groups)], axis=0
    )
    fwd = shared[: 2 * STATE]
    rev = turn_columns(shared[2 * STATE :], flip).astype(bf16)
    pairs = dot(jnp.concatenate([fwd, rev], axis=0), h_ref[...])
    turned = exact(split(pairs[2 * STATE :], 3), lambda part: turn_columns(part, flip))
    dwbct_ref[...] = (pairs[: 2 * STATE] + turned) * scaling


def spec(memory=pltpu.VMEM):
    return pl.BlockSpec(memory_space=memory)


def call(kernel, inputs, n_smem, outs, scratch, flops, moved):
    return pl.pallas_call(
        kernel,
        out_shape=outs,
        in_specs=[spec(pltpu.SMEM)] * n_smem + [spec()] * (len(inputs) - n_smem),
        out_specs=jax.tree.map(lambda _: spec(), outs),
        scratch_shapes=scratch,
        compiler_params=pltpu.CompilerParams(vmem_limit_bytes=VMEM_LIMIT),
        cost_estimate=pl.CostEstimate(flops=flops, bytes_accessed=moved, transcendentals=0),
    )(*inputs)


def shape(dims, dtype):
    return jax.ShapeDtypeStruct(dims, dtype)


def local(ctx_size, tp_size, hidden, w_in, w_bc, w_dt, dt_bias, a_log, d_skip, conv_w, w_out, d_out):
    own_rows, width = hidden.shape
    length = own_rows * tp_size * ctx_size
    head = w_out.shape[0]
    nz = tp_size // 4
    chunks = length // BLOCK
    t = lax.axis_index("tp")
    ids = jnp.stack([t >> 2, (t >> 1) & 1, t & 1, lax.axis_index("ctx")]).astype(jnp.int32)
    params = [dt_bias, a_log, d_skip]
    wcat, wrev, wpad, wturn, taps, late = call(
        prep_kernel,
        [w_in, w_bc.T, w_dt, w_out, conv_w, d_out],
        0,
        (
            shape((width, 2 * LANES), bf16),
            shape((width, 2 * LANES), bf16),
            shape((LANES, width), bf16),
            shape((LANES, width), bf16),
            shape((CONV, LANES), f32),
            shape(d_out.shape, bf16),
        ),
        [],
        2 * width * BLOCK * BLOCK,
        8 * width * LANES,
    )

    def across(value, flip_bits):
        return lax.ppermute(value, "tp", [(i, i ^ flip_bits) for i in range(tp_size)])

    def along(value, offset):
        return lax.ppermute(
            value, "ctx", [((i + offset) % ctx_size, i) for i in range(ctx_size)]
        )

    def gather(own):
        zs = [own] + [across(own, 4 * j) for j in range(1, nz)]
        groups = [range(0, nz // 2), range(nz // 2, nz)]
        coords, pieces = [], []
        for g, blocks in enumerate(groups):
            chunk = jnp.concatenate([zs[j] for j in blocks], axis=0)
            beside = across(chunk, 2)
            plane = [((0, 0), chunk), ((0, 1), beside)]
            for dc in range(1, ctx_size):
                ahead = along(chunk, dc)
                diagonal = across(ahead, 2) if g == 0 else along(beside, dc)
                plane += [((dc, 0), ahead), ((dc, 1), diagonal)]
            for (dc, dx), piece in plane:
                coords += [(dc, dx, 0, tuple(blocks)), (dc, dx, 1, tuple(blocks))]
                pieces += [piece, across(piece, 1)]
        return pieces, (tp_size, own_rows, tuple(coords))

    if own_rows % TILE_ROWS == 0:
        h_pieces, layout = gather(hidden)
        d_pieces, _ = gather(late)
        rows = [pltpu.VMEM((length, width), bf16)]
    else:
        h_pieces, d_pieces = (
            [lax.all_gather(a, ("ctx", "tp"), axis=0, tiled=True)] for a in (hidden, late)
        )
        layout, rows = (tp_size, own_rows, None), []
    n_pieces = len(h_pieces)
    extra = 4 * STATE * length // width
    half = tp_size * own_rows // 2
    full, low, states, gated = call(
        functools.partial(forward_kernel, n_pieces, layout),
        [ids, *params, *h_pieces, wcat, wrev, taps],
        4,
        (
            shape((2, length, 6 * LANES + BLOCK), f32),
            shape((2, length, 4 * LANES + BLOCK), bf16),
            shape((2, chunks + 1, LANES, LANES), f32),
            shape((length, 2 * LANES), bf16),
        ),
        rows,
        4 * length * width * BLOCK,
        16 * length * width,
    )
    send, keep, gcat = call(
        functools.partial(backward_kernel, n_pieces, layout),
        [ids, *params, *d_pieces, full, low, states, wcat, wrev, wpad, wturn, taps],
        4,
        (
            shape((extra + half, width), bf16),
            shape((extra + half, width), f32),
            shape((length, 4 * LANES), bf16),
        ),
        rows,
        4 * length * width * BLOCK,
        16 * length * width,
    )
    scaling = 1.0 / math.sqrt(length)
    got = across(send, 1)
    d_w_in, d_w_out = call(
        functools.partial(weight_kernel, n_pieces, n_pieces, layout, layout, scaling),
        [ids, *h_pieces, *d_pieces, gcat, gated],
        1,
        (
            shape((width, LANES), f32),
            shape((head, width), f32),
        ),
        rows * 2,
        8 * length * width * BLOCK,
        8 * length * width,
    )
    quarter = half // 2
    summed = keep + got.astype(f32)
    send = summed[: extra + quarter].astype(bf16)
    keep = jnp.concatenate(
        [summed[:extra].astype(bf16).astype(f32), summed[extra + quarter :]], axis=0
    )
    summed = keep + across(send, 2).astype(f32)
    got = []
    for j in range(1, nz):
        at = extra + j * own_rows
        piece = jnp.concatenate([summed[:extra], summed[at : at + own_rows]], axis=0)
        got.append(across(piece.astype(bf16), 4 * j))
    d_hidden, d_w_bc = call(
        functools.partial(last_kernel, len(got), n_pieces, layout, scaling),
        [ids, summed[: extra + own_rows], *got, *h_pieces],
        1,
        (shape((own_rows, width), bf16), shape((2 * STATE, width), f32)),
        rows,
        2 * length * width * LANES,
        4 * length * width,
    )
    return (d_hidden, d_w_in, d_w_out, d_w_bc.T)


def solution(mesh):
    in_specs = (
        P(("ctx", "tp"), None),
        P(None, "tp"),
        P(),
        P("tp", None),
        P("tp"),
        P("tp"),
        P("tp"),
        P(None, "tp"),
        P("tp", None),
        P(("ctx", "tp"), None),
    )
    out_specs = (P(("ctx", "tp"), None), P(None, "tp"), P("tp", None), P())
    body = functools.partial(local, mesh.shape["ctx"], mesh.shape["tp"])
    return jax.shard_map(body, mesh=mesh, in_specs=in_specs, out_specs=out_specs, check_vma=False)
```

time: 102 us -> 100 us (0.980)
  waiting for transfers between devices: 45.1 us -> 21.8 us
  starting transfers between devices: 15.9 us -> 35.9 us
  Pallas kernels: 26.8 us -> 32.4 us
  other arithmetic: 5.57 us -> 2.17 us
  local copies, waits for them, and re-layouts: 5.65 us -> 4.59 us
    ppermute x13 -> x33, starting transfers between devices: 12.8 us -> 28.6 us  [across(): lax.ppermute(value, 'tp', [(i, i ^ flip_bits) for i in range(tp_size)])]
    ppermute x1 -> x0, waiting for transfers between devices: 11.6 us -> none  [along_x(): return lax.ppermute(value, ('ctx', 'tp'), pairs)]
    ppermute x1 -> x6, waiting for transfers between devices: 9.36 us -> 2.35 us  [along(): lax.ppermute(value, 'ctx', [((i + offset) % ctx_size, i) for i in range(c...]
    ppermute x1 -> x6, starting transfers between devices: 0.51 us -> 7.3 us  [along(): lax.ppermute(value, 'ctx', [((i + offset) % ctx_size, i) for i in range(c...]
    pallas_call x4 -> x5, Pallas kernels: 26.8 us -> 32.4 us  [call(): pl.pallas_call(kernel, out_shape=outs, in_specs=[spec(pltpu.SMEM)] * n_sm...]
    ppermute x13 -> x33, waiting for transfers between devices: 24.1 us -> 19.4 us  [across(): lax.ppermute(value, 'tp', [(i, i ^ flip_bits) for i in range(tp_size)])]
    ppermute x1 -> x0, starting transfers between devices: 2.51 us -> none  [along_x(): return lax.ppermute(value, ('ctx', 'tp'), pairs)]
    concatenate x2 -> x0, other arithmetic: 2.01 us -> none  [the longest x1 1.36 us: local(): jnp.concatenate([w_in, w_bc, w_dt.T, jnp.zeros((width, 2 * LANES - 2 * he...]
  transfers between devices with their start and end apart: 15 -> 39, of which waited for: 8 -> 12; matrix products, arithmetic and copies ran while one was open for 5% -> 3% of each run, Pallas kernels for 9% -> 18%
where the time goes in v2:
time: 100 us
  starting transfers between devices  35.9 us (36%)
  Pallas kernels  32.4 us (32%)
  waiting for transfers between devices  21.8 us (22%)
  local copies, waits for them, and re-layouts  4.59 us (5%)
  between operations  3.11 us (3%)
  other arithmetic  2.17 us (2%)
    pallas_call x5, Pallas kernels, call(): pl.pallas_call(kernel, out_shape=outs, in_specs=[spec(pltpu.SMEM)] * n_sm...  32.4 us
    ppermute x33, starting transfers between devices, across(): lax.ppermute(value, 'tp', [(i, i ^ flip_bits) for i in range(tp_size)])  28.6 us
    ppermute x33, waiting for transfers between devices, across(): lax.ppermute(value, 'tp', [(i, i ^ flip_bits) for i in range(tp_size)])  19.4 us
    ppermute x6, starting transfers between devices, along(): lax.ppermute(value, 'ctx', [((i + offset) % ctx_size, i) for i in range(c...  7.3 us
    unnamed x72, local copies, waits for them, and re-layouts  3.74 us
    ppermute x6, waiting for transfers between devices, along(): lax.ppermute(value, 'ctx', [((i + offset) % ctx_size, i) for i in range(c...  2.35 us
  transfers between devices with their start and end apart: 39, of which 12 were waited for; matrix products, arithmetic and copies ran while one was open for 3% of the time, Pallas kernels for 18%

profile of v2, /device:TPU:0, one launch (start us, length us, event | category | flops | bytes accessed | tf_op | source)
XLA Modules:
  0.0 100.0 jit_solution(12106439879213368567)
XLA Ops:
  0.6 3.1 %collective-permute-start.17 = (bf16[16,2048]{1,0:T(8,128)(2,1)}, bf16[16,2048]{1,0:T(8,128)(2,1)S(1)}, u32[]{:S(2)}, u32[]{:S(2)}) collective-permute-start(bf16[16,2048]{1,0:T(8,128)(2,1)} %param.10), channel_id=1, source_target_pairs={{0,4},{1,5},{2,6},{3,7},{4,0},{5,1},{6,2},{7,3},{8,12},{9,13},{10,... | collective-permute-start | bytes 196616 | tf_op jit(solution)/shard_map/ppermute | solution.py:437
  3.7 2.5 %collective-permute-start.26 = (bf16[16,2048]{1,0:T(8,128)(2,1)}, bf16[16,2048]{1,0:T(8,128)(2,1)S(1)}, u32[]{:S(2)}, u32[]{:S(2)}) collective-permute-start(bf16[16,2048]{1,0:T(8,128)(2,1)} %param.10), channel_id=1, source_target_pairs={{0,12},{1,13},{2,14},{3,15},{4,8},{5,9},{6,10},{7,11},{8,4},{9,5},... | collective-permute-start | bytes 196616 | tf_op jit(solution)/shard_map/ppermute | solution.py:437
  6.3 3.4 %shard_map.129 = (bf16[2048,256]{1,0:T(8,128)(2,1)}, bf16[2048,256]{1,0:T(8,128)(2,1)}, bf16[128,2048]{1,0:T(8,128)(2,1)}, bf16[128,2048]{1,0:T(8,128)(2,1)}, f3...) custom-call(bf16[2048,128]{1,0:T(8,128)(2,1)} %win_ref.1, bf16[32,2048]{1,0:T(8,128)(2,1)} %bitcast.7, bf16[1,2048]{1,0:T(2,128)(2,1)} %wdt_ref.1, ...), custom_call_target="tpu_custom_call" | custom-call | flops 268435456 | bytes 2097152 | tf_op jit(solution)/shard_map/pallas_call | solution.py:395
  9.7 2.9 %collective-permute-start.9 = (bf16[16,2048]{1,0:T(8,128)(2,1)}, bf16[16,2048]{1,0:T(8,128)(2,1)S(1)}, u32[]{:S(2)}, u32[]{:S(2)}) collective-permute-start(bf16[16,2048]{1,0:T(8,128)(2,1)} %get-tuple-element.21), channel_id=1, source_target_pairs={{0,12},{1,13},{2,14},{3,15},{4,8},{5,9},{6,10},{7,11},{8,4},{9,5},... | collective-permute-start | bytes 196616 | tf_op jit(solution)/shard_map/ppermute | solution.py:437
  13.0 0.8 constant_dynamic-update-slice_fusion.5
  13.8 0.8 constant_dynamic-update-slice_fusion.1
  14.7 1.1 %collective-permute-start = (bf16[16,2048]{1,0:T(8,128)(2,1)}, bf16[16,2048]{1,0:T(8,128)(2,1)S(1)}, u32[]{:S(2)}, u32[]{:S(2)}) collective-permute-start(bf16[16,2048]{1,0:T(8,128)(2,1)} %get-tuple-element.21), channel_id=1, source_target_pairs={{0,4},{1,5},{2,6},{3,7},{4,0},{5,1},{6,2},{7,3},{8,12},{9,13},{10,... | collective-permute-start | bytes 196616 | tf_op jit(solution)/shard_map/ppermute | solution.py:437
  15.8 1.6 %collective-permute-start.21 = (bf16[32,2048]{1,0:T(8,128)(2,1)S(1)}, bf16[32,2048]{1,0:T(8,128)(2,1)S(1)}, u32[]{:S(2)}, u32[]{:S(2)}) collective-permute-start(bf16[32,2048]{1,0:T(8,128)(2,1)S(1)} %constant_dynamic-update-slice_fusion.4.refs_4_.refs_5_.refs_1_), channel_id=1, source_target_pairs={{16,0},{0,16},{17,1},{1,17},{18,2},{2,18},{19,3},{3,19},{20,4},{4,... | collective-permute-start | bytes 393224 | tf_op jit(solution)/shard_map/ppermute | solution.py:440
  17.4 1.6 %collective-permute-done.8 = bf16[16,2048]{1,0:T(8,128)(2,1)S(1)} collective-permute-done((bf16[16,2048]{1,0:T(8,128)(2,1)}, bf16[16,2048]{1,0:T(8,128)(2,1)S(1)}, u32[]{:S(2)}, u32[]{:S(2)}) %collective-permute-start.8) | collective-permute-done | bytes 65568 | tf_op jit(solution)/shard_map/ppermute | solution.py:437
  19.0 1.5 %collective-permute-start.19 = (bf16[32,2048]{1,0:T(8,128)(2,1)S(1)}, bf16[32,2048]{1,0:T(8,128)(2,1)S(1)}, u32[]{:S(2)}, u32[]{:S(2)}) collective-permute-start(bf16[32,2048]{1,0:T(8,128)(2,1)S(1)} %constant_dynamic-update-slice_fusion.4.refs_4_.refs_5_.refs_1_), channel_id=1, source_target_pairs={{0,2},{1,3},{2,0},{3,1},{4,6},{5,7},{6,4},{7,5},{8,10},{9,11},{10,... | collective-permute-start | bytes 393224 | tf_op jit(solution)/shard_map/ppermute | solution.py:437
  20.6 1.6 %collective-permute-start.30 = (bf16[32,2048]{1,0:T(8,128)(2,1)S(1)}, bf16[32,2048]{1,0:T(8,128)(2,1)S(1)}, u32[]{:S(2)}, u32[]{:S(2)}) collective-permute-start(bf16[32,2048]{1,0:T(8,128)(2,1)S(1)} %constant_dynamic-update-slice_fusion.6.refs_12_.refs_13_.refs_9_), channel_id=1, source_target_pairs={{16,0},{0,16},{17,1},{1,17},{18,2},{2,18},{19,3},{3,19},{20,4},{4,... | collective-permute-start | bytes 393224 | tf_op jit(solution)/shard_map/ppermute | solution.py:440
  22.8 1.1 %collective-permute-done.19.refs_6_.refs_7_.refs_3_ = bf16[32,2048]{1,0:T(8,128)(2,1)S(1)} collective-permute-done((bf16[32,2048]{1,0:T(8,128)(2,1)S(1)}, bf16[32,2048]{1,0:T(8,128)(2,1)S(1)}, u32[]{:S(2)}, u32[]{:S(2)}) %collective-permute-start.19) | collective-permute-done | bytes 131104 | tf_op jit(solution)/shard_map/ppermute | solution.py:437
  24.0 1.5 %collective-permute-start.4 = (bf16[32,2048]{1,0:T(8,128)(2,1)S(1)}, bf16[32,2048]{1,0:T(8,128)(2,1)S(1)}, u32[]{:S(2)}, u32[]{:S(2)}) collective-permute-start(bf16[32,2048]{1,0:T(8,128)(2,1)S(1)} %constant_dynamic-update-slice_fusion.refs_4_.refs_17_), channel_id=1, source_target_pairs={{16,0},{0,16},{17,1},{1,17},{18,2},{2,18},{19,3},{3,19},{20,4},{4,... | collective-permute-start | bytes 393224 | tf_op jit(solution)/shard_map/ppermute | solution.py:440
  25.5 2.4 %collective-permute-start.2 = (bf16[32,2048]{1,0:T(8,128)(2,1)S(1)}, bf16[32,2048]{1,0:T(8,128)(2,1)S(1)}, u32[]{:S(2)}, u32[]{:S(2)}) collective-permute-start(bf16[32,2048]{1,0:T(8,128)(2,1)S(1)} %constant_dynamic-update-slice_fusion.refs_4_.refs_17_), channel_id=1, source_target_pairs={{0,2},{1,3},{2,0},{3,1},{4,6},{5,7},{6,4},{7,5},{8,10},{9,11},{10,... | collective-permute-start | bytes 393224 | tf_op jit(solution)/shard_map/ppermute | solution.py:437
  29.1 1.3 %collective-permute-start.11 = (bf16[32,2048]{1,0:T(8,128)(2,1)S(1)}, bf16[32,2048]{1,0:T(8,128)(2,1)S(1)}, u32[]{:S(2)}, u32[]{:S(2)}) collective-permute-start(bf16[32,2048]{1,0:T(8,128)(2,1)S(1)} %constant_dynamic-update-slice_fusion.2.refs_12_.refs_25_), channel_id=1, source_target_pairs={{0,2},{1,3},{2,0},{3,1},{4,6},{5,7},{6,4},{7,5},{8,10},{9,11},{10,... | collective-permute-start | bytes 393224 | tf_op jit(solution)/shard_map/ppermute | solution.py:437
  30.4 1.2 %collective-permute-done.2.refs_6_.refs_19_ = bf16[32,2048]{1,0:T(8,128)(2,1)S(1)} collective-permute-done((bf16[32,2048]{1,0:T(8,128)(2,1)S(1)}, bf16[32,2048]{1,0:T(8,128)(2,1)S(1)}, u32[]{:S(2)}, u32[]{:S(2)}) %collective-permute-start.2) | collective-permute-done | bytes 131104 | tf_op jit(solution)/shard_map/ppermute | solution.py:437
  31.6 2.5 %collective-permute-start.23 = (bf16[32,2048]{1,0:T(8,128)(2,1)S(1)}, bf16[32,2048]{1,0:T(8,128)(2,1)S(1)}, u32[]{:S(2)}, u32[]{:S(2)}) collective-permute-start(bf16[32,2048]{1,0:T(8,128)(2,1)S(1)} %collective-permute-done.21.refs_8_.refs_9_.refs_5_), channel_id=1, source_target_pairs={{0,2},{1,3},{2,0},{3,1},{4,6},{5,7},{6,4},{7,5},{8,10},{9,11},{10,... | collective-permute-start | bytes 393224 | tf_op jit(solution)/shard_map/ppermute | solution.py:437
  34.9 1.6 %collective-permute-start.32 = (bf16[32,2048]{1,0:T(8,128)(2,1)S(1)}, bf16[32,2048]{1,0:T(8,128)(2,1)S(1)}, u32[]{:S(2)}, u32[]{:S(2)}) collective-permute-start(bf16[32,2048]{1,0:T(8,128)(2,1)S(1)} %collective-permute-done.28.refs_14_.refs_15_.refs_11_), channel_id=1, source_target_pairs={{16,0},{0,16},{17,1},{1,17},{18,2},{2,18},{19,3},{3,19},{20,4},{4,... | collective-permute-start | bytes 393224 | tf_op jit(solution)/shard_map/ppermute | solution.py:440
  37.0 2.1 %collective-permute-start.6 = (bf16[32,2048]{1,0:T(8,128)(2,1)S(1)}, bf16[32,2048]{1,0:T(8,128)(2,1)S(1)}, u32[]{:S(2)}, u32[]{:S(2)}) collective-permute-start(bf16[32,2048]{1,0:T(8,128)(2,1)S(1)} %collective-permute-done.4.refs_8_.refs_21_), channel_id=1, source_target_pairs={{0,2},{1,3},{2,0},{3,1},{4,6},{5,7},{6,4},{7,5},{8,10},{9,11},{10,... | collective-permute-start | bytes 393224 | tf_op jit(solution)/shard_map/ppermute | solution.py:437
  39.9 0.9 collective-permute-done.32.refs_18_.refs_19_.refs_15_
  41.3 1.8 %collective-permute-done.6.refs_10_.refs_23_ = bf16[32,2048]{1,0:T(8,128)(2,1)S(1)} collective-permute-done((bf16[32,2048]{1,0:T(8,128)(2,1)S(1)}, bf16[32,2048]{1,0:T(8,128)(2,1)S(1)}, u32[]{:S(2)}, u32[]{:S(2)}) %collective-permute-start.6) | collective-permute-done | bytes 131104 | tf_op jit(solution)/shard_map/ppermute | solution.py:437
  43.7 1.4 %collective-permute-done.15.refs_18_.refs_31_ = bf16[32,2048]{1,0:T(8,128)(2,1)} collective-permute-done((bf16[32,2048]{1,0:T(8,128)(2,1)S(1)}, bf16[32,2048]{1,0:T(8,128)(2,1)}, u32[]{:S(2)}, u32[]{:S(2)}) %collective-permute-start.15) | collective-permute-done | bytes 131104 | tf_op jit(solution)/shard_map/ppermute | solution.py:440
  48.4 8.6 %shard_map.130 = (f32[2,512,1024]{2,1,0:T(8,128)}, bf16[2,512,768]{2,1,0:T(8,128)(2,1)}, f32[2,3,128,128]{3,2,1,0:T(8,128)}, bf16[512,256]{1,0:T(8,128)(2,1)}) custom-call(s32[4]{0:T(128)} %pad_add_fusion.refs_0_, f32[1]{0:T(128)S(6)} %copy.18.refs_1_, f32[1]{0:T(128)S(6)} %copy.19.refs_2_, f32[1]{0:T(128)S(6)} %copy.20.refs_3_, bf16[32,2048]{1,0:T(8,128)(2,1)} %copy-done.1, ...), custom_call_target="tpu_custom_call" | custom-call | flops 1073741824 | bytes 16777216 | tf_op jit(solution)/shard_map/pallas_call | solution.py:395
  57.8 10.4 %shard_map.131 = (bf16[144,2048]{1,0:T(8,128)(2,1)}, f32[144,2048]{1,0:T(8,128)}, bf16[512,512]{1,0:T(8,128)(2,1)}) custom-call(s32[4]{0:T(128)} %pad_add_fusion.refs_0_, f32[1]{0:T(128)S(6)} %copy.18.refs_1_, f32[1]{0:T(128)S(6)} %copy.19.refs_2_, f32[1]{0:T(128)S(6)} %copy.20.refs_3_, bf16[32,2048]{1,0:T(8,128)(2,1)} %copy-done.17, ...), custom_call_target="tpu_custom_call" | custom-call | flops 1073741824 | bytes 16777216 | tf_op jit(solution)/shard_map/pallas_call | solution.py:395
  68.7 1.8 %collective-permute-done.34 = bf16[144,2048]{1,0:T(8,128)(2,1)S(1)} collective-permute-done((bf16[144,2048]{1,0:T(8,128)(2,1)}, bf16[144,2048]{1,0:T(8,128)(2,1)S(1)}, u32[]{:S(2)}, u32[]{:S(2)}) %collective-permute-start.34) | collective-permute-done | bytes 589856 | tf_op jit(solution)/shard_map/ppermute | solution.py:437
  70.5 1.4 %fusion.1 = (bf16[144,2048]{1,0:T(8,128)(2,1)S(1)}, f32[144,2048]{1,0:T(8,128)S(1)}) fusion(f32[144,2048]{1,0:T(8,128)} %get-tuple-element.30, bf16[144,2048]{1,0:T(8,128)(2,1)S(1)} %collective-permute-done.34), kind=kLoop, calls=%fused_computation.17 | loop fusion | flops 884736 | bytes 3538944 | tf_op jit(solution)/shard_map/convert.10
  72.7 9.4 %collective-permute-done.35 = bf16[80,2048]{1,0:T(8,128)(2,1)S(1)} collective-permute-done((bf16[80,2048]{1,0:T(8,128)(2,1)S(1)}, bf16[80,2048]{1,0:T(8,128)(2,1)S(1)}, u32[]{:S(2)}, u32[]{:S(2)}) %collective-permute-start.35) | collective-permute-done | bytes 327712 | tf_op jit(solution)/shard_map/ppermute | solution.py:437
  82.3 2.5 %collective-permute-start.38 = (bf16[32,2048]{1,0:T(8,128)(2,1)S(1)}, bf16[32,2048]{1,0:T(8,128)(2,1)S(1)}, u32[]{:S(2)}, u32[]{:S(2)}) collective-permute-start(bf16[32,2048]{1,0:T(8,128)(2,1)S(1)} %get-tuple-element.45), channel_id=1, source_target_pairs={{0,12},{1,13},{2,14},{3,15},{4,8},{5,9},{6,10},{7,11},{8,4},{9,5},... | collective-permute-start | bytes 393224 | tf_op jit(solution)/shard_map/ppermute | solution.py:437
  84.7 2.2 %collective-permute-start.36 = (bf16[32,2048]{1,0:T(8,128)(2,1)S(1)}, bf16[32,2048]{1,0:T(8,128)(2,1)S(1)}, u32[]{:S(2)}, u32[]{:S(2)}) collective-permute-start(bf16[32,2048]{1,0:T(8,128)(2,1)S(1)} %get-tuple-element.47), channel_id=1, source_target_pairs={{0,4},{1,5},{2,6},{3,7},{4,0},{5,1},{6,2},{7,3},{8,12},{9,13},{10,... | collective-permute-start | bytes 393224 | tf_op jit(solution)/shard_map/ppermute | solution.py:437
  86.9 6.3 %shard_map.133 = (f32[2048,128]{1,0:T(8,128)}, f32[64,2048]{1,0:T(8,128)}) custom-call(s32[4]{0:T(128)} %pad_add_fusion.refs_0_, bf16[32,2048]{1,0:T(8,128)(2,1)} %copy-done.1, bf16[32,2048]{1,0:T(8,128)(2,1)} %copy-done.4, bf16[32,2048]{1,0:T(8,128)(2,1)} %copy-done.3, bf16[32,2048]{1,0:T(8,128)(2,1)} %copy-done.10, bf16[32,2048]{1,0:T(8,128)(2,1)} %copy-done.2, ...), custom_call_target="tpu_custom_call" | custom-call | flops 2147483648 | bytes 8388608 | tf_op jit(solution)/shard_map/pallas_call | solution.py:395
  94.0 1.0 collective-permute-done.37.refs_3_
  96.2 3.8 %shard_map.132 = (bf16[16,2048]{1,0:T(8,128)(2,1)}, f32[32,2048]{1,0:T(8,128)}) custom-call(s32[4]{0:T(128)} %pad_add_fusion.refs_0_, f32[32,2048]{1,0:T(8,128)} %slice.42.refs_1_, bf16[32,2048]{1,0:T(8,128)(2,1)} %copy-done.20, bf16[32,2048]{1,0:T(8,128)(2,1)} %copy-done.19, bf16[32,2048]{1,0:T(8,128)(2,1)} %copy-done.18, bf16[32,2048]{1,0:T(8,128)(2,1)} %copy-done.1, ...), custom_call_target="tpu_custom_call" | custom-call | flops 268435456 | bytes 4194304 | tf_op jit(solution)/shard_map/pallas_call | solution.py:395
  (137 shorter events, 10.8 us)
Async XLA Ops:
  0.6 14.1 %collective-permute-start.17 = (bf16[16,2048]{1,0:T(8,128)(2,1)}, bf16[16,2048]{1,0:T(8,128)(2,1)S(1)}, u32[]{:S(2)}, u32[]{:S(2)}) collective-permute-start(bf16[16,2048]{1,0:T(8,128)(2,1)} %param.10), channel_id=1, source_target_pairs={{0,4},{1,5},{2,6},{3,7},{4,0},{5,1},{6,2},{7,3},{8,12},{9,13},{10,... | collective-permute-start | bytes 196616 | tf_op jit(solution)/shard_map/ppermute | solution.py:437
  3.7 16.8 %collective-permute-start.26 = (bf16[16,2048]{1,0:T(8,128)(2,1)}, bf16[16,2048]{1,0:T(8,128)(2,1)S(1)}, u32[]{:S(2)}, u32[]{:S(2)}) collective-permute-start(bf16[16,2048]{1,0:T(8,128)(2,1)} %param.10), channel_id=1, source_target_pairs={{0,12},{1,13},{2,14},{3,15},{4,8},{5,9},{6,10},{7,11},{8,4},{9,5},... | collective-permute-start | bytes 196616 | tf_op jit(solution)/shard_map/ppermute | solution.py:437
  6.2 9.6 %collective-permute-start.25 = (bf16[16,2048]{1,0:T(8,128)(2,1)}, bf16[16,2048]{1,0:T(8,128)(2,1)S(1)}, u32[]{:S(2)}, u32[]{:S(2)}) collective-permute-start(bf16[16,2048]{1,0:T(8,128)(2,1)} %param.10), channel_id=1, source_target_pairs={{0,8},{1,9},{2,10},{3,11},{4,12},{5,13},{6,14},{7,15},{8,0},{9,1},... | collective-permute-start | bytes 196616 | tf_op jit(solution)/shard_map/ppermute | solution.py:437
  9.7 12.5 %collective-permute-start.9 = (bf16[16,2048]{1,0:T(8,128)(2,1)}, bf16[16,2048]{1,0:T(8,128)(2,1)S(1)}, u32[]{:S(2)}, u32[]{:S(2)}) collective-permute-start(bf16[16,2048]{1,0:T(8,128)(2,1)} %get-tuple-element.21), channel_id=1, source_target_pairs={{0,12},{1,13},{2,14},{3,15},{4,8},{5,9},{6,10},{7,11},{8,4},{9,5},... | collective-permute-start | bytes 196616 | tf_op jit(solution)/shard_map/ppermute | solution.py:437
  12.7 6.3 %collective-permute-start.8 = (bf16[16,2048]{1,0:T(8,128)(2,1)}, bf16[16,2048]{1,0:T(8,128)(2,1)S(1)}, u32[]{:S(2)}, u32[]{:S(2)}) collective-permute-start(bf16[16,2048]{1,0:T(8,128)(2,1)} %get-tuple-element.21), channel_id=1, source_target_pairs={{0,8},{1,9},{2,10},{3,11},{4,12},{5,13},{6,14},{7,15},{8,0},{9,1},... | collective-permute-start | bytes 196616 | tf_op jit(solution)/shard_map/ppermute | solution.py:437
  14.7 5.9 %collective-permute-start = (bf16[16,2048]{1,0:T(8,128)(2,1)}, bf16[16,2048]{1,0:T(8,128)(2,1)S(1)}, u32[]{:S(2)}, u32[]{:S(2)}) collective-permute-start(bf16[16,2048]{1,0:T(8,128)(2,1)} %get-tuple-element.21), channel_id=1, source_target_pairs={{0,4},{1,5},{2,6},{3,7},{4,0},{5,1},{6,2},{7,3},{8,12},{9,13},{10,... | collective-permute-start | bytes 196616 | tf_op jit(solution)/shard_map/ppermute | solution.py:437
  15.8 7.0 %collective-permute-start.21 = (bf16[32,2048]{1,0:T(8,128)(2,1)S(1)}, bf16[32,2048]{1,0:T(8,128)(2,1)S(1)}, u32[]{:S(2)}, u32[]{:S(2)}) collective-permute-start(bf16[32,2048]{1,0:T(8,128)(2,1)S(1)} %constant_dynamic-update-slice_fusion.4.refs_4_.refs_5_.refs_1_), channel_id=1, source_target_pairs={{16,0},{0,16},{17,1},{1,17},{18,2},{2,18},{19,3},{3,19},{20,4},{4,... | collective-permute-start | bytes 393224 | tf_op jit(solution)/shard_map/ppermute | solution.py:440
  19.0 5.0 %collective-permute-start.19 = (bf16[32,2048]{1,0:T(8,128)(2,1)S(1)}, bf16[32,2048]{1,0:T(8,128)(2,1)S(1)}, u32[]{:S(2)}, u32[]{:S(2)}) collective-permute-start(bf16[32,2048]{1,0:T(8,128)(2,1)S(1)} %constant_dynamic-update-slice_fusion.4.refs_4_.refs_5_.refs_1_), channel_id=1, source_target_pairs={{0,2},{1,3},{2,0},{3,1},{4,6},{5,7},{6,4},{7,5},{8,10},{9,11},{10,... | collective-permute-start | bytes 393224 | tf_op jit(solution)/shard_map/ppermute | solution.py:437
  20.5 5.0 %collective-permute-start.18 = (bf16[32,2048]{1,0:T(8,128)(2,1)S(1)}, bf16[32,2048]{1,0:T(8,128)(2,1)S(1)}, u32[]{:S(2)}, u32[]{:S(2)}) collective-permute-start(bf16[32,2048]{1,0:T(8,128)(2,1)S(1)} %constant_dynamic-update-slice_fusion.4.refs_4_.refs_5_.refs_1_), channel_id=1, source_target_pairs={{0,1},{1,0},{2,3},{3,2},{4,5},{5,4},{6,7},{7,6},{8,9},{9,8},{10,11... | collective-permute-start | bytes 393224 | tf_op jit(solution)/shard_map/ppermute | solution.py:437
  20.6 7.3 %collective-permute-start.30 = (bf16[32,2048]{1,0:T(8,128)(2,1)S(1)}, bf16[32,2048]{1,0:T(8,128)(2,1)S(1)}, u32[]{:S(2)}, u32[]{:S(2)}) collective-permute-start(bf16[32,2048]{1,0:T(8,128)(2,1)S(1)} %constant_dynamic-update-slice_fusion.6.refs_12_.refs_13_.refs_9_), channel_id=1, source_target_pairs={{16,0},{0,16},{17,1},{1,17},{18,2},{2,18},{19,3},{3,19},{20,4},{4,... | collective-permute-start | bytes 393224 | tf_op jit(solution)/shard_map/ppermute | solution.py:440
  22.2 6.4 %collective-permute-start.28 = (bf16[32,2048]{1,0:T(8,128)(2,1)S(1)}, bf16[32,2048]{1,0:T(8,128)(2,1)S(1)}, u32[]{:S(2)}, u32[]{:S(2)}) collective-permute-start(bf16[32,2048]{1,0:T(8,128)(2,1)S(1)} %constant_dynamic-update-slice_fusion.6.refs_12_.refs_13_.refs_9_), channel_id=1, source_target_pairs={{0,2},{1,3},{2,0},{3,1},{4,6},{5,7},{6,4},{7,5},{8,10},{9,11},{10,... | collective-permute-start | bytes 393224 | tf_op jit(solution)/shard_map/ppermute | solution.py:437
  22.8 6.2 %collective-permute-start.27 = (bf16[32,2048]{1,0:T(8,128)(2,1)S(1)}, bf16[32,2048]{1,0:T(8,128)(2,1)S(1)}, u32[]{:S(2)}, u32[]{:S(2)}) collective-permute-start(bf16[32,2048]{1,0:T(8,128)(2,1)S(1)} %constant_dynamic-update-slice_fusion.6.refs_12_.refs_13_.refs_9_), channel_id=1, source_target_pairs={{0,1},{1,0},{2,3},{3,2},{4,5},{5,4},{6,7},{7,6},{8,9},{9,8},{10,11... | collective-permute-start | bytes 393224 | tf_op jit(solution)/shard_map/ppermute | solution.py:437
  24.0 6.4 %collective-permute-start.4 = (bf16[32,2048]{1,0:T(8,128)(2,1)S(1)}, bf16[32,2048]{1,0:T(8,128)(2,1)S(1)}, u32[]{:S(2)}, u32[]{:S(2)}) collective-permute-start(bf16[32,2048]{1,0:T(8,128)(2,1)S(1)} %constant_dynamic-update-slice_fusion.refs_4_.refs_17_), channel_id=1, source_target_pairs={{16,0},{0,16},{17,1},{1,17},{18,2},{2,18},{19,3},{3,19},{20,4},{4,... | collective-permute-start | bytes 393224 | tf_op jit(solution)/shard_map/ppermute | solution.py:440
  25.5 6.0 %collective-permute-start.2 = (bf16[32,2048]{1,0:T(8,128)(2,1)S(1)}, bf16[32,2048]{1,0:T(8,128)(2,1)S(1)}, u32[]{:S(2)}, u32[]{:S(2)}) collective-permute-start(bf16[32,2048]{1,0:T(8,128)(2,1)S(1)} %constant_dynamic-update-slice_fusion.refs_4_.refs_17_), channel_id=1, source_target_pairs={{0,2},{1,3},{2,0},{3,1},{4,6},{5,7},{6,4},{7,5},{8,10},{9,11},{10,... | collective-permute-start | bytes 393224 | tf_op jit(solution)/shard_map/ppermute | solution.py:437
  28.0 6.1 %collective-permute-start.1 = (bf16[32,2048]{1,0:T(8,128)(2,1)S(1)}, bf16[32,2048]{1,0:T(8,128)(2,1)S(1)}, u32[]{:S(2)}, u32[]{:S(2)}) collective-permute-start(bf16[32,2048]{1,0:T(8,128)(2,1)S(1)} %constant_dynamic-update-slice_fusion.refs_4_.refs_17_), channel_id=1, source_target_pairs={{0,1},{1,0},{2,3},{3,2},{4,5},{5,4},{6,7},{7,6},{8,9},{9,8},{10,11... | collective-permute-start | bytes 393224 | tf_op jit(solution)/shard_map/ppermute | solution.py:437
  28.6 5.4 %collective-permute-start.13 = (bf16[32,2048]{1,0:T(8,128)(2,1)S(1)}, bf16[32,2048]{1,0:T(8,128)(2,1)S(1)}, u32[]{:S(2)}, u32[]{:S(2)}) collective-permute-start(bf16[32,2048]{1,0:T(8,128)(2,1)S(1)} %constant_dynamic-update-slice_fusion.2.refs_12_.refs_25_), channel_id=1, source_target_pairs={{16,0},{0,16},{17,1},{1,17},{18,2},{2,18},{19,3},{3,19},{20,4},{4,... | collective-permute-start | bytes 393224 | tf_op jit(solution)/shard_map/ppermute | solution.py:440
  29.1 5.8 %collective-permute-start.11 = (bf16[32,2048]{1,0:T(8,128)(2,1)S(1)}, bf16[32,2048]{1,0:T(8,128)(2,1)S(1)}, u32[]{:S(2)}, u32[]{:S(2)}) collective-permute-start(bf16[32,2048]{1,0:T(8,128)(2,1)S(1)} %constant_dynamic-update-slice_fusion.2.refs_12_.refs_25_), channel_id=1, source_target_pairs={{0,2},{1,3},{2,0},{3,1},{4,6},{5,7},{6,4},{7,5},{8,10},{9,11},{10,... | collective-permute-start | bytes 393224 | tf_op jit(solution)/shard_map/ppermute | solution.py:437
  31.6 5.4 %collective-permute-start.23 = (bf16[32,2048]{1,0:T(8,128)(2,1)S(1)}, bf16[32,2048]{1,0:T(8,128)(2,1)S(1)}, u32[]{:S(2)}, u32[]{:S(2)}) collective-permute-start(bf16[32,2048]{1,0:T(8,128)(2,1)S(1)} %collective-permute-done.21.refs_8_.refs_9_.refs_5_), channel_id=1, source_target_pairs={{0,2},{1,3},{2,0},{3,1},{4,6},{5,7},{6,4},{7,5},{8,10},{9,11},{10,... | collective-permute-start | bytes 393224 | tf_op jit(solution)/shard_map/ppermute | solution.py:437
  34.1 5.0 %collective-permute-start.20 = (bf16[32,2048]{1,0:T(8,128)(2,1)S(1)}, bf16[32,2048]{1,0:T(8,128)(2,1)S(1)}, u32[]{:S(2)}, u32[]{:S(2)}) collective-permute-start(bf16[32,2048]{1,0:T(8,128)(2,1)S(1)} %collective-permute-done.19.refs_6_.refs_7_.refs_3_), channel_id=1, source_target_pairs={{0,1},{1,0},{2,3},{3,2},{4,5},{5,4},{6,7},{7,6},{8,9},{9,8},{10,11... | collective-permute-start | bytes 393224 | tf_op jit(solution)/shard_map/ppermute | solution.py:437
  34.9 5.9 %collective-permute-start.32 = (bf16[32,2048]{1,0:T(8,128)(2,1)S(1)}, bf16[32,2048]{1,0:T(8,128)(2,1)S(1)}, u32[]{:S(2)}, u32[]{:S(2)}) collective-permute-start(bf16[32,2048]{1,0:T(8,128)(2,1)S(1)} %collective-permute-done.28.refs_14_.refs_15_.refs_11_), channel_id=1, source_target_pairs={{16,0},{0,16},{17,1},{1,17},{18,2},{2,18},{19,3},{3,19},{20,4},{4,... | collective-permute-start | bytes 393224 | tf_op jit(solution)/shard_map/ppermute | solution.py:440
  37.0 6.2 %collective-permute-start.6 = (bf16[32,2048]{1,0:T(8,128)(2,1)S(1)}, bf16[32,2048]{1,0:T(8,128)(2,1)S(1)}, u32[]{:S(2)}, u32[]{:S(2)}) collective-permute-start(bf16[32,2048]{1,0:T(8,128)(2,1)S(1)} %collective-permute-done.4.refs_8_.refs_21_), channel_id=1, source_target_pairs={{0,2},{1,3},{2,0},{3,1},{4,6},{5,7},{6,4},{7,5},{8,10},{9,11},{10,... | collective-permute-start | bytes 393224 | tf_op jit(solution)/shard_map/ppermute | solution.py:437
  39.3 5.9 %collective-permute-start.15 = (bf16[32,2048]{1,0:T(8,128)(2,1)S(1)}, bf16[32,2048]{1,0:T(8,128)(2,1)}, u32[]{:S(2)}, u32[]{:S(2)}) collective-permute-start(bf16[32,2048]{1,0:T(8,128)(2,1)S(1)} %collective-permute-done.11.refs_14_.refs_27_), channel_id=1, source_target_pairs={{16,0},{0,16},{17,1},{1,17},{18,2},{2,18},{19,3},{3,19},{20,4},{4,... | collective-permute-start | bytes 393224 | tf_op jit(solution)/shard_map/ppermute | solution.py:440
  40.8 4.8 %collective-permute-start.33 = (bf16[32,2048]{1,0:T(8,128)(2,1)S(1)}, bf16[32,2048]{1,0:T(8,128)(2,1)S(1)}, u32[]{:S(2)}, u32[]{:S(2)}) collective-permute-start(bf16[32,2048]{1,0:T(8,128)(2,1)S(1)} %collective-permute-done.32.refs_18_.refs_19_.refs_15_), channel_id=1, source_target_pairs={{0,1},{1,0},{2,3},{3,2},{4,5},{5,4},{6,7},{7,6},{8,9},{9,8},{10,11... | collective-permute-start | bytes 393224 | tf_op jit(solution)/shard_map/ppermute | solution.py:437
  43.2 13.9 %collective-permute-start.12 = (bf16[32,2048]{1,0:T(8,128)(2,1)S(1)}, bf16[32,2048]{1,0:T(8,128)(2,1)S(1)}, u32[]{:S(2)}, u32[]{:S(2)}) collective-permute-start(bf16[32,2048]{1,0:T(8,128)(2,1)S(1)} %collective-permute-done.11.refs_14_.refs_27_), channel_id=1, source_target_pairs={{0,1},{1,0},{2,3},{3,2},{4,5},{5,4},{6,7},{7,6},{8,9},{9,8},{10,11... | collective-permute-start | bytes 393224 | tf_op jit(solution)/shard_map/ppermute | solution.py:437
  43.2 13.8 %collective-permute-start.3 = (bf16[32,2048]{1,0:T(8,128)(2,1)S(1)}, bf16[32,2048]{1,0:T(8,128)(2,1)S(1)}, u32[]{:S(2)}, u32[]{:S(2)}) collective-permute-start(bf16[32,2048]{1,0:T(8,128)(2,1)S(1)} %collective-permute-done.2.refs_6_.refs_19_), channel_id=1, source_target_pairs={{0,1},{1,0},{2,3},{3,2},{4,5},{5,4},{6,7},{7,6},{8,9},{9,8},{10,11... | collective-permute-start | bytes 393224 | tf_op jit(solution)/shard_map/ppermute | solution.py:437
  45.1 11.9 %collective-permute-start.14 = (bf16[32,2048]{1,0:T(8,128)(2,1)S(1)}, bf16[32,2048]{1,0:T(8,128)(2,1)S(1)}, u32[]{:S(2)}, u32[]{:S(2)}) collective-permute-start(bf16[32,2048]{1,0:T(8,128)(2,1)S(1)} %collective-permute-done.13.refs_16_.refs_29_), channel_id=1, source_target_pairs={{0,1},{1,0},{2,3},{3,2},{4,5},{5,4},{6,7},{7,6},{8,9},{9,8},{10,11... | collective-permute-start | bytes 393224 | tf_op jit(solution)/shard_map/ppermute | solution.py:437
  45.1 11.9 %collective-permute-start.7 = (bf16[32,2048]{1,0:T(8,128)(2,1)S(1)}, bf16[32,2048]{1,0:T(8,128)(2,1)S(1)}, u32[]{:S(2)}, u32[]{:S(2)}) collective-permute-start(bf16[32,2048]{1,0:T(8,128)(2,1)S(1)} %collective-permute-done.6.refs_10_.refs_23_), channel_id=1, source_target_pairs={{0,1},{1,0},{2,3},{3,2},{4,5},{5,4},{6,7},{7,6},{8,9},{9,8},{10,11... | collective-permute-start | bytes 393224 | tf_op jit(solution)/shard_map/ppermute | solution.py:437
  45.6 11.4 %collective-permute-start.16 = (bf16[32,2048]{1,0:T(8,128)(2,1)}, bf16[32,2048]{1,0:T(8,128)(2,1)S(1)}, u32[]{:S(2)}, u32[]{:S(2)}) collective-permute-start(bf16[32,2048]{1,0:T(8,128)(2,1)} %collective-permute-done.15.refs_18_.refs_31_), channel_id=1, source_target_pairs={{0,1},{1,0},{2,3},{3,2},{4,5},{5,4},{6,7},{7,6},{8,9},{9,8},{10,11... | collective-permute-start | bytes 393224 | tf_op jit(solution)/shard_map/ppermute | solution.py:437
  72.1 10.1 %collective-permute-start.35 = (bf16[80,2048]{1,0:T(8,128)(2,1)S(1)}, bf16[80,2048]{1,0:T(8,128)(2,1)S(1)}, u32[]{:S(2)}, u32[]{:S(2)}) collective-permute-start(bf16[80,2048]{1,0:T(8,128)(2,1)S(1)} %slice.41), channel_id=1, source_target_pairs={{0,2},{1,3},{2,0},{3,1},{4,6},{5,7},{6,4},{7,5},{8,10},{9,11},{10,... | collective-permute-start | bytes 983048 | tf_op jit(solution)/shard_map/ppermute | solution.py:437
  82.3 11.7 %collective-permute-start.38 = (bf16[32,2048]{1,0:T(8,128)(2,1)S(1)}, bf16[32,2048]{1,0:T(8,128)(2,1)S(1)}, u32[]{:S(2)}, u32[]{:S(2)}) collective-permute-start(bf16[32,2048]{1,0:T(8,128)(2,1)S(1)} %get-tuple-element.45), channel_id=1, source_target_pairs={{0,12},{1,13},{2,14},{3,15},{4,8},{5,9},{6,10},{7,11},{8,4},{9,5},... | collective-permute-start | bytes 393224 | tf_op jit(solution)/shard_map/ppermute | solution.py:437
  84.7 10.2 %collective-permute-start.37 = (bf16[32,2048]{1,0:T(8,128)(2,1)S(1)}, bf16[32,2048]{1,0:T(8,128)(2,1)S(1)}, u32[]{:S(2)}, u32[]{:S(2)}) collective-permute-start(bf16[32,2048]{1,0:T(8,128)(2,1)S(1)} %get-tuple-element.46), channel_id=1, source_target_pairs={{0,8},{1,9},{2,10},{3,11},{4,12},{5,13},{6,14},{7,15},{8,0},{9,1},... | collective-permute-start | bytes 393224 | tf_op jit(solution)/shard_map/ppermute | solution.py:437
  84.7 10.2 %collective-permute-start.36 = (bf16[32,2048]{1,0:T(8,128)(2,1)S(1)}, bf16[32,2048]{1,0:T(8,128)(2,1)S(1)}, u32[]{:S(2)}, u32[]{:S(2)}) collective-permute-start(bf16[32,2048]{1,0:T(8,128)(2,1)S(1)} %get-tuple-element.47), channel_id=1, source_target_pairs={{0,4},{1,5},{2,6},{3,7},{4,0},{5,1},{6,2},{7,3},{8,12},{9,13},{10,... | collective-permute-start | bytes 393224 | tf_op jit(solution)/shard_map/ppermute | solution.py:437
  (41 other events, 521.7 us)

commit v3 on v2

v3 whole, which is shorter than its diff:
```python
import functools
import math

import jax
import jax.numpy as jnp
from jax import lax
from jax.experimental import pallas as pl
from jax.experimental.pallas import tpu as pltpu
from jax.sharding import PartitionSpec as P

STATE = 16
CONV = 4
LANES = 128
BLOCK = 256
TILE_ROWS = 16
VMEM_LIMIT = 60 * 1024 * 1024
f32 = jnp.float32
bf16 = jnp.bfloat16


def dot(a, b):
    return jnp.dot(a, b, preferred_element_type=f32)


def dot_nt(a, b):
    return lax.dot_general(a, b, (((1,), (1,)), ((), ())), preferred_element_type=f32)


def dot_tn(a, b):
    return lax.dot_general(a, b, (((0,), (0,)), ((), ())), preferred_element_type=f32)


def iota(shape, dim):
    return lax.broadcasted_iota(jnp.int32, shape, dim)


def mirror(size):
    return jnp.where(iota((size, size), 0) + iota((size, size), 1) == size - 1, 1.0, 0.0).astype(
        bf16
    )


def split(value, terms):
    parts = []
    for _ in range(terms):
        part = value.astype(bf16)
        parts.append(part)
        value = value - part.astype(f32)
    return parts


def flip_rows(value, flip):
    count = value.shape[0] // BLOCK
    return jnp.concatenate(
        [dot(flip, value[(count - 1 - i) * BLOCK : (count - i) * BLOCK]) for i in range(count)],
        axis=0,
    )


def assemble(ids_ref, pieces, h_ref, d_ref, layout):
    tp_size, own_rows, coords = layout
    z, x, core, ctx = (ids_ref[i] for i in range(4))
    ctx_size = max(c[0] for c in coords) + 1
    for piece, (dc, dx, dcore, blocks) in zip(pieces, coords):
        from_ctx = lax.rem(ctx + dc, ctx_size)
        for k, j in enumerate(blocks):
            owner = ((z ^ j) * 2 + (x ^ dx)) * 2 + (core ^ dcore)
            at = pl.multiple_of((from_ctx * tp_size + owner) * own_rows, own_rows)
            base = 2 * k * own_rows
            h_ref[pl.ds(at, own_rows), :] = piece[base : base + own_rows, :]
            if d_ref is not None:
                d_ref[pl.ds(at, own_rows), :] = piece[base + own_rows : base + 2 * own_rows, :]


def turn_columns(value, flip):
    count = value.shape[1] // BLOCK
    return jnp.concatenate(
        [dot(value[:, (count - 1 - i) * BLOCK : (count - i) * BLOCK], flip) for i in range(count)],
        axis=1,
    )


def prep_kernel(win_ref, wbct_ref, wdt_ref, wout_ref, conv_ref, *outs):
    wall_ref, wallt_ref, gall_ref, taps_ref = outs
    flip = mirror(BLOCK)
    width = win_ref.shape[0]
    head = wout_ref.shape[0]
    count = width // BLOCK
    shared = 2 * STATE + 1
    for i in range(count):
        cols = slice(i * BLOCK, (i + 1) * BLOCK)
        rows = jnp.concatenate(
            [
                wbct_ref[:, cols].astype(f32),
                wdt_ref[:, cols].astype(f32),
                jnp.zeros((LANES - shared, BLOCK), f32),
            ],
            axis=0,
        )
        block = win_ref[cols, :]
        wall_ref[cols, :LANES] = block
        wall_ref[cols, LANES : 2 * LANES] = jnp.transpose(rows).astype(bf16)
        wallt_ref[:LANES, cols] = jnp.transpose(block.astype(f32)).astype(bf16)
        wallt_ref[LANES : 2 * LANES, cols] = rows.astype(bf16)
        out = jnp.concatenate(
            [wout_ref[:, cols].astype(f32), jnp.zeros((LANES - head, BLOCK), f32)], axis=0
        )
        gall_ref[cols, :LANES] = jnp.transpose(out).astype(bf16)
    for i in range(count):
        cols = slice(i * BLOCK, (i + 1) * BLOCK)
        back = slice((count - 1 - i) * BLOCK, (count - i) * BLOCK)
        wall_ref[cols, 2 * LANES :] = dot(flip, wall_ref[back, : 2 * LANES]).astype(bf16)
        gall_ref[cols, LANES:] = dot(flip, gall_ref[back, :LANES]).astype(bf16)
        wallt_ref[2 * LANES :, cols] = dot(wallt_ref[: 2 * LANES, back], flip).astype(bf16)
    tap = iota((CONV, LANES - head), 0)
    taps_ref[:, :head] = conv_ref[...]
    taps_ref[:, head:] = jnp.where(tap == CONV - 1, 1.0, 0.0)


def pack_kernel(*refs):
    out_ref = refs[-1]
    at = 0
    for ref in refs[:-2]:
        out_ref[at : at + ref.shape[0], :] = ref[...]
        at += ref.shape[0]


def own_source(shape, dim, ids_ref, tp_size, own_rows):
    z, x, core, ctx = (ids_ref[i] for i in range(4))
    nz = tp_size // 4
    row = iota(shape, dim)
    block = row // own_rows
    j = block % nz
    dx = 1 - (block // nz) % 2
    dcore = 1 - block // (2 * nz)
    owner = ((z ^ j) * 2 + (x ^ dx)) * 2 + (core ^ dcore)
    return (ctx * tp_size + owner) * own_rows + row % own_rows


def exact(parts, apply):
    return sum(apply(part) for part in parts)


def decay_rate(par_refs):
    return -jnp.exp(jnp.full((1, LANES), par_refs[1][0], f32))


def core_kernel(n_pieces, layout, *refs):
    ids_ref, par_refs = refs[0], refs[1:4]
    pieces = refs[4 : 4 + n_pieces]
    wall_ref, wallt_ref, gall_ref, taps_ref = refs[4 + n_pieces : 8 + n_pieces]
    send_ref, keep_ref, gcat_ref, gated_ref = refs[8 + n_pieces : 12 + n_pieces]
    tp_size, own_rows, coords = layout
    if coords is None:
        h_ref, d_ref = pieces
    else:
        h_ref, d_ref = refs[12 + n_pieces :]
        assemble(ids_ref, pieces, h_ref, d_ref, layout)
    length, width = h_ref.shape
    chunks = length // BLOCK
    flip = mirror(BLOCK)
    bias, rate, skip = par_refs[0][0], decay_rate(par_refs), par_refs[2][0]
    lane = iota((1, LANES), 1)
    low = lane < LANES // 2
    causal = iota((BLOCK, BLOCK), 0) >= iota((BLOCK, BLOCK), 1)
    tri = jnp.where(causal, 1.0, 0.0).astype(bf16)
    row_at = iota((length, LANES), 0)

    proj = dot(h_ref[...], wall_ref[...])
    grads = dot(d_ref[...], gall_ref[...])
    turned = [proj[:, 2 * LANES : 3 * LANES].astype(bf16)]
    turned += split(proj[:, 3 * LANES :], 3) + split(grads[:, LANES:], 2)
    turned = flip_rows(jnp.concatenate(turned, axis=1), flip)
    turned = [turned[:, i * LANES : (i + 1) * LANES] for i in range(6)]
    strands = (
        (
            proj[:, :LANES].astype(bf16).astype(f32),
            proj[:, LANES : 2 * LANES],
            grads[:, :LANES],
        ),
        (turned[0], turned[1] + turned[2] + turned[3], turned[4] + turned[5]),
    )
    small = []
    for s, (xz, rest, grad_g) in enumerate(strands):
        pre = taps_ref[CONV - 1 : CONV, :] * xz
        for shift in range(1, CONV):
            moved = jnp.where(row_at >= shift, pltpu.roll(xz, shift, 0), 0.0)
            pre += taps_ref[CONV - 1 - shift : CONV - shift, :] * moved
        sig = jax.nn.sigmoid(pre)
        u = pre * sig
        slope = sig * (1.0 + pre * (1.0 - sig))
        u_other = pltpu.roll(u, LANES // 2, 1)
        raw = jnp.broadcast_to(rest[:, 2 * STATE : 2 * STATE + 1], (length, LANES)) + bias
        dt = jnp.maximum(raw, 0.0) + jnp.log1p(jnp.exp(-jnp.abs(raw)))
        b_all = jnp.where(lane < STATE, rest, 0.0)
        c_all = jnp.where(lane < STATE, pltpu.roll(rest, LANES - STATE, 1), 0.0)
        w_all = dt * u
        g_y = jnp.where(low, grad_g * u_other, 0.0)
        state = jnp.zeros((LANES, LANES), f32)
        saved, outs = [], []
        for c in range(chunks):
            rows = slice(c * BLOCK, (c + 1) * BLOCK)
            log_keep = dot(tri, jnp.concatenate(split(dt[rows] * rate, 3), axis=1))
            log_keep = (
                log_keep[:, :LANES] + log_keep[:, LANES : 2 * LANES] + log_keep[:, 2 * LANES :]
            )
            across = jnp.transpose(log_keep)[0:1, :]
            gap = jnp.concatenate([log_keep] * (BLOCK // LANES), axis=1) - across
            decay = jnp.exp(jnp.where(causal, gap, -jnp.inf))
            b_low, c_low = b_all[rows].astype(bf16), c_all[rows].astype(bf16)
            w_low = w_all[rows].astype(bf16)
            mixed = (dot_nt(c_low, b_low) * decay).astype(bf16)
            last = log_keep[BLOCK - 1 : BLOCK, :]
            enter = jnp.exp(log_keep)
            leave = jnp.exp(last - log_keep)
            b_left = (leave * b_all[rows]).astype(bf16)
            out = dot(mixed, w_low) + enter * dot(c_low, state.astype(bf16))
            before = state
            state = jnp.exp(last) * state + dot_tn(b_left, w_low)
            saved.append(
                (decay, mixed, b_low, c_low, w_low, b_left, enter, leave, last, before, state)
            )
            outs.append(out)
        out = jnp.concatenate(outs, axis=0)
        y = out + skip * u
        gated = jnp.where(low, y * u_other, 0.0).astype(bf16)
        g_gate = jnp.where(low, grad_g * y, 0.0)
        d_state = jnp.zeros((LANES, LANES), f32)
        d_w, g_b, g_c, g_a = [None] * chunks, [None] * chunks, [None] * chunks, [None] * chunks
        for c in reversed(range(chunks)):
            rows = slice(c * BLOCK, (c + 1) * BLOCK)
            decay, mixed, b_low, c_low, w_low, b_left, enter, leave, last, before, after = saved[c]
            gy = g_y[rows]
            gy_low = gy.astype(bf16)
            ds_low = d_state.astype(bf16)
            dw = dot_tn(mixed, gy_low) + dot(b_left, ds_low)
            d_scores = (dot_nt(gy_low, w_low) * decay).astype(bf16)
            g_c[c] = dot(d_scores, b_low) + enter * dot_nt(gy_low, before.astype(bf16))
            g_b[c] = dot_tn(d_scores, c_low) + leave * dot_nt(w_low, ds_low)
            d_log = jnp.sum(
                jnp.where(low, gy * outs[c] - w_all[rows] * dw, 0.0), axis=1, keepdims=True
            )
            at_end = jnp.sum(jnp.where(low, after * d_state, 0.0))
            d_log = jnp.broadcast_to(d_log, (BLOCK, LANES))
            d_sum = dot_tn(tri, jnp.concatenate(split(d_log, 2), axis=1))
            d_sum = d_sum[:, :LANES] + d_sum[:, LANES:] + at_end
            g_a[c] = rate * d_sum + jnp.sum(
                jnp.where(low, u[rows] * dw, 0.0), axis=1, keepdims=True
            )
            d_w[c] = dw
            carried = (enter * c_all[rows]).astype(bf16)
            d_state = jnp.exp(last) * d_state + dot_tn(carried, gy_low)
        d_w = jnp.concatenate(d_w, axis=0)
        g_b = jnp.concatenate(g_b, axis=0)
        g_c = jnp.concatenate(g_c, axis=0)
        g_raw = jnp.concatenate(g_a, axis=0) * jax.nn.sigmoid(raw)
        d_u = jnp.where(low, skip * g_y + dt * d_w, pltpu.roll(g_gate, LANES // 2, 1))
        d_pre = d_u * slope
        g_xz = taps_ref[CONV - 1 : CONV, :] * d_pre
        for shift in range(1, CONV):
            moved = jnp.where(
                row_at < length - shift, pltpu.roll(d_pre, length - shift, 0), 0.0
            )
            g_xz += taps_ref[CONV - 1 - shift : CONV - shift, :] * moved
        shared = jnp.where(lane < STATE, g_b, 0.0) + jnp.where(
            (lane >= STATE) & (lane < 2 * STATE), pltpu.roll(g_c, STATE, 1), 0.0
        )
        g_rest = shared + jnp.where(lane == 2 * STATE, g_raw, 0.0)
        result = jnp.concatenate([g_xz.astype(bf16), g_rest.astype(bf16), gated], axis=1)
        small.append(shared)
        if s == 1:
            result = flip_rows(result, flip).astype(bf16)
        gcat_ref[:, 2 * s * LANES : 2 * (s + 1) * LANES] = result[:, : 2 * LANES]
        gated_ref[:, s * LANES : (s + 1) * LANES] = result[:, 2 * LANES :]

    pair = small[0] + pltpu.roll(small[1], 2 * STATE, 1)
    shared_t = jnp.transpose(pair)[: 4 * STATE].astype(bf16)
    groups = width // length
    step = 4 * STATE // groups
    for i in range(groups):
        part = shared_t[i * step : (i + 1) * step, :]
        send_ref[0:step, i * length : (i + 1) * length] = part
        keep_ref[0:step, i * length : (i + 1) * length] = part.astype(f32)
    own = tp_size * own_rows
    source = own_source((own, length), 0, ids_ref, tp_size, own_rows)
    pick = jnp.where(source == iota((own, length), 1), 1.0, 0.0).astype(bf16)
    picked = dot(pick, gcat_ref[...]).astype(bf16)
    half = own // 2
    part = dot(picked, wallt_ref[...])
    send_ref[step:, :] = part[:half].astype(bf16)
    keep_ref[step:, :] = part[half:]


def weight_kernel(n_pieces, layout, scaling, *refs):
    ids_ref = refs[0]
    pieces = refs[1 : 1 + n_pieces]
    gcat_ref, gated_ref, dwin_ref, dwout_ref = refs[1 + n_pieces : 5 + n_pieces]
    if layout[2] is None:
        h_ref, d_ref = pieces
    else:
        h_ref, d_ref = refs[5 + n_pieces :]
        assemble(ids_ref, pieces, h_ref, d_ref, layout)
    flip = mirror(BLOCK)
    columns = h_ref.shape[1] // BLOCK
    head = dwout_ref.shape[0]
    g_f = gcat_ref[:, 0:LANES]
    g_r = gcat_ref[:, 2 * LANES : 3 * LANES]
    y_f = gated_ref[:, 0:LANES]
    y_r = gated_ref[:, LANES:]
    for i in range(columns):
        cols = slice(i * BLOCK, (i + 1) * BLOCK)
        back = slice((columns - 1 - i) * BLOCK, (columns - i) * BLOCK)
        turned = dot(h_ref[:, back], flip).astype(bf16)
        grad = dot_tn(g_f, h_ref[:, cols]) + dot_tn(g_r, turned)
        dwin_ref[cols, :] = jnp.transpose(grad * scaling)
        turned = dot(d_ref[:, back], flip).astype(bf16)
        grad = dot_tn(y_f, d_ref[:, cols]) + dot_tn(y_r, turned)
        dwout_ref[:, cols] = grad[:head] * scaling


def last_kernel(n_got, n_pieces, layout, scaling, *refs):
    ids_ref, own_ref = refs[:2]
    got_refs = refs[2 : 2 + n_got]
    pieces = refs[2 + n_got : 2 + n_got + n_pieces]
    refs = refs[2 + n_got + n_pieces :]
    dhid_ref, dwbct_ref = refs[:2]
    if layout[2] is None:
        h_ref = pieces[0]
    else:
        h_ref = refs[2]
        assemble(ids_ref, pieces, h_ref, None, layout)
    flip = mirror(BLOCK)
    length, width = h_ref.shape
    own_rows = layout[1]
    groups = width // length
    extra = 4 * STATE // groups
    total = own_ref[extra : extra + own_rows, :]
    for got in got_refs:
        total += got[extra : extra + own_rows, :].astype(f32)
    dhid_ref[...] = total.astype(bf16)
    sums = [own_ref[:extra, :].astype(bf16).astype(f32)]
    sums += [got[:extra, :].astype(f32) for got in got_refs]
    while len(sums) > 1:
        sums = [a + b for a, b in zip(sums[0::2], sums[1::2])]
    shared = sums[0].astype(bf16)
    shared = jnp.concatenate(
        [shared[:, i * length : (i + 1) * length] for i in range(groups)], axis=0
    )
    fwd = shared[: 2 * STATE]
    rev = turn_columns(shared[2 * STATE :], flip).astype(bf16)
    pairs = dot(jnp.concatenate([fwd, rev], axis=0), h_ref[...])
    turned = exact(split(pairs[2 * STATE :], 3), lambda part: turn_columns(part, flip))
    dwbct_ref[...] = (pairs[: 2 * STATE] + turned) * scaling


def spec(memory=pltpu.VMEM):
    return pl.BlockSpec(memory_space=memory)


def call(kernel, inputs, n_smem, outs, scratch, flops, moved):
    return pl.pallas_call(
        kernel,
        out_shape=outs,
        in_specs=[spec(pltpu.SMEM)] * n_smem + [spec()] * (len(inputs) - n_smem),
        out_specs=jax.tree.map(lambda _: spec(), outs),
        scratch_shapes=scratch,
        compiler_params=pltpu.CompilerParams(vmem_limit_bytes=VMEM_LIMIT),
        cost_estimate=pl.CostEstimate(flops=flops, bytes_accessed=moved, transcendentals=0),
    )(*inputs)


def shape(dims, dtype):
    return jax.ShapeDtypeStruct(dims, dtype)


def local(ctx_size, tp_size, hidden, w_in, w_bc, w_dt, dt_bias, a_log, d_skip, conv_w, w_out, d_out):
    own_rows, width = hidden.shape
    length = own_rows * tp_size * ctx_size
    head = w_out.shape[0]
    nz = tp_size // 4
    chunks = length // BLOCK
    t = lax.axis_index("tp")
    ids = jnp.stack([t >> 2, (t >> 1) & 1, t & 1, lax.axis_index("ctx")]).astype(jnp.int32)
    params = [dt_bias, a_log, d_skip]
    wall, wallt, gall, taps = call(
        prep_kernel,
        [w_in, w_bc.T, w_dt, w_out, conv_w],
        0,
        (
            shape((width, 4 * LANES), bf16),
            shape((4 * LANES, width), bf16),
            shape((width, 2 * LANES), bf16),
            shape((CONV, LANES), f32),
        ),
        [],
        6 * width * BLOCK * BLOCK,
        20 * width * LANES,
    )

    def across(value, flip_bits):
        return lax.ppermute(value, "tp", [(i, i ^ flip_bits) for i in range(tp_size)])

    def along(value, offset):
        return lax.ppermute(
            value, "ctx", [((i + offset) % ctx_size, i) for i in range(ctx_size)]
        )

    def pack(parts):
        rows = sum(part.shape[0] for part in parts)
        return pl.pallas_call(
            pack_kernel,
            out_shape=shape((rows, width), bf16),
            in_specs=[spec()] * len(parts) + [spec(pl.ANY)],
            out_specs=spec(),
        )(*parts, taps)

    def column(own, count):
        if count == 1:
            return [own]
        half = count // 2
        return column(own, half) + column(across(own, 4 * half), half)

    if own_rows % TILE_ROWS == 0:
        zs = column(jnp.concatenate([hidden, d_out], axis=0), nz)
        coords, pieces = [], []
        for g, blocks in enumerate([range(0, nz // 2), range(nz // 2, nz)]):
            parts = [zs[j] for j in blocks]
            chunk = pack(parts) if g else jnp.concatenate(parts, axis=0)
            beside = across(chunk, 2)
            plane = [((0, 0), chunk), ((0, 1), beside)]
            for dc in range(1, ctx_size):
                ahead = along(chunk, dc)
                diagonal = along(beside, dc) if g else across(ahead, 2)
                plane += [((dc, 0), ahead), ((dc, 1), diagonal)]
            for (dc, dx), piece in plane:
                coords += [(dc, dx, 0, tuple(blocks)), (dc, dx, 1, tuple(blocks))]
                pieces += [piece, across(piece, 1)]
        layout = (tp_size, own_rows, tuple(coords))
        rows = [pltpu.VMEM((length, width), bf16)]
    else:
        pieces = [lax.all_gather(a, ("ctx", "tp"), axis=0, tiled=True) for a in (hidden, d_out)]
        layout, rows = (tp_size, own_rows, None), []
    h_pieces = pieces if rows else pieces[:1]
    n_pieces = len(pieces)
    extra = 4 * STATE * length // width
    half = tp_size * own_rows // 2
    send, keep, gcat, gated = call(
        functools.partial(core_kernel, n_pieces, layout),
        [ids, *params, *pieces, wall, wallt, gall, taps],
        4,
        (
            shape((extra + half, width), bf16),
            shape((extra + half, width), f32),
            shape((length, 4 * LANES), bf16),
            shape((length, 2 * LANES), bf16),
        ),
        rows * 2,
        8 * length * width * BLOCK,
        8 * length * width,
    )
    scaling = 1.0 / math.sqrt(length)
    got = across(send, 1)
    d_w_in, d_w_out = call(
        functools.partial(weight_kernel, n_pieces, layout, scaling),
        [ids, *pieces, gcat, gated],
        1,
        (
            shape((width, LANES), f32),
            shape((head, width), f32),
        ),
        rows * 2,
        8 * length * width * BLOCK,
        8 * length * width,
    )
    quarter = half // 2
    summed = keep + got.astype(f32)
    send = summed[: extra + quarter].astype(bf16)
    keep = jnp.concatenate(
        [summed[:extra].astype(bf16).astype(f32), summed[extra + quarter :]], axis=0
    )
    summed = keep + across(send, 2).astype(f32)
    got = []
    for j in range(1, nz):
        at = extra + j * own_rows
        piece = jnp.concatenate([summed[:extra], summed[at : at + own_rows]], axis=0)
        got.append(across(piece.astype(bf16), 4 * j))
    d_hidden, d_w_bc = call(
        functools.partial(last_kernel, len(got), len(h_pieces), layout, scaling),
        [ids, summed[: extra + own_rows], *got, *h_pieces],
        1,
        (shape((own_rows, width), bf16), shape((2 * STATE, width), f32)),
        rows,
        2 * length * width * LANES,
        4 * length * width,
    )
    return (d_hidden, d_w_in, d_w_out, d_w_bc.T)


def solution(mesh):
    in_specs = (
        P(("ctx", "tp"), None),
        P(None, "tp"),
        P(),
        P("tp", None),
        P("tp"),
        P("tp"),
        P("tp"),
        P(None, "tp"),
        P("tp", None),
        P(("ctx", "tp"), None),
    )
    out_specs = (P(("ctx", "tp"), None), P(None, "tp"), P("tp", None), P())
    body = functools.partial(local, mesh.shape["ctx"], mesh.shape["tp"])
    return jax.shard_map(body, mesh=mesh, in_specs=in_specs, out_specs=out_specs, check_vma=False)
```

time: 100 us -> 87.4 us (0.87)
  starting transfers between devices: 35.9 us -> 23.7 us
  Pallas kernels: 32.4 us -> 29.4 us
  waiting for transfers between devices: 21.8 us -> 23.7 us
    ppermute x33 -> x19, starting transfers between devices: 28.6 us -> 19.4 us  [across(): lax.ppermute(value, 'tp', [(i, i ^ flip_bits) for i in range(tp_size)])]
    pallas_call x5 -> x4, Pallas kernels: 32.4 us -> 27.7 us  [call(): pl.pallas_call(kernel, out_shape=outs, in_specs=[spec(pltpu.SMEM)] * n_sm...]
    ppermute x6 -> x3, starting transfers between devices: 7.3 us -> 4.29 us  [along(): lax.ppermute(value, 'ctx', [((i + offset) % ctx_size, i) for i in range(c...]
    ppermute x33 -> x19, waiting for transfers between devices: 19.4 us -> 22.2 us  [across(): lax.ppermute(value, 'tp', [(i, i ^ flip_bits) for i in range(tp_size)])]
    pallas_call x0 -> x1, Pallas kernels: none -> 1.71 us  [pack(): pl.pallas_call(pack_kernel, out_shape=shape((rows, width), bf16), in_spec...]
    ppermute x6 -> x3, waiting for transfers between devices: 2.35 us -> 1.51 us  [along(): lax.ppermute(value, 'ctx', [((i + offset) % ctx_size, i) for i in range(c...]
    unnamed x72 -> x37, local copies, waits for them, and re-layouts: 3.74 us -> 3.59 us
  transfers between devices with their start and end apart: 39 -> 22, of which waited for: 12 -> 8; matrix products, arithmetic and copies ran while one was open for 3% -> 2% of each run, Pallas kernels for 18% -> 14%
where the time goes in v3:
time: 87.4 us; the launch traced here: 87.1 us
  Pallas kernels  29.4 us (34%)
  starting transfers between devices  23.7 us (27%)
  waiting for transfers between devices  23.7 us (27%)
  local copies, waits for them, and re-layouts  5.26 us (6%)
  between operations  2.87 us (3%)
  other arithmetic  2.17 us (2%)
    pallas_call x4, Pallas kernels, call(): pl.pallas_call(kernel, out_shape=outs, in_specs=[spec(pltpu.SMEM)] * n_sm...  27.7 us
    ppermute x19, waiting for transfers between devices, across(): lax.ppermute(value, 'tp', [(i, i ^ flip_bits) for i in range(tp_size)])  22.2 us
    ppermute x19, starting transfers between devices, across(): lax.ppermute(value, 'tp', [(i, i ^ flip_bits) for i in range(tp_size)])  19.4 us
    ppermute x3, starting transfers between devices, along(): lax.ppermute(value, 'ctx', [((i + offset) % ctx_size, i) for i in range(c...  4.29 us
    unnamed x37, local copies, waits for them, and re-layouts  3.59 us
  transfers between devices with their start and end apart: 22, of which 8 were waited for; matrix products, arithmetic and copies ran while one was open for 2% of the time, Pallas kernels for 14%

profile of v3, /device:TPU:0, one launch (start us, length us, event | category | flops | bytes accessed | tf_op | source)
XLA Modules:
  0.0 87.1 jit_solution(3773932301764994951)
XLA Ops:
  0.6 0.8 constant_dynamic-update-slice_fusion.1
  1.5 0.9 constant_dynamic-update-slice_fusion
  2.3 4.1 %collective-permute-start.8 = (bf16[32,2048]{1,0:T(8,128)(2,1)S(1)}, bf16[32,2048]{1,0:T(8,128)(2,1)S(1)}, u32[]{:S(2)}, u32[]{:S(2)}) collective-permute-start(bf16[32,2048]{1,0:T(8,128)(2,1)S(1)} %get-tuple-element.38), channel_id=1, source_target_pairs={{0,8},{1,9},{2,10},{3,11},{4,12},{5,13},{6,14},{7,15},{8,0},{9,1},... | collective-permute-start | bytes 393224 | tf_op jit(solution)/shard_map/ppermute | solution.py:401
  6.4 1.6 %collective-permute-start = (bf16[32,2048]{1,0:T(8,128)(2,1)S(1)}, bf16[32,2048]{1,0:T(8,128)(2,1)S(1)}, u32[]{:S(2)}, u32[]{:S(2)}) collective-permute-start(bf16[32,2048]{1,0:T(8,128)(2,1)S(1)} %get-tuple-element.38), channel_id=1, source_target_pairs={{0,4},{1,5},{2,6},{3,7},{4,0},{5,1},{6,2},{7,3},{8,12},{9,13},{10,... | collective-permute-start | bytes 393224 | tf_op jit(solution)/shard_map/ppermute | solution.py:401
  8.0 4.6 %shard_map.129 = (bf16[2048,512]{1,0:T(8,128)(2,1)}, bf16[512,2048]{1,0:T(8,128)(2,1)}, bf16[2048,256]{1,0:T(8,128)(2,1)}, f32[4,128]{1,0:T(4,128)}) custom-call(bf16[2048,128]{1,0:T(8,128)(2,1)} %win_ref.1, bf16[32,2048]{1,0:T(8,128)(2,1)} %bitcast.7, bf16[1,2048]{1,0:T(2,128)(2,1)} %wdt_ref.1, bf16[64,2048]{1,0:T(8,128)(2,1)} %wout_ref.1, f32[4,64]{1,0:T(4,128)} %conv_ref.1), custom_call_target="tpu_custom_call" | custom-call | flops 805306368 | bytes 5242880 | tf_op jit(solution)/shard_map/pallas_call | solution.py:361
  12.9 0.6 collective-permute-start.9
  13.5 1.6 %collective-permute-start.4 = (bf16[64,2048]{1,0:T(8,128)(2,1)S(1)}, bf16[64,2048]{1,0:T(8,128)(2,1)S(1)}, u32[]{:S(2)}, u32[]{:S(2)}) collective-permute-start(bf16[64,2048]{1,0:T(8,128)(2,1)S(1)} %constant_dynamic-update-slice_fusion.2.refs_4_.refs_5_.refs_1_), channel_id=1, source_target_pairs={{16,0},{0,16},{17,1},{1,17},{18,2},{2,18},{19,3},{3,19},{20,4},{4,... | collective-permute-start | bytes 786440 | tf_op jit(solution)/shard_map/ppermute | solution.py:404
  15.1 1.5 %collective-permute-start.2 = (bf16[64,2048]{1,0:T(8,128)(2,1)S(1)}, bf16[64,2048]{1,0:T(8,128)(2,1)S(1)}, u32[]{:S(2)}, u32[]{:S(2)}) collective-permute-start(bf16[64,2048]{1,0:T(8,128)(2,1)S(1)} %constant_dynamic-update-slice_fusion.2.refs_4_.refs_5_.refs_1_), channel_id=1, source_target_pairs={{0,2},{1,3},{2,0},{3,1},{4,6},{5,7},{6,4},{7,5},{8,10},{9,11},{10,... | collective-permute-start | bytes 786440 | tf_op jit(solution)/shard_map/ppermute | solution.py:401
  16.6 1.2 %collective-permute-done.9.refs_1_ = bf16[32,2048]{1,0:T(8,128)(2,1)S(1)} collective-permute-done((bf16[32,2048]{1,0:T(8,128)(2,1)S(1)}, bf16[32,2048]{1,0:T(8,128)(2,1)S(1)}, u32[]{:S(2)}, u32[]{:S(2)}) %collective-permute-start.9) | collective-permute-done | bytes 131104 | tf_op jit(solution)/shard_map/ppermute | solution.py:401
  17.8 0.7 copy-done.17
  18.5 1.7 %shard_map.130.refs_12_.refs_13_.refs_9_ = bf16[64,2048]{1,0:T(8,128)(2,1)} custom-call(bf16[32,2048]{1,0:T(8,128)(2,1)} %copy-done.16, bf16[32,2048]{1,0:T(8,128)(2,1)} %copy-done.17, f32[4,128]{1,0:T(4,128)} %get-tuple-element.16.refs_2_.refs_23_), custom_call_target="tpu_custom_call" | custom-call | tf_op jit(solution)/shard_map/pallas_call | solution.py:410
  20.2 1.5 %collective-permute-start.11 = (bf16[64,2048]{1,0:T(8,128)(2,1)}, bf16[64,2048]{1,0:T(8,128)(2,1)S(1)}, u32[]{:S(2)}, u32[]{:S(2)}) collective-permute-start(bf16[64,2048]{1,0:T(8,128)(2,1)} %shard_map.130.refs_12_.refs_13_.refs_9_), channel_id=1, source_target_pairs={{0,2},{1,3},{2,0},{3,1},{4,6},{5,7},{6,4},{7,5},{8,10},{9,11},{10,... | collective-permute-start | bytes 786440 | tf_op jit(solution)/shard_map/ppermute | solution.py:401
  21.7 1.5 %collective-permute-start.13 = (bf16[64,2048]{1,0:T(8,128)(2,1)}, bf16[64,2048]{1,0:T(8,128)(2,1)S(1)}, u32[]{:S(2)}, u32[]{:S(2)}) collective-permute-start(bf16[64,2048]{1,0:T(8,128)(2,1)} %shard_map.130.refs_12_.refs_13_.refs_9_), channel_id=1, source_target_pairs={{16,0},{0,16},{17,1},{1,17},{18,2},{2,18},{19,3},{3,19},{20,4},{4,... | collective-permute-start | bytes 786440 | tf_op jit(solution)/shard_map/ppermute | solution.py:404
  23.3 2.4 %collective-permute-start.6 = (bf16[64,2048]{1,0:T(8,128)(2,1)S(1)}, bf16[64,2048]{1,0:T(8,128)(2,1)S(1)}, u32[]{:S(2)}, u32[]{:S(2)}) collective-permute-start(bf16[64,2048]{1,0:T(8,128)(2,1)S(1)} %collective-permute-done.4.refs_8_.refs_9_.refs_5_), channel_id=1, source_target_pairs={{0,2},{1,3},{2,0},{3,1},{4,6},{5,7},{6,4},{7,5},{8,10},{9,11},{10,... | collective-permute-start | bytes 786440 | tf_op jit(solution)/shard_map/ppermute | solution.py:401
  25.6 4.0 %collective-permute-done.11.refs_14_.refs_15_.refs_11_ = bf16[64,2048]{1,0:T(8,128)(2,1)S(1)} collective-permute-done((bf16[64,2048]{1,0:T(8,128)(2,1)}, bf16[64,2048]{1,0:T(8,128)(2,1)S(1)}, u32[]{:S(2)}, u32[]{:S(2)}) %collective-permute-start.11) | collective-permute-done | bytes 262176 | tf_op jit(solution)/shard_map/ppermute | solution.py:401
  29.6 1.2 %collective-permute-start.15 = (bf16[64,2048]{1,0:T(8,128)(2,1)S(1)}, bf16[64,2048]{1,0:T(8,128)(2,1)S(1)}, u32[]{:S(2)}, u32[]{:S(2)}) collective-permute-start(bf16[64,2048]{1,0:T(8,128)(2,1)S(1)} %collective-permute-done.11.refs_14_.refs_15_.refs_11_), channel_id=1, source_target_pairs={{16,0},{0,16},{17,1},{1,17},{18,2},{2,18},{19,3},{3,19},{20,4},{4,... | collective-permute-start | bytes 786440 | tf_op jit(solution)/shard_map/ppermute | solution.py:404
  31.3 2.6 %collective-permute-done.6.refs_10_.refs_11_.refs_7_ = bf16[64,2048]{1,0:T(8,128)(2,1)S(1)} collective-permute-done((bf16[64,2048]{1,0:T(8,128)(2,1)S(1)}, bf16[64,2048]{1,0:T(8,128)(2,1)S(1)}, u32[]{:S(2)}, u32[]{:S(2)}) %collective-permute-start.6) | collective-permute-done | bytes 262176 | tf_op jit(solution)/shard_map/ppermute | solution.py:401
  34.5 1.5 %collective-permute-done.15.refs_18_.refs_19_.refs_15_ = bf16[64,2048]{1,0:T(8,128)(2,1)S(1)} collective-permute-done((bf16[64,2048]{1,0:T(8,128)(2,1)S(1)}, bf16[64,2048]{1,0:T(8,128)(2,1)S(1)}, u32[]{:S(2)}, u32[]{:S(2)}) %collective-permute-start.15) | collective-permute-done | bytes 262176 | tf_op jit(solution)/shard_map/ppermute | solution.py:404
  38.0 0.6 pad_add_fusion.refs_0_
  39.5 12.5 %shard_map.131 = (bf16[144,2048]{1,0:T(8,128)(2,1)}, f32[144,2048]{1,0:T(8,128)}, bf16[512,512]{1,0:T(8,128)(2,1)}, bf16[512,256]{1,0:T(8,128)(2,1)}) custom-call(s32[4]{0:T(128)} %pad_add_fusion.refs_0_, f32[1]{0:T(128)S(6)} %copy.17.refs_1_, f32[1]{0:T(128)S(6)} %copy.18.refs_2_, f32[1]{0:T(128)S(6)} %copy.19.refs_3_, bf16[64,2048]{1,0:T(8,128)(2,1)} %copy-done, ...), custom_call_target="tpu_custom_call" | custom-call | flops 2147483648 | bytes 8388608 | tf_op jit(solution)/shard_map/pallas_call | solution.py:361
  52.6 1.8 %collective-permute-done.17 = bf16[144,2048]{1,0:T(8,128)(2,1)S(1)} collective-permute-done((bf16[144,2048]{1,0:T(8,128)(2,1)}, bf16[144,2048]{1,0:T(8,128)(2,1)S(1)}, u32[]{:S(2)}, u32[]{:S(2)}) %collective-permute-start.17) | collective-permute-done | bytes 589856 | tf_op jit(solution)/shard_map/ppermute | solution.py:401
  54.4 1.4 %fusion.1 = (bf16[144,2048]{1,0:T(8,128)(2,1)S(1)}, f32[144,2048]{1,0:T(8,128)S(1)}) fusion(f32[144,2048]{1,0:T(8,128)} %get-tuple-element.20, bf16[144,2048]{1,0:T(8,128)(2,1)S(1)} %collective-permute-done.17), kind=kLoop, calls=%fused_computation.14 | loop fusion | flops 884736 | bytes 3538944 | tf_op jit(solution)/shard_map/convert.10
  55.9 1.7 %collective-permute-start.18 = (bf16[80,2048]{1,0:T(8,128)(2,1)S(1)}, bf16[80,2048]{1,0:T(8,128)(2,1)S(1)}, u32[]{:S(2)}, u32[]{:S(2)}) collective-permute-start(bf16[80,2048]{1,0:T(8,128)(2,1)S(1)} %slice.41), channel_id=1, source_target_pairs={{0,2},{1,3},{2,0},{3,1},{4,6},{5,7},{6,4},{7,5},{8,10},{9,11},{10,... | collective-permute-start | bytes 983048 | tf_op jit(solution)/shard_map/ppermute | solution.py:401
  57.6 8.3 %collective-permute-done.18 = bf16[80,2048]{1,0:T(8,128)(2,1)S(1)} collective-permute-done((bf16[80,2048]{1,0:T(8,128)(2,1)S(1)}, bf16[80,2048]{1,0:T(8,128)(2,1)S(1)}, u32[]{:S(2)}, u32[]{:S(2)}) %collective-permute-start.18) | collective-permute-done | bytes 327712 | tf_op jit(solution)/shard_map/ppermute | solution.py:401
  66.2 3.7 %collective-permute-start.21 = (bf16[32,2048]{1,0:T(8,128)(2,1)S(1)}, bf16[32,2048]{1,0:T(8,128)(2,1)S(1)}, u32[]{:S(2)}, u32[]{:S(2)}) collective-permute-start(bf16[32,2048]{1,0:T(8,128)(2,1)S(1)} %get-tuple-element.35), channel_id=1, source_target_pairs={{0,12},{1,13},{2,14},{3,15},{4,8},{5,9},{6,10},{7,11},{8,4},{9,5},... | collective-permute-start | bytes 393224 | tf_op jit(solution)/shard_map/ppermute | solution.py:401
  69.9 0.7 collective-permute-start.19
  70.6 6.2 %shard_map.133 = (f32[2048,128]{1,0:T(8,128)}, f32[64,2048]{1,0:T(8,128)}) custom-call(s32[4]{0:T(128)} %pad_add_fusion.refs_0_, bf16[64,2048]{1,0:T(8,128)(2,1)} %copy-done, bf16[64,2048]{1,0:T(8,128)(2,1)} %copy-done.3, bf16[64,2048]{1,0:T(8,128)(2,1)} %copy-done.2, bf16[64,2048]{1,0:T(8,128)(2,1)} %copy-done.10, bf16[64,2048]{1,0:T(8,128)(2,1)} %copy-done.1, ...), custom_call_target="tpu_custom_call" | custom-call | flops 2147483648 | bytes 8388608 | tf_op jit(solution)/shard_map/pallas_call | solution.py:361
  76.8 0.7 slice.42.refs_1_
  77.5 3.9 %collective-permute-done.20.refs_3_ = bf16[32,2048]{1,0:T(8,128)(2,1)S(1)} collective-permute-done((bf16[32,2048]{1,0:T(8,128)(2,1)S(1)}, bf16[32,2048]{1,0:T(8,128)(2,1)S(1)}, u32[]{:S(2)}, u32[]{:S(2)}) %collective-permute-start.20) | collective-permute-done | bytes 131104 | tf_op jit(solution)/shard_map/ppermute | solution.py:401
  81.4 0.6 copy-done.14
  82.1 0.6 copy-done.15
  82.7 4.4 %shard_map.132 = (bf16[16,2048]{1,0:T(8,128)(2,1)}, f32[32,2048]{1,0:T(8,128)}) custom-call(s32[4]{0:T(128)} %pad_add_fusion.refs_0_, f32[32,2048]{1,0:T(8,128)} %slice.42.refs_1_, bf16[32,2048]{1,0:T(8,128)(2,1)} %copy-done.15, bf16[32,2048]{1,0:T(8,128)(2,1)} %copy-done.14, bf16[32,2048]{1,0:T(8,128)(2,1)} %copy-done.13, bf16[64,2048]{1,0:T(8,128)(2,1)} %copy-done, ...), custom_call_target="tpu_custom_call" | custom-call | flops 268435456 | bytes 4194304 | tf_op jit(solution)/shard_map/pallas_call | solution.py:361
  (66 shorter events, 2.8 us)
Async XLA Ops:
  2.3 10.5 %collective-permute-start.8 = (bf16[32,2048]{1,0:T(8,128)(2,1)S(1)}, bf16[32,2048]{1,0:T(8,128)(2,1)S(1)}, u32[]{:S(2)}, u32[]{:S(2)}) collective-permute-start(bf16[32,2048]{1,0:T(8,128)(2,1)S(1)} %get-tuple-element.38), channel_id=1, source_target_pairs={{0,8},{1,9},{2,10},{3,11},{4,12},{5,13},{6,14},{7,15},{8,0},{9,1},... | collective-permute-start | bytes 393224 | tf_op jit(solution)/shard_map/ppermute | solution.py:401
  6.4 7.0 %collective-permute-start = (bf16[32,2048]{1,0:T(8,128)(2,1)S(1)}, bf16[32,2048]{1,0:T(8,128)(2,1)S(1)}, u32[]{:S(2)}, u32[]{:S(2)}) collective-permute-start(bf16[32,2048]{1,0:T(8,128)(2,1)S(1)} %get-tuple-element.38), channel_id=1, source_target_pairs={{0,4},{1,5},{2,6},{3,7},{4,0},{5,1},{6,2},{7,3},{8,12},{9,13},{10,... | collective-permute-start | bytes 393224 | tf_op jit(solution)/shard_map/ppermute | solution.py:401
  12.9 5.0 %copy-start.16 = (bf16[32,2048]{1,0:T(8,128)(2,1)}, bf16[32,2048]{1,0:T(8,128)(2,1)S(1)}, u32[]{:S(2)}) copy-start(bf16[32,2048]{1,0:T(8,128)(2,1)S(1)} %collective-permute-done.8.refs_0_) | copy-start | bytes 393220
  12.9 5.0 %collective-permute-start.9 = (bf16[32,2048]{1,0:T(8,128)(2,1)S(1)}, bf16[32,2048]{1,0:T(8,128)(2,1)S(1)}, u32[]{:S(2)}, u32[]{:S(2)}) collective-permute-start(bf16[32,2048]{1,0:T(8,128)(2,1)S(1)} %collective-permute-done.8.refs_0_), channel_id=1, source_target_pairs={{0,4},{1,5},{2,6},{3,7},{4,0},{5,1},{6,2},{7,3},{8,12},{9,13},{10,... | collective-permute-start | bytes 393224 | tf_op jit(solution)/shard_map/ppermute | solution.py:401
  13.5 25.1 %copy-start = (bf16[64,2048]{1,0:T(8,128)(2,1)}, bf16[64,2048]{1,0:T(8,128)(2,1)S(1)}, u32[]{:S(2)}) copy-start(bf16[64,2048]{1,0:T(8,128)(2,1)S(1)} %constant_dynamic-update-slice_fusion.2.refs_4_.refs_5_.refs_1_) | copy-start | bytes 786436
  13.5 9.8 %collective-permute-start.4 = (bf16[64,2048]{1,0:T(8,128)(2,1)S(1)}, bf16[64,2048]{1,0:T(8,128)(2,1)S(1)}, u32[]{:S(2)}, u32[]{:S(2)}) collective-permute-start(bf16[64,2048]{1,0:T(8,128)(2,1)S(1)} %constant_dynamic-update-slice_fusion.2.refs_4_.refs_5_.refs_1_), channel_id=1, source_target_pairs={{16,0},{0,16},{17,1},{1,17},{18,2},{2,18},{19,3},{3,19},{20,4},{4,... | collective-permute-start | bytes 786440 | tf_op jit(solution)/shard_map/ppermute | solution.py:404
  15.1 8.2 %collective-permute-start.2 = (bf16[64,2048]{1,0:T(8,128)(2,1)S(1)}, bf16[64,2048]{1,0:T(8,128)(2,1)S(1)}, u32[]{:S(2)}, u32[]{:S(2)}) collective-permute-start(bf16[64,2048]{1,0:T(8,128)(2,1)S(1)} %constant_dynamic-update-slice_fusion.2.refs_4_.refs_5_.refs_1_), channel_id=1, source_target_pairs={{0,2},{1,3},{2,0},{3,1},{4,6},{5,7},{6,4},{7,5},{8,10},{9,11},{10,... | collective-permute-start | bytes 786440 | tf_op jit(solution)/shard_map/ppermute | solution.py:401
  16.6 9.1 %collective-permute-start.1 = (bf16[64,2048]{1,0:T(8,128)(2,1)S(1)}, bf16[64,2048]{1,0:T(8,128)(2,1)S(1)}, u32[]{:S(2)}, u32[]{:S(2)}) collective-permute-start(bf16[64,2048]{1,0:T(8,128)(2,1)S(1)} %constant_dynamic-update-slice_fusion.2.refs_4_.refs_5_.refs_1_), channel_id=1, source_target_pairs={{0,1},{1,0},{2,3},{3,2},{4,5},{5,4},{6,7},{7,6},{8,9},{9,8},{10,11... | collective-permute-start | bytes 786440 | tf_op jit(solution)/shard_map/ppermute | solution.py:401
  20.2 9.5 %collective-permute-start.11 = (bf16[64,2048]{1,0:T(8,128)(2,1)}, bf16[64,2048]{1,0:T(8,128)(2,1)S(1)}, u32[]{:S(2)}, u32[]{:S(2)}) collective-permute-start(bf16[64,2048]{1,0:T(8,128)(2,1)} %shard_map.130.refs_12_.refs_13_.refs_9_), channel_id=1, source_target_pairs={{0,2},{1,3},{2,0},{3,1},{4,6},{5,7},{6,4},{7,5},{8,10},{9,11},{10,... | collective-permute-start | bytes 786440 | tf_op jit(solution)/shard_map/ppermute | solution.py:401
  21.7 9.1 %collective-permute-start.13 = (bf16[64,2048]{1,0:T(8,128)(2,1)}, bf16[64,2048]{1,0:T(8,128)(2,1)S(1)}, u32[]{:S(2)}, u32[]{:S(2)}) collective-permute-start(bf16[64,2048]{1,0:T(8,128)(2,1)} %shard_map.130.refs_12_.refs_13_.refs_9_), channel_id=1, source_target_pairs={{16,0},{0,16},{17,1},{1,17},{18,2},{2,18},{19,3},{3,19},{20,4},{4,... | collective-permute-start | bytes 786440 | tf_op jit(solution)/shard_map/ppermute | solution.py:404
  23.2 15.4 %copy-start.1 = (bf16[64,2048]{1,0:T(8,128)(2,1)}, bf16[64,2048]{1,0:T(8,128)(2,1)S(1)}, u32[]{:S(2)}) copy-start(bf16[64,2048]{1,0:T(8,128)(2,1)S(1)} %collective-permute-done.4.refs_8_.refs_9_.refs_5_) | copy-start | bytes 786436
  23.2 7.6 %collective-permute-start.10 = (bf16[64,2048]{1,0:T(8,128)(2,1)}, bf16[64,2048]{1,0:T(8,128)(2,1)S(1)}, u32[]{:S(2)}, u32[]{:S(2)}) collective-permute-start(bf16[64,2048]{1,0:T(8,128)(2,1)} %shard_map.130.refs_12_.refs_13_.refs_9_), channel_id=1, source_target_pairs={{0,1},{1,0},{2,3},{3,2},{4,5},{5,4},{6,7},{7,6},{8,9},{9,8},{10,11... | collective-permute-start | bytes 786440 | tf_op jit(solution)/shard_map/ppermute | solution.py:401
  23.3 15.4 %copy-start.2 = (bf16[64,2048]{1,0:T(8,128)(2,1)}, bf16[64,2048]{1,0:T(8,128)(2,1)S(1)}, u32[]{:S(2)}) copy-start(bf16[64,2048]{1,0:T(8,128)(2,1)S(1)} %collective-permute-done.2.refs_6_.refs_7_.refs_3_) | copy-start | bytes 786436
  23.3 10.7 %collective-permute-start.6 = (bf16[64,2048]{1,0:T(8,128)(2,1)S(1)}, bf16[64,2048]{1,0:T(8,128)(2,1)S(1)}, u32[]{:S(2)}, u32[]{:S(2)}) collective-permute-start(bf16[64,2048]{1,0:T(8,128)(2,1)S(1)} %collective-permute-done.4.refs_8_.refs_9_.refs_5_), channel_id=1, source_target_pairs={{0,2},{1,3},{2,0},{3,1},{4,6},{5,7},{6,4},{7,5},{8,10},{9,11},{10,... | collective-permute-start | bytes 786440 | tf_op jit(solution)/shard_map/ppermute | solution.py:401
  25.6 13.0 %copy-start.3 = (bf16[64,2048]{1,0:T(8,128)(2,1)}, bf16[64,2048]{1,0:T(8,128)(2,1)S(1)}, u32[]{:S(2)}) copy-start(bf16[64,2048]{1,0:T(8,128)(2,1)S(1)} %collective-permute-done.1.refs_5_.refs_6_.refs_2_) | copy-start | bytes 786436
  25.6 8.4 %collective-permute-start.5 = (bf16[64,2048]{1,0:T(8,128)(2,1)S(1)}, bf16[64,2048]{1,0:T(8,128)(2,1)S(1)}, u32[]{:S(2)}, u32[]{:S(2)}) collective-permute-start(bf16[64,2048]{1,0:T(8,128)(2,1)S(1)} %collective-permute-done.4.refs_8_.refs_9_.refs_5_), channel_id=1, source_target_pairs={{0,1},{1,0},{2,3},{3,2},{4,5},{5,4},{6,7},{7,6},{8,9},{9,8},{10,11... | collective-permute-start | bytes 786440 | tf_op jit(solution)/shard_map/ppermute | solution.py:401
  29.6 9.0 %copy-start.4 = (bf16[64,2048]{1,0:T(8,128)(2,1)}, bf16[64,2048]{1,0:T(8,128)(2,1)S(1)}, u32[]{:S(2)}) copy-start(bf16[64,2048]{1,0:T(8,128)(2,1)S(1)} %collective-permute-done.11.refs_14_.refs_15_.refs_11_) | copy-start | bytes 786436
  29.6 6.4 %collective-permute-start.15 = (bf16[64,2048]{1,0:T(8,128)(2,1)S(1)}, bf16[64,2048]{1,0:T(8,128)(2,1)S(1)}, u32[]{:S(2)}, u32[]{:S(2)}) collective-permute-start(bf16[64,2048]{1,0:T(8,128)(2,1)S(1)} %collective-permute-done.11.refs_14_.refs_15_.refs_11_), channel_id=1, source_target_pairs={{16,0},{0,16},{17,1},{1,17},{18,2},{2,18},{19,3},{3,19},{20,4},{4,... | collective-permute-start | bytes 786440 | tf_op jit(solution)/shard_map/ppermute | solution.py:404
  30.8 7.9 %copy-start.5 = (bf16[64,2048]{1,0:T(8,128)(2,1)}, bf16[64,2048]{1,0:T(8,128)(2,1)S(1)}, u32[]{:S(2)}) copy-start(bf16[64,2048]{1,0:T(8,128)(2,1)S(1)} %collective-permute-done.13.refs_16_.refs_17_.refs_13_) | copy-start | bytes 786436
  30.8 7.7 %collective-permute-start.3 = (bf16[64,2048]{1,0:T(8,128)(2,1)S(1)}, bf16[64,2048]{1,0:T(8,128)(2,1)S(1)}, u32[]{:S(2)}, u32[]{:S(2)}) collective-permute-start(bf16[64,2048]{1,0:T(8,128)(2,1)S(1)} %collective-permute-done.2.refs_6_.refs_7_.refs_3_), channel_id=1, source_target_pairs={{0,1},{1,0},{2,3},{3,2},{4,5},{5,4},{6,7},{7,6},{8,9},{9,8},{10,11... | collective-permute-start | bytes 786440 | tf_op jit(solution)/shard_map/ppermute | solution.py:401
  30.8 7.8 %copy-start.6 = (bf16[64,2048]{1,0:T(8,128)(2,1)}, bf16[64,2048]{1,0:T(8,128)(2,1)S(1)}, u32[]{:S(2)}) copy-start(bf16[64,2048]{1,0:T(8,128)(2,1)S(1)} %collective-permute-done.10.refs_13_.refs_14_.refs_10_) | copy-start | bytes 786436
  30.9 7.7 %collective-permute-start.12 = (bf16[64,2048]{1,0:T(8,128)(2,1)S(1)}, bf16[64,2048]{1,0:T(8,128)(2,1)S(1)}, u32[]{:S(2)}, u32[]{:S(2)}) collective-permute-start(bf16[64,2048]{1,0:T(8,128)(2,1)S(1)} %collective-permute-done.11.refs_14_.refs_15_.refs_11_), channel_id=1, source_target_pairs={{0,1},{1,0},{2,3},{3,2},{4,5},{5,4},{6,7},{7,6},{8,9},{9,8},{10,11... | collective-permute-start | bytes 786440 | tf_op jit(solution)/shard_map/ppermute | solution.py:401
  34.0 4.7 %copy-start.7 = (bf16[64,2048]{1,0:T(8,128)(2,1)}, bf16[64,2048]{1,0:T(8,128)(2,1)S(1)}, u32[]{:S(2)}) copy-start(bf16[64,2048]{1,0:T(8,128)(2,1)S(1)} %collective-permute-done.6.refs_10_.refs_11_.refs_7_) | copy-start | bytes 786436
  34.0 4.6 %collective-permute-start.14 = (bf16[64,2048]{1,0:T(8,128)(2,1)S(1)}, bf16[64,2048]{1,0:T(8,128)(2,1)S(1)}, u32[]{:S(2)}, u32[]{:S(2)}) collective-permute-start(bf16[64,2048]{1,0:T(8,128)(2,1)S(1)} %collective-permute-done.13.refs_16_.refs_17_.refs_13_), channel_id=1, source_target_pairs={{0,1},{1,0},{2,3},{3,2},{4,5},{5,4},{6,7},{7,6},{8,9},{9,8},{10,11... | collective-permute-start | bytes 786440 | tf_op jit(solution)/shard_map/ppermute | solution.py:401
  34.0 4.7 %copy-start.8 = (bf16[64,2048]{1,0:T(8,128)(2,1)}, bf16[64,2048]{1,0:T(8,128)(2,1)S(1)}, u32[]{:S(2)}) copy-start(bf16[64,2048]{1,0:T(8,128)(2,1)S(1)} %collective-permute-done.5.refs_9_.refs_10_.refs_6_) | copy-start | bytes 786436
  34.0 4.6 %collective-permute-start.7 = (bf16[64,2048]{1,0:T(8,128)(2,1)S(1)}, bf16[64,2048]{1,0:T(8,128)(2,1)}, u32[]{:S(2)}, u32[]{:S(2)}) collective-permute-start(bf16[64,2048]{1,0:T(8,128)(2,1)S(1)} %collective-permute-done.6.refs_10_.refs_11_.refs_7_), channel_id=1, source_target_pairs={{0,1},{1,0},{2,3},{3,2},{4,5},{5,4},{6,7},{7,6},{8,9},{9,8},{10,11... | collective-permute-start | bytes 786440 | tf_op jit(solution)/shard_map/ppermute | solution.py:401
  36.0 2.6 %collective-permute-start.16 = (bf16[64,2048]{1,0:T(8,128)(2,1)S(1)}, bf16[64,2048]{1,0:T(8,128)(2,1)}, u32[]{:S(2)}, u32[]{:S(2)}) collective-permute-start(bf16[64,2048]{1,0:T(8,128)(2,1)S(1)} %collective-permute-done.15.refs_18_.refs_19_.refs_15_), channel_id=1, source_target_pairs={{0,1},{1,0},{2,3},{3,2},{4,5},{5,4},{6,7},{7,6},{8,9},{9,8},{10,11... | collective-permute-start | bytes 786440 | tf_op jit(solution)/shard_map/ppermute | solution.py:401
  52.0 2.4 %collective-permute-start.17 = (bf16[144,2048]{1,0:T(8,128)(2,1)}, bf16[144,2048]{1,0:T(8,128)(2,1)S(1)}, u32[]{:S(2)}, u32[]{:S(2)}) collective-permute-start(bf16[144,2048]{1,0:T(8,128)(2,1)} %get-tuple-element.21), channel_id=1, source_target_pairs={{0,1},{1,0},{2,3},{3,2},{4,5},{5,4},{6,7},{7,6},{8,9},{9,8},{10,11... | collective-permute-start | bytes 1769480 | tf_op jit(solution)/shard_map/ppermute | solution.py:401
  55.9 10.1 %collective-permute-start.18 = (bf16[80,2048]{1,0:T(8,128)(2,1)S(1)}, bf16[80,2048]{1,0:T(8,128)(2,1)S(1)}, u32[]{:S(2)}, u32[]{:S(2)}) collective-permute-start(bf16[80,2048]{1,0:T(8,128)(2,1)S(1)} %slice.41), channel_id=1, source_target_pairs={{0,2},{1,3},{2,0},{3,1},{4,6},{5,7},{6,4},{7,5},{8,10},{9,11},{10,... | collective-permute-start | bytes 983048 | tf_op jit(solution)/shard_map/ppermute | solution.py:401
  66.2 11.4 %collective-permute-start.21 = (bf16[32,2048]{1,0:T(8,128)(2,1)S(1)}, bf16[32,2048]{1,0:T(8,128)(2,1)S(1)}, u32[]{:S(2)}, u32[]{:S(2)}) collective-permute-start(bf16[32,2048]{1,0:T(8,128)(2,1)S(1)} %get-tuple-element.35), channel_id=1, source_target_pairs={{0,12},{1,13},{2,14},{3,15},{4,8},{5,9},{6,10},{7,11},{8,4},{9,5},... | collective-permute-start | bytes 393224 | tf_op jit(solution)/shard_map/ppermute | solution.py:401
  69.9 11.5 %collective-permute-start.20 = (bf16[32,2048]{1,0:T(8,128)(2,1)S(1)}, bf16[32,2048]{1,0:T(8,128)(2,1)S(1)}, u32[]{:S(2)}, u32[]{:S(2)}) collective-permute-start(bf16[32,2048]{1,0:T(8,128)(2,1)S(1)} %get-tuple-element.36), channel_id=1, source_target_pairs={{0,8},{1,9},{2,10},{3,11},{4,12},{5,13},{6,14},{7,15},{8,0},{9,1},... | collective-permute-start | bytes 393224 | tf_op jit(solution)/shard_map/ppermute | solution.py:401
  69.9 11.5 %collective-permute-start.19 = (bf16[32,2048]{1,0:T(8,128)(2,1)S(1)}, bf16[32,2048]{1,0:T(8,128)(2,1)S(1)}, u32[]{:S(2)}, u32[]{:S(2)}) collective-permute-start(bf16[32,2048]{1,0:T(8,128)(2,1)S(1)} %get-tuple-element.37), channel_id=1, source_target_pairs={{0,4},{1,5},{2,6},{3,7},{4,0},{5,1},{6,2},{7,3},{8,12},{9,13},{10,... | collective-permute-start | bytes 393224 | tf_op jit(solution)/shard_map/ppermute | solution.py:401
  (8 other events, 10.9 us)

commit v4 on v3

--- a/solution.py
+++ b/solution.py
@@ -13,7 +13,6 @@
 LANES = 128
 BLOCK = 256
 TILE_ROWS = 16
-VMEM_LIMIT = 60 * 1024 * 1024
 f32 = jnp.float32
 bf16 = jnp.bfloat16
 
@@ -57,19 +56,50 @@
     )
 
 
-def assemble(ids_ref, pieces, h_ref, d_ref, layout):
+def owners(ids_ref, layout):
     tp_size, own_rows, coords = layout
     z, x, core, ctx = (ids_ref[i] for i in range(4))
     ctx_size = max(c[0] for c in coords) + 1
-    for piece, (dc, dx, dcore, blocks) in zip(pieces, coords):
+    for p, (dc, dx, dcore, blocks) in enumerate(coords):
         from_ctx = lax.rem(ctx + dc, ctx_size)
         for k, j in enumerate(blocks):
             owner = ((z ^ j) * 2 + (x ^ dx)) * 2 + (core ^ dcore)
             at = pl.multiple_of((from_ctx * tp_size + owner) * own_rows, own_rows)
-            base = 2 * k * own_rows
-            h_ref[pl.ds(at, own_rows), :] = piece[base : base + own_rows, :]
-            if d_ref is not None:
-                d_ref[pl.ds(at, own_rows), :] = piece[base + own_rows : base + 2 * own_rows, :]
+            yield p, k, at
+
+
+def assemble(ids_ref, pieces, h_ref, d_ref, layout):
+    own_rows = layout[1]
+    for p, k, at in owners(ids_ref, layout):
+        piece = pieces[p]
+        half = piece.shape[0] // 2
+        h_rows = slice(k * own_rows, (k + 1) * own_rows)
+        d_rows = slice(half + k * own_rows, half + (k + 1) * own_rows)
+        h_ref[pl.ds(at, own_rows), :] = piece[h_rows, :]
+        d_ref[pl.ds(at, own_rows), :] = piece[d_rows, :]
+
+
+def project(pieces, wall_ref, gall_ref):
+    half = pieces[0].shape[0] // 2
+    h = jnp.concatenate([piece[:half, :] for piece in pieces], axis=0)
+    d = jnp.concatenate([piece[half:, :] for piece in pieces], axis=0)
+    return dot(h, wall_ref[...]), dot(d, gall_ref[...])
+
+
+def pack_kernel(n_parts, own_rows, *refs):
+    parts, out_ref = refs[:n_parts], refs[-1]
+    half = n_parts * own_rows
+    for k, ref in enumerate(parts):
+        out_ref[k * own_rows : (k + 1) * own_rows, :] = ref[:own_rows, :]
+        if ref.shape[0] > own_rows:
+            rows = slice(half + k * own_rows, half + (k + 1) * own_rows)
+            out_ref[rows, :] = ref[own_rows:, :]
+
+
+def early_kernel(*refs):
+    pieces = refs[:-4]
+    wall_ref, gall_ref, proj_ref, grad_ref = refs[-4:]
+    proj_ref[...], grad_ref[...] = project(pieces, wall_ref, gall_ref)
 
 
 def turn_columns(value, flip):
@@ -80,8 +110,8 @@
     )
 
 
-def prep_kernel(win_ref, wbct_ref, wdt_ref, wout_ref, conv_ref, *outs):
-    wall_ref, wallt_ref, gall_ref, taps_ref = outs
+def prep_kernel(ids_ref, win_ref, wbct_ref, wdt_ref, wout_ref, conv_ref, *refs):
+    wall_ref, wallt_ref, gall_ref, taps_ref = refs[-4:]
     flip = mirror(BLOCK)
     width = win_ref.shape[0]
     head = wout_ref.shape[0]
@@ -117,14 +147,6 @@
     taps_ref[:, head:] = jnp.where(tap == CONV - 1, 1.0, 0.0)
 
 
-def pack_kernel(*refs):
-    out_ref = refs[-1]
-    at = 0
-    for ref in refs[:-2]:
-        out_ref[at : at + ref.shape[0], :] = ref[...]
-        at += ref.shape[0]
-
-
 def own_source(shape, dim, ids_ref, tp_size, own_rows):
     z, x, core, ctx = (ids_ref[i] for i in range(4))
     nz = tp_size // 4
@@ -148,15 +170,23 @@
 def core_kernel(n_pieces, layout, *refs):
     ids_ref, par_refs = refs[0], refs[1:4]
     pieces = refs[4 : 4 + n_pieces]
-    wall_ref, wallt_ref, gall_ref, taps_ref = refs[4 + n_pieces : 8 + n_pieces]
-    send_ref, keep_ref, gcat_ref, gated_ref = refs[8 + n_pieces : 12 + n_pieces]
+    early_refs = refs[4 + n_pieces : 6 + n_pieces]
+    wall_ref, wallt_ref, gall_ref, taps_ref = refs[6 + n_pieces : 10 + n_pieces]
+    send_ref, keep_ref, gcat_ref, gated_ref = refs[10 + n_pieces : 14 + n_pieces]
     tp_size, own_rows, coords = layout
     if coords is None:
-        h_ref, d_ref = pieces
+        proj, grads = early_refs[0][...], early_refs[1][...]
     else:
-        h_ref, d_ref = refs[12 + n_pieces :]
-        assemble(ids_ref, pieces, h_ref, d_ref, layout)
-    length, width = h_ref.shape
+        proj_ref, grad_ref = refs[14 + n_pieces :]
+        halves = [[ref[...] for ref in early_refs], project(pieces, wall_ref, gall_ref)]
+        for p, k, at in owners(ids_ref, layout):
+            blocks = len(coords[p][3])
+            source = halves[p // n_pieces]
+            first = ((p % n_pieces) * blocks + k) * own_rows
+            proj_ref[pl.ds(at, own_rows), :] = source[0][first : first + own_rows]
+            grad_ref[pl.ds(at, own_rows), :] = source[1][first : first + own_rows]
+        proj, grads = proj_ref[...], grad_ref[...]
+    length, width = proj.shape[0], wall_ref.shape[0]
     chunks = length // BLOCK
     flip = mirror(BLOCK)
     bias, rate, skip = par_refs[0][0], decay_rate(par_refs), par_refs[2][0]
@@ -166,8 +196,6 @@
     tri = jnp.where(causal, 1.0, 0.0).astype(bf16)
     row_at = iota((length, LANES), 0)
 
-    proj = dot(h_ref[...], wall_ref[...])
-    grads = dot(d_ref[...], gall_ref[...])
     turned = [proj[:, 2 * LANES : 3 * LANES].astype(bf16)]
     turned += split(proj[:, 3 * LANES :], 3) + split(grads[:, LANES:], 2)
     turned = flip_rows(jnp.concatenate(turned, axis=1), flip)
@@ -180,8 +208,8 @@
         ),
         (turned[0], turned[1] + turned[2] + turned[3], turned[4] + turned[5]),
     )
-    small = []
-    for s, (xz, rest, grad_g) in enumerate(strands):
+
+    def gates(xz, rest, grad_g):
         pre = taps_ref[CONV - 1 : CONV, :] * xz
         for shift in range(1, CONV):
             moved = jnp.where(row_at >= shift, pltpu.roll(xz, shift, 0), 0.0)
@@ -194,66 +222,68 @@
         dt = jnp.maximum(raw, 0.0) + jnp.log1p(jnp.exp(-jnp.abs(raw)))
         b_all = jnp.where(lane < STATE, rest, 0.0)
         c_all = jnp.where(lane < STATE, pltpu.roll(rest, LANES - STATE, 1), 0.0)
-        w_all = dt * u
         g_y = jnp.where(low, grad_g * u_other, 0.0)
-        state = jnp.zeros((LANES, LANES), f32)
-        saved, outs = [], []
-        for c in range(chunks):
-            rows = slice(c * BLOCK, (c + 1) * BLOCK)
-            log_keep = dot(tri, jnp.concatenate(split(dt[rows] * rate, 3), axis=1))
-            log_keep = (
-                log_keep[:, :LANES] + log_keep[:, LANES : 2 * LANES] + log_keep[:, 2 * LANES :]
-            )
-            across = jnp.transpose(log_keep)[0:1, :]
-            gap = jnp.concatenate([log_keep] * (BLOCK // LANES), axis=1) - across
-            decay = jnp.exp(jnp.where(causal, gap, -jnp.inf))
-            b_low, c_low = b_all[rows].astype(bf16), c_all[rows].astype(bf16)
-            w_low = w_all[rows].astype(bf16)
-            mixed = (dot_nt(c_low, b_low) * decay).astype(bf16)
-            last = log_keep[BLOCK - 1 : BLOCK, :]
-            enter = jnp.exp(log_keep)
-            leave = jnp.exp(last - log_keep)
-            b_left = (leave * b_all[rows]).astype(bf16)
-            out = dot(mixed, w_low) + enter * dot(c_low, state.astype(bf16))
-            before = state
-            state = jnp.exp(last) * state + dot_tn(b_left, w_low)
-            saved.append(
-                (decay, mixed, b_low, c_low, w_low, b_left, enter, leave, last, before, state)
-            )
-            outs.append(out)
-        out = jnp.concatenate(outs, axis=0)
-        y = out + skip * u
+        return u, slope, u_other, dt, jax.nn.sigmoid(raw), b_all, c_all, dt * u, g_y, grad_g
+
+    def enter_chunk(c, gate, state):
+        rows = slice(c * BLOCK, (c + 1) * BLOCK)
+        dt, b_all, c_all, w_all = gate[3][rows], gate[5][rows], gate[6][rows], gate[7][rows]
+        log_keep = dot(tri, jnp.concatenate(split(dt * rate, 3), axis=1))
+        log_keep = log_keep[:, :LANES] + log_keep[:, LANES : 2 * LANES] + log_keep[:, 2 * LANES :]
+        across = jnp.transpose(log_keep)[0:1, :]
+        gap = jnp.concatenate([log_keep] * (BLOCK // LANES), axis=1) - across
+        decay = jnp.exp(jnp.where(causal, gap, -jnp.inf))
+        b_low, c_low, w_low = b_all.astype(bf16), c_all.astype(bf16), w_all.astype(bf16)
+        mixed = (dot_nt(c_low, b_low) * decay).astype(bf16)
+        last = log_keep[BLOCK - 1 : BLOCK, :]
+        enter = jnp.exp(log_keep)
+        leave = jnp.exp(last - log_keep)
+        b_left = (leave * b_all).astype(bf16)
+        out = dot(mixed, w_low) + enter * dot(c_low, state.astype(bf16))
+        after = jnp.exp(last) * state + dot_tn(b_left, w_low)
+        return out, decay, mixed, b_low, c_low, w_low, b_left, enter, leave, last, state, after
+
+    def leave_chunk(c, gate, saved, d_state):
+        rows = slice(c * BLOCK, (c + 1) * BLOCK)
+        u, c_all, w_all, gy = gate[0][rows], gate[6][rows], gate[7][rows], gate[8][rows]
+        out, decay, mixed, b_low, c_low, w_low, b_left, enter, leave, last, before, after = saved
+        gy_low = gy.astype(bf16)
+        ds_low = d_state.astype(bf16)
+        dw = dot_tn(mixed, gy_low) + dot(b_left, ds_low)
+        d_scores = (dot_nt(gy_low, w_low) * decay).astype(bf16)
+        g_c = dot(d_scores, b_low) + enter * dot_nt(gy_low, before.astype(bf16))
+        g_b = dot_tn(d_scores, c_low) + leave * dot_nt(w_low, ds_low)
+        d_log = jnp.sum(jnp.where(low, gy * out - w_all * dw, 0.0), axis=1, keepdims=True)
+        at_end = jnp.sum(jnp.where(low, after * d_state, 0.0))
+        d_log = jnp.broadcast_to(d_log, (BLOCK, LANES))
+        d_sum = dot_tn(tri, jnp.concatenate(split(d_log, 2), axis=1))
+        d_sum = d_sum[:, :LANES] + d_sum[:, LANES:] + at_end
+        g_a = rate * d_sum + jnp.sum(jnp.where(low, u * dw, 0.0), axis=1, keepdims=True)
+        carried = (enter * c_all).astype(bf16)
+        return dw, g_b, g_c, g_a, jnp.exp(last) * d_state + dot_tn(carried, gy_low)
+
+    gate = [gates(*strand) for strand in strands]
+    saved = [[], []]
+    state = [jnp.zeros((LANES, LANES), f32)] * 2
+    for c in range(chunks):
+        for s in range(2):
+            saved[s].append(enter_chunk(c, gate[s], state[s]))
+            state[s] = saved[s][c][-1]
+    state = [jnp.zeros((LANES, LANES), f32)] * 2
+    grads = [[None] * chunks, [None] * chunks]
+    for c in reversed(range(chunks)):
+        for s in range(2):
+            *grads[s][c], state[s] = leave_chunk(c, gate[s], saved[s][c], state[s])
+    small = []
+    for s in range(2):
+        u, slope, u_other, dt, dt_slope, _, _, _, g_y, grad_g = gate[s]
+        y = jnp.concatenate([part[0] for part in saved[s]], axis=0) + skip * u
         gated = jnp.where(low, y * u_other, 0.0).astype(bf16)
         g_gate = jnp.where(low, grad_g * y, 0.0)
-        d_state = jnp.zeros((LANES, LANES), f32)
-        d_w, g_b, g_c, g_a = [None] * chunks, [None] * chunks, [None] * chunks, [None] * chunks
-        for c in reversed(range(chunks)):
-            rows = slice(c * BLOCK, (c + 1) * BLOCK)
-            decay, mixed, b_low, c_low, w_low, b_left, enter, leave, last, before, after = saved[c]
-            gy = g_y[rows]
-            gy_low = gy.astype(bf16)
-            ds_low = d_state.astype(bf16)
-            dw = dot_tn(mixed, gy_low) + dot(b_left, ds_low)
-            d_scores = (dot_nt(gy_low, w_low) * decay).astype(bf16)
-            g_c[c] = dot(d_scores, b_low) + enter * dot_nt(gy_low, before.astype(bf16))
-            g_b[c] = dot_tn(d_scores, c_low) + leave * dot_nt(w_low, ds_low)
-            d_log = jnp.sum(
-                jnp.where(low, gy * outs[c] - w_all[rows] * dw, 0.0), axis=1, keepdims=True
-            )
-            at_end = jnp.sum(jnp.where(low, after * d_state, 0.0))
-            d_log = jnp.broadcast_to(d_log, (BLOCK, LANES))
-            d_sum = dot_tn(tri, jnp.concatenate(split(d_log, 2), axis=1))
-            d_sum = d_sum[:, :LANES] + d_sum[:, LANES:] + at_end
-            g_a[c] = rate * d_sum + jnp.sum(
-                jnp.where(low, u[rows] * dw, 0.0), axis=1, keepdims=True
-            )
-            d_w[c] = dw
-            carried = (enter * c_all[rows]).astype(bf16)
-            d_state = jnp.exp(last) * d_state + dot_tn(carried, gy_low)
-        d_w = jnp.concatenate(d_w, axis=0)
-        g_b = jnp.concatenate(g_b, axis=0)
-        g_c = jnp.concatenate(g_c, axis=0)
-        g_raw = jnp.concatenate(g_a, axis=0) * jax.nn.sigmoid(raw)
+        d_w, g_b, g_c, g_a = (
+            jnp.concatenate([part[i] for part in grads[s]], axis=0) for i in range(4)
+        )
+        g_raw = g_a * dt_slope
         d_u = jnp.where(low, skip * g_y + dt * d_w, pltpu.roll(g_gate, LANES // 2, 1))
         d_pre = d_u * slope
         g_xz = taps_ref[CONV - 1 : CONV, :] * d_pre
@@ -294,11 +324,11 @@
 def weight_kernel(n_pieces, layout, scaling, *refs):
     ids_ref = refs[0]
     pieces = refs[1 : 1 + n_pieces]
-    gcat_ref, gated_ref, dwin_ref, dwout_ref = refs[1 + n_pieces : 5 + n_pieces]
+    gcat_ref, gated_ref, _, dwin_ref, dwout_ref = refs[1 + n_pieces : 6 + n_pieces]
     if layout[2] is None:
         h_ref, d_ref = pieces
     else:
-        h_ref, d_ref = refs[5 + n_pieces :]
+        h_ref, d_ref = refs[6 + n_pieces :]
         assemble(ids_ref, pieces, h_ref, d_ref, layout)
     flip = mirror(BLOCK)
     columns = h_ref.shape[1] // BLOCK
@@ -318,20 +348,21 @@
         dwout_ref[:, cols] = grad[:head] * scaling
 
 
-def last_kernel(n_got, n_pieces, layout, scaling, *refs):
-    ids_ref, own_ref = refs[:2]
-    got_refs = refs[2 : 2 + n_got]
-    pieces = refs[2 + n_got : 2 + n_got + n_pieces]
-    refs = refs[2 + n_got + n_pieces :]
-    dhid_ref, dwbct_ref = refs[:2]
-    if layout[2] is None:
-        h_ref = pieces[0]
-    else:
-        h_ref = refs[2]
-        assemble(ids_ref, pieces, h_ref, None, layout)
+def stage_kernel(extra, own_rows, keep_ref, got_ref, _, own_ref, *piece_refs):
+    shared = keep_ref[:extra, :] + got_ref[:extra, :].astype(f32)
+    own_ref[:extra, :] = shared
+    for j, ref in enumerate([own_ref, *piece_refs]):
+        rows = slice(extra + j * own_rows, extra + (j + 1) * own_rows)
+        value = keep_ref[rows, :] + got_ref[rows, :].astype(f32)
+        ref[extra:, :] = value.astype(ref.dtype)
+        if j:
+            ref[:extra, :] = shared.astype(bf16)
+
+
+def last_kernel(own_rows, scaling, own_ref, h_ref, *refs):
+    got_refs, (dhid_ref, dwbct_ref) = refs[:-2], refs[-2:]
     flip = mirror(BLOCK)
     length, width = h_ref.shape
-    own_rows = layout[1]
     groups = width // length
     extra = 4 * STATE // groups
     total = own_ref[extra : extra + own_rows, :]
@@ -357,14 +388,16 @@
     return pl.BlockSpec(memory_space=memory)
 
 
-def call(kernel, inputs, n_smem, outs, scratch, flops, moved):
+def call(kernel, inputs, n_smem, outs, scratch, flops, moved, unread=0, vmem=32):
     return pl.pallas_call(
         kernel,
         out_shape=outs,
-        in_specs=[spec(pltpu.SMEM)] * n_smem + [spec()] * (len(inputs) - n_smem),
+        in_specs=[spec(pltpu.SMEM)] * n_smem
+        + [spec()] * (len(inputs) - n_smem - unread)
+        + [spec(pl.ANY)] * unread,
         out_specs=jax.tree.map(lambda _: spec(), outs),
         scratch_shapes=scratch,
-        compiler_params=pltpu.CompilerParams(vmem_limit_bytes=VMEM_LIMIT),
+        compiler_params=pltpu.CompilerParams(vmem_limit_bytes=vmem * 1024 * 1024),
         cost_estimate=pl.CostEstimate(flops=flops, bytes_accessed=moved, transcendentals=0),
     )(*inputs)
 
@@ -382,21 +415,6 @@
     t = lax.axis_index("tp")
     ids = jnp.stack([t >> 2, (t >> 1) & 1, t & 1, lax.axis_index("ctx")]).astype(jnp.int32)
     params = [dt_bias, a_log, d_skip]
-    wall, wallt, gall, taps = call(
-        prep_kernel,
-        [w_in, w_bc.T, w_dt, w_out, conv_w],
-        0,
-        (
-            shape((width, 4 * LANES), bf16),
-            shape((4 * LANES, width), bf16),
-            shape((width, 2 * LANES), bf16),
-            shape((CONV, LANES), f32),
-        ),
-        [],
-        6 * width * BLOCK * BLOCK,
-        20 * width * LANES,
-    )
-
     def across(value, flip_bits):
         return lax.ppermute(value, "tp", [(i, i ^ flip_bits) for i in range(tp_size)])
 
@@ -405,14 +423,34 @@
             value, "ctx", [((i + offset) % ctx_size, i) for i in range(ctx_size)]
         )
 
-    def pack(parts):
-        rows = sum(part.shape[0] for part in parts)
-        return pl.pallas_call(
-            pack_kernel,
-            out_shape=shape((rows, width), bf16),
-            in_specs=[spec()] * len(parts) + [spec(pl.ANY)],
-            out_specs=spec(),
-        )(*parts, taps)
+    def prepare(*begun):
+        return call(
+            prep_kernel,
+            [ids, w_in, w_bc.T, w_dt, w_out, conv_w, *begun],
+            1,
+            (
+                shape((width, 4 * LANES), bf16),
+                shape((4 * LANES, width), bf16),
+                shape((width, 2 * LANES), bf16),
+                shape((CONV, LANES), f32),
+            ),
+            [],
+            6 * width * BLOCK * BLOCK,
+            20 * width * LANES,
+            len(begun),
+        )
+
+    def pack(parts, rows, *after):
+        return call(
+            functools.partial(pack_kernel, len(parts), own_rows),
+            [*parts, *after],
+            0,
+            shape((rows, width), bf16),
+            [],
+            0,
+            4 * rows * width,
+            len(after),
+        )
 
     def column(own, count):
         if count == 1:
@@ -421,11 +459,12 @@
         return column(own, half) + column(across(own, 4 * half), half)
 
     if own_rows % TILE_ROWS == 0:
-        zs = column(jnp.concatenate([hidden, d_out], axis=0), nz)
+        zs = column(pack([hidden, d_out], 2 * own_rows), nz)
         coords, pieces = [], []
         for g, blocks in enumerate([range(0, nz // 2), range(nz // 2, nz)]):
-            parts = [zs[j] for j in blocks]
-            chunk = pack(parts) if g else jnp.concatenate(parts, axis=0)
+            chunk = pack([zs[j] for j in blocks], nz * own_rows, *([taps] if g else []))
+            if g == 0:
+                wall, wallt, gall, taps = prepare(chunk, zs[nz // 2])
             beside = across(chunk, 2)
             plane = [((0, 0), chunk), ((0, 1), beside)]
             for dc in range(1, ctx_size):
@@ -436,17 +475,30 @@
                 coords += [(dc, dx, 0, tuple(blocks)), (dc, dx, 1, tuple(blocks))]
                 pieces += [piece, across(piece, 1)]
         layout = (tp_size, own_rows, tuple(coords))
-        rows = [pltpu.VMEM((length, width), bf16)]
+        early, late = pieces[: len(pieces) // 2], pieces[len(pieces) // 2 :]
     else:
         pieces = [lax.all_gather(a, ("ctx", "tp"), axis=0, tiled=True) for a in (hidden, d_out)]
-        layout, rows = (tp_size, own_rows, None), []
-    h_pieces = pieces if rows else pieces[:1]
-    n_pieces = len(pieces)
+        layout = (tp_size, own_rows, None)
+        wall, wallt, gall, taps = prepare()
+        early, late = [jnp.concatenate(pieces, axis=0)], []
+    ordered = layout[2] is None
+    vmem = 60 if ordered else 32
+    early_rows = sum(piece.shape[0] for piece in early) // 2
+    early = call(
+        early_kernel,
+        [*early, wall, gall],
+        0,
+        (shape((early_rows, 4 * LANES), f32), shape((early_rows, 2 * LANES), f32)),
+        [],
+        2 * early_rows * width * 6 * LANES,
+        4 * early_rows * width,
+        vmem=vmem,
+    )
     extra = 4 * STATE * length // width
     half = tp_size * own_rows // 2
     send, keep, gcat, gated = call(
-        functools.partial(core_kernel, n_pieces, layout),
-        [ids, *params, *pieces, wall, wallt, gall, taps],
+        functools.partial(core_kernel, len(late), layout),
+        [ids, *params, *late, *early, wall, wallt, gall, taps],
         4,
         (
             shape((extra + half, width), bf16),
@@ -454,42 +506,55 @@
             shape((length, 4 * LANES), bf16),
             shape((length, 2 * LANES), bf16),
         ),
-        rows * 2,
+        []
+        if ordered
+        else [pltpu.VMEM((length, 4 * LANES), f32), pltpu.VMEM((length, 2 * LANES), f32)],
         8 * length * width * BLOCK,
         8 * length * width,
+        vmem=vmem,
     )
     scaling = 1.0 / math.sqrt(length)
     got = across(send, 1)
-    d_w_in, d_w_out = call(
-        functools.partial(weight_kernel, n_pieces, layout, scaling),
-        [ids, *pieces, gcat, gated],
-        1,
-        (
-            shape((width, LANES), f32),
-            shape((head, width), f32),
-        ),
-        rows * 2,
-        8 * length * width * BLOCK,
-        8 * length * width,
-    )
     quarter = half // 2
     summed = keep + got.astype(f32)
     send = summed[: extra + quarter].astype(bf16)
     keep = jnp.concatenate(
         [summed[:extra].astype(bf16).astype(f32), summed[extra + quarter :]], axis=0
     )
-    summed = keep + across(send, 2).astype(f32)
-    got = []
-    for j in range(1, nz):
-        at = extra + j * own_rows
-        piece = jnp.concatenate([summed[:extra], summed[at : at + own_rows]], axis=0)
-        got.append(across(piece.astype(bf16), 4 * j))
+    got = across(send, 2)
+    outs = (shape((width, LANES), f32), shape((head, width), f32))
+    if not ordered:
+        outs += (shape((length, width), bf16),)
+    d_w_in, d_w_out, *in_order = call(
+        functools.partial(weight_kernel, len(pieces), layout, scaling),
+        [ids, *pieces, gcat, gated, send],
+        1,
+        outs,
+        [] if ordered else [pltpu.VMEM((length, width), bf16)],
+        8 * length * width * BLOCK,
+        8 * length * width,
+        1,
+        vmem=vmem,
+    )
+    in_order = in_order[0] if in_order else pieces[0]
+    own, *send = call(
+        functools.partial(stage_kernel, extra, own_rows),
+        [keep, got, d_w_out],
+        0,
+        (shape((extra + own_rows, width), f32),)
+        + (shape((extra + own_rows, width), bf16),) * (nz - 1),
+        [],
+        4 * quarter * width,
+        10 * quarter * width,
+        1,
+    )
+    got = [across(piece, 4 * (j + 1)) for j, piece in enumerate(send)]
     d_hidden, d_w_bc = call(
-        functools.partial(last_kernel, len(got), len(h_pieces), layout, scaling),
-        [ids, summed[: extra + own_rows], *got, *h_pieces],
-        1,
+        functools.partial(last_kernel, own_rows, scaling),
+        [own, in_order, *got],
+        0,
         (shape((own_rows, width), bf16), shape((2 * STATE, width), f32)),
-        rows,
+        [],
         2 * length * width * LANES,
         4 * length * width,
     )

time: 87.4 us -> 77.7 us (0.89)
  Pallas kernels: 29.4 us -> 15.6 us
  waiting for transfers between devices: 23.7 us -> 32.6 us
  starting transfers between devices: 23.7 us -> 20.1 us
  other arithmetic: 2.17 us -> 0.31 us
    pallas_call x4 -> x9, Pallas kernels: 27.7 us -> 15.6 us  [call(): pl.pallas_call(kernel, out_shape=outs, in_specs=[spec(pltpu.SMEM)] * n_sm...]
    ppermute x19, waiting for transfers between devices: 22.2 us -> 31.3 us  [across(): lax.ppermute(value, 'tp', [(i, i ^ flip_bits) for i in range(tp_size)])]
    unnamed x37 -> x16, local copies, waits for them, and re-layouts: 3.59 us -> 5.95 us
    ppermute x19, starting transfers between devices: 19.4 us -> 17.5 us  [across(): lax.ppermute(value, 'tp', [(i, i ^ flip_bits) for i in range(tp_size)])]
    pallas_call x1 -> x0, Pallas kernels: 1.71 us -> none  [pack(): pl.pallas_call(pack_kernel, out_shape=shape((rows, width), bf16), in_spec...]
    ppermute x3, starting transfers between devices: 4.29 us -> 2.6 us  [along(): lax.ppermute(value, 'ctx', [((i + offset) % ctx_size, i) for i in range(c...]
    another operation x2 -> x1, other arithmetic: 1.52 us -> 0.18 us
  transfers between devices with their start and end apart: 22 -> 22, of which waited for: 8 -> 8; matrix products, arithmetic and copies ran while one was open for 2% -> 0% of each run, Pallas kernels for 14% -> 9%
where the time goes in v4:
time: 77.7 us; the launch traced here: 77.3 us
  waiting for transfers between devices  32.6 us (42%)
  starting transfers between devices  20.1 us (26%)
  Pallas kernels  15.6 us (20%)
  local copies, waits for them, and re-layouts  6.01 us (8%)
  between operations  2.74 us (4%)
    ppermute x19, waiting for transfers between devices, across(): lax.ppermute(value, 'tp', [(i, i ^ flip_bits) for i in range(tp_size)])  31.3 us
    ppermute x19, starting transfers between devices, across(): lax.ppermute(value, 'tp', [(i, i ^ flip_bits) for i in range(tp_size)])  17.5 us
    pallas_call x9, Pallas kernels, call(): pl.pallas_call(kernel, out_shape=outs, in_specs=[spec(pltpu.SMEM)] * n_sm...  15.6 us
    unnamed x16, local copies, waits for them, and re-layouts  5.95 us
    ppermute x3, starting transfers between devices, along(): lax.ppermute(value, 'ctx', [((i + offset) % ctx_size, i) for i in range(c...  2.6 us
  transfers between devices with their start and end apart: 22, of which 8 were waited for; matrix products, arithmetic and copies ran while one was open for 0% of the time, Pallas kernels for 9%

profile of v4, /device:TPU:0, one launch (start us, length us, event | category | flops | bytes accessed | tf_op | source)
XLA Modules:
  0.0 77.3 jit_solution(9006698155402984657)
XLA Ops:
  0.6 0.8 %copy-done.1 = bf16[16,2048]{1,0:T(8,128)(2,1)S(1)} copy-done((bf16[16,2048]{1,0:T(8,128)(2,1)S(1)}, bf16[16,2048]{1,0:T(8,128)(2,1)}, u32[]{:S(2)}) %copy-start.1) | copy-done | bytes 65560
  1.5 0.8 %copy-done.2 = bf16[16,2048]{1,0:T(8,128)(2,1)S(1)} copy-done((bf16[16,2048]{1,0:T(8,128)(2,1)S(1)}, bf16[16,2048]{1,0:T(8,128)(2,1)}, u32[]{:S(2)}) %copy-start.2) | copy-done | bytes 65560
  2.3 4.1 %collective-permute-start = (bf16[32,2048]{1,0:T(8,128)(2,1)S(1)}, bf16[32,2048]{1,0:T(8,128)(2,1)S(1)}, u32[]{:S(2)}, u32[]{:S(2)}) collective-permute-start(bf16[32,2048]{1,0:T(8,128)(2,1)S(1)} %shard_map.129.refs_0_), channel_id=1, source_target_pairs={{0,8},{1,9},{2,10},{3,11},{4,12},{5,13},{6,14},{7,15},{8,0},{9,1},... | collective-permute-start | bytes 393224 | tf_op jit(solution)/shard_map/ppermute | solution.py:419
  6.4 1.6 %collective-permute-start.2 = (bf16[32,2048]{1,0:T(8,128)(2,1)S(1)}, bf16[32,2048]{1,0:T(8,128)(2,1)S(1)}, u32[]{:S(2)}, u32[]{:S(2)}) collective-permute-start(bf16[32,2048]{1,0:T(8,128)(2,1)S(1)} %shard_map.129.refs_0_), channel_id=1, source_target_pairs={{0,4},{1,5},{2,6},{3,7},{4,0},{5,1},{6,2},{7,3},{8,12},{9,13},{10,... | collective-permute-start | bytes 393224 | tf_op jit(solution)/shard_map/ppermute | solution.py:419
  8.0 4.8 %collective-permute-done.refs_1_.refs_0_ = bf16[32,2048]{1,0:T(8,128)(2,1)S(1)} collective-permute-done((bf16[32,2048]{1,0:T(8,128)(2,1)S(1)}, bf16[32,2048]{1,0:T(8,128)(2,1)S(1)}, u32[]{:S(2)}, u32[]{:S(2)}) %collective-permute-start) | collective-permute-done | bytes 131104 | tf_op jit(solution)/shard_map/ppermute | solution.py:419
  12.8 0.6 collective-permute-start.1
  13.6 1.6 %collective-permute-start.13 = (bf16[64,2048]{1,0:T(8,128)(2,1)S(1)}, bf16[64,2048]{1,0:T(8,128)(2,1)S(1)}, u32[]{:S(2)}, u32[]{:S(2)}) collective-permute-start(bf16[64,2048]{1,0:T(8,128)(2,1)S(1)} %shard_map.130.refs_0_.refs_1_), channel_id=1, source_target_pairs={{16,0},{0,16},{17,1},{1,17},{18,2},{2,18},{19,3},{3,19},{20,4},{4,... | collective-permute-start | bytes 786440 | tf_op jit(solution)/shard_map/ppermute | solution.py:422
  15.1 1.5 %collective-permute-start.11 = (bf16[64,2048]{1,0:T(8,128)(2,1)S(1)}, bf16[64,2048]{1,0:T(8,128)(2,1)S(1)}, u32[]{:S(2)}, u32[]{:S(2)}) collective-permute-start(bf16[64,2048]{1,0:T(8,128)(2,1)S(1)} %shard_map.130.refs_0_.refs_1_), channel_id=1, source_target_pairs={{0,2},{1,3},{2,0},{3,1},{4,6},{5,7},{6,4},{7,5},{8,10},{9,11},{10,... | collective-permute-start | bytes 786440 | tf_op jit(solution)/shard_map/ppermute | solution.py:419
  16.6 1.0 %copy-done.3 = bf16[2048,128]{1,0:T(8,128)(2,1)S(1)} copy-done((bf16[2048,128]{1,0:T(8,128)(2,1)S(1)}, bf16[2048,128]{1,0:T(8,128)(2,1)}, u32[]{:S(2)}) %copy-start.3) | copy-done | bytes 524312
  17.7 0.9 %copy-done.4 = bf16[64,2048]{1,0:T(8,128)(2,1)S(1)} copy-done((bf16[64,2048]{1,0:T(8,128)(2,1)S(1)}, bf16[64,2048]{1,0:T(8,128)(2,1)}, u32[]{:S(2)}) %copy-start.4) | copy-done | bytes 262168
  18.6 0.9 %copy-done.5 = bf16[2048,32]{0,1:T(8,128)(2,1)S(1)} copy-done((bf16[2048,32]{0,1:T(8,128)(2,1)S(1)}, bf16[2048,32]{0,1:T(8,128)(2,1)}, u32[]{:S(2)}) %copy-start.5) | copy-done | bytes 131096
  19.5 0.7 copy-done.6
  20.2 0.7 copy-done.7
  20.9 1.7 %shard_map.131 = (bf16[2048,512]{1,0:T(8,128)(2,1)S(1)}, bf16[512,2048]{1,0:T(8,128)(2,1)S(1)}, bf16[2048,256]{1,0:T(8,128)(2,1)S(1)}, f32[4,128]{1,0:T(4,128)S(1)}) custom-call(s32[4]{0:T(128)S(1)} %pad_add_fusion.ids_ref.refs_0_, bf16[2048,128]{1,0:T(8,128)(2,1)S(1)} %copy-done.3, bf16[32,2048]{1,0:T(8,128)(2,1)S(1)} %bitcast.6, ...), custom_call_target="tpu_custom_call" | custom-call | flops 805306368 | bytes 5242880 | tf_op jit(solution)/shard_map/pallas_call | solution.py:392
  22.6 0.6 collective-permute-start.4
  23.2 1.5 %collective-permute-start.15 = (bf16[64,2048]{1,0:T(8,128)(2,1)S(1)}, bf16[64,2048]{1,0:T(8,128)(2,1)S(1)}, u32[]{:S(2)}, u32[]{:S(2)}) collective-permute-start(bf16[64,2048]{1,0:T(8,128)(2,1)S(1)} %collective-permute-done.13.refs_4_.refs_5_), channel_id=1, source_target_pairs={{0,2},{1,3},{2,0},{3,1},{4,6},{5,7},{6,4},{7,5},{8,10},{9,11},{10,... | collective-permute-start | bytes 786440 | tf_op jit(solution)/shard_map/ppermute | solution.py:419
  25.8 6.0 %collective-permute-done.4.refs_6_.refs_11_ = bf16[64,2048]{1,0:T(8,128)(2,1)S(1)} collective-permute-done((bf16[64,2048]{1,0:T(8,128)(2,1)S(1)}, bf16[64,2048]{1,0:T(8,128)(2,1)S(1)}, u32[]{:S(2)}, u32[]{:S(2)}) %collective-permute-start.4) | collective-permute-done | bytes 262176 | tf_op jit(solution)/shard_map/ppermute | solution.py:419
  32.3 4.7 %collective-permute-done.15.refs_6_.refs_7_ = bf16[64,2048]{1,0:T(8,128)(2,1)S(1)} collective-permute-done((bf16[64,2048]{1,0:T(8,128)(2,1)S(1)}, bf16[64,2048]{1,0:T(8,128)(2,1)S(1)}, u32[]{:S(2)}, u32[]{:S(2)}) %collective-permute-start.15) | collective-permute-done | bytes 262176 | tf_op jit(solution)/shard_map/ppermute | solution.py:419
  38.1 1.3 %collective-permute-done.8.refs_10_.refs_15_ = bf16[64,2048]{1,0:T(8,128)(2,1)S(1)} collective-permute-done((bf16[64,2048]{1,0:T(8,128)(2,1)S(1)}, bf16[64,2048]{1,0:T(8,128)(2,1)S(1)}, u32[]{:S(2)}, u32[]{:S(2)}) %collective-permute-start.8) | collective-permute-done | bytes 262176 | tf_op jit(solution)/shard_map/ppermute | solution.py:422
  41.3 1.0 %shard_map.133 = (f32[256,512]{1,0:T(8,128)S(1)}, f32[256,256]{1,0:T(8,128)S(1)}) custom-call(bf16[64,2048]{1,0:T(8,128)(2,1)S(1)} %shard_map.130.refs_0_.refs_1_, bf16[64,2048]{1,0:T(8,128)(2,1)S(1)} %collective-permute-done.10.refs_1_.refs_2_, bf16[64,2048]{1,0:T(8,128)(2,1)S(1)} %collective-permute-done.11.refs_2_.refs_3_, ...), custom_call_target="tpu_custom_call" | custom-call | flops 805306368 | bytes 2097152 | tf_op jit(solution)/shard_map/pallas_call | solution.py:392
  42.4 6.5 %shard_map.134 = (bf16[144,2048]{1,0:T(8,128)(2,1)S(1)}, f32[144,2048]{1,0:T(8,128)S(1)}, bf16[512,512]{1,0:T(8,128)(2,1)S(1)}, bf16[512,256]{1,0:T(8,128)(2,1)S(1)}) custom-call(s32[4]{0:T(128)S(1)} %pad_add_fusion.ids_ref.refs_0_, f32[1]{0:T(128)S(6)} %copy.14.refs_1_, f32[1]{0:T(128)S(6)} %copy.15.refs_2_, f32[1]{0:T(128)S(6)} %copy.16.refs_3_, ...), custom_call_target="tpu_custom_call" | custom-call | flops 2147483648 | bytes 8388608 | tf_op jit(solution)/shard_map/pallas_call | solution.py:392
  48.9 0.6 collective-permute-start.17
  49.5 1.6 %collective-permute-done.17 = bf16[144,2048]{1,0:T(8,128)(2,1)S(1)} collective-permute-done((bf16[144,2048]{1,0:T(8,128)(2,1)S(1)}, bf16[144,2048]{1,0:T(8,128)(2,1)S(1)}, u32[]{:S(2)}, u32[]{:S(2)}) %collective-permute-start.17) | collective-permute-done | bytes 589856 | tf_op jit(solution)/shard_map/ppermute | solution.py:419
  51.3 0.6 collective-permute-start.18
  51.9 4.4 %shard_map.135 = (f32[2048,128]{1,0:T(8,128)}, f32[64,2048]{1,0:T(8,128)}, bf16[512,2048]{1,0:T(8,128)(2,1)S(1)}) custom-call(s32[4]{0:T(128)S(1)} %pad_add_fusion.ids_ref.refs_0_, bf16[64,2048]{1,0:T(8,128)(2,1)S(1)} %shard_map.130.refs_0_.refs_1_, bf16[64,2048]{1,0:T(8,128)(2,1)S(1)} %collective-permute-done.10.refs_1_.refs_2_, ...), custom_call_target="tpu_custom_call" | custom-call | flops 2147483648 | bytes 8388608 | tf_op jit(solution)/shard_map/pallas_call | solution.py:392
  56.4 5.0 %collective-permute-done.18.got_ref = bf16[80,2048]{1,0:T(8,128)(2,1)S(1)} collective-permute-done((bf16[80,2048]{1,0:T(8,128)(2,1)S(1)}, bf16[80,2048]{1,0:T(8,128)(2,1)S(1)}, u32[]{:S(2)}, u32[]{:S(2)}) %collective-permute-start.18) | collective-permute-done | bytes 327712 | tf_op jit(solution)/shard_map/ppermute | solution.py:419
  61.5 1.5 %collective-permute-start.19 = (bf16[32,2048]{1,0:T(8,128)(2,1)S(1)}, bf16[32,2048]{1,0:T(8,128)(2,1)S(1)}, u32[]{:S(2)}, u32[]{:S(2)}) collective-permute-start(bf16[32,2048]{1,0:T(8,128)(2,1)S(1)} %get-tuple-element.36), channel_id=1, source_target_pairs={{0,4},{1,5},{2,6},{3,7},{4,0},{5,1},{6,2},{7,3},{8,12},{9,13},{10,... | collective-permute-start | bytes 393224 | tf_op jit(solution)/shard_map/ppermute | solution.py:419
  63.0 2.0 %collective-permute-start.20 = (bf16[32,2048]{1,0:T(8,128)(2,1)S(1)}, bf16[32,2048]{1,0:T(8,128)(2,1)S(1)}, u32[]{:S(2)}, u32[]{:S(2)}) collective-permute-start(bf16[32,2048]{1,0:T(8,128)(2,1)S(1)} %get-tuple-element.37), channel_id=1, source_target_pairs={{0,8},{1,9},{2,10},{3,11},{4,12},{5,13},{6,14},{7,15},{8,0},{9,1},... | collective-permute-start | bytes 393224 | tf_op jit(solution)/shard_map/ppermute | solution.py:419
  65.0 1.4 %collective-permute-start.21 = (bf16[32,2048]{1,0:T(8,128)(2,1)S(1)}, bf16[32,2048]{1,0:T(8,128)(2,1)S(1)}, u32[]{:S(2)}, u32[]{:S(2)}) collective-permute-start(bf16[32,2048]{1,0:T(8,128)(2,1)S(1)} %get-tuple-element.38), channel_id=1, source_target_pairs={{0,12},{1,13},{2,14},{3,15},{4,8},{5,9},{6,10},{7,11},{8,4},{9,5},... | collective-permute-start | bytes 393224 | tf_op jit(solution)/shard_map/ppermute | solution.py:419
  66.4 2.1 %collective-permute-done.19.refs_0_ = bf16[32,2048]{1,0:T(8,128)(2,1)S(1)} collective-permute-done((bf16[32,2048]{1,0:T(8,128)(2,1)S(1)}, bf16[32,2048]{1,0:T(8,128)(2,1)S(1)}, u32[]{:S(2)}, u32[]{:S(2)}) %collective-permute-start.19) | collective-permute-done | bytes 131104 | tf_op jit(solution)/shard_map/ppermute | solution.py:419
  68.5 7.0 %collective-permute-done.20.refs_1_ = bf16[32,2048]{1,0:T(8,128)(2,1)S(1)} collective-permute-done((bf16[32,2048]{1,0:T(8,128)(2,1)S(1)}, bf16[32,2048]{1,0:T(8,128)(2,1)S(1)}, u32[]{:S(2)}, u32[]{:S(2)}) %collective-permute-start.20) | collective-permute-done | bytes 131104 | tf_op jit(solution)/shard_map/ppermute | solution.py:419
  75.4 1.9 %shard_map.137 = (bf16[16,2048]{1,0:T(8,128)(2,1)}, f32[32,2048]{1,0:T(8,128)}) custom-call(f32[32,2048]{1,0:T(8,128)S(1)} %get-tuple-element.34.own_ref, bf16[512,2048]{1,0:T(8,128)(2,1)S(1)} %get-tuple-element.35.h_ref, bf16[32,2048]{1,0:T(8,128)(2,1)S(1)} %collective-permute-done.19.refs_0_, bf16[32,2048]{1,0:T(8,128)(2,1)S(1)} %collective-permute-done.20.refs_1_, ...), custom_call_target="tpu_custom_call" | custom-call | flops 268435456 | bytes 4194304 | tf_op jit(solution)/shard_map/pallas_call | solution.py:392
  (43 shorter events, 3.1 us)
Async XLA Ops:
  0.6 0.8 %copy-start.1 = (bf16[16,2048]{1,0:T(8,128)(2,1)S(1)}, bf16[16,2048]{1,0:T(8,128)(2,1)}, u32[]{:S(2)}) copy-start(bf16[16,2048]{1,0:T(8,128)(2,1)} %refs_0_.1) | copy-start | bytes 196612
  1.5 0.8 %copy-start.2 = (bf16[16,2048]{1,0:T(8,128)(2,1)S(1)}, bf16[16,2048]{1,0:T(8,128)(2,1)}, u32[]{:S(2)}) copy-start(bf16[16,2048]{1,0:T(8,128)(2,1)} %refs_1_.2) | copy-start | bytes 196612
  2.3 10.5 %collective-permute-start = (bf16[32,2048]{1,0:T(8,128)(2,1)S(1)}, bf16[32,2048]{1,0:T(8,128)(2,1)S(1)}, u32[]{:S(2)}, u32[]{:S(2)}) collective-permute-start(bf16[32,2048]{1,0:T(8,128)(2,1)S(1)} %shard_map.129.refs_0_), channel_id=1, source_target_pairs={{0,8},{1,9},{2,10},{3,11},{4,12},{5,13},{6,14},{7,15},{8,0},{9,1},... | collective-permute-start | bytes 393224 | tf_op jit(solution)/shard_map/ppermute | solution.py:419
  6.4 7.1 %collective-permute-start.2 = (bf16[32,2048]{1,0:T(8,128)(2,1)S(1)}, bf16[32,2048]{1,0:T(8,128)(2,1)S(1)}, u32[]{:S(2)}, u32[]{:S(2)}) collective-permute-start(bf16[32,2048]{1,0:T(8,128)(2,1)S(1)} %shard_map.129.refs_0_), channel_id=1, source_target_pairs={{0,4},{1,5},{2,6},{3,7},{4,0},{5,1},{6,2},{7,3},{8,12},{9,13},{10,... | collective-permute-start | bytes 393224 | tf_op jit(solution)/shard_map/ppermute | solution.py:419
  12.8 9.8 %collective-permute-start.1 = (bf16[32,2048]{1,0:T(8,128)(2,1)S(1)}, bf16[32,2048]{1,0:T(8,128)(2,1)S(1)}, u32[]{:S(2)}, u32[]{:S(2)}) collective-permute-start(bf16[32,2048]{1,0:T(8,128)(2,1)S(1)} %collective-permute-done.refs_1_.refs_0_), channel_id=1, source_target_pairs={{0,4},{1,5},{2,6},{3,7},{4,0},{5,1},{6,2},{7,3},{8,12},{9,13},{10,... | collective-permute-start | bytes 393224 | tf_op jit(solution)/shard_map/ppermute | solution.py:419
  13.6 9.7 %collective-permute-start.13 = (bf16[64,2048]{1,0:T(8,128)(2,1)S(1)}, bf16[64,2048]{1,0:T(8,128)(2,1)S(1)}, u32[]{:S(2)}, u32[]{:S(2)}) collective-permute-start(bf16[64,2048]{1,0:T(8,128)(2,1)S(1)} %shard_map.130.refs_0_.refs_1_), channel_id=1, source_target_pairs={{16,0},{0,16},{17,1},{1,17},{18,2},{2,18},{19,3},{3,19},{20,4},{4,... | collective-permute-start | bytes 786440 | tf_op jit(solution)/shard_map/ppermute | solution.py:422
  15.1 10.1 %collective-permute-start.11 = (bf16[64,2048]{1,0:T(8,128)(2,1)S(1)}, bf16[64,2048]{1,0:T(8,128)(2,1)S(1)}, u32[]{:S(2)}, u32[]{:S(2)}) collective-permute-start(bf16[64,2048]{1,0:T(8,128)(2,1)S(1)} %shard_map.130.refs_0_.refs_1_), channel_id=1, source_target_pairs={{0,2},{1,3},{2,0},{3,1},{4,6},{5,7},{6,4},{7,5},{8,10},{9,11},{10,... | collective-permute-start | bytes 786440 | tf_op jit(solution)/shard_map/ppermute | solution.py:419
  16.6 8.6 %collective-permute-start.10 = (bf16[64,2048]{1,0:T(8,128)(2,1)S(1)}, bf16[64,2048]{1,0:T(8,128)(2,1)S(1)}, u32[]{:S(2)}, u32[]{:S(2)}) collective-permute-start(bf16[64,2048]{1,0:T(8,128)(2,1)S(1)} %shard_map.130.refs_0_.refs_1_), channel_id=1, source_target_pairs={{0,1},{1,0},{2,3},{3,2},{4,5},{5,4},{6,7},{7,6},{8,9},{9,8},{10,11... | collective-permute-start | bytes 786440 | tf_op jit(solution)/shard_map/ppermute | solution.py:419
  16.6 1.0 %copy-start.3 = (bf16[2048,128]{1,0:T(8,128)(2,1)S(1)}, bf16[2048,128]{1,0:T(8,128)(2,1)}, u32[]{:S(2)}) copy-start(bf16[2048,128]{1,0:T(8,128)(2,1)} %win_ref.1) | copy-start | bytes 1572868
  17.7 0.9 %copy-start.4 = (bf16[64,2048]{1,0:T(8,128)(2,1)S(1)}, bf16[64,2048]{1,0:T(8,128)(2,1)}, u32[]{:S(2)}) copy-start(bf16[64,2048]{1,0:T(8,128)(2,1)} %wout_ref.1) | copy-start | bytes 786436
  18.6 0.9 %copy-start.5 = (bf16[2048,32]{0,1:T(8,128)(2,1)S(1)}, bf16[2048,32]{0,1:T(8,128)(2,1)}, u32[]{:S(2)}) copy-start(bf16[2048,32]{0,1:T(8,128)(2,1)} %param.12) | copy-start | bytes 393220
  19.5 0.7 copy-start.6
  20.2 0.7 copy-start.7
  22.6 9.2 %collective-permute-start.4 = (bf16[64,2048]{1,0:T(8,128)(2,1)S(1)}, bf16[64,2048]{1,0:T(8,128)(2,1)S(1)}, u32[]{:S(2)}, u32[]{:S(2)}) collective-permute-start(bf16[64,2048]{1,0:T(8,128)(2,1)S(1)} %shard_map.132.refs_4_.refs_9_), channel_id=1, source_target_pairs={{0,2},{1,3},{2,0},{3,1},{4,6},{5,7},{6,4},{7,5},{8,10},{9,11},{10,... | collective-permute-start | bytes 786440 | tf_op jit(solution)/shard_map/ppermute | solution.py:419
  23.2 13.8 %collective-permute-start.15 = (bf16[64,2048]{1,0:T(8,128)(2,1)S(1)}, bf16[64,2048]{1,0:T(8,128)(2,1)S(1)}, u32[]{:S(2)}, u32[]{:S(2)}) collective-permute-start(bf16[64,2048]{1,0:T(8,128)(2,1)S(1)} %collective-permute-done.13.refs_4_.refs_5_), channel_id=1, source_target_pairs={{0,2},{1,3},{2,0},{3,1},{4,6},{5,7},{6,4},{7,5},{8,10},{9,11},{10,... | collective-permute-start | bytes 786440 | tf_op jit(solution)/shard_map/ppermute | solution.py:419
  24.7 12.3 %collective-permute-start.6 = (bf16[64,2048]{1,0:T(8,128)(2,1)S(1)}, bf16[64,2048]{1,0:T(8,128)(2,1)S(1)}, u32[]{:S(2)}, u32[]{:S(2)}) collective-permute-start(bf16[64,2048]{1,0:T(8,128)(2,1)S(1)} %shard_map.132.refs_4_.refs_9_), channel_id=1, source_target_pairs={{16,0},{0,16},{17,1},{1,17},{18,2},{2,18},{19,3},{3,19},{20,4},{4,... | collective-permute-start | bytes 786440 | tf_op jit(solution)/shard_map/ppermute | solution.py:422
  25.3 12.3 %collective-permute-start.14 = (bf16[64,2048]{1,0:T(8,128)(2,1)S(1)}, bf16[64,2048]{1,0:T(8,128)(2,1)S(1)}, u32[]{:S(2)}, u32[]{:S(2)}) collective-permute-start(bf16[64,2048]{1,0:T(8,128)(2,1)S(1)} %collective-permute-done.13.refs_4_.refs_5_), channel_id=1, source_target_pairs={{0,1},{1,0},{2,3},{3,2},{4,5},{5,4},{6,7},{7,6},{8,9},{9,8},{10,11... | collective-permute-start | bytes 786440 | tf_op jit(solution)/shard_map/ppermute | solution.py:419
  25.3 12.4 %collective-permute-start.12 = (bf16[64,2048]{1,0:T(8,128)(2,1)S(1)}, bf16[64,2048]{1,0:T(8,128)(2,1)S(1)}, u32[]{:S(2)}, u32[]{:S(2)}) collective-permute-start(bf16[64,2048]{1,0:T(8,128)(2,1)S(1)} %collective-permute-done.11.refs_2_.refs_3_), channel_id=1, source_target_pairs={{0,1},{1,0},{2,3},{3,2},{4,5},{5,4},{6,7},{7,6},{8,9},{9,8},{10,11... | collective-permute-start | bytes 786440 | tf_op jit(solution)/shard_map/ppermute | solution.py:419
  31.8 7.6 %collective-permute-start.8 = (bf16[64,2048]{1,0:T(8,128)(2,1)S(1)}, bf16[64,2048]{1,0:T(8,128)(2,1)S(1)}, u32[]{:S(2)}, u32[]{:S(2)}) collective-permute-start(bf16[64,2048]{1,0:T(8,128)(2,1)S(1)} %collective-permute-done.4.refs_6_.refs_11_), channel_id=1, source_target_pairs={{16,0},{0,16},{17,1},{1,17},{18,2},{2,18},{19,3},{3,19},{20,4},{4,... | collective-permute-start | bytes 786440 | tf_op jit(solution)/shard_map/ppermute | solution.py:422
  37.0 4.3 %collective-permute-start.16 = (bf16[64,2048]{1,0:T(8,128)(2,1)S(1)}, bf16[64,2048]{1,0:T(8,128)(2,1)S(1)}, u32[]{:S(2)}, u32[]{:S(2)}) collective-permute-start(bf16[64,2048]{1,0:T(8,128)(2,1)S(1)} %collective-permute-done.15.refs_6_.refs_7_), channel_id=1, source_target_pairs={{0,1},{1,0},{2,3},{3,2},{4,5},{5,4},{6,7},{7,6},{8,9},{9,8},{10,11... | collective-permute-start | bytes 786440 | tf_op jit(solution)/shard_map/ppermute | solution.py:419
  37.1 5.3 %collective-permute-start.3 = (bf16[64,2048]{1,0:T(8,128)(2,1)S(1)}, bf16[64,2048]{1,0:T(8,128)(2,1)S(1)}, u32[]{:S(2)}, u32[]{:S(2)}) collective-permute-start(bf16[64,2048]{1,0:T(8,128)(2,1)S(1)} %shard_map.132.refs_4_.refs_9_), channel_id=1, source_target_pairs={{0,1},{1,0},{2,3},{3,2},{4,5},{5,4},{6,7},{7,6},{8,9},{9,8},{10,11... | collective-permute-start | bytes 786440 | tf_op jit(solution)/shard_map/ppermute | solution.py:419
  37.6 4.8 %collective-permute-start.5 = (bf16[64,2048]{1,0:T(8,128)(2,1)S(1)}, bf16[64,2048]{1,0:T(8,128)(2,1)S(1)}, u32[]{:S(2)}, u32[]{:S(2)}) collective-permute-start(bf16[64,2048]{1,0:T(8,128)(2,1)S(1)} %collective-permute-done.4.refs_6_.refs_11_), channel_id=1, source_target_pairs={{0,1},{1,0},{2,3},{3,2},{4,5},{5,4},{6,7},{7,6},{8,9},{9,8},{10,11... | collective-permute-start | bytes 786440 | tf_op jit(solution)/shard_map/ppermute | solution.py:419
  37.6 4.7 %collective-permute-start.7 = (bf16[64,2048]{1,0:T(8,128)(2,1)S(1)}, bf16[64,2048]{1,0:T(8,128)(2,1)S(1)}, u32[]{:S(2)}, u32[]{:S(2)}) collective-permute-start(bf16[64,2048]{1,0:T(8,128)(2,1)S(1)} %collective-permute-done.6.refs_8_.refs_13_), channel_id=1, source_target_pairs={{0,1},{1,0},{2,3},{3,2},{4,5},{5,4},{6,7},{7,6},{8,9},{9,8},{10,11... | collective-permute-start | bytes 786440 | tf_op jit(solution)/shard_map/ppermute | solution.py:419
  39.4 3.0 %collective-permute-start.9 = (bf16[64,2048]{1,0:T(8,128)(2,1)S(1)}, bf16[64,2048]{1,0:T(8,128)(2,1)S(1)}, u32[]{:S(2)}, u32[]{:S(2)}) collective-permute-start(bf16[64,2048]{1,0:T(8,128)(2,1)S(1)} %collective-permute-done.8.refs_10_.refs_15_), channel_id=1, source_target_pairs={{0,1},{1,0},{2,3},{3,2},{4,5},{5,4},{6,7},{7,6},{8,9},{9,8},{10,11... | collective-permute-start | bytes 786440 | tf_op jit(solution)/shard_map/ppermute | solution.py:419
  48.9 2.2 %collective-permute-start.17 = (bf16[144,2048]{1,0:T(8,128)(2,1)S(1)}, bf16[144,2048]{1,0:T(8,128)(2,1)S(1)}, u32[]{:S(2)}, u32[]{:S(2)}) collective-permute-start(bf16[144,2048]{1,0:T(8,128)(2,1)S(1)} %get-tuple-element.30), channel_id=1, source_target_pairs={{0,1},{1,0},{2,3},{3,2},{4,5},{5,4},{6,7},{7,6},{8,9},{9,8},{10,11... | collective-permute-start | bytes 1769480 | tf_op jit(solution)/shard_map/ppermute | solution.py:419
  51.3 10.1 %collective-permute-start.18 = (bf16[80,2048]{1,0:T(8,128)(2,1)S(1)}, bf16[80,2048]{1,0:T(8,128)(2,1)S(1)}, u32[]{:S(2)}, u32[]{:S(2)}) collective-permute-start(bf16[80,2048]{1,0:T(8,128)(2,1)S(1)} %slice.16.refs_19_), channel_id=1, source_target_pairs={{0,2},{1,3},{2,0},{3,1},{4,6},{5,7},{6,4},{7,5},{8,10},{9,11},{10,... | collective-permute-start | bytes 983048 | tf_op jit(solution)/shard_map/ppermute | solution.py:419
  56.3 5.1 %copy-start = (f32[64,2048]{1,0:T(8,128)S(1)}, f32[64,2048]{1,0:T(8,128)}, u32[]{:S(2)}) copy-start(f32[64,2048]{1,0:T(8,128)} %get-tuple-element.21._) | copy-start | bytes 1572868
  61.5 7.0 %collective-permute-start.19 = (bf16[32,2048]{1,0:T(8,128)(2,1)S(1)}, bf16[32,2048]{1,0:T(8,128)(2,1)S(1)}, u32[]{:S(2)}, u32[]{:S(2)}) collective-permute-start(bf16[32,2048]{1,0:T(8,128)(2,1)S(1)} %get-tuple-element.36), channel_id=1, source_target_pairs={{0,4},{1,5},{2,6},{3,7},{4,0},{5,1},{6,2},{7,3},{8,12},{9,13},{10,... | collective-permute-start | bytes 393224 | tf_op jit(solution)/shard_map/ppermute | solution.py:419
  63.0 12.5 %collective-permute-start.20 = (bf16[32,2048]{1,0:T(8,128)(2,1)S(1)}, bf16[32,2048]{1,0:T(8,128)(2,1)S(1)}, u32[]{:S(2)}, u32[]{:S(2)}) collective-permute-start(bf16[32,2048]{1,0:T(8,128)(2,1)S(1)} %get-tuple-element.37), channel_id=1, source_target_pairs={{0,8},{1,9},{2,10},{3,11},{4,12},{5,13},{6,14},{7,15},{8,0},{9,1},... | collective-permute-start | bytes 393224 | tf_op jit(solution)/shard_map/ppermute | solution.py:419
  65.0 10.5 %collective-permute-start.21 = (bf16[32,2048]{1,0:T(8,128)(2,1)S(1)}, bf16[32,2048]{1,0:T(8,128)(2,1)S(1)}, u32[]{:S(2)}, u32[]{:S(2)}) collective-permute-start(bf16[32,2048]{1,0:T(8,128)(2,1)S(1)} %get-tuple-element.38), channel_id=1, source_target_pairs={{0,12},{1,13},{2,14},{3,15},{4,8},{5,9},{6,10},{7,11},{8,4},{9,5},... | collective-permute-start | bytes 393224 | tf_op jit(solution)/shard_map/ppermute | solution.py:419

commit v5 on v4

--- a/solution.py
+++ b/solution.py
@@ -96,6 +96,15 @@
             out_ref[rows, :] = ref[own_rows:, :]
 
 
+def first_kernel(hidden_ref, dout_ref, out_ref, sem):
+    rows = hidden_ref.shape[0]
+    fetch([hidden_ref, dout_ref], [out_ref.at[:rows], out_ref.at[rows:]], sem)
+
+
+def copy_kernel(value_ref, _, out_ref):
+    out_ref[...] = value_ref[...]
+
+
 def early_kernel(*refs):
     pieces = refs[:-4]
     wall_ref, gall_ref, proj_ref, grad_ref = refs[-4:]
@@ -110,7 +119,19 @@
     )
 
 
-def prep_kernel(ids_ref, win_ref, wbct_ref, wdt_ref, wout_ref, conv_ref, *refs):
+def fetch(sources, targets, sem):
+    copies = [
+        pltpu.make_async_copy(source, target, sem.at[i])
+        for i, (source, target) in enumerate(zip(sources, targets))
+    ]
+    for copy in copies:
+        copy.start()
+    for copy in copies:
+        copy.wait()
+
+
+def prep_kernel(ids_ref, *refs):
+    win_ref, wbct_ref, wdt_ref, wout_ref, conv_ref = refs[:5]
     wall_ref, wallt_ref, gall_ref, taps_ref = refs[-4:]
     flip = mirror(BLOCK)
     width = win_ref.shape[0]
@@ -348,32 +369,23 @@
         dwout_ref[:, cols] = grad[:head] * scaling
 
 
-def stage_kernel(extra, own_rows, keep_ref, got_ref, _, own_ref, *piece_refs):
-    shared = keep_ref[:extra, :] + got_ref[:extra, :].astype(f32)
-    own_ref[:extra, :] = shared
+def stage_kernel(own_rows, keep_ref, got_ref, _, own_ref, *piece_refs):
     for j, ref in enumerate([own_ref, *piece_refs]):
-        rows = slice(extra + j * own_rows, extra + (j + 1) * own_rows)
+        rows = slice(j * own_rows, (j + 1) * own_rows)
         value = keep_ref[rows, :] + got_ref[rows, :].astype(f32)
-        ref[extra:, :] = value.astype(ref.dtype)
-        if j:
-            ref[:extra, :] = shared.astype(bf16)
-
-
-def last_kernel(own_rows, scaling, own_ref, h_ref, *refs):
+        ref[...] = value.astype(ref.dtype)
+
+
+def last_kernel(scaling, own_ref, h_ref, shared_ref, other_ref, *refs):
     got_refs, (dhid_ref, dwbct_ref) = refs[:-2], refs[-2:]
     flip = mirror(BLOCK)
     length, width = h_ref.shape
     groups = width // length
-    extra = 4 * STATE // groups
-    total = own_ref[extra : extra + own_rows, :]
+    total = own_ref[...]
     for got in got_refs:
-        total += got[extra : extra + own_rows, :].astype(f32)
+        total += got[...].astype(f32)
     dhid_ref[...] = total.astype(bf16)
-    sums = [own_ref[:extra, :].astype(bf16).astype(f32)]
-    sums += [got[:extra, :].astype(f32) for got in got_refs]
-    while len(sums) > 1:
-        sums = [a + b for a, b in zip(sums[0::2], sums[1::2])]
-    shared = sums[0].astype(bf16)
+    shared = (shared_ref[...].astype(f32) + other_ref[...].astype(f32)).astype(bf16)
     shared = jnp.concatenate(
         [shared[:, i * length : (i + 1) * length] for i in range(groups)], axis=0
     )
@@ -388,13 +400,13 @@
     return pl.BlockSpec(memory_space=memory)
 
 
-def call(kernel, inputs, n_smem, outs, scratch, flops, moved, unread=0, vmem=32):
+def call(kernel, inputs, n_smem, outs, scratch, flops, moved, unread=0, vmem=32, far=False):
     return pl.pallas_call(
         kernel,
         out_shape=outs,
         in_specs=[spec(pltpu.SMEM)] * n_smem
         + [spec()] * (len(inputs) - n_smem - unread)
-        + [spec(pl.ANY)] * unread,
+        + [spec(pltpu.HBM if far else pl.ANY)] * unread,
         out_specs=jax.tree.map(lambda _: spec(), outs),
         scratch_shapes=scratch,
         compiler_params=pltpu.CompilerParams(vmem_limit_bytes=vmem * 1024 * 1024),
@@ -440,16 +452,15 @@
             len(begun),
         )
 
-    def pack(parts, rows, *after):
+    def pack(parts, rows):
         return call(
             functools.partial(pack_kernel, len(parts), own_rows),
-            [*parts, *after],
+            parts,
             0,
             shape((rows, width), bf16),
             [],
             0,
             4 * rows * width,
-            len(after),
         )
 
     def column(own, count):
@@ -458,22 +469,40 @@
         half = count // 2
         return column(own, half) + column(across(own, 4 * half), half)
 
+    def after(value):
+        return call(
+            copy_kernel, [value, taps], 0, shape(value.shape, bf16), [], 0, 4 * value.size, 1
+        )
+
     if own_rows % TILE_ROWS == 0:
-        zs = column(pack([hidden, d_out], 2 * own_rows), nz)
-        coords, pieces = [], []
+        both = call(
+            first_kernel,
+            [hidden, d_out],
+            0,
+            shape((2 * own_rows, width), bf16),
+            [pltpu.SemaphoreType.DMA((2,))],
+            0,
+            8 * own_rows * width,
+            2,
+            vmem=48,
+            far=True,
+        )
+        zs = column(both, nz)
+        coords, pieces, planes = [], [], []
         for g, blocks in enumerate([range(0, nz // 2), range(nz // 2, nz)]):
-            chunk = pack([zs[j] for j in blocks], nz * own_rows, *([taps] if g else []))
-            if g == 0:
-                wall, wallt, gall, taps = prepare(chunk, zs[nz // 2])
+            chunk = pack([zs[j] for j in blocks], nz * own_rows)
             beside = across(chunk, 2)
             plane = [((0, 0), chunk), ((0, 1), beside)]
             for dc in range(1, ctx_size):
                 ahead = along(chunk, dc)
                 diagonal = along(beside, dc) if g else across(ahead, 2)
                 plane += [((dc, 0), ahead), ((dc, 1), diagonal)]
+            planes.append((tuple(blocks), plane))
+        wall, wallt, gall, taps = prepare(chunk)
+        for g, (blocks, plane) in enumerate(planes):
             for (dc, dx), piece in plane:
-                coords += [(dc, dx, 0, tuple(blocks)), (dc, dx, 1, tuple(blocks))]
-                pieces += [piece, across(piece, 1)]
+                coords += [(dc, dx, 0, blocks), (dc, dx, 1, blocks)]
+                pieces += [piece, across(after(piece) if dc and dx and not g else piece, 1)]
         layout = (tp_size, own_rows, tuple(coords))
         early, late = pieces[: len(pieces) // 2], pieces[len(pieces) // 2 :]
     else:
@@ -517,11 +546,14 @@
     got = across(send, 1)
     quarter = half // 2
     summed = keep + got.astype(f32)
-    send = summed[: extra + quarter].astype(bf16)
-    keep = jnp.concatenate(
-        [summed[:extra].astype(bf16).astype(f32), summed[extra + quarter :]], axis=0
-    )
+    shared = summed[:extra].astype(bf16)
+    send = summed[extra : extra + quarter].astype(bf16)
+    keep = summed[extra + quarter :]
     got = across(send, 2)
+    step = nz // 2
+    while step:
+        shared = (shared.astype(f32) + across(shared, 4 * step).astype(f32)).astype(bf16)
+        step //= 2
     outs = (shape((width, LANES), f32), shape((head, width), f32))
     if not ordered:
         outs += (shape((length, width), bf16),)
@@ -538,11 +570,10 @@
     )
     in_order = in_order[0] if in_order else pieces[0]
     own, *send = call(
-        functools.partial(stage_kernel, extra, own_rows),
+        functools.partial(stage_kernel, own_rows),
         [keep, got, d_w_out],
         0,
-        (shape((extra + own_rows, width), f32),)
-        + (shape((extra + own_rows, width), bf16),) * (nz - 1),
+        (shape((own_rows, width), f32),) + (shape((own_rows, width), bf16),) * (nz - 1),
         [],
         4 * quarter * width,
         10 * quarter * width,
@@ -550,8 +581,8 @@
     )
     got = [across(piece, 4 * (j + 1)) for j, piece in enumerate(send)]
     d_hidden, d_w_bc = call(
-        functools.partial(last_kernel, own_rows, scaling),
-        [own, in_order, *got],
+        functools.partial(last_kernel, scaling),
+        [own, in_order, shared, across(shared, 2), *got],
         0,
         (shape((own_rows, width), bf16), shape((2 * STATE, width), f32)),
         [],

time: 77.7 us -> 75.7 us (0.974)
  starting transfers between devices: 20.1 us -> 26.9 us
  waiting for transfers between devices: 32.6 us -> 27.9 us
  local copies, waits for them, and re-layouts: 6.01 us -> 1.75 us
    ppermute x19 -> x22, waiting for transfers between devices: 31.3 us -> 26 us  [across(): lax.ppermute(value, 'tp', [(i, i ^ flip_bits) for i in range(tp_size)])]
    ppermute x19 -> x22, starting transfers between devices: 17.5 us -> 22 us  [across(): lax.ppermute(value, 'tp', [(i, i ^ flip_bits) for i in range(tp_size)])]
    unnamed x16, local copies, waits for them, and re-layouts: 5.95 us -> 1.69 us
    ppermute x3, starting transfers between devices: 2.6 us -> 4.95 us  [along(): lax.ppermute(value, 'ctx', [((i + offset) % ctx_size, i) for i in range(c...]
    pallas_call x9 -> x10, Pallas kernels: 15.6 us -> 15.7 us  [call(): pl.pallas_call(kernel, out_shape=outs, in_specs=[spec(pltpu.SMEM)] * n_sm...]
  transfers between devices with their start and end apart: 22 -> 25, of which waited for: 8 -> 11; matrix products, arithmetic and copies ran while one was open for 0% -> 0% of each run, Pallas kernels for 9% -> 10%
where the time goes in v5:
time: 75.7 us; the launch traced here: 75.4 us
  waiting for transfers between devices  27.9 us (37%)
  starting transfers between devices  26.9 us (36%)
  Pallas kernels  15.7 us (21%)
  between operations  2.8 us (4%)
  local copies, waits for them, and re-layouts  1.75 us (2%)
    ppermute x22, waiting for transfers between devices, across(): lax.ppermute(value, 'tp', [(i, i ^ flip_bits) for i in range(tp_size)])  26 us
    ppermute x22, starting transfers between devices, across(): lax.ppermute(value, 'tp', [(i, i ^ flip_bits) for i in range(tp_size)])  22 us
    pallas_call x10, Pallas kernels, call(): pl.pallas_call(kernel, out_shape=outs, in_specs=[spec(pltpu.SMEM)] * n_sm...  15.7 us
    ppermute x3, starting transfers between devices, along(): lax.ppermute(value, 'ctx', [((i + offset) % ctx_size, i) for i in range(c...  4.95 us
    ppermute x3, waiting for transfers between devices, along(): lax.ppermute(value, 'ctx', [((i + offset) % ctx_size, i) for i in range(c...  1.92 us
    unnamed x16, local copies, waits for them, and re-layouts  1.69 us
  transfers between devices with their start and end apart: 25, of which 11 were waited for; matrix products, arithmetic and copies ran while one was open for 0% of the time, Pallas kernels for 10%

profile of v5, /device:TPU:0, one launch (start us, length us, event | category | flops | bytes accessed | tf_op | source)
XLA Modules:
  0.0 75.4 jit_solution(15195065137242412872)
XLA Ops:
  0.6 0.8 %copy-done.1 = bf16[16,2048]{1,0:T(8,128)(2,1)S(1)} copy-done((bf16[16,2048]{1,0:T(8,128)(2,1)S(1)}, bf16[16,2048]{1,0:T(8,128)(2,1)}, u32[]{:S(2)}) %copy-start.1) | copy-done | bytes 65560
  1.5 0.8 %copy-done.2 = bf16[16,2048]{1,0:T(8,128)(2,1)S(1)} copy-done((bf16[16,2048]{1,0:T(8,128)(2,1)S(1)}, bf16[16,2048]{1,0:T(8,128)(2,1)}, u32[]{:S(2)}) %copy-start.2) | copy-done | bytes 65560
  2.5 3.1 %collective-permute-start.9 = (bf16[32,2048]{1,0:T(8,128)(2,1)S(1)}, bf16[32,2048]{1,0:T(8,128)(2,1)S(1)}, u32[]{:S(2)}, u32[]{:S(2)}) collective-permute-start(bf16[32,2048]{1,0:T(8,128)(2,1)S(1)} %shard_map.129.refs_0_), channel_id=1, source_target_pairs={{0,4},{1,5},{2,6},{3,7},{4,0},{5,1},{6,2},{7,3},{8,12},{9,13},{10,... | collective-permute-start | bytes 393224 | tf_op jit(solution)/shard_map/ppermute | solution.py:431
  5.6 2.6 %collective-permute-start = (bf16[32,2048]{1,0:T(8,128)(2,1)S(1)}, bf16[32,2048]{1,0:T(8,128)(2,1)S(1)}, u32[]{:S(2)}, u32[]{:S(2)}) collective-permute-start(bf16[32,2048]{1,0:T(8,128)(2,1)S(1)} %shard_map.129.refs_0_), channel_id=1, source_target_pairs={{0,8},{1,9},{2,10},{3,11},{4,12},{5,13},{6,14},{7,15},{8,0},{9,1},... | collective-permute-start | bytes 393224 | tf_op jit(solution)/shard_map/ppermute | solution.py:431
  8.2 2.8 %collective-permute-done.9.refs_1_ = bf16[32,2048]{1,0:T(8,128)(2,1)S(1)} collective-permute-done((bf16[32,2048]{1,0:T(8,128)(2,1)S(1)}, bf16[32,2048]{1,0:T(8,128)(2,1)S(1)}, u32[]{:S(2)}, u32[]{:S(2)}) %collective-permute-start.9) | collective-permute-done | bytes 131104 | tf_op jit(solution)/shard_map/ppermute | solution.py:431
  11.0 1.9 %collective-permute-start.13 = (bf16[64,2048]{1,0:T(8,128)(2,1)S(1)}, bf16[64,2048]{1,0:T(8,128)(2,1)S(1)}, u32[]{:S(2)}, u32[]{:S(2)}) collective-permute-start(bf16[64,2048]{1,0:T(8,128)(2,1)S(1)} %shard_map.131.refs_0_.refs_1_), channel_id=1, source_target_pairs={{16,0},{0,16},{17,1},{1,17},{18,2},{2,18},{19,3},{3,19},{20,4},{4,... | collective-permute-start | bytes 786440 | tf_op jit(solution)/shard_map/ppermute | solution.py:434
  12.9 1.4 %collective-permute-done.refs_0_ = bf16[32,2048]{1,0:T(8,128)(2,1)S(1)} collective-permute-done((bf16[32,2048]{1,0:T(8,128)(2,1)S(1)}, bf16[32,2048]{1,0:T(8,128)(2,1)S(1)}, u32[]{:S(2)}, u32[]{:S(2)}) %collective-permute-start) | collective-permute-done | bytes 131104 | tf_op jit(solution)/shard_map/ppermute | solution.py:431
  14.8 1.5 %collective-permute-start.11 = (bf16[64,2048]{1,0:T(8,128)(2,1)S(1)}, bf16[64,2048]{1,0:T(8,128)(2,1)S(1)}, u32[]{:S(2)}, u32[]{:S(2)}) collective-permute-start(bf16[64,2048]{1,0:T(8,128)(2,1)S(1)} %shard_map.131.refs_0_.refs_1_), channel_id=1, source_target_pairs={{0,2},{1,3},{2,0},{3,1},{4,6},{5,7},{6,4},{7,5},{8,10},{9,11},{10,... | collective-permute-start | bytes 786440 | tf_op jit(solution)/shard_map/ppermute | solution.py:431
  16.3 3.0 %collective-permute-done.1.refs_1_ = bf16[32,2048]{1,0:T(8,128)(2,1)S(1)} collective-permute-done((bf16[32,2048]{1,0:T(8,128)(2,1)S(1)}, bf16[32,2048]{1,0:T(8,128)(2,1)S(1)}, u32[]{:S(2)}, u32[]{:S(2)}) %collective-permute-start.1) | collective-permute-done | bytes 131104 | tf_op jit(solution)/shard_map/ppermute | solution.py:431
  19.3 1.6 %collective-permute-start.3 = (bf16[64,2048]{1,0:T(8,128)(2,1)S(1)}, bf16[64,2048]{1,0:T(8,128)(2,1)S(1)}, u32[]{:S(2)}, u32[]{:S(2)}) collective-permute-start(bf16[64,2048]{1,0:T(8,128)(2,1)S(1)} %shard_map.130.refs_5_.refs_4_.refs_9_), channel_id=1, source_target_pairs={{0,2},{1,3},{2,0},{3,1},{4,6},{5,7},{6,4},{7,5},{8,10},{9,11},{10,... | collective-permute-start | bytes 786440 | tf_op jit(solution)/shard_map/ppermute | solution.py:431
  21.4 1.5 %collective-permute-start.5 = (bf16[64,2048]{1,0:T(8,128)(2,1)S(1)}, bf16[64,2048]{1,0:T(8,128)(2,1)S(1)}, u32[]{:S(2)}, u32[]{:S(2)}) collective-permute-start(bf16[64,2048]{1,0:T(8,128)(2,1)S(1)} %shard_map.130.refs_5_.refs_4_.refs_9_), channel_id=1, source_target_pairs={{16,0},{0,16},{17,1},{1,17},{18,2},{2,18},{19,3},{3,19},{20,4},{4,... | collective-permute-start | bytes 786440 | tf_op jit(solution)/shard_map/ppermute | solution.py:434
  22.9 1.1 %collective-permute-done.11.refs_2_.refs_3_ = bf16[64,2048]{1,0:T(8,128)(2,1)S(1)} collective-permute-done((bf16[64,2048]{1,0:T(8,128)(2,1)S(1)}, bf16[64,2048]{1,0:T(8,128)(2,1)S(1)}, u32[]{:S(2)}, u32[]{:S(2)}) %collective-permute-start.11) | collective-permute-done | bytes 262176 | tf_op jit(solution)/shard_map/ppermute | solution.py:431
  24.0 5.6 %collective-permute-done.3.refs_6_.refs_11_ = bf16[64,2048]{1,0:T(8,128)(2,1)S(1)} collective-permute-done((bf16[64,2048]{1,0:T(8,128)(2,1)S(1)}, bf16[64,2048]{1,0:T(8,128)(2,1)S(1)}, u32[]{:S(2)}, u32[]{:S(2)}) %collective-permute-start.3) | collective-permute-done | bytes 262176 | tf_op jit(solution)/shard_map/ppermute | solution.py:431
  29.7 3.2 %collective-permute-done.15.value_ref.refs_6_.refs_7_ = bf16[64,2048]{1,0:T(8,128)(2,1)S(1)} collective-permute-done((bf16[64,2048]{1,0:T(8,128)(2,1)S(1)}, bf16[64,2048]{1,0:T(8,128)(2,1)S(1)}, u32[]{:S(2)}, u32[]{:S(2)}) %collective-permute-start.15) | collective-permute-done | bytes 262176 | tf_op jit(solution)/shard_map/ppermute | solution.py:431
  32.8 1.5 %collective-permute-start.7 = (bf16[64,2048]{1,0:T(8,128)(2,1)S(1)}, bf16[64,2048]{1,0:T(8,128)(2,1)S(1)}, u32[]{:S(2)}, u32[]{:S(2)}) collective-permute-start(bf16[64,2048]{1,0:T(8,128)(2,1)S(1)} %collective-permute-done.3.refs_6_.refs_11_), channel_id=1, source_target_pairs={{16,0},{0,16},{17,1},{1,17},{18,2},{2,18},{19,3},{3,19},{20,4},{4,... | collective-permute-start | bytes 786440 | tf_op jit(solution)/shard_map/ppermute | solution.py:434
  34.4 1.7 %shard_map.132 = (bf16[2048,512]{1,0:T(8,128)(2,1)S(1)}, bf16[512,2048]{1,0:T(8,128)(2,1)S(1)}, bf16[2048,256]{1,0:T(8,128)(2,1)S(1)}, f32[4,128]{1,0:T(4,128)S(1)}) custom-call(s32[4]{0:T(128)S(1)} %pad_add_fusion.ids_ref.refs_0_, bf16[2048,128]{1,0:T(8,128)(2,1)S(1)} %copy-done.3, bf16[32,2048]{1,0:T(8,128)(2,1)S(1)} %bitcast.6, ...), custom_call_target="tpu_custom_call" | custom-call | flops 805306368 | bytes 5242880 | tf_op jit(solution)/shard_map/pallas_call | solution.py:404
  37.3 1.9 %collective-permute-done.7.refs_10_.refs_15_ = bf16[64,2048]{1,0:T(8,128)(2,1)S(1)} collective-permute-done((bf16[64,2048]{1,0:T(8,128)(2,1)S(1)}, bf16[64,2048]{1,0:T(8,128)(2,1)S(1)}, u32[]{:S(2)}, u32[]{:S(2)}) %collective-permute-start.7) | collective-permute-done | bytes 262176 | tf_op jit(solution)/shard_map/ppermute | solution.py:434
  41.1 1.0 %shard_map.134 = (f32[256,512]{1,0:T(8,128)S(1)}, f32[256,256]{1,0:T(8,128)S(1)}) custom-call(bf16[64,2048]{1,0:T(8,128)(2,1)S(1)} %shard_map.131.refs_0_.refs_1_, bf16[64,2048]{1,0:T(8,128)(2,1)S(1)} %collective-permute-done.10.refs_1_.refs_2_, bf16[64,2048]{1,0:T(8,128)(2,1)S(1)} %collective-permute-done.11.refs_2_.refs_3_, ...), custom_call_target="tpu_custom_call" | custom-call | flops 805306368 | bytes 2097152 | tf_op jit(solution)/shard_map/pallas_call | solution.py:404
  42.2 6.5 %shard_map.135 = (bf16[144,2048]{1,0:T(8,128)(2,1)S(1)}, f32[144,2048]{1,0:T(8,128)S(1)}, bf16[512,512]{1,0:T(8,128)(2,1)S(1)}, bf16[512,256]{1,0:T(8,128)(2,1)S(1)}) custom-call(s32[4]{0:T(128)S(1)} %pad_add_fusion.ids_ref.refs_0_, f32[1]{0:T(128)S(6)} %copy.14.refs_1_, f32[1]{0:T(128)S(6)} %copy.15.refs_2_, f32[1]{0:T(128)S(6)} %copy.16.refs_3_, ...), custom_call_target="tpu_custom_call" | custom-call | flops 2147483648 | bytes 8388608 | tf_op jit(solution)/shard_map/pallas_call | solution.py:404
  48.7 0.6 collective-permute-start.17
  49.2 1.6 %collective-permute-done.17 = bf16[144,2048]{1,0:T(8,128)(2,1)S(1)} collective-permute-done((bf16[144,2048]{1,0:T(8,128)(2,1)S(1)}, bf16[144,2048]{1,0:T(8,128)(2,1)S(1)}, u32[]{:S(2)}, u32[]{:S(2)}) %collective-permute-start.17) | collective-permute-done | bytes 589856 | tf_op jit(solution)/shard_map/ppermute | solution.py:431
  51.1 2.7 %collective-permute-start.19 = (bf16[16,2048]{1,0:T(8,128)(2,1)S(1)}, bf16[16,2048]{1,0:T(8,128)(2,1)S(1)}, u32[]{:S(2)}, u32[]{:S(2)}) collective-permute-start(bf16[16,2048]{1,0:T(8,128)(2,1)S(1)} %slice.16), channel_id=1, source_target_pairs={{0,8},{1,9},{2,10},{3,11},{4,12},{5,13},{6,14},{7,15},{8,0},{9,1},... | collective-permute-start | bytes 196616 | tf_op jit(solution)/shard_map/ppermute | solution.py:431
  53.8 1.6 %collective-permute-start.18 = (bf16[64,2048]{1,0:T(8,128)(2,1)S(1)}, bf16[64,2048]{1,0:T(8,128)(2,1)S(1)}, u32[]{:S(2)}, u32[]{:S(2)}) collective-permute-start(bf16[64,2048]{1,0:T(8,128)(2,1)S(1)} %slice.15.refs_19_), channel_id=1, source_target_pairs={{0,2},{1,3},{2,0},{3,1},{4,6},{5,7},{6,4},{7,5},{8,10},{9,11},{10,... | collective-permute-start | bytes 786440 | tf_op jit(solution)/shard_map/ppermute | solution.py:431
  55.3 2.5 %collective-permute-done.19 = bf16[16,2048]{1,0:T(8,128)(2,1)S(1)} collective-permute-done((bf16[16,2048]{1,0:T(8,128)(2,1)S(1)}, bf16[16,2048]{1,0:T(8,128)(2,1)S(1)}, u32[]{:S(2)}, u32[]{:S(2)}) %collective-permute-start.19) | collective-permute-done | bytes 65568 | tf_op jit(solution)/shard_map/ppermute | solution.py:431
  57.9 4.4 %shard_map.136 = (f32[2048,128]{1,0:T(8,128)}, f32[64,2048]{1,0:T(8,128)}, bf16[512,2048]{1,0:T(8,128)(2,1)S(1)}) custom-call(s32[4]{0:T(128)S(1)} %pad_add_fusion.ids_ref.refs_0_, bf16[64,2048]{1,0:T(8,128)(2,1)S(1)} %shard_map.131.refs_0_.refs_1_, bf16[64,2048]{1,0:T(8,128)(2,1)S(1)} %collective-permute-done.10.refs_1_.refs_2_, ...), custom_call_target="tpu_custom_call" | custom-call | flops 2147483648 | bytes 8388608 | tf_op jit(solution)/shard_map/pallas_call | solution.py:404
  62.4 1.6 %collective-permute-start.21 = (bf16[16,2048]{1,0:T(8,128)(2,1)S(1)}, bf16[16,2048]{1,0:T(8,128)(2,1)S(1)}, u32[]{:S(2)}, u32[]{:S(2)}) collective-permute-start(bf16[16,2048]{1,0:T(8,128)(2,1)S(1)} %add_convert_fusion.shared_ref), channel_id=1, source_target_pairs={{0,2},{1,3},{2,0},{3,1},{4,6},{5,7},{6,4},{7,5},{8,10},{9,11},{10,... | collective-permute-start | bytes 196616 | tf_op jit(solution)/shard_map/ppermute | solution.py:431
  64.0 2.1 %collective-permute-start.22 = (bf16[16,2048]{1,0:T(8,128)(2,1)S(1)}, bf16[16,2048]{1,0:T(8,128)(2,1)S(1)}, u32[]{:S(2)}, u32[]{:S(2)}) collective-permute-start(bf16[16,2048]{1,0:T(8,128)(2,1)S(1)} %get-tuple-element.36), channel_id=1, source_target_pairs={{0,4},{1,5},{2,6},{3,7},{4,0},{5,1},{6,2},{7,3},{8,12},{9,13},{10,... | collective-permute-start | bytes 196616 | tf_op jit(solution)/shard_map/ppermute | solution.py:431
  66.1 1.3 %collective-permute-start.23 = (bf16[16,2048]{1,0:T(8,128)(2,1)S(1)}, bf16[16,2048]{1,0:T(8,128)(2,1)S(1)}, u32[]{:S(2)}, u32[]{:S(2)}) collective-permute-start(bf16[16,2048]{1,0:T(8,128)(2,1)S(1)} %get-tuple-element.37), channel_id=1, source_target_pairs={{0,8},{1,9},{2,10},{3,11},{4,12},{5,13},{6,14},{7,15},{8,0},{9,1},... | collective-permute-start | bytes 196616 | tf_op jit(solution)/shard_map/ppermute | solution.py:431
  67.4 1.4 %collective-permute-start.24 = (bf16[16,2048]{1,0:T(8,128)(2,1)S(1)}, bf16[16,2048]{1,0:T(8,128)(2,1)S(1)}, u32[]{:S(2)}, u32[]{:S(2)}) collective-permute-start(bf16[16,2048]{1,0:T(8,128)(2,1)S(1)} %get-tuple-element.38), channel_id=1, source_target_pairs={{0,12},{1,13},{2,14},{3,15},{4,8},{5,9},{6,10},{7,11},{8,4},{9,5},... | collective-permute-start | bytes 196616 | tf_op jit(solution)/shard_map/ppermute | solution.py:431
  68.7 3.6 %collective-permute-done.23.refs_1_ = bf16[16,2048]{1,0:T(8,128)(2,1)S(1)} collective-permute-done((bf16[16,2048]{1,0:T(8,128)(2,1)S(1)}, bf16[16,2048]{1,0:T(8,128)(2,1)S(1)}, u32[]{:S(2)}, u32[]{:S(2)}) %collective-permute-start.23) | collective-permute-done | bytes 65568 | tf_op jit(solution)/shard_map/ppermute | solution.py:431
  72.3 1.2 %collective-permute-done.24.refs_2_ = bf16[16,2048]{1,0:T(8,128)(2,1)S(1)} collective-permute-done((bf16[16,2048]{1,0:T(8,128)(2,1)S(1)}, bf16[16,2048]{1,0:T(8,128)(2,1)S(1)}, u32[]{:S(2)}, u32[]{:S(2)}) %collective-permute-start.24) | collective-permute-done | bytes 65568 | tf_op jit(solution)/shard_map/ppermute | solution.py:431
  73.5 1.9 %shard_map.138 = (bf16[16,2048]{1,0:T(8,128)(2,1)}, f32[32,2048]{1,0:T(8,128)}) custom-call(f32[16,2048]{1,0:T(8,128)S(1)} %get-tuple-element.34.own_ref, bf16[512,2048]{1,0:T(8,128)(2,1)S(1)} %get-tuple-element.35.h_ref, bf16[16,2048]{1,0:T(8,128)(2,1)S(1)} %add_convert_fusion.shared_ref, bf16[16,2048]{1,0:T(8,128)(2,1)S(1)} %collective-permute-done.21.other_ref, ...), custom_call_target="tpu_custom_call" | custom-call | flops 268435456 | bytes 4194304 | tf_op jit(solution)/shard_map/pallas_call | solution.py:404
  (51 shorter events, 2.9 us)
Async XLA Ops:
  0.6 0.8 %copy-start.1 = (bf16[16,2048]{1,0:T(8,128)(2,1)S(1)}, bf16[16,2048]{1,0:T(8,128)(2,1)}, u32[]{:S(2)}) copy-start(bf16[16,2048]{1,0:T(8,128)(2,1)} %hidden_ref.1) | copy-start | bytes 196612
  2.3 32.1 %copy-start.3 = (bf16[2048,128]{1,0:T(8,128)(2,1)S(1)}, bf16[2048,128]{1,0:T(8,128)(2,1)}, u32[]{:S(2)}) copy-start(bf16[2048,128]{1,0:T(8,128)(2,1)} %refs_0_.1) | copy-start | bytes 1572868
  2.3 32.1 %copy-start.4 = (bf16[64,2048]{1,0:T(8,128)(2,1)S(1)}, bf16[64,2048]{1,0:T(8,128)(2,1)}, u32[]{:S(2)}) copy-start(bf16[64,2048]{1,0:T(8,128)(2,1)} %refs_3_.2) | copy-start | bytes 786436
  2.3 32.1 %copy-start.5 = (bf16[2048,32]{0,1:T(8,128)(2,1)S(1)}, bf16[2048,32]{0,1:T(8,128)(2,1)}, u32[]{:S(2)}) copy-start(bf16[2048,32]{0,1:T(8,128)(2,1)} %param.12) | copy-start | bytes 393220
  2.3 32.1 %copy-start.6 = (bf16[1,2048]{1,0:T(2,128)(2,1)S(1)}, bf16[1,2048]{1,0:T(2,128)(2,1)}, u32[]{:S(2)}) copy-start(bf16[1,2048]{1,0:T(2,128)(2,1)} %refs_2_.2) | copy-start | bytes 12292
  2.3 32.1 %copy-start.7 = (f32[4,64]{1,0:T(4,128)S(1)}, f32[4,64]{1,0:T(4,128)}, u32[]{:S(2)}) copy-start(f32[4,64]{1,0:T(4,128)} %refs_4_.1) | copy-start | bytes 3076
  2.5 8.4 %collective-permute-start.9 = (bf16[32,2048]{1,0:T(8,128)(2,1)S(1)}, bf16[32,2048]{1,0:T(8,128)(2,1)S(1)}, u32[]{:S(2)}, u32[]{:S(2)}) collective-permute-start(bf16[32,2048]{1,0:T(8,128)(2,1)S(1)} %shard_map.129.refs_0_), channel_id=1, source_target_pairs={{0,4},{1,5},{2,6},{3,7},{4,0},{5,1},{6,2},{7,3},{8,12},{9,13},{10,... | collective-permute-start | bytes 393224 | tf_op jit(solution)/shard_map/ppermute | solution.py:431
  5.6 8.7 %collective-permute-start = (bf16[32,2048]{1,0:T(8,128)(2,1)S(1)}, bf16[32,2048]{1,0:T(8,128)(2,1)S(1)}, u32[]{:S(2)}, u32[]{:S(2)}) collective-permute-start(bf16[32,2048]{1,0:T(8,128)(2,1)S(1)} %shard_map.129.refs_0_), channel_id=1, source_target_pairs={{0,8},{1,9},{2,10},{3,11},{4,12},{5,13},{6,14},{7,15},{8,0},{9,1},... | collective-permute-start | bytes 393224 | tf_op jit(solution)/shard_map/ppermute | solution.py:431
  11.0 9.9 %collective-permute-start.13 = (bf16[64,2048]{1,0:T(8,128)(2,1)S(1)}, bf16[64,2048]{1,0:T(8,128)(2,1)S(1)}, u32[]{:S(2)}, u32[]{:S(2)}) collective-permute-start(bf16[64,2048]{1,0:T(8,128)(2,1)S(1)} %shard_map.131.refs_0_.refs_1_), channel_id=1, source_target_pairs={{16,0},{0,16},{17,1},{1,17},{18,2},{2,18},{19,3},{3,19},{20,4},{4,... | collective-permute-start | bytes 786440 | tf_op jit(solution)/shard_map/ppermute | solution.py:434
  14.3 5.0 %collective-permute-start.1 = (bf16[32,2048]{1,0:T(8,128)(2,1)S(1)}, bf16[32,2048]{1,0:T(8,128)(2,1)S(1)}, u32[]{:S(2)}, u32[]{:S(2)}) collective-permute-start(bf16[32,2048]{1,0:T(8,128)(2,1)S(1)} %collective-permute-done.refs_0_), channel_id=1, source_target_pairs={{0,4},{1,5},{2,6},{3,7},{4,0},{5,1},{6,2},{7,3},{8,12},{9,13},{10,... | collective-permute-start | bytes 393224 | tf_op jit(solution)/shard_map/ppermute | solution.py:431
  14.8 9.2 %collective-permute-start.11 = (bf16[64,2048]{1,0:T(8,128)(2,1)S(1)}, bf16[64,2048]{1,0:T(8,128)(2,1)S(1)}, u32[]{:S(2)}, u32[]{:S(2)}) collective-permute-start(bf16[64,2048]{1,0:T(8,128)(2,1)S(1)} %shard_map.131.refs_0_.refs_1_), channel_id=1, source_target_pairs={{0,2},{1,3},{2,0},{3,1},{4,6},{5,7},{6,4},{7,5},{8,10},{9,11},{10,... | collective-permute-start | bytes 786440 | tf_op jit(solution)/shard_map/ppermute | solution.py:431
  19.3 10.3 %collective-permute-start.3 = (bf16[64,2048]{1,0:T(8,128)(2,1)S(1)}, bf16[64,2048]{1,0:T(8,128)(2,1)S(1)}, u32[]{:S(2)}, u32[]{:S(2)}) collective-permute-start(bf16[64,2048]{1,0:T(8,128)(2,1)S(1)} %shard_map.130.refs_5_.refs_4_.refs_9_), channel_id=1, source_target_pairs={{0,2},{1,3},{2,0},{3,1},{4,6},{5,7},{6,4},{7,5},{8,10},{9,11},{10,... | collective-permute-start | bytes 786440 | tf_op jit(solution)/shard_map/ppermute | solution.py:431
  20.9 11.9 %collective-permute-start.15 = (bf16[64,2048]{1,0:T(8,128)(2,1)S(1)}, bf16[64,2048]{1,0:T(8,128)(2,1)S(1)}, u32[]{:S(2)}, u32[]{:S(2)}) collective-permute-start(bf16[64,2048]{1,0:T(8,128)(2,1)S(1)} %collective-permute-done.13.refs_4_.refs_5_), channel_id=1, source_target_pairs={{0,2},{1,3},{2,0},{3,1},{4,6},{5,7},{6,4},{7,5},{8,10},{9,11},{10,... | collective-permute-start | bytes 786440 | tf_op jit(solution)/shard_map/ppermute | solution.py:431
  21.4 14.7 %collective-permute-start.10 = (bf16[64,2048]{1,0:T(8,128)(2,1)S(1)}, bf16[64,2048]{1,0:T(8,128)(2,1)S(1)}, u32[]{:S(2)}, u32[]{:S(2)}) collective-permute-start(bf16[64,2048]{1,0:T(8,128)(2,1)S(1)} %shard_map.131.refs_0_.refs_1_), channel_id=1, source_target_pairs={{0,1},{1,0},{2,3},{3,2},{4,5},{5,4},{6,7},{7,6},{8,9},{9,8},{10,11... | collective-permute-start | bytes 786440 | tf_op jit(solution)/shard_map/ppermute | solution.py:431
  21.4 14.8 %collective-permute-start.5 = (bf16[64,2048]{1,0:T(8,128)(2,1)S(1)}, bf16[64,2048]{1,0:T(8,128)(2,1)S(1)}, u32[]{:S(2)}, u32[]{:S(2)}) collective-permute-start(bf16[64,2048]{1,0:T(8,128)(2,1)S(1)} %shard_map.130.refs_5_.refs_4_.refs_9_), channel_id=1, source_target_pairs={{16,0},{0,16},{17,1},{1,17},{18,2},{2,18},{19,3},{3,19},{20,4},{4,... | collective-permute-start | bytes 786440 | tf_op jit(solution)/shard_map/ppermute | solution.py:434
  24.0 12.7 %collective-permute-start.14 = (bf16[64,2048]{1,0:T(8,128)(2,1)S(1)}, bf16[64,2048]{1,0:T(8,128)(2,1)S(1)}, u32[]{:S(2)}, u32[]{:S(2)}) collective-permute-start(bf16[64,2048]{1,0:T(8,128)(2,1)S(1)} %collective-permute-done.13.refs_4_.refs_5_), channel_id=1, source_target_pairs={{0,1},{1,0},{2,3},{3,2},{4,5},{5,4},{6,7},{7,6},{8,9},{9,8},{10,11... | collective-permute-start | bytes 786440 | tf_op jit(solution)/shard_map/ppermute | solution.py:431
  29.6 7.2 %collective-permute-start.12 = (bf16[64,2048]{1,0:T(8,128)(2,1)S(1)}, bf16[64,2048]{1,0:T(8,128)(2,1)S(1)}, u32[]{:S(2)}, u32[]{:S(2)}) collective-permute-start(bf16[64,2048]{1,0:T(8,128)(2,1)S(1)} %collective-permute-done.11.refs_2_.refs_3_), channel_id=1, source_target_pairs={{0,1},{1,0},{2,3},{3,2},{4,5},{5,4},{6,7},{7,6},{8,9},{9,8},{10,11... | collective-permute-start | bytes 786440 | tf_op jit(solution)/shard_map/ppermute | solution.py:431
  32.8 6.4 %collective-permute-start.7 = (bf16[64,2048]{1,0:T(8,128)(2,1)S(1)}, bf16[64,2048]{1,0:T(8,128)(2,1)S(1)}, u32[]{:S(2)}, u32[]{:S(2)}) collective-permute-start(bf16[64,2048]{1,0:T(8,128)(2,1)S(1)} %collective-permute-done.3.refs_6_.refs_11_), channel_id=1, source_target_pairs={{16,0},{0,16},{17,1},{1,17},{18,2},{2,18},{19,3},{3,19},{20,4},{4,... | collective-permute-start | bytes 786440 | tf_op jit(solution)/shard_map/ppermute | solution.py:434
  36.2 5.0 %collective-permute-start.16 = (bf16[64,2048]{1,0:T(8,128)(2,1)S(1)}, bf16[64,2048]{1,0:T(8,128)(2,1)S(1)}, u32[]{:S(2)}, u32[]{:S(2)}) collective-permute-start(bf16[64,2048]{1,0:T(8,128)(2,1)S(1)} %shard_map.133), channel_id=1, source_target_pairs={{0,1},{1,0},{2,3},{3,2},{4,5},{5,4},{6,7},{7,6},{8,9},{9,8},{10,11... | collective-permute-start | bytes 786440 | tf_op jit(solution)/shard_map/ppermute | solution.py:431
  36.3 5.9 %collective-permute-start.2 = (bf16[64,2048]{1,0:T(8,128)(2,1)S(1)}, bf16[64,2048]{1,0:T(8,128)(2,1)S(1)}, u32[]{:S(2)}, u32[]{:S(2)}) collective-permute-start(bf16[64,2048]{1,0:T(8,128)(2,1)S(1)} %shard_map.130.refs_5_.refs_4_.refs_9_), channel_id=1, source_target_pairs={{0,1},{1,0},{2,3},{3,2},{4,5},{5,4},{6,7},{7,6},{8,9},{9,8},{10,11... | collective-permute-start | bytes 786440 | tf_op jit(solution)/shard_map/ppermute | solution.py:431
  36.8 5.4 %collective-permute-start.4 = (bf16[64,2048]{1,0:T(8,128)(2,1)S(1)}, bf16[64,2048]{1,0:T(8,128)(2,1)S(1)}, u32[]{:S(2)}, u32[]{:S(2)}) collective-permute-start(bf16[64,2048]{1,0:T(8,128)(2,1)S(1)} %collective-permute-done.3.refs_6_.refs_11_), channel_id=1, source_target_pairs={{0,1},{1,0},{2,3},{3,2},{4,5},{5,4},{6,7},{7,6},{8,9},{9,8},{10,11... | collective-permute-start | bytes 786440 | tf_op jit(solution)/shard_map/ppermute | solution.py:431
  36.8 5.3 %collective-permute-start.6 = (bf16[64,2048]{1,0:T(8,128)(2,1)S(1)}, bf16[64,2048]{1,0:T(8,128)(2,1)S(1)}, u32[]{:S(2)}, u32[]{:S(2)}) collective-permute-start(bf16[64,2048]{1,0:T(8,128)(2,1)S(1)} %collective-permute-done.5.refs_8_.refs_13_), channel_id=1, source_target_pairs={{0,1},{1,0},{2,3},{3,2},{4,5},{5,4},{6,7},{7,6},{8,9},{9,8},{10,11... | collective-permute-start | bytes 786440 | tf_op jit(solution)/shard_map/ppermute | solution.py:431
  39.2 3.0 %collective-permute-start.8 = (bf16[64,2048]{1,0:T(8,128)(2,1)S(1)}, bf16[64,2048]{1,0:T(8,128)(2,1)S(1)}, u32[]{:S(2)}, u32[]{:S(2)}) collective-permute-start(bf16[64,2048]{1,0:T(8,128)(2,1)S(1)} %collective-permute-done.7.refs_10_.refs_15_), channel_id=1, source_target_pairs={{0,1},{1,0},{2,3},{3,2},{4,5},{5,4},{6,7},{7,6},{8,9},{9,8},{10,11... | collective-permute-start | bytes 786440 | tf_op jit(solution)/shard_map/ppermute | solution.py:431
  48.7 2.2 %collective-permute-start.17 = (bf16[144,2048]{1,0:T(8,128)(2,1)S(1)}, bf16[144,2048]{1,0:T(8,128)(2,1)S(1)}, u32[]{:S(2)}, u32[]{:S(2)}) collective-permute-start(bf16[144,2048]{1,0:T(8,128)(2,1)S(1)} %get-tuple-element.30), channel_id=1, source_target_pairs={{0,1},{1,0},{2,3},{3,2},{4,5},{5,4},{6,7},{7,6},{8,9},{9,8},{10,11... | collective-permute-start | bytes 1769480 | tf_op jit(solution)/shard_map/ppermute | solution.py:431
  51.1 6.7 %collective-permute-start.19 = (bf16[16,2048]{1,0:T(8,128)(2,1)S(1)}, bf16[16,2048]{1,0:T(8,128)(2,1)S(1)}, u32[]{:S(2)}, u32[]{:S(2)}) collective-permute-start(bf16[16,2048]{1,0:T(8,128)(2,1)S(1)} %slice.16), channel_id=1, source_target_pairs={{0,8},{1,9},{2,10},{3,11},{4,12},{5,13},{6,14},{7,15},{8,0},{9,1},... | collective-permute-start | bytes 196616 | tf_op jit(solution)/shard_map/ppermute | solution.py:431
  53.8 10.2 %collective-permute-start.18 = (bf16[64,2048]{1,0:T(8,128)(2,1)S(1)}, bf16[64,2048]{1,0:T(8,128)(2,1)S(1)}, u32[]{:S(2)}, u32[]{:S(2)}) collective-permute-start(bf16[64,2048]{1,0:T(8,128)(2,1)S(1)} %slice.15.refs_19_), channel_id=1, source_target_pairs={{0,2},{1,3},{2,0},{3,1},{4,6},{5,7},{6,4},{7,5},{8,10},{9,11},{10,... | collective-permute-start | bytes 786440 | tf_op jit(solution)/shard_map/ppermute | solution.py:431
  57.8 4.5 %collective-permute-start.20 = (bf16[16,2048]{1,0:T(8,128)(2,1)S(1)}, bf16[16,2048]{1,0:T(8,128)(2,1)S(1)}, u32[]{:S(2)}, u32[]{:S(2)}) collective-permute-start(bf16[16,2048]{1,0:T(8,128)(2,1)S(1)} %add_convert_fusion.1), channel_id=1, source_target_pairs={{0,4},{1,5},{2,6},{3,7},{4,0},{5,1},{6,2},{7,3},{8,12},{9,13},{10,... | collective-permute-start | bytes 196616 | tf_op jit(solution)/shard_map/ppermute | solution.py:431
  62.3 1.6 %copy-start = (f32[64,2048]{1,0:T(8,128)S(1)}, f32[64,2048]{1,0:T(8,128)}, u32[]{:S(2)}) copy-start(f32[64,2048]{1,0:T(8,128)} %get-tuple-element.21._) | copy-start | bytes 1572868
  62.4 6.4 %collective-permute-start.21 = (bf16[16,2048]{1,0:T(8,128)(2,1)S(1)}, bf16[16,2048]{1,0:T(8,128)(2,1)S(1)}, u32[]{:S(2)}, u32[]{:S(2)}) collective-permute-start(bf16[16,2048]{1,0:T(8,128)(2,1)S(1)} %add_convert_fusion.shared_ref), channel_id=1, source_target_pairs={{0,2},{1,3},{2,0},{3,1},{4,6},{5,7},{6,4},{7,5},{8,10},{9,11},{10,... | collective-permute-start | bytes 196616 | tf_op jit(solution)/shard_map/ppermute | solution.py:431
  64.0 4.7 %collective-permute-start.22 = (bf16[16,2048]{1,0:T(8,128)(2,1)S(1)}, bf16[16,2048]{1,0:T(8,128)(2,1)S(1)}, u32[]{:S(2)}, u32[]{:S(2)}) collective-permute-start(bf16[16,2048]{1,0:T(8,128)(2,1)S(1)} %get-tuple-element.36), channel_id=1, source_target_pairs={{0,4},{1,5},{2,6},{3,7},{4,0},{5,1},{6,2},{7,3},{8,12},{9,13},{10,... | collective-permute-start | bytes 196616 | tf_op jit(solution)/shard_map/ppermute | solution.py:431
  66.1 6.3 %collective-permute-start.23 = (bf16[16,2048]{1,0:T(8,128)(2,1)S(1)}, bf16[16,2048]{1,0:T(8,128)(2,1)S(1)}, u32[]{:S(2)}, u32[]{:S(2)}) collective-permute-start(bf16[16,2048]{1,0:T(8,128)(2,1)S(1)} %get-tuple-element.37), channel_id=1, source_target_pairs={{0,8},{1,9},{2,10},{3,11},{4,12},{5,13},{6,14},{7,15},{8,0},{9,1},... | collective-permute-start | bytes 196616 | tf_op jit(solution)/shard_map/ppermute | solution.py:431
  67.4 6.2 %collective-permute-start.24 = (bf16[16,2048]{1,0:T(8,128)(2,1)S(1)}, bf16[16,2048]{1,0:T(8,128)(2,1)S(1)}, u32[]{:S(2)}, u32[]{:S(2)}) collective-permute-start(bf16[16,2048]{1,0:T(8,128)(2,1)S(1)} %get-tuple-element.38), channel_id=1, source_target_pairs={{0,12},{1,13},{2,14},{3,15},{4,8},{5,9},{6,10},{7,11},{8,4},{9,5},... | collective-permute-start | bytes 196616 | tf_op jit(solution)/shard_map/ppermute | solution.py:431
  (1 other events, 0.8 us)

commit v6 on v5

--- a/solution.py
+++ b/solution.py
@@ -96,13 +96,9 @@
             out_ref[rows, :] = ref[own_rows:, :]
 
 
-def first_kernel(hidden_ref, dout_ref, out_ref, sem):
-    rows = hidden_ref.shape[0]
-    fetch([hidden_ref, dout_ref], [out_ref.at[:rows], out_ref.at[rows:]], sem)
-
-
-def copy_kernel(value_ref, _, out_ref):
-    out_ref[...] = value_ref[...]
+def copy_kernel(count, *refs):
+    for value_ref, out_ref in zip(refs[:count], refs[len(refs) - count :]):
+        out_ref[...] = value_ref[...]
 
 
 def early_kernel(*refs):
@@ -117,17 +113,6 @@
         [dot(value[:, (count - 1 - i) * BLOCK : (count - i) * BLOCK], flip) for i in range(count)],
         axis=1,
     )
-
-
-def fetch(sources, targets, sem):
-    copies = [
-        pltpu.make_async_copy(source, target, sem.at[i])
-        for i, (source, target) in enumerate(zip(sources, targets))
-    ]
-    for copy in copies:
-        copy.start()
-    for copy in copies:
-        copy.wait()
 
 
 def prep_kernel(ids_ref, *refs):
@@ -345,11 +330,12 @@
 def weight_kernel(n_pieces, layout, scaling, *refs):
     ids_ref = refs[0]
     pieces = refs[1 : 1 + n_pieces]
-    gcat_ref, gated_ref, _, dwin_ref, dwout_ref = refs[1 + n_pieces : 6 + n_pieces]
+    gcat_ref, gated_ref, _, dwin_ref, dwout_ref, mark_ref = refs[1 + n_pieces : 7 + n_pieces]
+    mark_ref[...] = jnp.zeros_like(mark_ref)
     if layout[2] is None:
         h_ref, d_ref = pieces
     else:
-        h_ref, d_ref = refs[6 + n_pieces :]
+        h_ref, d_ref = refs[7 + n_pieces :]
         assemble(ids_ref, pieces, h_ref, d_ref, layout)
     flip = mirror(BLOCK)
     columns = h_ref.shape[1] // BLOCK
@@ -369,7 +355,12 @@
         dwout_ref[:, cols] = grad[:head] * scaling
 
 
-def stage_kernel(own_rows, keep_ref, got_ref, _, own_ref, *piece_refs):
+def add_kernel(a_ref, b_ref, _, out_ref):
+    rows = slice(0, out_ref.shape[0])
+    out_ref[...] = (a_ref[rows, :].astype(f32) + b_ref[rows, :].astype(f32)).astype(bf16)
+
+
+def stage_kernel(own_rows, keep_ref, got_ref, own_ref, *piece_refs):
     for j, ref in enumerate([own_ref, *piece_refs]):
         rows = slice(j * own_rows, (j + 1) * own_rows)
         value = keep_ref[rows, :] + got_ref[rows, :].astype(f32)
@@ -400,13 +391,13 @@
     return pl.BlockSpec(memory_space=memory)
 
 
-def call(kernel, inputs, n_smem, outs, scratch, flops, moved, unread=0, vmem=32, far=False):
+def call(kernel, inputs, n_smem, outs, scratch, flops, moved, unread=0, vmem=32):
     return pl.pallas_call(
         kernel,
         out_shape=outs,
         in_specs=[spec(pltpu.SMEM)] * n_smem
         + [spec()] * (len(inputs) - n_smem - unread)
-        + [spec(pltpu.HBM if far else pl.ANY)] * unread,
+        + [spec(pl.ANY)] * unread,
         out_specs=jax.tree.map(lambda _: spec(), outs),
         scratch_shapes=scratch,
         compiler_params=pltpu.CompilerParams(vmem_limit_bytes=vmem * 1024 * 1024),
@@ -469,40 +460,48 @@
         half = count // 2
         return column(own, half) + column(across(own, 4 * half), half)
 
-    def after(value):
+    def after(first, value):
+        outs = (shape(value.shape, bf16),)
         return call(
-            copy_kernel, [value, taps], 0, shape(value.shape, bf16), [], 0, 4 * value.size, 1
-        )
+            functools.partial(copy_kernel, 1), [value, first], 0, outs, [], 0, 4 * value.size, 1
+        )[0]
 
     if own_rows % TILE_ROWS == 0:
-        both = call(
-            first_kernel,
-            [hidden, d_out],
-            0,
-            shape((2 * own_rows, width), bf16),
-            [pltpu.SemaphoreType.DMA((2,))],
-            0,
-            8 * own_rows * width,
-            2,
-            vmem=48,
-            far=True,
+        low = jnp.array(-jnp.inf, bf16)
+        both = jnp.maximum(
+            lax.pad(hidden, low, [(0, own_rows, 0), (0, 0, 0)]),
+            lax.pad(d_out, low, [(own_rows, 0, 0), (0, 0, 0)]),
         )
         zs = column(both, nz)
         coords, pieces, planes = [], [], []
-        for g, blocks in enumerate([range(0, nz // 2), range(nz // 2, nz)]):
+        for blocks in (range(0, nz // 2), range(nz // 2, nz)):
             chunk = pack([zs[j] for j in blocks], nz * own_rows)
-            beside = across(chunk, 2)
+            ahead = [along(chunk, dc) for dc in range(1, ctx_size)]
+            planes.append((chunk, across(chunk, 2), ahead, tuple(blocks)))
+        (_, beside_a, ahead_a, _), (chunk_b, beside_b, ahead_b, _) = planes
+        wall, wallt, gall, taps = prepare(chunk_b)
+        count = len(ahead_a)
+        *forward_a, forward_b = call(
+            functools.partial(copy_kernel, count + 1),
+            [*ahead_a, beside_b, *ahead_b, beside_a],
+            0,
+            (shape(beside_b.shape, bf16),) * (count + 1),
+            [],
+            0,
+            8 * beside_b.size,
+            count + 1,
+        )
+        diagonals = (
+            [after(taps, across(piece, 2)) for piece in forward_a],
+            [along(forward_b, dc + 1) for dc in range(count)],
+        )
+        for (chunk, beside, ahead, blocks), diagonal in zip(planes, diagonals):
             plane = [((0, 0), chunk), ((0, 1), beside)]
-            for dc in range(1, ctx_size):
-                ahead = along(chunk, dc)
-                diagonal = along(beside, dc) if g else across(ahead, 2)
-                plane += [((dc, 0), ahead), ((dc, 1), diagonal)]
-            planes.append((tuple(blocks), plane))
-        wall, wallt, gall, taps = prepare(chunk)
-        for g, (blocks, plane) in enumerate(planes):
+            for dc in range(count):
+                plane += [((dc + 1, 0), ahead[dc]), ((dc + 1, 1), diagonal[dc])]
             for (dc, dx), piece in plane:
                 coords += [(dc, dx, 0, blocks), (dc, dx, 1, blocks)]
-                pieces += [piece, across(after(piece) if dc and dx and not g else piece, 1)]
+                pieces += [piece, across(piece, 1)]
         layout = (tp_size, own_rows, tuple(coords))
         early, late = pieces[: len(pieces) // 2], pieces[len(pieces) // 2 :]
     else:
@@ -545,19 +544,29 @@
     scaling = 1.0 / math.sqrt(length)
     got = across(send, 1)
     quarter = half // 2
-    summed = keep + got.astype(f32)
-    shared = summed[:extra].astype(bf16)
-    send = summed[extra : extra + quarter].astype(bf16)
-    keep = summed[extra + quarter :]
+    at = extra + quarter
+    given, own_given = got, keep
+    send = (keep[extra:at] + got[extra:at].astype(f32)).astype(bf16)
+    keep = keep[at:] + got[at:].astype(f32)
+    sent = send
     got = across(send, 2)
-    step = nz // 2
-    while step:
-        shared = (shared.astype(f32) + across(shared, 4 * step).astype(f32)).astype(bf16)
-        step //= 2
-    outs = (shape((width, LANES), f32), shape((head, width), f32))
+
+    def add_shared(a, b, *first):
+        return call(
+            add_kernel,
+            [a, b, *first],
+            0,
+            shape((extra, width), bf16),
+            [],
+            extra * width,
+            6 * extra * width,
+            1,
+        )
+
+    outs = (shape((width, LANES), f32), shape((head, width), f32), shape((8, LANES), f32))
     if not ordered:
         outs += (shape((length, width), bf16),)
-    d_w_in, d_w_out, *in_order = call(
+    d_w_in, d_w_out, mark, *in_order = call(
         functools.partial(weight_kernel, len(pieces), layout, scaling),
         [ids, *pieces, gcat, gated, send],
         1,
@@ -571,14 +580,18 @@
     in_order = in_order[0] if in_order else pieces[0]
     own, *send = call(
         functools.partial(stage_kernel, own_rows),
-        [keep, got, d_w_out],
+        [keep, got],
         0,
         (shape((own_rows, width), f32),) + (shape((own_rows, width), bf16),) * (nz - 1),
         [],
         4 * quarter * width,
         10 * quarter * width,
-        1,
-    )
+    )
+    shared = add_shared(own_given, given, sent)
+    step = nz // 2
+    while step:
+        shared = add_shared(shared, across(shared, 4 * step), mark if step > 1 else own)
+        step //= 2
     got = [across(piece, 4 * (j + 1)) for j, piece in enumerate(send)]
     d_hidden, d_w_bc = call(
         functools.partial(last_kernel, scaling),

time: 75.7 us -> 70.7 us (0.934)
  waiting for transfers between devices: 27.9 us -> 23.5 us
  local copies, waits for them, and re-layouts: 1.75 us -> 0.02 us
  other arithmetic: 0.29 us -> 1.16 us
    ppermute x22, waiting for transfers between devices: 26 us -> 16 us  [across(): lax.ppermute(value, 'tp', [(i, i ^ flip_bits) for i in range(tp_size)])]
    ppermute x3, waiting for transfers between devices: 1.92 us -> 7.47 us  [along(): lax.ppermute(value, 'ctx', [((i + offset) % ctx_size, i) for i in range(c...]
    unnamed x16 -> x10, local copies, waits for them, and re-layouts: 1.69 us -> 0.02 us
    max x0 -> x1, other arithmetic: none -> 0.95 us  [local(): jnp.maximum(lax.pad(hidden, low, [(0, own_rows, 0), (0, 0, 0)]), lax.pad(...]
    ppermute x22, starting transfers between devices: 22 us -> 22.8 us  [across(): lax.ppermute(value, 'tp', [(i, i ^ flip_bits) for i in range(tp_size)])]
    pallas_call x10 -> x13, Pallas kernels: 15.7 us -> 15.6 us  [call(): pl.pallas_call(kernel, out_shape=outs, in_specs=[spec(pltpu.SMEM)] * n_sm...]
  transfers between devices with their start and end apart: 25 -> 25, of which waited for: 11 -> 9; matrix products, arithmetic and copies ran while one was open for 0% -> 0% of each run, Pallas kernels for 10% -> 10%
where the time goes in v6:
time: 70.7 us; the launch traced here: 70.5 us
  starting transfers between devices  27.5 us (39%)
  waiting for transfers between devices  23.5 us (33%)
  Pallas kernels  15.6 us (22%)
  between operations  2.77 us (4%)
  other arithmetic  1.16 us (2%)
    ppermute x22, starting transfers between devices, across(): lax.ppermute(value, 'tp', [(i, i ^ flip_bits) for i in range(tp_size)])  22.8 us
    ppermute x22, waiting for transfers between devices, across(): lax.ppermute(value, 'tp', [(i, i ^ flip_bits) for i in range(tp_size)])  16 us
    pallas_call x13, Pallas kernels, call(): pl.pallas_call(kernel, out_shape=outs, in_specs=[spec(pltpu.SMEM)] * n_sm...  15.6 us
    ppermute x3, waiting for transfers between devices, along(): lax.ppermute(value, 'ctx', [((i + offset) % ctx_size, i) for i in range(c...  7.47 us
    ppermute x3, starting transfers between devices, along(): lax.ppermute(value, 'ctx', [((i + offset) % ctx_size, i) for i in range(c...  4.67 us
  transfers between devices with their start and end apart: 25, of which 9 were waited for; matrix products, arithmetic and copies ran while one was open for 0% of the time, Pallas kernels for 10%

profile of v6, /device:TPU:0, one launch (start us, length us, event | category | flops | bytes accessed | tf_op | source)
XLA Modules:
  0.0 70.5 jit_solution(9243680790157972890)
XLA Ops:
  0.7 1.0 %pad_maximum_fusion.refs_0_ = bf16[32,2048]{1,0:T(8,128)(2,1)S(1)} fusion(bf16[16,2048]{1,0:T(8,128)(2,1)} %param.19, bf16[16,2048]{1,0:T(8,128)(2,1)} %param.10), kind=kLoop, calls=%fused_computation.2 | loop fusion | flops 262144 | bytes 262144 | tf_op jit(solution)/shard_map/max | solution.py:471
  1.6 4.1 %collective-permute-start = (bf16[32,2048]{1,0:T(8,128)(2,1)S(1)}, bf16[32,2048]{1,0:T(8,128)(2,1)S(1)}, u32[]{:S(2)}, u32[]{:S(2)}) collective-permute-start(bf16[32,2048]{1,0:T(8,128)(2,1)S(1)} %pad_maximum_fusion.refs_0_), channel_id=1, source_target_pairs={{0,8},{1,9},{2,10},{3,11},{4,12},{5,13},{6,14},{7,15},{8,0},{9,1},... | collective-permute-start | bytes 393224 | tf_op jit(solution)/shard_map/ppermute | solution.py:422
  5.7 1.6 %collective-permute-start.7 = (bf16[32,2048]{1,0:T(8,128)(2,1)S(1)}, bf16[32,2048]{1,0:T(8,128)(2,1)S(1)}, u32[]{:S(2)}, u32[]{:S(2)}) collective-permute-start(bf16[32,2048]{1,0:T(8,128)(2,1)S(1)} %pad_maximum_fusion.refs_0_), channel_id=1, source_target_pairs={{0,4},{1,5},{2,6},{3,7},{4,0},{5,1},{6,2},{7,3},{8,12},{9,13},{10,... | collective-permute-start | bytes 393224 | tf_op jit(solution)/shard_map/ppermute | solution.py:422
  7.3 4.8 %collective-permute-done.refs_0_ = bf16[32,2048]{1,0:T(8,128)(2,1)S(1)} collective-permute-done((bf16[32,2048]{1,0:T(8,128)(2,1)S(1)}, bf16[32,2048]{1,0:T(8,128)(2,1)S(1)}, u32[]{:S(2)}, u32[]{:S(2)}) %collective-permute-start) | collective-permute-done | bytes 131104 | tf_op jit(solution)/shard_map/ppermute | solution.py:422
  12.2 0.6 collective-permute-start.1
  12.8 1.6 %collective-permute-start.9 = (bf16[64,2048]{1,0:T(8,128)(2,1)S(1)}, bf16[64,2048]{1,0:T(8,128)(2,1)S(1)}, u32[]{:S(2)}, u32[]{:S(2)}) collective-permute-start(bf16[64,2048]{1,0:T(8,128)(2,1)S(1)} %shard_map.130.refs_0_.refs_1_), channel_id=1, source_target_pairs={{0,2},{1,3},{2,0},{3,1},{4,6},{5,7},{6,4},{7,5},{8,10},{9,11},{10,... | collective-permute-start | bytes 786440 | tf_op jit(solution)/shard_map/ppermute | solution.py:422
  14.4 1.5 %collective-permute-start.8 = (bf16[64,2048]{1,0:T(8,128)(2,1)S(1)}, bf16[64,2048]{1,0:T(8,128)(2,1)S(1)}, u32[]{:S(2)}, u32[]{:S(2)}) collective-permute-start(bf16[64,2048]{1,0:T(8,128)(2,1)S(1)} %shard_map.130.refs_0_.refs_1_), channel_id=1, source_target_pairs={{16,0},{0,16},{17,1},{1,17},{18,2},{2,18},{19,3},{3,19},{20,4},{4,... | collective-permute-start | bytes 786440 | tf_op jit(solution)/shard_map/ppermute | solution.py:425
  15.9 1.2 %collective-permute-done.1.refs_1_ = bf16[32,2048]{1,0:T(8,128)(2,1)S(1)} collective-permute-done((bf16[32,2048]{1,0:T(8,128)(2,1)S(1)}, bf16[32,2048]{1,0:T(8,128)(2,1)S(1)}, u32[]{:S(2)}, u32[]{:S(2)}) %collective-permute-start.1) | collective-permute-done | bytes 131104 | tf_op jit(solution)/shard_map/ppermute | solution.py:422
  17.1 1.6 %collective-permute-start.5 = (bf16[64,2048]{1,0:T(8,128)(2,1)S(1)}, bf16[64,2048]{1,0:T(8,128)(2,1)S(1)}, u32[]{:S(2)}, u32[]{:S(2)}) collective-permute-start(bf16[64,2048]{1,0:T(8,128)(2,1)S(1)} %shard_map.129.refs_5_.refs_4_.refs_9_), channel_id=1, source_target_pairs={{16,0},{0,16},{17,1},{1,17},{18,2},{2,18},{19,3},{3,19},{20,4},{4,... | collective-permute-start | bytes 786440 | tf_op jit(solution)/shard_map/ppermute | solution.py:425
  18.8 1.5 %collective-permute-start.3 = (bf16[64,2048]{1,0:T(8,128)(2,1)S(1)}, bf16[64,2048]{1,0:T(8,128)(2,1)S(1)}, u32[]{:S(2)}, u32[]{:S(2)}) collective-permute-start(bf16[64,2048]{1,0:T(8,128)(2,1)S(1)} %shard_map.129.refs_5_.refs_4_.refs_9_), channel_id=1, source_target_pairs={{0,2},{1,3},{2,0},{3,1},{4,6},{5,7},{6,4},{7,5},{8,10},{9,11},{10,... | collective-permute-start | bytes 786440 | tf_op jit(solution)/shard_map/ppermute | solution.py:422
  20.3 1.8 %collective-permute-done.9.refs_3_.refs_2_ = bf16[64,2048]{1,0:T(8,128)(2,1)S(1)} collective-permute-done((bf16[64,2048]{1,0:T(8,128)(2,1)S(1)}, bf16[64,2048]{1,0:T(8,128)(2,1)S(1)}, u32[]{:S(2)}, u32[]{:S(2)}) %collective-permute-start.9) | collective-permute-done | bytes 262176 | tf_op jit(solution)/shard_map/ppermute | solution.py:422
  22.1 1.5 %collective-permute-done.8.refs_0_.refs_4_.refs_5_ = bf16[64,2048]{1,0:T(8,128)(2,1)S(1)} collective-permute-done((bf16[64,2048]{1,0:T(8,128)(2,1)S(1)}, bf16[64,2048]{1,0:T(8,128)(2,1)S(1)}, u32[]{:S(2)}, u32[]{:S(2)}) %collective-permute-start.8) | collective-permute-done | bytes 262176 | tf_op jit(solution)/shard_map/ppermute | solution.py:425
  23.6 4.0 %collective-permute-done.5.refs_2_.refs_8_.refs_13_ = bf16[64,2048]{1,0:T(8,128)(2,1)S(1)} collective-permute-done((bf16[64,2048]{1,0:T(8,128)(2,1)S(1)}, bf16[64,2048]{1,0:T(8,128)(2,1)S(1)}, u32[]{:S(2)}, u32[]{:S(2)}) %collective-permute-start.5) | collective-permute-done | bytes 262176 | tf_op jit(solution)/shard_map/ppermute | solution.py:425
  27.7 0.6 collective-permute-start.15
  28.3 0.5 collective-permute-start.13
  28.8 1.5 %collective-permute-start.10 = (bf16[64,2048]{1,0:T(8,128)(2,1)S(1)}, bf16[64,2048]{1,0:T(8,128)(2,1)S(1)}, u32[]{:S(2)}, u32[]{:S(2)}) collective-permute-start(bf16[64,2048]{1,0:T(8,128)(2,1)S(1)} %get-tuple-element.26), channel_id=1, source_target_pairs={{16,0},{0,16},{17,1},{1,17},{18,2},{2,18},{19,3},{3,19},{20,4},{4,... | collective-permute-start | bytes 786440 | tf_op jit(solution)/shard_map/ppermute | solution.py:425
  30.4 1.7 %shard_map.132 = (bf16[2048,512]{1,0:T(8,128)(2,1)S(1)}, bf16[512,2048]{1,0:T(8,128)(2,1)S(1)}, bf16[2048,256]{1,0:T(8,128)(2,1)S(1)}, f32[4,128]{1,0:T(4,128)S(1)}) custom-call(s32[4]{0:T(128)S(1)} %pad_add_fusion.ids_ref.refs_0_, bf16[2048,128]{1,0:T(8,128)(2,1)S(1)} %copy-done, bf16[32,2048]{1,0:T(8,128)(2,1)S(1)} %bitcast.6, ...), custom_call_target="tpu_custom_call" | custom-call | flops 805306368 | bytes 5242880 | tf_op jit(solution)/shard_map/pallas_call | solution.py:395
  32.1 2.4 %collective-permute-done.15.refs_0_ = bf16[64,2048]{1,0:T(8,128)(2,1)S(1)} collective-permute-done((bf16[64,2048]{1,0:T(8,128)(2,1)S(1)}, bf16[64,2048]{1,0:T(8,128)(2,1)S(1)}, u32[]{:S(2)}, u32[]{:S(2)}) %collective-permute-start.15) | collective-permute-done | bytes 262176 | tf_op jit(solution)/shard_map/ppermute | solution.py:422
  35.6 1.9 %collective-permute-done.10.refs_10_.refs_15_ = bf16[64,2048]{1,0:T(8,128)(2,1)S(1)} collective-permute-done((bf16[64,2048]{1,0:T(8,128)(2,1)S(1)}, bf16[64,2048]{1,0:T(8,128)(2,1)S(1)}, u32[]{:S(2)}, u32[]{:S(2)}) %collective-permute-start.10) | collective-permute-done | bytes 262176 | tf_op jit(solution)/shard_map/ppermute | solution.py:425
  39.5 1.0 %shard_map.134 = (f32[256,512]{1,0:T(8,128)S(1)}, f32[256,256]{1,0:T(8,128)S(1)}) custom-call(bf16[64,2048]{1,0:T(8,128)(2,1)S(1)} %shard_map.130.refs_0_.refs_1_, bf16[64,2048]{1,0:T(8,128)(2,1)S(1)} %collective-permute-done.12.refs_1_.refs_2_, bf16[64,2048]{1,0:T(8,128)(2,1)S(1)} %collective-permute-done.9.refs_3_.refs_2_, ...), custom_call_target="tpu_custom_call" | custom-call | flops 805306368 | bytes 2097152 | tf_op jit(solution)/shard_map/pallas_call | solution.py:395
  40.5 6.5 %shard_map.135 = (bf16[144,2048]{1,0:T(8,128)(2,1)S(1)}, f32[144,2048]{1,0:T(8,128)S(1)}, bf16[512,512]{1,0:T(8,128)(2,1)S(1)}, bf16[512,256]{1,0:T(8,128)(2,1)S(1)}) custom-call(s32[4]{0:T(128)S(1)} %pad_add_fusion.ids_ref.refs_0_, f32[1]{0:T(128)S(6)} %copy.14.refs_1_, f32[1]{0:T(128)S(6)} %copy.15.refs_2_, f32[1]{0:T(128)S(6)} %copy.16.refs_3_, ...), custom_call_target="tpu_custom_call" | custom-call | flops 2147483648 | bytes 8388608 | tf_op jit(solution)/shard_map/pallas_call | solution.py:395
  47.0 0.6 collective-permute-start.17
  47.6 1.6 %collective-permute-done.17.b_ref = bf16[144,2048]{1,0:T(8,128)(2,1)S(1)} collective-permute-done((bf16[144,2048]{1,0:T(8,128)(2,1)S(1)}, bf16[144,2048]{1,0:T(8,128)(2,1)S(1)}, u32[]{:S(2)}, u32[]{:S(2)}) %collective-permute-start.17) | collective-permute-done | bytes 589856 | tf_op jit(solution)/shard_map/ppermute | solution.py:422
  49.3 1.6 %collective-permute-start.18 = (bf16[64,2048]{1,0:T(8,128)(2,1)S(1)}, bf16[64,2048]{1,0:T(8,128)(2,1)S(1)}, u32[]{:S(2)}, u32[]{:S(2)}) collective-permute-start(bf16[64,2048]{1,0:T(8,128)(2,1)S(1)} %get-tuple-element.48.refs_19_._), channel_id=1, source_target_pairs={{0,2},{1,3},{2,0},{3,1},{4,6},{5,7},{6,4},{7,5},{8,10},{9,11},{10,... | collective-permute-start | bytes 786440 | tf_op jit(solution)/shard_map/ppermute | solution.py:422
  50.9 3.4 %collective-permute-start.19 = (bf16[16,2048]{1,0:T(8,128)(2,1)S(1)}, bf16[16,2048]{1,0:T(8,128)(2,1)S(1)}, u32[]{:S(2)}, u32[]{:S(2)}) collective-permute-start(bf16[16,2048]{1,0:T(8,128)(2,1)S(1)} %shard_map.138.a_ref), channel_id=1, source_target_pairs={{0,8},{1,9},{2,10},{3,11},{4,12},{5,13},{6,14},{7,15},{8,0},{9,1},... | collective-permute-start | bytes 196616 | tf_op jit(solution)/shard_map/ppermute | solution.py:422
  54.4 4.4 %shard_map.137 = (f32[2048,128]{1,0:T(8,128)}, f32[64,2048]{1,0:T(8,128)}, f32[8,128]{1,0:T(8,128)S(1)}, bf16[512,2048]{1,0:T(8,128)(2,1)S(1)}) custom-call(s32[4]{0:T(128)S(1)} %pad_add_fusion.ids_ref.refs_0_, bf16[64,2048]{1,0:T(8,128)(2,1)S(1)} %shard_map.130.refs_0_.refs_1_, bf16[64,2048]{1,0:T(8,128)(2,1)S(1)} %collective-permute-done.12.refs_1_.refs_2_, ...), custom_call_target="tpu_custom_call" | custom-call | flops 2147483648 | bytes 8388608 | tf_op jit(solution)/shard_map/pallas_call | solution.py:395
  59.2 1.8 %collective-permute-start.22 = (bf16[16,2048]{1,0:T(8,128)(2,1)S(1)}, bf16[16,2048]{1,0:T(8,128)(2,1)S(1)}, u32[]{:S(2)}, u32[]{:S(2)}) collective-permute-start(bf16[16,2048]{1,0:T(8,128)(2,1)S(1)} %get-tuple-element.41), channel_id=1, source_target_pairs={{0,4},{1,5},{2,6},{3,7},{4,0},{5,1},{6,2},{7,3},{8,12},{9,13},{10,... | collective-permute-start | bytes 196616 | tf_op jit(solution)/shard_map/ppermute | solution.py:422
  61.0 0.8 %collective-permute-start.23 = (bf16[16,2048]{1,0:T(8,128)(2,1)S(1)}, bf16[16,2048]{1,0:T(8,128)(2,1)S(1)}, u32[]{:S(2)}, u32[]{:S(2)}) collective-permute-start(bf16[16,2048]{1,0:T(8,128)(2,1)S(1)} %get-tuple-element.42), channel_id=1, source_target_pairs={{0,8},{1,9},{2,10},{3,11},{4,12},{5,13},{6,14},{7,15},{8,0},{9,1},... | collective-permute-start | bytes 196616 | tf_op jit(solution)/shard_map/ppermute | solution.py:422
  61.8 1.8 %collective-permute-start.24 = (bf16[16,2048]{1,0:T(8,128)(2,1)S(1)}, bf16[16,2048]{1,0:T(8,128)(2,1)S(1)}, u32[]{:S(2)}, u32[]{:S(2)}) collective-permute-start(bf16[16,2048]{1,0:T(8,128)(2,1)S(1)} %get-tuple-element.43), channel_id=1, source_target_pairs={{0,12},{1,13},{2,14},{3,15},{4,8},{5,9},{6,10},{7,11},{8,4},{9,5},... | collective-permute-start | bytes 196616 | tf_op jit(solution)/shard_map/ppermute | solution.py:422
  63.7 0.9 %collective-permute-start.21 = (bf16[16,2048]{1,0:T(8,128)(2,1)S(1)}, bf16[16,2048]{1,0:T(8,128)(2,1)S(1)}, u32[]{:S(2)}, u32[]{:S(2)}) collective-permute-start(bf16[16,2048]{1,0:T(8,128)(2,1)S(1)} %shard_map.140.shared_ref), channel_id=1, source_target_pairs={{0,2},{1,3},{2,0},{3,1},{4,6},{5,7},{6,4},{7,5},{8,10},{9,11},{10,... | collective-permute-start | bytes 196616 | tf_op jit(solution)/shard_map/ppermute | solution.py:422
  64.5 4.1 %collective-permute-done.23.refs_1_ = bf16[16,2048]{1,0:T(8,128)(2,1)S(1)} collective-permute-done((bf16[16,2048]{1,0:T(8,128)(2,1)S(1)}, bf16[16,2048]{1,0:T(8,128)(2,1)S(1)}, u32[]{:S(2)}, u32[]{:S(2)}) %collective-permute-start.23) | collective-permute-done | bytes 65568 | tf_op jit(solution)/shard_map/ppermute | solution.py:422
  68.6 1.9 %shard_map.141 = (bf16[16,2048]{1,0:T(8,128)(2,1)}, f32[32,2048]{1,0:T(8,128)}) custom-call(f32[16,2048]{1,0:T(8,128)S(1)} %get-tuple-element.36._.own_ref, bf16[512,2048]{1,0:T(8,128)(2,1)S(1)} %get-tuple-element.39.h_ref, bf16[16,2048]{1,0:T(8,128)(2,1)S(1)} %shard_map.140.shared_ref, bf16[16,2048]{1,0:T(8,128)(2,1)S(1)} %collective-permute-done.21.other_ref, ...), custom_call_target="tpu_custom_call" | custom-call | flops 268435456 | bytes 4194304 | tf_op jit(solution)/shard_map/pallas_call | solution.py:395
  (44 shorter events, 1.9 us)
Async XLA Ops:
  0.6 29.8 %copy-start.1 = (bf16[64,2048]{1,0:T(8,128)(2,1)S(1)}, bf16[64,2048]{1,0:T(8,128)(2,1)}, u32[]{:S(2)}) copy-start(bf16[64,2048]{1,0:T(8,128)(2,1)} %refs_3_.2) | copy-start | bytes 786436
  0.6 29.8 %copy-start.4 = (f32[4,64]{1,0:T(4,128)S(1)}, f32[4,64]{1,0:T(4,128)}, u32[]{:S(2)}) copy-start(f32[4,64]{1,0:T(4,128)} %refs_4_.1) | copy-start | bytes 3076
  0.7 29.7 %copy-start.3 = (bf16[1,2048]{1,0:T(2,128)(2,1)S(1)}, bf16[1,2048]{1,0:T(2,128)(2,1)}, u32[]{:S(2)}) copy-start(bf16[1,2048]{1,0:T(2,128)(2,1)} %refs_2_.2) | copy-start | bytes 12292
  0.7 29.7 %copy-start.2 = (bf16[2048,32]{0,1:T(8,128)(2,1)S(1)}, bf16[2048,32]{0,1:T(8,128)(2,1)}, u32[]{:S(2)}) copy-start(bf16[2048,32]{0,1:T(8,128)(2,1)} %param.12) | copy-start | bytes 393220
  0.7 29.7 %copy-start = (bf16[2048,128]{1,0:T(8,128)(2,1)S(1)}, bf16[2048,128]{1,0:T(8,128)(2,1)}, u32[]{:S(2)}) copy-start(bf16[2048,128]{1,0:T(8,128)(2,1)} %refs_0_.1) | copy-start | bytes 1572868
  1.6 10.5 %collective-permute-start = (bf16[32,2048]{1,0:T(8,128)(2,1)S(1)}, bf16[32,2048]{1,0:T(8,128)(2,1)S(1)}, u32[]{:S(2)}, u32[]{:S(2)}) collective-permute-start(bf16[32,2048]{1,0:T(8,128)(2,1)S(1)} %pad_maximum_fusion.refs_0_), channel_id=1, source_target_pairs={{0,8},{1,9},{2,10},{3,11},{4,12},{5,13},{6,14},{7,15},{8,0},{9,1},... | collective-permute-start | bytes 393224 | tf_op jit(solution)/shard_map/ppermute | solution.py:422
  5.7 7.0 %collective-permute-start.7 = (bf16[32,2048]{1,0:T(8,128)(2,1)S(1)}, bf16[32,2048]{1,0:T(8,128)(2,1)S(1)}, u32[]{:S(2)}, u32[]{:S(2)}) collective-permute-start(bf16[32,2048]{1,0:T(8,128)(2,1)S(1)} %pad_maximum_fusion.refs_0_), channel_id=1, source_target_pairs={{0,4},{1,5},{2,6},{3,7},{4,0},{5,1},{6,2},{7,3},{8,12},{9,13},{10,... | collective-permute-start | bytes 393224 | tf_op jit(solution)/shard_map/ppermute | solution.py:422
  12.2 5.0 %collective-permute-start.1 = (bf16[32,2048]{1,0:T(8,128)(2,1)S(1)}, bf16[32,2048]{1,0:T(8,128)(2,1)S(1)}, u32[]{:S(2)}, u32[]{:S(2)}) collective-permute-start(bf16[32,2048]{1,0:T(8,128)(2,1)S(1)} %collective-permute-done.refs_0_), channel_id=1, source_target_pairs={{0,4},{1,5},{2,6},{3,7},{4,0},{5,1},{6,2},{7,3},{8,12},{9,13},{10,... | collective-permute-start | bytes 393224 | tf_op jit(solution)/shard_map/ppermute | solution.py:422
  12.8 9.3 %collective-permute-start.9 = (bf16[64,2048]{1,0:T(8,128)(2,1)S(1)}, bf16[64,2048]{1,0:T(8,128)(2,1)S(1)}, u32[]{:S(2)}, u32[]{:S(2)}) collective-permute-start(bf16[64,2048]{1,0:T(8,128)(2,1)S(1)} %shard_map.130.refs_0_.refs_1_), channel_id=1, source_target_pairs={{0,2},{1,3},{2,0},{3,1},{4,6},{5,7},{6,4},{7,5},{8,10},{9,11},{10,... | collective-permute-start | bytes 786440 | tf_op jit(solution)/shard_map/ppermute | solution.py:422
  14.4 9.2 %collective-permute-start.8 = (bf16[64,2048]{1,0:T(8,128)(2,1)S(1)}, bf16[64,2048]{1,0:T(8,128)(2,1)S(1)}, u32[]{:S(2)}, u32[]{:S(2)}) collective-permute-start(bf16[64,2048]{1,0:T(8,128)(2,1)S(1)} %shard_map.130.refs_0_.refs_1_), channel_id=1, source_target_pairs={{16,0},{0,16},{17,1},{1,17},{18,2},{2,18},{19,3},{3,19},{20,4},{4,... | collective-permute-start | bytes 786440 | tf_op jit(solution)/shard_map/ppermute | solution.py:425
  17.1 10.5 %collective-permute-start.5 = (bf16[64,2048]{1,0:T(8,128)(2,1)S(1)}, bf16[64,2048]{1,0:T(8,128)(2,1)S(1)}, u32[]{:S(2)}, u32[]{:S(2)}) collective-permute-start(bf16[64,2048]{1,0:T(8,128)(2,1)S(1)} %shard_map.129.refs_5_.refs_4_.refs_9_), channel_id=1, source_target_pairs={{16,0},{0,16},{17,1},{1,17},{18,2},{2,18},{19,3},{3,19},{20,4},{4,... | collective-permute-start | bytes 786440 | tf_op jit(solution)/shard_map/ppermute | solution.py:425
  18.8 8.9 %collective-permute-start.3 = (bf16[64,2048]{1,0:T(8,128)(2,1)S(1)}, bf16[64,2048]{1,0:T(8,128)(2,1)S(1)}, u32[]{:S(2)}, u32[]{:S(2)}) collective-permute-start(bf16[64,2048]{1,0:T(8,128)(2,1)S(1)} %shard_map.129.refs_5_.refs_4_.refs_9_), channel_id=1, source_target_pairs={{0,2},{1,3},{2,0},{3,1},{4,6},{5,7},{6,4},{7,5},{8,10},{9,11},{10,... | collective-permute-start | bytes 786440 | tf_op jit(solution)/shard_map/ppermute | solution.py:422
  27.7 6.8 %collective-permute-start.15 = (bf16[64,2048]{1,0:T(8,128)(2,1)S(1)}, bf16[64,2048]{1,0:T(8,128)(2,1)S(1)}, u32[]{:S(2)}, u32[]{:S(2)}) collective-permute-start(bf16[64,2048]{1,0:T(8,128)(2,1)S(1)} %get-tuple-element.27), channel_id=1, source_target_pairs={{0,2},{1,3},{2,0},{3,1},{4,6},{5,7},{6,4},{7,5},{8,10},{9,11},{10,... | collective-permute-start | bytes 786440 | tf_op jit(solution)/shard_map/ppermute | solution.py:422
  28.3 6.3 %collective-permute-start.12 = (bf16[64,2048]{1,0:T(8,128)(2,1)S(1)}, bf16[64,2048]{1,0:T(8,128)(2,1)S(1)}, u32[]{:S(2)}, u32[]{:S(2)}) collective-permute-start(bf16[64,2048]{1,0:T(8,128)(2,1)S(1)} %shard_map.130.refs_0_.refs_1_), channel_id=1, source_target_pairs={{0,1},{1,0},{2,3},{3,2},{4,5},{5,4},{6,7},{7,6},{8,9},{9,8},{10,11... | collective-permute-start | bytes 786440 | tf_op jit(solution)/shard_map/ppermute | solution.py:422
  28.3 6.8 %collective-permute-start.13 = (bf16[64,2048]{1,0:T(8,128)(2,1)S(1)}, bf16[64,2048]{1,0:T(8,128)(2,1)S(1)}, u32[]{:S(2)}, u32[]{:S(2)}) collective-permute-start(bf16[64,2048]{1,0:T(8,128)(2,1)S(1)} %collective-permute-done.9.refs_3_.refs_2_), channel_id=1, source_target_pairs={{0,1},{1,0},{2,3},{3,2},{4,5},{5,4},{6,7},{7,6},{8,9},{9,8},{10,11... | collective-permute-start | bytes 786440 | tf_op jit(solution)/shard_map/ppermute | solution.py:422
  28.8 6.4 %collective-permute-start.14 = (bf16[64,2048]{1,0:T(8,128)(2,1)S(1)}, bf16[64,2048]{1,0:T(8,128)(2,1)S(1)}, u32[]{:S(2)}, u32[]{:S(2)}) collective-permute-start(bf16[64,2048]{1,0:T(8,128)(2,1)S(1)} %collective-permute-done.8.refs_0_.refs_4_.refs_5_), channel_id=1, source_target_pairs={{0,1},{1,0},{2,3},{3,2},{4,5},{5,4},{6,7},{7,6},{8,9},{9,8},{10,11... | collective-permute-start | bytes 786440 | tf_op jit(solution)/shard_map/ppermute | solution.py:422
  28.8 8.7 %collective-permute-start.10 = (bf16[64,2048]{1,0:T(8,128)(2,1)S(1)}, bf16[64,2048]{1,0:T(8,128)(2,1)S(1)}, u32[]{:S(2)}, u32[]{:S(2)}) collective-permute-start(bf16[64,2048]{1,0:T(8,128)(2,1)S(1)} %get-tuple-element.26), channel_id=1, source_target_pairs={{16,0},{0,16},{17,1},{1,17},{18,2},{2,18},{19,3},{3,19},{20,4},{4,... | collective-permute-start | bytes 786440 | tf_op jit(solution)/shard_map/ppermute | solution.py:425
  34.5 5.0 %collective-permute-start.16 = (bf16[64,2048]{1,0:T(8,128)(2,1)S(1)}, bf16[64,2048]{1,0:T(8,128)(2,1)S(1)}, u32[]{:S(2)}, u32[]{:S(2)}) collective-permute-start(bf16[64,2048]{1,0:T(8,128)(2,1)S(1)} %shard_map.133.refs_6_.refs_7_), channel_id=1, source_target_pairs={{0,1},{1,0},{2,3},{3,2},{4,5},{5,4},{6,7},{7,6},{8,9},{9,8},{10,11... | collective-permute-start | bytes 786440 | tf_op jit(solution)/shard_map/ppermute | solution.py:422
  34.6 5.9 %collective-permute-start.2 = (bf16[64,2048]{1,0:T(8,128)(2,1)S(1)}, bf16[64,2048]{1,0:T(8,128)(2,1)S(1)}, u32[]{:S(2)}, u32[]{:S(2)}) collective-permute-start(bf16[64,2048]{1,0:T(8,128)(2,1)S(1)} %shard_map.129.refs_5_.refs_4_.refs_9_), channel_id=1, source_target_pairs={{0,1},{1,0},{2,3},{3,2},{4,5},{5,4},{6,7},{7,6},{8,9},{9,8},{10,11... | collective-permute-start | bytes 786440 | tf_op jit(solution)/shard_map/ppermute | solution.py:422
  35.1 5.4 %collective-permute-start.6 = (bf16[64,2048]{1,0:T(8,128)(2,1)S(1)}, bf16[64,2048]{1,0:T(8,128)(2,1)S(1)}, u32[]{:S(2)}, u32[]{:S(2)}) collective-permute-start(bf16[64,2048]{1,0:T(8,128)(2,1)S(1)} %collective-permute-done.5.refs_2_.refs_8_.refs_13_), channel_id=1, source_target_pairs={{0,1},{1,0},{2,3},{3,2},{4,5},{5,4},{6,7},{7,6},{8,9},{9,8},{10,11... | collective-permute-start | bytes 786440 | tf_op jit(solution)/shard_map/ppermute | solution.py:422
  35.2 5.3 %collective-permute-start.4 = (bf16[64,2048]{1,0:T(8,128)(2,1)S(1)}, bf16[64,2048]{1,0:T(8,128)(2,1)S(1)}, u32[]{:S(2)}, u32[]{:S(2)}) collective-permute-start(bf16[64,2048]{1,0:T(8,128)(2,1)S(1)} %collective-permute-done.3.refs_1_.refs_6_.refs_11_), channel_id=1, source_target_pairs={{0,1},{1,0},{2,3},{3,2},{4,5},{5,4},{6,7},{7,6},{8,9},{9,8},{10,11... | collective-permute-start | bytes 786440 | tf_op jit(solution)/shard_map/ppermute | solution.py:422
  37.5 3.0 %collective-permute-start.11 = (bf16[64,2048]{1,0:T(8,128)(2,1)S(1)}, bf16[64,2048]{1,0:T(8,128)(2,1)S(1)}, u32[]{:S(2)}, u32[]{:S(2)}) collective-permute-start(bf16[64,2048]{1,0:T(8,128)(2,1)S(1)} %collective-permute-done.10.refs_10_.refs_15_), channel_id=1, source_target_pairs={{0,1},{1,0},{2,3},{3,2},{4,5},{5,4},{6,7},{7,6},{8,9},{9,8},{10,11... | collective-permute-start | bytes 786440 | tf_op jit(solution)/shard_map/ppermute | solution.py:422
  47.0 2.2 %collective-permute-start.17 = (bf16[144,2048]{1,0:T(8,128)(2,1)S(1)}, bf16[144,2048]{1,0:T(8,128)(2,1)S(1)}, u32[]{:S(2)}, u32[]{:S(2)}) collective-permute-start(bf16[144,2048]{1,0:T(8,128)(2,1)S(1)} %get-tuple-element.35), channel_id=1, source_target_pairs={{0,1},{1,0},{2,3},{3,2},{4,5},{5,4},{6,7},{7,6},{8,9},{9,8},{10,11... | collective-permute-start | bytes 1769480 | tf_op jit(solution)/shard_map/ppermute | solution.py:422
  49.3 9.8 %collective-permute-start.18 = (bf16[64,2048]{1,0:T(8,128)(2,1)S(1)}, bf16[64,2048]{1,0:T(8,128)(2,1)S(1)}, u32[]{:S(2)}, u32[]{:S(2)}) collective-permute-start(bf16[64,2048]{1,0:T(8,128)(2,1)S(1)} %get-tuple-element.48.refs_19_._), channel_id=1, source_target_pairs={{0,2},{1,3},{2,0},{3,1},{4,6},{5,7},{6,4},{7,5},{8,10},{9,11},{10,... | collective-permute-start | bytes 786440 | tf_op jit(solution)/shard_map/ppermute | solution.py:422
  50.9 7.8 %collective-permute-start.19 = (bf16[16,2048]{1,0:T(8,128)(2,1)S(1)}, bf16[16,2048]{1,0:T(8,128)(2,1)S(1)}, u32[]{:S(2)}, u32[]{:S(2)}) collective-permute-start(bf16[16,2048]{1,0:T(8,128)(2,1)S(1)} %shard_map.138.a_ref), channel_id=1, source_target_pairs={{0,8},{1,9},{2,10},{3,11},{4,12},{5,13},{6,14},{7,15},{8,0},{9,1},... | collective-permute-start | bytes 196616 | tf_op jit(solution)/shard_map/ppermute | solution.py:422
  58.8 4.9 %collective-permute-start.20 = (bf16[16,2048]{1,0:T(8,128)(2,1)S(1)}, bf16[16,2048]{1,0:T(8,128)(2,1)S(1)}, u32[]{:S(2)}, u32[]{:S(2)}) collective-permute-start(bf16[16,2048]{1,0:T(8,128)(2,1)S(1)} %shard_map.139.a_ref), channel_id=1, source_target_pairs={{0,4},{1,5},{2,6},{3,7},{4,0},{5,1},{6,2},{7,3},{8,12},{9,13},{10,... | collective-permute-start | bytes 196616 | tf_op jit(solution)/shard_map/ppermute | solution.py:422
  59.2 5.4 %collective-permute-start.22 = (bf16[16,2048]{1,0:T(8,128)(2,1)S(1)}, bf16[16,2048]{1,0:T(8,128)(2,1)S(1)}, u32[]{:S(2)}, u32[]{:S(2)}) collective-permute-start(bf16[16,2048]{1,0:T(8,128)(2,1)S(1)} %get-tuple-element.41), channel_id=1, source_target_pairs={{0,4},{1,5},{2,6},{3,7},{4,0},{5,1},{6,2},{7,3},{8,12},{9,13},{10,... | collective-permute-start | bytes 196616 | tf_op jit(solution)/shard_map/ppermute | solution.py:422
  61.0 7.6 %collective-permute-start.23 = (bf16[16,2048]{1,0:T(8,128)(2,1)S(1)}, bf16[16,2048]{1,0:T(8,128)(2,1)S(1)}, u32[]{:S(2)}, u32[]{:S(2)}) collective-permute-start(bf16[16,2048]{1,0:T(8,128)(2,1)S(1)} %get-tuple-element.42), channel_id=1, source_target_pairs={{0,8},{1,9},{2,10},{3,11},{4,12},{5,13},{6,14},{7,15},{8,0},{9,1},... | collective-permute-start | bytes 196616 | tf_op jit(solution)/shard_map/ppermute | solution.py:422
  61.8 6.9 %collective-permute-start.24 = (bf16[16,2048]{1,0:T(8,128)(2,1)S(1)}, bf16[16,2048]{1,0:T(8,128)(2,1)S(1)}, u32[]{:S(2)}, u32[]{:S(2)}) collective-permute-start(bf16[16,2048]{1,0:T(8,128)(2,1)S(1)} %get-tuple-element.43), channel_id=1, source_target_pairs={{0,12},{1,13},{2,14},{3,15},{4,8},{5,9},{6,10},{7,11},{8,4},{9,5},... | collective-permute-start | bytes 196616 | tf_op jit(solution)/shard_map/ppermute | solution.py:422
  63.7 5.0 %collective-permute-start.21 = (bf16[16,2048]{1,0:T(8,128)(2,1)S(1)}, bf16[16,2048]{1,0:T(8,128)(2,1)S(1)}, u32[]{:S(2)}, u32[]{:S(2)}) collective-permute-start(bf16[16,2048]{1,0:T(8,128)(2,1)S(1)} %shard_map.140.shared_ref), channel_id=1, source_target_pairs={{0,2},{1,3},{2,0},{3,1},{4,6},{5,7},{6,4},{7,5},{8,10},{9,11},{10,... | collective-permute-start | bytes 196616 | tf_op jit(solution)/shard_map/ppermute | solution.py:422

commit v7 on v6

--- a/solution.py
+++ b/solution.py
@@ -154,14 +154,11 @@
 
 
 def own_source(shape, dim, ids_ref, tp_size, own_rows):
-    z, x, core, ctx = (ids_ref[i] for i in range(4))
-    nz = tp_size // 4
+    core, ctx = ids_ref[2], ids_ref[3]
     row = iota(shape, dim)
     block = row // own_rows
-    j = block % nz
-    dx = 1 - (block // nz) % 2
-    dcore = 1 - block // (2 * nz)
-    owner = ((z ^ j) * 2 + (x ^ dx)) * 2 + (core ^ dcore)
+    chips = tp_size // 2
+    owner = (block % chips) * 2 + (core ^ (1 - block // chips))
     return (ctx * tp_size + owner) * own_rows + row % own_rows
 
 
@@ -360,21 +357,13 @@
     out_ref[...] = (a_ref[rows, :].astype(f32) + b_ref[rows, :].astype(f32)).astype(bf16)
 
 
-def stage_kernel(own_rows, keep_ref, got_ref, own_ref, *piece_refs):
-    for j, ref in enumerate([own_ref, *piece_refs]):
-        rows = slice(j * own_rows, (j + 1) * own_rows)
-        value = keep_ref[rows, :] + got_ref[rows, :].astype(f32)
-        ref[...] = value.astype(ref.dtype)
-
-
-def last_kernel(scaling, own_ref, h_ref, shared_ref, other_ref, *refs):
-    got_refs, (dhid_ref, dwbct_ref) = refs[:-2], refs[-2:]
+def last_kernel(own_rows, scaling, got_ref, h_ref, shared_ref, other_ref, dhid_ref, dwbct_ref):
     flip = mirror(BLOCK)
     length, width = h_ref.shape
     groups = width // length
-    total = own_ref[...]
-    for got in got_refs:
-        total += got[...].astype(f32)
+    total = jnp.zeros((own_rows, width), f32)
+    for i in range(got_ref.shape[0] // own_rows):
+        total += got_ref[i * own_rows : (i + 1) * own_rows, :].astype(f32)
     dhid_ref[...] = total.astype(bf16)
     shared = (shared_ref[...].astype(f32) + other_ref[...].astype(f32)).astype(bf16)
     shared = jnp.concatenate(
@@ -543,13 +532,12 @@
     )
     scaling = 1.0 / math.sqrt(length)
     got = across(send, 1)
-    quarter = half // 2
-    at = extra + quarter
+    send_rows = (keep[extra:] + got[extra:].astype(f32)).astype(bf16)
     given, own_given = got, keep
-    send = (keep[extra:at] + got[extra:at].astype(f32)).astype(bf16)
-    keep = keep[at:] + got[at:].astype(f32)
-    sent = send
-    got = across(send, 2)
+    places = [[chip * 2 + core for chip in range(tp_size // 2)] for core in range(2)]
+    got = lax.all_to_all(
+        send_rows, "tp", split_axis=0, concat_axis=0, axis_index_groups=places, tiled=True
+    )
 
     def add_shared(a, b, *first):
         return call(
@@ -568,7 +556,7 @@
         outs += (shape((length, width), bf16),)
     d_w_in, d_w_out, mark, *in_order = call(
         functools.partial(weight_kernel, len(pieces), layout, scaling),
-        [ids, *pieces, gcat, gated, send],
+        [ids, *pieces, gcat, gated, send_rows],
         1,
         outs,
         [] if ordered else [pltpu.VMEM((length, width), bf16)],
@@ -578,24 +566,14 @@
         vmem=vmem,
     )
     in_order = in_order[0] if in_order else pieces[0]
-    own, *send = call(
-        functools.partial(stage_kernel, own_rows),
-        [keep, got],
-        0,
-        (shape((own_rows, width), f32),) + (shape((own_rows, width), bf16),) * (nz - 1),
-        [],
-        4 * quarter * width,
-        10 * quarter * width,
-    )
-    shared = add_shared(own_given, given, sent)
+    shared = add_shared(own_given, given, send_rows)
     step = nz // 2
     while step:
-        shared = add_shared(shared, across(shared, 4 * step), mark if step > 1 else own)
+        shared = add_shared(shared, across(shared, 4 * step), send_rows if step > 1 else mark)
         step //= 2
-    got = [across(piece, 4 * (j + 1)) for j, piece in enumerate(send)]
     d_hidden, d_w_bc = call(
-        functools.partial(last_kernel, scaling),
-        [own, in_order, shared, across(shared, 2), *got],
+        functools.partial(last_kernel, own_rows, scaling),
+        [got, in_order, shared, across(shared, 2)],
         0,
         (shape((own_rows, width), bf16), shape((2 * STATE, width), f32)),
         [],

time: 70.7 us -> 101 us (1.43)
  local copies, waits for them, and re-layouts: 0.02 us -> 15.9 us
  waiting for transfers between devices: 23.5 us -> 36 us
    unnamed x10 -> x70, local copies, waits for them, and re-layouts: 0.02 us -> 15.9 us
    ppermute x22 -> x18, waiting for transfers between devices: 16 us -> 28.7 us  [across(): lax.ppermute(value, 'tp', [(i, i ^ flip_bits) for i in range(tp_size)])]
    ppermute x22 -> x18, starting transfers between devices: 22.8 us -> 16.5 us  [across(): lax.ppermute(value, 'tp', [(i, i ^ flip_bits) for i in range(tp_size)])]
    all_to_all x0 -> x1, starting transfers between devices: none -> 5.59 us  [local(): lax.all_to_all(send_rows, 'tp', split_axis=0, concat_axis=0, axis_index_g...]
    pallas_call x13 -> x12, Pallas kernels: 15.6 us -> 16.3 us  [call(): pl.pallas_call(kernel, out_shape=outs, in_specs=[spec(pltpu.SMEM)] * n_sm...]
  transfers between devices with their start and end apart: 25 -> 22, of which waited for: 9 -> 10; matrix products, arithmetic and copies ran while one was open for 0% -> 0% of each run, Pallas kernels for 10% -> 7%
where the time goes in v7:
time: 101 us; the launch traced here: 99.9 us
  waiting for transfers between devices  36 us (36%)
  starting transfers between devices  26.8 us (27%)
  Pallas kernels  16.3 us (16%)
  local copies, waits for them, and re-layouts  15.9 us (16%)
  between operations  2.96 us (3%)
  other arithmetic  1.93 us (2%)
    ppermute x18, waiting for transfers between devices, across(): lax.ppermute(value, 'tp', [(i, i ^ flip_bits) for i in range(tp_size)])  28.7 us
    ppermute x18, starting transfers between devices, across(): lax.ppermute(value, 'tp', [(i, i ^ flip_bits) for i in range(tp_size)])  16.5 us
    pallas_call x12, Pallas kernels, call(): pl.pallas_call(kernel, out_shape=outs, in_specs=[spec(pltpu.SMEM)] * n_sm...  16.3 us
    unnamed x70, local copies, waits for them, and re-layouts  15.9 us
    ppermute x3, waiting for transfers between devices, along(): lax.ppermute(value, 'ctx', [((i + offset) % ctx_size, i) for i in range(c...  7.25 us
    all_to_all x1, starting transfers between devices, local(): lax.all_to_all(send_rows, 'tp', split_axis=0, concat_axis=0, axis_index_g...  5.59 us
    ppermute x3, starting transfers between devices, along(): lax.ppermute(value, 'ctx', [((i + offset) % ctx_size, i) for i in range(c...  4.67 us
  transfers between devices with their start and end apart: 22, of which 10 were waited for; matrix products, arithmetic and copies ran while one was open for 0% of the time, Pallas kernels for 7%

profile of v7, /device:TPU:0, one launch (start us, length us, event | category | flops | bytes accessed | tf_op | source)
XLA Modules:
  0.0 99.9 jit_solution(12220703962685275452)
XLA Ops:
  1.6 4.1 %collective-permute-start = (bf16[32,2048]{1,0:T(8,128)(2,1)S(1)}, bf16[32,2048]{1,0:T(8,128)(2,1)S(1)}, u32[]{:S(2)}, u32[]{:S(2)}) collective-permute-start(bf16[32,2048]{1,0:T(8,128)(2,1)S(1)} %pad_maximum_fusion.refs_0_), channel_id=1, source_target_pairs={{0,8},{1,9},{2,10},{3,11},{4,12},{5,13},{6,14},{7,15},{8,0},{9,1},... | collective-permute-start | bytes 393224 | tf_op jit(solution)/shard_map/ppermute | solution.py:411
  5.7 1.6 %collective-permute-start.7 = (bf16[32,2048]{1,0:T(8,128)(2,1)S(1)}, bf16[32,2048]{1,0:T(8,128)(2,1)S(1)}, u32[]{:S(2)}, u32[]{:S(2)}) collective-permute-start(bf16[32,2048]{1,0:T(8,128)(2,1)S(1)} %pad_maximum_fusion.refs_0_), channel_id=1, source_target_pairs={{0,4},{1,5},{2,6},{3,7},{4,0},{5,1},{6,2},{7,3},{8,12},{9,13},{10,... | collective-permute-start | bytes 393224 | tf_op jit(solution)/shard_map/ppermute | solution.py:411
  7.3 4.8 %collective-permute-done.refs_0_ = bf16[32,2048]{1,0:T(8,128)(2,1)S(1)} collective-permute-done((bf16[32,2048]{1,0:T(8,128)(2,1)S(1)}, bf16[32,2048]{1,0:T(8,128)(2,1)S(1)}, u32[]{:S(2)}, u32[]{:S(2)}) %collective-permute-start) | collective-permute-done | bytes 131104 | tf_op jit(solution)/shard_map/ppermute | solution.py:411
  12.8 1.6 %collective-permute-start.9 = (bf16[64,2048]{1,0:T(8,128)(2,1)S(1)}, bf16[64,2048]{1,0:T(8,128)(2,1)S(1)}, u32[]{:S(2)}, u32[]{:S(2)}) collective-permute-start(bf16[64,2048]{1,0:T(8,128)(2,1)S(1)} %shard_map.130.refs_0_.refs_1_), channel_id=1, source_target_pairs={{0,2},{1,3},{2,0},{3,1},{4,6},{5,7},{6,4},{7,5},{8,10},{9,11},{10,... | collective-permute-start | bytes 786440 | tf_op jit(solution)/shard_map/ppermute | solution.py:411
  14.3 1.5 %collective-permute-start.8 = (bf16[64,2048]{1,0:T(8,128)(2,1)S(1)}, bf16[64,2048]{1,0:T(8,128)(2,1)S(1)}, u32[]{:S(2)}, u32[]{:S(2)}) collective-permute-start(bf16[64,2048]{1,0:T(8,128)(2,1)S(1)} %shard_map.130.refs_0_.refs_1_), channel_id=1, source_target_pairs={{16,0},{0,16},{17,1},{1,17},{18,2},{2,18},{19,3},{3,19},{20,4},{4,... | collective-permute-start | bytes 786440 | tf_op jit(solution)/shard_map/ppermute | solution.py:414
  15.8 1.2 %collective-permute-done.1.refs_1_ = bf16[32,2048]{1,0:T(8,128)(2,1)S(1)} collective-permute-done((bf16[32,2048]{1,0:T(8,128)(2,1)S(1)}, bf16[32,2048]{1,0:T(8,128)(2,1)S(1)}, u32[]{:S(2)}, u32[]{:S(2)}) %collective-permute-start.1) | collective-permute-done | bytes 131104 | tf_op jit(solution)/shard_map/ppermute | solution.py:411
  17.1 1.6 %collective-permute-start.5 = (bf16[64,2048]{1,0:T(8,128)(2,1)S(1)}, bf16[64,2048]{1,0:T(8,128)(2,1)S(1)}, u32[]{:S(2)}, u32[]{:S(2)}) collective-permute-start(bf16[64,2048]{1,0:T(8,128)(2,1)S(1)} %shard_map.129.refs_5_.refs_4_.refs_9_), channel_id=1, source_target_pairs={{16,0},{0,16},{17,1},{1,17},{18,2},{2,18},{19,3},{3,19},{20,4},{4,... | collective-permute-start | bytes 786440 | tf_op jit(solution)/shard_map/ppermute | solution.py:414
  18.7 1.5 %collective-permute-start.3 = (bf16[64,2048]{1,0:T(8,128)(2,1)S(1)}, bf16[64,2048]{1,0:T(8,128)(2,1)S(1)}, u32[]{:S(2)}, u32[]{:S(2)}) collective-permute-start(bf16[64,2048]{1,0:T(8,128)(2,1)S(1)} %shard_map.129.refs_5_.refs_4_.refs_9_), channel_id=1, source_target_pairs={{0,2},{1,3},{2,0},{3,1},{4,6},{5,7},{6,4},{7,5},{8,10},{9,11},{10,... | collective-permute-start | bytes 786440 | tf_op jit(solution)/shard_map/ppermute | solution.py:411
  20.2 1.8 %collective-permute-done.9.refs_3_.refs_2_ = bf16[64,2048]{1,0:T(8,128)(2,1)S(1)} collective-permute-done((bf16[64,2048]{1,0:T(8,128)(2,1)S(1)}, bf16[64,2048]{1,0:T(8,128)(2,1)S(1)}, u32[]{:S(2)}, u32[]{:S(2)}) %collective-permute-start.9) | collective-permute-done | bytes 262176 | tf_op jit(solution)/shard_map/ppermute | solution.py:411
  22.0 1.5 %collective-permute-done.8.refs_0_.refs_4_.refs_5_ = bf16[64,2048]{1,0:T(8,128)(2,1)S(1)} collective-permute-done((bf16[64,2048]{1,0:T(8,128)(2,1)S(1)}, bf16[64,2048]{1,0:T(8,128)(2,1)S(1)}, u32[]{:S(2)}, u32[]{:S(2)}) %collective-permute-start.8) | collective-permute-done | bytes 262176 | tf_op jit(solution)/shard_map/ppermute | solution.py:414
  23.6 4.0 %collective-permute-done.5.refs_2_.refs_8_.refs_13_ = bf16[64,2048]{1,0:T(8,128)(2,1)S(1)} collective-permute-done((bf16[64,2048]{1,0:T(8,128)(2,1)S(1)}, bf16[64,2048]{1,0:T(8,128)(2,1)S(1)}, u32[]{:S(2)}, u32[]{:S(2)}) %collective-permute-start.5) | collective-permute-done | bytes 262176 | tf_op jit(solution)/shard_map/ppermute | solution.py:414
  29.5 1.5 %collective-permute-start.10 = (bf16[64,2048]{1,0:T(8,128)(2,1)S(1)}, bf16[64,2048]{1,0:T(8,128)(2,1)S(1)}, u32[]{:S(2)}, u32[]{:S(2)}) collective-permute-start(bf16[64,2048]{1,0:T(8,128)(2,1)S(1)} %get-tuple-element.22), channel_id=1, source_target_pairs={{16,0},{0,16},{17,1},{1,17},{18,2},{2,18},{19,3},{3,19},{20,4},{4,... | collective-permute-start | bytes 786440 | tf_op jit(solution)/shard_map/ppermute | solution.py:414
  31.1 1.0 %copy-done.26 = bf16[2048,128]{1,0:T(8,128)(2,1)S(1)} copy-done((bf16[2048,128]{1,0:T(8,128)(2,1)S(1)}, bf16[2048,128]{1,0:T(8,128)(2,1)}, u32[]{:S(2)}) %copy-start.26) | copy-done | bytes 524312
  32.2 1.7 %shard_map.132 = (bf16[2048,512]{1,0:T(8,128)(2,1)S(1)}, bf16[512,2048]{1,0:T(8,128)(2,1)S(1)}, bf16[2048,256]{1,0:T(8,128)(2,1)S(1)}, f32[4,128]{1,0:T(4,128)S(1)}) custom-call(s32[4]{0:T(128)S(1)} %pad_add_fusion.ids_ref.refs_0_, bf16[2048,128]{1,0:T(8,128)(2,1)S(1)} %copy-done.26, bf16[32,2048]{1,0:T(8,128)(2,1)S(1)} %bitcast.9, ...), custom_call_target="tpu_custom_call" | custom-call | flops 805306368 | bytes 5242880 | tf_op jit(solution)/shard_map/pallas_call | solution.py:384
  33.9 1.6 %collective-permute-done.15.refs_0_ = bf16[64,2048]{1,0:T(8,128)(2,1)S(1)} collective-permute-done((bf16[64,2048]{1,0:T(8,128)(2,1)}, bf16[64,2048]{1,0:T(8,128)(2,1)S(1)}, u32[]{:S(2)}, u32[]{:S(2)}) %collective-permute-start.15) | collective-permute-done | bytes 262176 | tf_op jit(solution)/shard_map/ppermute | solution.py:411
  36.5 1.7 %collective-permute-done.10.refs_10_.refs_15_ = bf16[64,2048]{1,0:T(8,128)(2,1)S(1)} collective-permute-done((bf16[64,2048]{1,0:T(8,128)(2,1)S(1)}, bf16[64,2048]{1,0:T(8,128)(2,1)S(1)}, u32[]{:S(2)}, u32[]{:S(2)}) %collective-permute-start.10) | collective-permute-done | bytes 262176 | tf_op jit(solution)/shard_map/ppermute | solution.py:414
  40.2 1.0 %shard_map.134 = (f32[256,512]{1,0:T(8,128)S(1)}, f32[256,256]{1,0:T(8,128)S(1)}) custom-call(bf16[64,2048]{1,0:T(8,128)(2,1)S(1)} %shard_map.130.refs_0_.refs_1_, bf16[64,2048]{1,0:T(8,128)(2,1)S(1)} %collective-permute-done.12.refs_1_.refs_2_, bf16[64,2048]{1,0:T(8,128)(2,1)S(1)} %collective-permute-done.9.refs_3_.refs_2_, ...), custom_call_target="tpu_custom_call" | custom-call | flops 805306368 | bytes 2097152 | tf_op jit(solution)/shard_map/pallas_call | solution.py:384
  41.4 6.4 %shard_map.135 = (bf16[144,2048]{1,0:T(8,128)(2,1)S(1)}, f32[144,2048]{1,0:T(8,128)S(1)}, bf16[512,512]{1,0:T(8,128)(2,1)S(1)}, bf16[512,256]{1,0:T(8,128)(2,1)S(1)}) custom-call(s32[4]{0:T(128)S(1)} %pad_add_fusion.ids_ref.refs_0_, f32[1]{0:T(128)S(6)} %copy.14.refs_1_, f32[1]{0:T(128)S(6)} %copy.15.refs_2_, f32[1]{0:T(128)S(6)} %copy.16.refs_3_, ...), custom_call_target="tpu_custom_call" | custom-call | flops 2147483648 | bytes 8388608 | tf_op jit(solution)/shard_map/pallas_call | solution.py:384
  49.9 1.6 %collective-permute-done.17.b_ref = bf16[144,2048]{1,0:T(8,128)(2,1)S(1)} collective-permute-done((bf16[144,2048]{1,0:T(8,128)(2,1)S(1)}, bf16[144,2048]{1,0:T(8,128)(2,1)S(1)}, u32[]{:S(2)}, u32[]{:S(2)}) %collective-permute-start.17) | collective-permute-done | bytes 589856 | tf_op jit(solution)/shard_map/ppermute | solution.py:411
  52.4 5.6 %all-to-all-start = ((bf16[8,16,2048]{2,1,0:T(8,128)(2,1)}), bf16[8,16,2048]{2,1,0:T(8,128)(2,1)S(1)}, u32[]{:S(2)}, u32[]{:S(2)}) async-start(bf16[8,16,2048]{2,1,0:T(8,128)(2,1)} %bitcast.5), calls=%async_computation | async-start | bytes 1048576 | tf_op jit(solution)/shard_map/all_to_all | solution.py:538
  58.0 3.0 %collective-permute-start.18 = (bf16[16,2048]{1,0:T(8,128)(2,1)S(1)}, bf16[16,2048]{1,0:T(8,128)(2,1)S(1)}, u32[]{:S(2)}, u32[]{:S(2)}) collective-permute-start(bf16[16,2048]{1,0:T(8,128)(2,1)S(1)} %shard_map.137.a_ref), channel_id=1, source_target_pairs={{0,8},{1,9},{2,10},{3,11},{4,12},{5,13},{6,14},{7,15},{8,0},{9,1},... | collective-permute-start | bytes 196616 | tf_op jit(solution)/shard_map/ppermute | solution.py:411
  61.0 14.8 %collective-permute-done.18.b_ref = bf16[16,2048]{1,0:T(8,128)(2,1)S(1)} collective-permute-done((bf16[16,2048]{1,0:T(8,128)(2,1)S(1)}, bf16[16,2048]{1,0:T(8,128)(2,1)S(1)}, u32[]{:S(2)}, u32[]{:S(2)}) %collective-permute-start.18) | collective-permute-done | bytes 65568 | tf_op jit(solution)/shard_map/ppermute | solution.py:411
  77.9 0.9 copy-done.5
  78.8 0.9 copy-done.7
  80.7 0.9 copy-done.11
  81.7 0.9 copy-done.13
  83.6 0.9 copy-done.17
  84.5 0.9 copy-done.19
  89.3 4.4 %shard_map.136 = (f32[2048,128]{1,0:T(8,128)}, f32[64,2048]{1,0:T(8,128)}, f32[8,128]{1,0:T(8,128)S(1)}, bf16[512,2048]{1,0:T(8,128)(2,1)S(1)}) custom-call(s32[4]{0:T(128)S(1)} %pad_add_fusion.ids_ref.refs_0_, bf16[64,2048]{1,0:T(8,128)(2,1)S(1)} %shard_map.130.refs_0_.refs_1_, bf16[64,2048]{1,0:T(8,128)(2,1)S(1)} %copy-done.9, ...), custom_call_target="tpu_custom_call" | custom-call | flops 2147483648 | bytes 8388608 | tf_op jit(solution)/shard_map/pallas_call | solution.py:384
  93.6 1.5 %collective-permute-start.20 = (bf16[16,2048]{1,0:T(8,128)(2,1)S(1)}, bf16[16,2048]{1,0:T(8,128)(2,1)S(1)}, u32[]{:S(2)}, u32[]{:S(2)}) collective-permute-start(bf16[16,2048]{1,0:T(8,128)(2,1)S(1)} %shard_map.139.shared_ref), channel_id=1, source_target_pairs={{0,2},{1,3},{2,0},{3,1},{4,6},{5,7},{6,4},{7,5},{8,10},{9,11},{10,... | collective-permute-start | bytes 196616 | tf_op jit(solution)/shard_map/ppermute | solution.py:411
  95.2 2.8 %collective-permute-done.20.other_ref = bf16[16,2048]{1,0:T(8,128)(2,1)S(1)} collective-permute-done((bf16[16,2048]{1,0:T(8,128)(2,1)S(1)}, bf16[16,2048]{1,0:T(8,128)(2,1)S(1)}, u32[]{:S(2)}, u32[]{:S(2)}) %collective-permute-start.20) | collective-permute-done | bytes 65568 | tf_op jit(solution)/shard_map/ppermute | solution.py:411
  98.0 1.9 %shard_map.140 = (bf16[16,2048]{1,0:T(8,128)(2,1)}, f32[32,2048]{1,0:T(8,128)}) custom-call(bf16[128,2048]{1,0:T(8,128)(2,1)S(1)} %bitcast.8, bf16[512,2048]{1,0:T(8,128)(2,1)S(1)} %get-tuple-element.34.h_ref, bf16[16,2048]{1,0:T(8,128)(2,1)S(1)} %shard_map.139.shared_ref, bf16[16,2048]{1,0:T(8,128)(2,1)S(1)} %collective-permute-done.20.other_ref), custom_call_target="tpu_custom_call" | custom-call | flops 268435456 | bytes 4194304 | tf_op jit(solution)/shard_map/pallas_call | solution.py:384
  (97 shorter events, 15.4 us)
Async XLA Ops:
  0.6 30.5 %copy-start.29 = (bf16[64,2048]{1,0:T(8,128)(2,1)S(1)}, bf16[64,2048]{1,0:T(8,128)(2,1)}, u32[]{:S(2)}) copy-start(bf16[64,2048]{1,0:T(8,128)(2,1)} %refs_3_.2) | copy-start | bytes 786436
  0.6 30.5 %copy-start.34 = (f32[4,64]{1,0:T(4,128)S(1)}, f32[4,64]{1,0:T(4,128)}, u32[]{:S(2)}) copy-start(f32[4,64]{1,0:T(4,128)} %refs_4_.1) | copy-start | bytes 3076
  0.7 30.5 %copy-start.33 = (bf16[1,2048]{1,0:T(2,128)(2,1)S(1)}, bf16[1,2048]{1,0:T(2,128)(2,1)}, u32[]{:S(2)}) copy-start(bf16[1,2048]{1,0:T(2,128)(2,1)} %refs_2_.2) | copy-start | bytes 12292
  0.7 30.5 %copy-start.32 = (bf16[2048,32]{0,1:T(8,128)(2,1)S(1)}, bf16[2048,32]{0,1:T(8,128)(2,1)}, u32[]{:S(2)}) copy-start(bf16[2048,32]{0,1:T(8,128)(2,1)} %param.12) | copy-start | bytes 393220
  1.6 10.5 %collective-permute-start = (bf16[32,2048]{1,0:T(8,128)(2,1)S(1)}, bf16[32,2048]{1,0:T(8,128)(2,1)S(1)}, u32[]{:S(2)}, u32[]{:S(2)}) collective-permute-start(bf16[32,2048]{1,0:T(8,128)(2,1)S(1)} %pad_maximum_fusion.refs_0_), channel_id=1, source_target_pairs={{0,8},{1,9},{2,10},{3,11},{4,12},{5,13},{6,14},{7,15},{8,0},{9,1},... | collective-permute-start | bytes 393224 | tf_op jit(solution)/shard_map/ppermute | solution.py:411
  5.7 7.0 %collective-permute-start.7 = (bf16[32,2048]{1,0:T(8,128)(2,1)S(1)}, bf16[32,2048]{1,0:T(8,128)(2,1)S(1)}, u32[]{:S(2)}, u32[]{:S(2)}) collective-permute-start(bf16[32,2048]{1,0:T(8,128)(2,1)S(1)} %pad_maximum_fusion.refs_0_), channel_id=1, source_target_pairs={{0,4},{1,5},{2,6},{3,7},{4,0},{5,1},{6,2},{7,3},{8,12},{9,13},{10,... | collective-permute-start | bytes 393224 | tf_op jit(solution)/shard_map/ppermute | solution.py:411
  12.1 5.0 %collective-permute-start.1 = (bf16[32,2048]{1,0:T(8,128)(2,1)S(1)}, bf16[32,2048]{1,0:T(8,128)(2,1)S(1)}, u32[]{:S(2)}, u32[]{:S(2)}) collective-permute-start(bf16[32,2048]{1,0:T(8,128)(2,1)S(1)} %collective-permute-done.refs_0_), channel_id=1, source_target_pairs={{0,4},{1,5},{2,6},{3,7},{4,0},{5,1},{6,2},{7,3},{8,12},{9,13},{10,... | collective-permute-start | bytes 393224 | tf_op jit(solution)/shard_map/ppermute | solution.py:411
  12.8 9.3 %collective-permute-start.9 = (bf16[64,2048]{1,0:T(8,128)(2,1)S(1)}, bf16[64,2048]{1,0:T(8,128)(2,1)S(1)}, u32[]{:S(2)}, u32[]{:S(2)}) collective-permute-start(bf16[64,2048]{1,0:T(8,128)(2,1)S(1)} %shard_map.130.refs_0_.refs_1_), channel_id=1, source_target_pairs={{0,2},{1,3},{2,0},{3,1},{4,6},{5,7},{6,4},{7,5},{8,10},{9,11},{10,... | collective-permute-start | bytes 786440 | tf_op jit(solution)/shard_map/ppermute | solution.py:411
  14.3 9.2 %collective-permute-start.8 = (bf16[64,2048]{1,0:T(8,128)(2,1)S(1)}, bf16[64,2048]{1,0:T(8,128)(2,1)S(1)}, u32[]{:S(2)}, u32[]{:S(2)}) collective-permute-start(bf16[64,2048]{1,0:T(8,128)(2,1)S(1)} %shard_map.130.refs_0_.refs_1_), channel_id=1, source_target_pairs={{16,0},{0,16},{17,1},{1,17},{18,2},{2,18},{19,3},{3,19},{20,4},{4,... | collective-permute-start | bytes 786440 | tf_op jit(solution)/shard_map/ppermute | solution.py:414
  17.1 10.5 %collective-permute-start.5 = (bf16[64,2048]{1,0:T(8,128)(2,1)S(1)}, bf16[64,2048]{1,0:T(8,128)(2,1)S(1)}, u32[]{:S(2)}, u32[]{:S(2)}) collective-permute-start(bf16[64,2048]{1,0:T(8,128)(2,1)S(1)} %shard_map.129.refs_5_.refs_4_.refs_9_), channel_id=1, source_target_pairs={{16,0},{0,16},{17,1},{1,17},{18,2},{2,18},{19,3},{3,19},{20,4},{4,... | collective-permute-start | bytes 786440 | tf_op jit(solution)/shard_map/ppermute | solution.py:414
  18.7 8.9 %collective-permute-start.3 = (bf16[64,2048]{1,0:T(8,128)(2,1)S(1)}, bf16[64,2048]{1,0:T(8,128)(2,1)S(1)}, u32[]{:S(2)}, u32[]{:S(2)}) collective-permute-start(bf16[64,2048]{1,0:T(8,128)(2,1)S(1)} %shard_map.129.refs_5_.refs_4_.refs_9_), channel_id=1, source_target_pairs={{0,2},{1,3},{2,0},{3,1},{4,6},{5,7},{6,4},{7,5},{8,10},{9,11},{10,... | collective-permute-start | bytes 786440 | tf_op jit(solution)/shard_map/ppermute | solution.py:411
  22.0 18.2 %copy-start = (bf16[64,2048]{1,0:T(8,128)(2,1)}, bf16[64,2048]{1,0:T(8,128)(2,1)S(1)}, u32[]{:S(2)}) copy-start(bf16[64,2048]{1,0:T(8,128)(2,1)S(1)} %collective-permute-done.9.refs_3_.refs_2_) | copy-start | bytes 786436
  23.6 16.7 %copy-start.2 = (bf16[64,2048]{1,0:T(8,128)(2,1)}, bf16[64,2048]{1,0:T(8,128)(2,1)S(1)}, u32[]{:S(2)}) copy-start(bf16[64,2048]{1,0:T(8,128)(2,1)S(1)} %collective-permute-done.8.refs_0_.refs_4_.refs_5_) | copy-start | bytes 786436
  27.6 13.7 %copy-start.4 = (bf16[64,2048]{1,0:T(8,128)(2,1)}, bf16[64,2048]{1,0:T(8,128)(2,1)S(1)}, u32[]{:S(2)}) copy-start(bf16[64,2048]{1,0:T(8,128)(2,1)S(1)} %collective-permute-done.5.refs_2_.refs_8_.refs_13_) | copy-start | bytes 786436
  27.6 13.8 %copy-start.6 = (bf16[64,2048]{1,0:T(8,128)(2,1)}, bf16[64,2048]{1,0:T(8,128)(2,1)S(1)}, u32[]{:S(2)}) copy-start(bf16[64,2048]{1,0:T(8,128)(2,1)S(1)} %collective-permute-done.3.refs_1_.refs_6_.refs_11_) | copy-start | bytes 786436
  28.5 7.0 %collective-permute-start.15 = (bf16[64,2048]{1,0:T(8,128)(2,1)}, bf16[64,2048]{1,0:T(8,128)(2,1)S(1)}, u32[]{:S(2)}, u32[]{:S(2)}) collective-permute-start(bf16[64,2048]{1,0:T(8,128)(2,1)} %get-tuple-element.23), channel_id=1, source_target_pairs={{0,2},{1,3},{2,0},{3,1},{4,6},{5,7},{6,4},{7,5},{8,10},{9,11},{10,... | collective-permute-start | bytes 786440 | tf_op jit(solution)/shard_map/ppermute | solution.py:411
  29.0 6.5 %collective-permute-start.12 = (bf16[64,2048]{1,0:T(8,128)(2,1)S(1)}, bf16[64,2048]{1,0:T(8,128)(2,1)S(1)}, u32[]{:S(2)}, u32[]{:S(2)}) collective-permute-start(bf16[64,2048]{1,0:T(8,128)(2,1)S(1)} %shard_map.130.refs_0_.refs_1_), channel_id=1, source_target_pairs={{0,1},{1,0},{2,3},{3,2},{4,5},{5,4},{6,7},{7,6},{8,9},{9,8},{10,11... | collective-permute-start | bytes 786440 | tf_op jit(solution)/shard_map/ppermute | solution.py:411
  29.0 7.0 %collective-permute-start.13 = (bf16[64,2048]{1,0:T(8,128)(2,1)S(1)}, bf16[64,2048]{1,0:T(8,128)(2,1)S(1)}, u32[]{:S(2)}, u32[]{:S(2)}) collective-permute-start(bf16[64,2048]{1,0:T(8,128)(2,1)S(1)} %collective-permute-done.9.refs_3_.refs_2_), channel_id=1, source_target_pairs={{0,1},{1,0},{2,3},{3,2},{4,5},{5,4},{6,7},{7,6},{8,9},{9,8},{10,11... | collective-permute-start | bytes 786440 | tf_op jit(solution)/shard_map/ppermute | solution.py:411
  29.5 6.6 %collective-permute-start.14 = (bf16[64,2048]{1,0:T(8,128)(2,1)S(1)}, bf16[64,2048]{1,0:T(8,128)(2,1)S(1)}, u32[]{:S(2)}, u32[]{:S(2)}) collective-permute-start(bf16[64,2048]{1,0:T(8,128)(2,1)S(1)} %collective-permute-done.8.refs_0_.refs_4_.refs_5_), channel_id=1, source_target_pairs={{0,1},{1,0},{2,3},{3,2},{4,5},{5,4},{6,7},{7,6},{8,9},{9,8},{10,11... | collective-permute-start | bytes 786440 | tf_op jit(solution)/shard_map/ppermute | solution.py:411
  29.5 8.7 %collective-permute-start.10 = (bf16[64,2048]{1,0:T(8,128)(2,1)S(1)}, bf16[64,2048]{1,0:T(8,128)(2,1)S(1)}, u32[]{:S(2)}, u32[]{:S(2)}) collective-permute-start(bf16[64,2048]{1,0:T(8,128)(2,1)S(1)} %get-tuple-element.22), channel_id=1, source_target_pairs={{16,0},{0,16},{17,1},{1,17},{18,2},{2,18},{19,3},{3,19},{20,4},{4,... | collective-permute-start | bytes 786440 | tf_op jit(solution)/shard_map/ppermute | solution.py:414
  35.4 4.7 %collective-permute-start.16 = (bf16[64,2048]{1,0:T(8,128)(2,1)S(1)}, bf16[64,2048]{1,0:T(8,128)(2,1)S(1)}, u32[]{:S(2)}, u32[]{:S(2)}) collective-permute-start(bf16[64,2048]{1,0:T(8,128)(2,1)S(1)} %shard_map.133.refs_6_.refs_7_), channel_id=1, source_target_pairs={{0,1},{1,0},{2,3},{3,2},{4,5},{5,4},{6,7},{7,6},{8,9},{9,8},{10,11... | collective-permute-start | bytes 786440 | tf_op jit(solution)/shard_map/ppermute | solution.py:411
  35.5 5.7 %collective-permute-start.2 = (bf16[64,2048]{1,0:T(8,128)(2,1)S(1)}, bf16[64,2048]{1,0:T(8,128)(2,1)S(1)}, u32[]{:S(2)}, u32[]{:S(2)}) collective-permute-start(bf16[64,2048]{1,0:T(8,128)(2,1)S(1)} %shard_map.129.refs_5_.refs_4_.refs_9_), channel_id=1, source_target_pairs={{0,1},{1,0},{2,3},{3,2},{4,5},{5,4},{6,7},{7,6},{8,9},{9,8},{10,11... | collective-permute-start | bytes 786440 | tf_op jit(solution)/shard_map/ppermute | solution.py:411
  36.0 5.3 %collective-permute-start.6 = (bf16[64,2048]{1,0:T(8,128)(2,1)S(1)}, bf16[64,2048]{1,0:T(8,128)(2,1)S(1)}, u32[]{:S(2)}, u32[]{:S(2)}) collective-permute-start(bf16[64,2048]{1,0:T(8,128)(2,1)S(1)} %collective-permute-done.5.refs_2_.refs_8_.refs_13_), channel_id=1, source_target_pairs={{0,1},{1,0},{2,3},{3,2},{4,5},{5,4},{6,7},{7,6},{8,9},{9,8},{10,11... | collective-permute-start | bytes 786440 | tf_op jit(solution)/shard_map/ppermute | solution.py:411
  36.1 5.2 %collective-permute-start.4 = (bf16[64,2048]{1,0:T(8,128)(2,1)S(1)}, bf16[64,2048]{1,0:T(8,128)(2,1)S(1)}, u32[]{:S(2)}, u32[]{:S(2)}) collective-permute-start(bf16[64,2048]{1,0:T(8,128)(2,1)S(1)} %collective-permute-done.3.refs_1_.refs_6_.refs_11_), channel_id=1, source_target_pairs={{0,1},{1,0},{2,3},{3,2},{4,5},{5,4},{6,7},{7,6},{8,9},{9,8},{10,11... | collective-permute-start | bytes 786440 | tf_op jit(solution)/shard_map/ppermute | solution.py:411
  38.2 3.1 %collective-permute-start.11 = (bf16[64,2048]{1,0:T(8,128)(2,1)S(1)}, bf16[64,2048]{1,0:T(8,128)(2,1)S(1)}, u32[]{:S(2)}, u32[]{:S(2)}) collective-permute-start(bf16[64,2048]{1,0:T(8,128)(2,1)S(1)} %collective-permute-done.10.refs_10_.refs_15_), channel_id=1, source_target_pairs={{0,1},{1,0},{2,3},{3,2},{4,5},{5,4},{6,7},{7,6},{8,9},{9,8},{10,11... | collective-permute-start | bytes 786440 | tf_op jit(solution)/shard_map/ppermute | solution.py:411
  41.3 6.5 %copy-start.18 = (bf16[64,2048]{1,0:T(8,128)(2,1)}, bf16[64,2048]{1,0:T(8,128)(2,1)S(1)}, u32[]{:S(2)}) copy-start(bf16[64,2048]{1,0:T(8,128)(2,1)S(1)} %collective-permute-done.2.refs_5_.refs_10_) | copy-start | bytes 786436
  49.4 2.1 %collective-permute-start.17 = (bf16[144,2048]{1,0:T(8,128)(2,1)S(1)}, bf16[144,2048]{1,0:T(8,128)(2,1)S(1)}, u32[]{:S(2)}, u32[]{:S(2)}) collective-permute-start(bf16[144,2048]{1,0:T(8,128)(2,1)S(1)} %get-tuple-element.31), channel_id=1, source_target_pairs={{0,1},{1,0},{2,3},{3,2},{4,5},{5,4},{6,7},{7,6},{8,9},{9,8},{10,11... | collective-permute-start | bytes 1769480 | tf_op jit(solution)/shard_map/ppermute | solution.py:411
  52.4 45.5 %all-to-all-start = ((bf16[8,16,2048]{2,1,0:T(8,128)(2,1)}), bf16[8,16,2048]{2,1,0:T(8,128)(2,1)S(1)}, u32[]{:S(2)}, u32[]{:S(2)}) async-start(bf16[8,16,2048]{2,1,0:T(8,128)(2,1)} %bitcast.5), calls=%async_computation | async-start | bytes 1048576 | tf_op jit(solution)/shard_map/all_to_all | solution.py:538
  58.0 17.9 %copy-start.28 = (bf16[512,512]{1,0:T(8,128)(2,1)S(1)}, bf16[512,512]{1,0:T(8,128)(2,1)}, u32[]{:S(2)}) copy-start(bf16[512,512]{1,0:T(8,128)(2,1)} %copy-done.27) | copy-start | bytes 1572868
  58.0 17.8 %collective-permute-start.18 = (bf16[16,2048]{1,0:T(8,128)(2,1)S(1)}, bf16[16,2048]{1,0:T(8,128)(2,1)S(1)}, u32[]{:S(2)}, u32[]{:S(2)}) collective-permute-start(bf16[16,2048]{1,0:T(8,128)(2,1)S(1)} %shard_map.137.a_ref), channel_id=1, source_target_pairs={{0,8},{1,9},{2,10},{3,11},{4,12},{5,13},{6,14},{7,15},{8,0},{9,1},... | collective-permute-start | bytes 196616 | tf_op jit(solution)/shard_map/ppermute | solution.py:411
  75.9 17.8 %collective-permute-start.19 = (bf16[16,2048]{1,0:T(8,128)(2,1)S(1)}, bf16[16,2048]{1,0:T(8,128)(2,1)S(1)}, u32[]{:S(2)}, u32[]{:S(2)}) collective-permute-start(bf16[16,2048]{1,0:T(8,128)(2,1)S(1)} %shard_map.138.a_ref), channel_id=1, source_target_pairs={{0,4},{1,5},{2,6},{3,7},{4,0},{5,1},{6,2},{7,3},{8,12},{9,13},{10,... | collective-permute-start | bytes 196616 | tf_op jit(solution)/shard_map/ppermute | solution.py:411
  93.6 4.3 %collective-permute-start.20 = (bf16[16,2048]{1,0:T(8,128)(2,1)S(1)}, bf16[16,2048]{1,0:T(8,128)(2,1)S(1)}, u32[]{:S(2)}, u32[]{:S(2)}) collective-permute-start(bf16[16,2048]{1,0:T(8,128)(2,1)S(1)} %shard_map.139.shared_ref), channel_id=1, source_target_pairs={{0,2},{1,3},{2,0},{3,1},{4,6},{5,7},{6,4},{7,5},{8,10},{9,11},{10,... | collective-permute-start | bytes 196616 | tf_op jit(solution)/shard_map/ppermute | solution.py:411
  (25 other events, 55.7 us)

commit v8 on v6

--- a/solution.py
+++ b/solution.py
@@ -57,7 +57,7 @@
 
 
 def owners(ids_ref, layout):
-    tp_size, own_rows, coords = layout
+    tp_size, own_rows, coords, _ = layout
     z, x, core, ctx = (ids_ref[i] for i in range(4))
     ctx_size = max(c[0] for c in coords) + 1
     for p, (dc, dx, dcore, blocks) in enumerate(coords):
@@ -80,9 +80,8 @@
 
 
 def project(pieces, wall_ref, gall_ref):
-    half = pieces[0].shape[0] // 2
-    h = jnp.concatenate([piece[:half, :] for piece in pieces], axis=0)
-    d = jnp.concatenate([piece[half:, :] for piece in pieces], axis=0)
+    h = jnp.concatenate([piece[: piece.shape[0] // 2, :] for piece in pieces], axis=0)
+    d = jnp.concatenate([piece[piece.shape[0] // 2 :, :] for piece in pieces], axis=0)
     return dot(h, wall_ref[...]), dot(d, gall_ref[...])
 
 
@@ -96,9 +95,8 @@
             out_ref[rows, :] = ref[own_rows:, :]
 
 
-def copy_kernel(count, *refs):
-    for value_ref, out_ref in zip(refs[:count], refs[len(refs) - count :]):
-        out_ref[...] = value_ref[...]
+def copy_kernel(value_ref, *refs):
+    refs[-1][...] = value_ref[...]
 
 
 def early_kernel(*refs):
@@ -179,18 +177,20 @@
     early_refs = refs[4 + n_pieces : 6 + n_pieces]
     wall_ref, wallt_ref, gall_ref, taps_ref = refs[6 + n_pieces : 10 + n_pieces]
     send_ref, keep_ref, gcat_ref, gated_ref = refs[10 + n_pieces : 14 + n_pieces]
-    tp_size, own_rows, coords = layout
+    tp_size, own_rows, coords, n_early = layout
     if coords is None:
         proj, grads = early_refs[0][...], early_refs[1][...]
     else:
         proj_ref, grad_ref = refs[14 + n_pieces :]
-        halves = [[ref[...] for ref in early_refs], project(pieces, wall_ref, gall_ref)]
+        parts = [[ref[...] for ref in early_refs], project(pieces, wall_ref, gall_ref)]
+        first = 0
         for p, k, at in owners(ids_ref, layout):
-            blocks = len(coords[p][3])
-            source = halves[p // n_pieces]
-            first = ((p % n_pieces) * blocks + k) * own_rows
+            if p == n_early and k == 0:
+                first = 0
+            source = parts[p >= n_early]
             proj_ref[pl.ds(at, own_rows), :] = source[0][first : first + own_rows]
             grad_ref[pl.ds(at, own_rows), :] = source[1][first : first + own_rows]
+            first += own_rows
         proj, grads = proj_ref[...], grad_ref[...]
     length, width = proj.shape[0], wall_ref.shape[0]
     chunks = length // BLOCK
@@ -421,10 +421,8 @@
     def across(value, flip_bits):
         return lax.ppermute(value, "tp", [(i, i ^ flip_bits) for i in range(tp_size)])
 
-    def along(value, offset):
-        return lax.ppermute(
-            value, "ctx", [((i + offset) % ctx_size, i) for i in range(ctx_size)]
-        )
+    def along(value):
+        return lax.ppermute(value, "ctx", [(0, 1), (1, 0)])
 
     def prepare(*begun):
         return call(
@@ -443,76 +441,65 @@
             len(begun),
         )
 
-    def pack(parts, rows):
+    def pack(parts, *first):
+        rows = sum(part.shape[0] for part in parts)
         return call(
             functools.partial(pack_kernel, len(parts), own_rows),
-            parts,
+            [*parts, *first],
             0,
             shape((rows, width), bf16),
             [],
             0,
             4 * rows * width,
-        )
-
-    def column(own, count):
-        if count == 1:
-            return [own]
-        half = count // 2
-        return column(own, half) + column(across(own, 4 * half), half)
-
-    def after(first, value):
-        outs = (shape(value.shape, bf16),)
+            len(first),
+        )
+
+    def after(value, *first):
         return call(
-            functools.partial(copy_kernel, 1), [value, first], 0, outs, [], 0, 4 * value.size, 1
-        )[0]
-
-    if own_rows % TILE_ROWS == 0:
+            copy_kernel,
+            [value, *first],
+            0,
+            shape(value.shape, bf16),
+            [],
+            0,
+            4 * value.size,
+            len(first),
+        )
+
+    if own_rows % TILE_ROWS == 0 and (ctx_size, nz) == (2, 4):
         low = jnp.array(-jnp.inf, bf16)
-        both = jnp.maximum(
+        own = jnp.maximum(
             lax.pad(hidden, low, [(0, own_rows, 0), (0, 0, 0)]),
             lax.pad(d_out, low, [(own_rows, 0, 0), (0, 0, 0)]),
         )
-        zs = column(both, nz)
-        coords, pieces, planes = [], [], []
-        for blocks in (range(0, nz // 2), range(nz // 2, nz)):
-            chunk = pack([zs[j] for j in blocks], nz * own_rows)
-            ahead = [along(chunk, dc) for dc in range(1, ctx_size)]
-            planes.append((chunk, across(chunk, 2), ahead, tuple(blocks)))
-        (_, beside_a, ahead_a, _), (chunk_b, beside_b, ahead_b, _) = planes
+        z_near, z_far = across(own, 4), across(own, 8)
+        chunk_a = pack([own, z_near])
+        chunk_b = pack([z_far, across(z_far, 4)])
+        direct = [[part, across(part, 2), along(part)] for part in (chunk_a, chunk_b)]
+        (_, a_x, a_c), (_, b_x, b_c) = direct
+        beside_a = [across(part, 1) for part in direct[0]]
         wall, wallt, gall, taps = prepare(chunk_b)
-        count = len(ahead_a)
-        *forward_a, forward_b = call(
-            functools.partial(copy_kernel, count + 1),
-            [*ahead_a, beside_b, *ahead_b, beside_a],
-            0,
-            (shape(beside_b.shape, bf16),) * (count + 1),
-            [],
-            0,
-            8 * beside_b.size,
-            count + 1,
-        )
-        diagonals = (
-            [after(taps, across(piece, 2)) for piece in forward_a],
-            [along(forward_b, dc + 1) for dc in range(count)],
-        )
-        for (chunk, beside, ahead, blocks), diagonal in zip(planes, diagonals):
-            plane = [((0, 0), chunk), ((0, 1), beside)]
-            for dc in range(count):
-                plane += [((dc + 1, 0), ahead[dc]), ((dc + 1, 1), diagonal[dc])]
-            for (dc, dx), piece in plane:
-                coords += [(dc, dx, 0, blocks), (dc, dx, 1, blocks)]
-                pieces += [piece, across(piece, 1)]
-        layout = (tp_size, own_rows, tuple(coords))
-        early, late = pieces[: len(pieces) // 2], pieces[len(pieces) // 2 :]
+        a_d = across(after(a_c, a_x, b_x, b_c, *beside_a), 2)
+        b_d = along(after(b_x, a_x, a_c, b_c, *beside_a))
+        beside = [beside_a, [across(part, 1) for part in direct[1]]]
+        early, coords = [], []
+        blocks = ((0, 1), (2, 3))
+        for g in range(2):
+            for place, part, other in zip(((0, 0), (0, 1), (1, 0)), direct[g], beside[g]):
+                early += [part, other]
+                coords += [(*place, 0, blocks[g]), (*place, 1, blocks[g])]
+        coords += [(1, 1, core, blocks[g]) for g in range(2) for core in range(2)]
+        layout = (tp_size, own_rows, tuple(coords), len(early))
+        late, pieces = None, None
     else:
         pieces = [lax.all_gather(a, ("ctx", "tp"), axis=0, tiled=True) for a in (hidden, d_out)]
-        layout = (tp_size, own_rows, None)
+        layout = (tp_size, own_rows, None, 0)
         wall, wallt, gall, taps = prepare()
         early, late = [jnp.concatenate(pieces, axis=0)], []
     ordered = layout[2] is None
     vmem = 60 if ordered else 32
     early_rows = sum(piece.shape[0] for piece in early) // 2
-    early = call(
+    projected = call(
         early_kernel,
         [*early, wall, gall],
         0,
@@ -522,11 +509,14 @@
         4 * early_rows * width,
         vmem=vmem,
     )
+    if not ordered:
+        late = [a_d, across(after(a_d, projected[0]), 1), b_d, across(b_d, 1)]
+        pieces = early + late
     extra = 4 * STATE * length // width
     half = tp_size * own_rows // 2
     send, keep, gcat, gated = call(
         functools.partial(core_kernel, len(late), layout),
-        [ids, *params, *late, *early, wall, wallt, gall, taps],
+        [ids, *params, *late, *projected, wall, wallt, gall, taps],
         4,
         (
             shape((extra + half, width), bf16),

time: 70.7 us -> 66.9 us (0.946)
  starting transfers between devices: 27.5 us -> 24.7 us
  waiting for transfers between devices: 23.5 us -> 22.6 us
    ppermute x22, starting transfers between devices: 22.8 us -> 21.1 us  [across(): lax.ppermute(value, 'tp', [(i, i ^ flip_bits) for i in range(tp_size)])]
    ppermute x3, starting transfers between devices: 4.67 us -> 3.62 us  [along(): return lax.ppermute(value, 'ctx', [(0, 1), (1, 0)])]
    ppermute x22, waiting for transfers between devices: 16 us -> 15.1 us  [across(): lax.ppermute(value, 'tp', [(i, i ^ flip_bits) for i in range(tp_size)])]
    pallas_call x13 -> x14, Pallas kernels: 15.6 us -> 15.5 us  [call(): pl.pallas_call(kernel, out_shape=outs, in_specs=[spec(pltpu.SMEM)] * n_sm...]
  transfers between devices with their start and end apart: 25 -> 25, of which waited for: 9 -> 10; matrix products, arithmetic and copies ran while one was open for 0% -> 0% of each run, Pallas kernels for 10% -> 12%
where the time goes in v8:
time: 66.9 us; the launch traced here: 66.7 us
  starting transfers between devices  24.7 us (37%)
  waiting for transfers between devices  22.6 us (34%)
  Pallas kernels  15.5 us (23%)
  between operations  2.76 us (4%)
  other arithmetic  1.09 us (2%)
    ppermute x22, starting transfers between devices, across(): lax.ppermute(value, 'tp', [(i, i ^ flip_bits) for i in range(tp_size)])  21.1 us
    pallas_call x14, Pallas kernels, call(): pl.pallas_call(kernel, out_shape=outs, in_specs=[spec(pltpu.SMEM)] * n_sm...  15.5 us
    ppermute x22, waiting for transfers between devices, across(): lax.ppermute(value, 'tp', [(i, i ^ flip_bits) for i in range(tp_size)])  15.1 us
    ppermute x3, waiting for transfers between devices, along(): return lax.ppermute(value, 'ctx', [(0, 1), (1, 0)])  7.5 us
    ppermute x3, starting transfers between devices, along(): return lax.ppermute(value, 'ctx', [(0, 1), (1, 0)])  3.62 us
  transfers between devices with their start and end apart: 25, of which 10 were waited for; matrix products, arithmetic and copies ran while one was open for 0% of the time, Pallas kernels for 12%

profile of v8, /device:TPU:0, one launch (start us, length us, event | category | flops | bytes accessed | tf_op | source)
XLA Modules:
  0.0 66.7 jit_solution(8371347290609289141)
XLA Ops:
  0.6 0.9 %pad_maximum_fusion.refs_0_ = bf16[32,2048]{1,0:T(8,128)(2,1)S(1)} fusion(bf16[16,2048]{1,0:T(8,128)(2,1)} %param.19, bf16[16,2048]{1,0:T(8,128)(2,1)} %param.10), kind=kLoop, calls=%fused_computation.2 | loop fusion | flops 262144 | bytes 262144 | tf_op jit(solution)/shard_map/max | solution.py:471
  1.5 3.1 %collective-permute-start = (bf16[32,2048]{1,0:T(8,128)(2,1)S(1)}, bf16[32,2048]{1,0:T(8,128)(2,1)S(1)}, u32[]{:S(2)}, u32[]{:S(2)}) collective-permute-start(bf16[32,2048]{1,0:T(8,128)(2,1)S(1)} %pad_maximum_fusion.refs_0_), channel_id=1, source_target_pairs={{0,4},{1,5},{2,6},{3,7},{4,0},{5,1},{6,2},{7,3},{8,12},{9,13},{10,... | collective-permute-start | bytes 393224 | tf_op jit(solution)/shard_map/ppermute | solution.py:422
  4.6 2.6 %collective-permute-start.3 = (bf16[32,2048]{1,0:T(8,128)(2,1)S(1)}, bf16[32,2048]{1,0:T(8,128)(2,1)S(1)}, u32[]{:S(2)}, u32[]{:S(2)}) collective-permute-start(bf16[32,2048]{1,0:T(8,128)(2,1)S(1)} %pad_maximum_fusion.refs_0_), channel_id=1, source_target_pairs={{0,8},{1,9},{2,10},{3,11},{4,12},{5,13},{6,14},{7,15},{8,0},{9,1},... | collective-permute-start | bytes 393224 | tf_op jit(solution)/shard_map/ppermute | solution.py:422
  7.2 2.8 %collective-permute-done.refs_1_ = bf16[32,2048]{1,0:T(8,128)(2,1)S(1)} collective-permute-done((bf16[32,2048]{1,0:T(8,128)(2,1)S(1)}, bf16[32,2048]{1,0:T(8,128)(2,1)S(1)}, u32[]{:S(2)}, u32[]{:S(2)}) %collective-permute-start) | collective-permute-done | bytes 131104 | tf_op jit(solution)/shard_map/ppermute | solution.py:422
  10.0 1.9 %collective-permute-start.2 = (bf16[64,2048]{1,0:T(8,128)(2,1)S(1)}, bf16[64,2048]{1,0:T(8,128)(2,1)S(1)}, u32[]{:S(2)}, u32[]{:S(2)}) collective-permute-start(bf16[64,2048]{1,0:T(8,128)(2,1)S(1)} %shard_map.129.refs_0_.refs_1_), channel_id=1, source_target_pairs={{0,2},{1,3},{2,0},{3,1},{4,6},{5,7},{6,4},{7,5},{8,10},{9,11},{10,... | collective-permute-start | bytes 786440 | tf_op jit(solution)/shard_map/ppermute | solution.py:422
  11.9 1.5 %collective-permute-start.1 = (bf16[64,2048]{1,0:T(8,128)(2,1)S(1)}, bf16[64,2048]{1,0:T(8,128)(2,1)S(1)}, u32[]{:S(2)}, u32[]{:S(2)}) collective-permute-start(bf16[64,2048]{1,0:T(8,128)(2,1)S(1)} %shard_map.129.refs_0_.refs_1_), channel_id=1, source_target_pairs={{0,16},{16,0},{1,17},{17,1},{2,18},{18,2},{3,19},{19,3},{4,20},{20... | collective-permute-start | bytes 786440 | tf_op jit(solution)/shard_map/ppermute | solution.py:425
  13.8 4.6 %collective-permute-done.4.refs_1_ = bf16[32,2048]{1,0:T(8,128)(2,1)S(1)} collective-permute-done((bf16[32,2048]{1,0:T(8,128)(2,1)S(1)}, bf16[32,2048]{1,0:T(8,128)(2,1)S(1)}, u32[]{:S(2)}, u32[]{:S(2)}) %collective-permute-start.4) | collective-permute-done | bytes 131104 | tf_op jit(solution)/shard_map/ppermute | solution.py:422
  18.4 1.5 %collective-permute-start.6 = (bf16[64,2048]{1,0:T(8,128)(2,1)S(1)}, bf16[64,2048]{1,0:T(8,128)(2,1)S(1)}, u32[]{:S(2)}, u32[]{:S(2)}) collective-permute-start(bf16[64,2048]{1,0:T(8,128)(2,1)S(1)} %shard_map.130.refs_5_.refs_6_.refs_7_), channel_id=1, source_target_pairs={{0,16},{16,0},{1,17},{17,1},{2,18},{18,2},{3,19},{19,3},{4,20},{20... | collective-permute-start | bytes 786440 | tf_op jit(solution)/shard_map/ppermute | solution.py:425
  19.9 1.5 %collective-permute-start.5 = (bf16[64,2048]{1,0:T(8,128)(2,1)S(1)}, bf16[64,2048]{1,0:T(8,128)(2,1)S(1)}, u32[]{:S(2)}, u32[]{:S(2)}) collective-permute-start(bf16[64,2048]{1,0:T(8,128)(2,1)S(1)} %shard_map.130.refs_5_.refs_6_.refs_7_), channel_id=1, source_target_pairs={{0,2},{1,3},{2,0},{3,1},{4,6},{5,7},{6,4},{7,5},{8,10},{9,11},{10,... | collective-permute-start | bytes 786440 | tf_op jit(solution)/shard_map/ppermute | solution.py:422
  21.4 0.5 collective-permute-start.9
  22.0 2.8 %collective-permute-done.6.refs_2_.refs_10_.refs_11_ = bf16[64,2048]{1,0:T(8,128)(2,1)S(1)} collective-permute-done((bf16[64,2048]{1,0:T(8,128)(2,1)S(1)}, bf16[64,2048]{1,0:T(8,128)(2,1)S(1)}, u32[]{:S(2)}, u32[]{:S(2)}) %collective-permute-start.6) | collective-permute-done | bytes 262176 | tf_op jit(solution)/shard_map/ppermute | solution.py:425
  24.8 1.5 %collective-permute-done.5.refs_1_.refs_8_.value_ref.refs_9_ = bf16[64,2048]{1,0:T(8,128)(2,1)S(1)} collective-permute-done((bf16[64,2048]{1,0:T(8,128)(2,1)S(1)}, bf16[64,2048]{1,0:T(8,128)(2,1)S(1)}, u32[]{:S(2)}, u32[]{:S(2)}) %collective-permute-start.5) | collective-permute-done | bytes 262176 | tf_op jit(solution)/shard_map/ppermute | solution.py:422
  26.4 1.6 %collective-permute-start.10 = (bf16[64,2048]{1,0:T(8,128)(2,1)S(1)}, bf16[64,2048]{1,0:T(8,128)(2,1)S(1)}, u32[]{:S(2)}, u32[]{:S(2)}) collective-permute-start(bf16[64,2048]{1,0:T(8,128)(2,1)S(1)} %shard_map.131), channel_id=1, source_target_pairs={{0,2},{1,3},{2,0},{3,1},{4,6},{5,7},{6,4},{7,5},{8,10},{9,11},{10,... | collective-permute-start | bytes 786440 | tf_op jit(solution)/shard_map/ppermute | solution.py:422
  27.9 0.6 collective-permute-start.15
  28.6 1.7 %shard_map.132 = (bf16[2048,512]{1,0:T(8,128)(2,1)S(1)}, bf16[512,2048]{1,0:T(8,128)(2,1)S(1)}, bf16[2048,256]{1,0:T(8,128)(2,1)S(1)}, f32[4,128]{1,0:T(4,128)S(1)}) custom-call(s32[4]{0:T(128)S(1)} %pad_add_fusion.ids_ref.refs_0_, bf16[2048,128]{1,0:T(8,128)(2,1)S(1)} %copy-done, bf16[32,2048]{1,0:T(8,128)(2,1)S(1)} %bitcast.6, ...), custom_call_target="tpu_custom_call" | custom-call | flops 805306368 | bytes 5242880 | tf_op jit(solution)/shard_map/pallas_call | solution.py:395
  30.3 1.4 %shard_map.133 = (f32[384,512]{1,0:T(8,128)S(1)}, f32[384,256]{1,0:T(8,128)S(1)}) custom-call(bf16[64,2048]{1,0:T(8,128)(2,1)S(1)} %shard_map.129.refs_0_.refs_1_, bf16[64,2048]{1,0:T(8,128)(2,1)S(1)} %collective-permute-done.7.refs_3_.refs_1_.refs_2_, bf16[64,2048]{1,0:T(8,128)(2,1)S(1)} %collective-permute-done.2.refs_0_.refs_2_.refs_3_, ...), custom_call_target="tpu_custom_call" | custom-call | flops 1207959552 | bytes 3145728 | tf_op jit(solution)/shard_map/pallas_call | solution.py:395
  31.8 4.7 %collective-permute-done.15.refs_6_.refs_15_ = bf16[64,2048]{1,0:T(8,128)(2,1)S(1)} collective-permute-done((bf16[64,2048]{1,0:T(8,128)(2,1)S(1)}, bf16[64,2048]{1,0:T(8,128)(2,1)S(1)}, u32[]{:S(2)}, u32[]{:S(2)}) %collective-permute-start.15) | collective-permute-done | bytes 262176 | tf_op jit(solution)/shard_map/ppermute | solution.py:425
  36.5 0.6 collective-permute-start.14
  39.0 5.9 %shard_map.136 = (bf16[144,2048]{1,0:T(8,128)(2,1)S(1)}, f32[144,2048]{1,0:T(8,128)S(1)}, bf16[512,512]{1,0:T(8,128)(2,1)S(1)}, bf16[512,256]{1,0:T(8,128)(2,1)S(1)}) custom-call(s32[4]{0:T(128)S(1)} %pad_add_fusion.ids_ref.refs_0_, f32[1]{0:T(128)S(6)} %copy.14.refs_1_, f32[1]{0:T(128)S(6)} %copy.15.refs_2_, f32[1]{0:T(128)S(6)} %copy.16.refs_3_, ...), custom_call_target="tpu_custom_call" | custom-call | flops 2147483648 | bytes 8388608 | tf_op jit(solution)/shard_map/pallas_call | solution.py:395
  45.0 2.0 %collective-permute-done.17.b_ref = bf16[144,2048]{1,0:T(8,128)(2,1)S(1)} collective-permute-done((bf16[144,2048]{1,0:T(8,128)(2,1)S(1)}, bf16[144,2048]{1,0:T(8,128)(2,1)S(1)}, u32[]{:S(2)}, u32[]{:S(2)}) %collective-permute-start.17) | collective-permute-done | bytes 589856 | tf_op jit(solution)/shard_map/ppermute | solution.py:422
  47.1 0.6 collective-permute-start.18
  47.8 1.1 %collective-permute-start.19 = (bf16[16,2048]{1,0:T(8,128)(2,1)S(1)}, bf16[16,2048]{1,0:T(8,128)(2,1)S(1)}, u32[]{:S(2)}, u32[]{:S(2)}) collective-permute-start(bf16[16,2048]{1,0:T(8,128)(2,1)S(1)} %shard_map.139.a_ref), channel_id=1, source_target_pairs={{0,8},{1,9},{2,10},{3,11},{4,12},{5,13},{6,14},{7,15},{8,0},{9,1},... | collective-permute-start | bytes 196616 | tf_op jit(solution)/shard_map/ppermute | solution.py:422
  48.8 4.4 %shard_map.138 = (f32[2048,128]{1,0:T(8,128)}, f32[64,2048]{1,0:T(8,128)}, f32[8,128]{1,0:T(8,128)S(1)}, bf16[512,2048]{1,0:T(8,128)(2,1)S(1)}) custom-call(s32[4]{0:T(128)S(1)} %pad_add_fusion.ids_ref.refs_0_, bf16[64,2048]{1,0:T(8,128)(2,1)S(1)} %shard_map.129.refs_0_.refs_1_, bf16[64,2048]{1,0:T(8,128)(2,1)S(1)} %collective-permute-done.7.refs_3_.refs_1_.refs_2_, ...), custom_call_target="tpu_custom_call" | custom-call | flops 2147483648 | bytes 8388608 | tf_op jit(solution)/shard_map/pallas_call | solution.py:395
  53.2 0.7 collective-permute-done.19.b_ref
  53.9 1.4 %collective-permute-start.20 = (bf16[16,2048]{1,0:T(8,128)(2,1)S(1)}, bf16[16,2048]{1,0:T(8,128)(2,1)S(1)}, u32[]{:S(2)}, u32[]{:S(2)}) collective-permute-start(bf16[16,2048]{1,0:T(8,128)(2,1)S(1)} %shard_map.140.a_ref), channel_id=1, source_target_pairs={{0,4},{1,5},{2,6},{3,7},{4,0},{5,1},{6,2},{7,3},{8,12},{9,13},{10,... | collective-permute-start | bytes 196616 | tf_op jit(solution)/shard_map/ppermute | solution.py:422
  55.6 0.5 collective-permute-start.22
  56.1 2.6 %collective-permute-start.23 = (bf16[16,2048]{1,0:T(8,128)(2,1)S(1)}, bf16[16,2048]{1,0:T(8,128)(2,1)S(1)}, u32[]{:S(2)}, u32[]{:S(2)}) collective-permute-start(bf16[16,2048]{1,0:T(8,128)(2,1)S(1)} %get-tuple-element.38), channel_id=1, source_target_pairs={{0,8},{1,9},{2,10},{3,11},{4,12},{5,13},{6,14},{7,15},{8,0},{9,1},... | collective-permute-start | bytes 196616 | tf_op jit(solution)/shard_map/ppermute | solution.py:422
  58.7 1.4 %collective-permute-start.24 = (bf16[16,2048]{1,0:T(8,128)(2,1)S(1)}, bf16[16,2048]{1,0:T(8,128)(2,1)S(1)}, u32[]{:S(2)}, u32[]{:S(2)}) collective-permute-start(bf16[16,2048]{1,0:T(8,128)(2,1)S(1)} %get-tuple-element.39), channel_id=1, source_target_pairs={{0,12},{1,13},{2,14},{3,15},{4,8},{5,9},{6,10},{7,11},{8,4},{9,5},... | collective-permute-start | bytes 196616 | tf_op jit(solution)/shard_map/ppermute | solution.py:422
  60.1 1.3 %collective-permute-start.21 = (bf16[16,2048]{1,0:T(8,128)(2,1)S(1)}, bf16[16,2048]{1,0:T(8,128)(2,1)S(1)}, u32[]{:S(2)}, u32[]{:S(2)}) collective-permute-start(bf16[16,2048]{1,0:T(8,128)(2,1)S(1)} %shard_map.141.shared_ref), channel_id=1, source_target_pairs={{0,2},{1,3},{2,0},{3,1},{4,6},{5,7},{6,4},{7,5},{8,10},{9,11},{10,... | collective-permute-start | bytes 196616 | tf_op jit(solution)/shard_map/ppermute | solution.py:422
  61.4 1.8 %collective-permute-done.23.refs_1_ = bf16[16,2048]{1,0:T(8,128)(2,1)S(1)} collective-permute-done((bf16[16,2048]{1,0:T(8,128)(2,1)S(1)}, bf16[16,2048]{1,0:T(8,128)(2,1)S(1)}, u32[]{:S(2)}, u32[]{:S(2)}) %collective-permute-start.23) | collective-permute-done | bytes 65568 | tf_op jit(solution)/shard_map/ppermute | solution.py:422
  63.3 1.5 %collective-permute-done.24.refs_2_ = bf16[16,2048]{1,0:T(8,128)(2,1)S(1)} collective-permute-done((bf16[16,2048]{1,0:T(8,128)(2,1)S(1)}, bf16[16,2048]{1,0:T(8,128)(2,1)S(1)}, u32[]{:S(2)}, u32[]{:S(2)}) %collective-permute-start.24) | collective-permute-done | bytes 65568 | tf_op jit(solution)/shard_map/ppermute | solution.py:422
  64.8 1.9 %shard_map.142 = (bf16[16,2048]{1,0:T(8,128)(2,1)}, f32[32,2048]{1,0:T(8,128)}) custom-call(f32[16,2048]{1,0:T(8,128)S(1)} %get-tuple-element.32._.own_ref, bf16[512,2048]{1,0:T(8,128)(2,1)S(1)} %get-tuple-element.35.h_ref, bf16[16,2048]{1,0:T(8,128)(2,1)S(1)} %shard_map.141.shared_ref, bf16[16,2048]{1,0:T(8,128)(2,1)S(1)} %collective-permute-done.21.other_ref, ...), custom_call_target="tpu_custom_call" | custom-call | flops 268435456 | bytes 4194304 | tf_op jit(solution)/shard_map/pallas_call | solution.py:395
  (45 shorter events, 1.3 us)
Async XLA Ops:
  1.5 8.4 %collective-permute-start = (bf16[32,2048]{1,0:T(8,128)(2,1)S(1)}, bf16[32,2048]{1,0:T(8,128)(2,1)S(1)}, u32[]{:S(2)}, u32[]{:S(2)}) collective-permute-start(bf16[32,2048]{1,0:T(8,128)(2,1)S(1)} %pad_maximum_fusion.refs_0_), channel_id=1, source_target_pairs={{0,4},{1,5},{2,6},{3,7},{4,0},{5,1},{6,2},{7,3},{8,12},{9,13},{10,... | collective-permute-start | bytes 393224 | tf_op jit(solution)/shard_map/ppermute | solution.py:422
  4.6 8.8 %collective-permute-start.3 = (bf16[32,2048]{1,0:T(8,128)(2,1)S(1)}, bf16[32,2048]{1,0:T(8,128)(2,1)S(1)}, u32[]{:S(2)}, u32[]{:S(2)}) collective-permute-start(bf16[32,2048]{1,0:T(8,128)(2,1)S(1)} %pad_maximum_fusion.refs_0_), channel_id=1, source_target_pairs={{0,8},{1,9},{2,10},{3,11},{4,12},{5,13},{6,14},{7,15},{8,0},{9,1},... | collective-permute-start | bytes 393224 | tf_op jit(solution)/shard_map/ppermute | solution.py:422
  10.0 11.4 %collective-permute-start.2 = (bf16[64,2048]{1,0:T(8,128)(2,1)S(1)}, bf16[64,2048]{1,0:T(8,128)(2,1)S(1)}, u32[]{:S(2)}, u32[]{:S(2)}) collective-permute-start(bf16[64,2048]{1,0:T(8,128)(2,1)S(1)} %shard_map.129.refs_0_.refs_1_), channel_id=1, source_target_pairs={{0,2},{1,3},{2,0},{3,1},{4,6},{5,7},{6,4},{7,5},{8,10},{9,11},{10,... | collective-permute-start | bytes 786440 | tf_op jit(solution)/shard_map/ppermute | solution.py:422
  11.9 9.5 %collective-permute-start.1 = (bf16[64,2048]{1,0:T(8,128)(2,1)S(1)}, bf16[64,2048]{1,0:T(8,128)(2,1)S(1)}, u32[]{:S(2)}, u32[]{:S(2)}) collective-permute-start(bf16[64,2048]{1,0:T(8,128)(2,1)S(1)} %shard_map.129.refs_0_.refs_1_), channel_id=1, source_target_pairs={{0,16},{16,0},{1,17},{17,1},{2,18},{18,2},{3,19},{19,3},{4,20},{20... | collective-permute-start | bytes 786440 | tf_op jit(solution)/shard_map/ppermute | solution.py:425
  13.4 5.0 %collective-permute-start.4 = (bf16[32,2048]{1,0:T(8,128)(2,1)S(1)}, bf16[32,2048]{1,0:T(8,128)(2,1)S(1)}, u32[]{:S(2)}, u32[]{:S(2)}) collective-permute-start(bf16[32,2048]{1,0:T(8,128)(2,1)S(1)} %collective-permute-done.3.refs_0_), channel_id=1, source_target_pairs={{0,4},{1,5},{2,6},{3,7},{4,0},{5,1},{6,2},{7,3},{8,12},{9,13},{10,... | collective-permute-start | bytes 393224 | tf_op jit(solution)/shard_map/ppermute | solution.py:422
  13.8 8.1 %collective-permute-start.7 = (bf16[64,2048]{1,0:T(8,128)(2,1)S(1)}, bf16[64,2048]{1,0:T(8,128)(2,1)S(1)}, u32[]{:S(2)}, u32[]{:S(2)}) collective-permute-start(bf16[64,2048]{1,0:T(8,128)(2,1)S(1)} %shard_map.129.refs_0_.refs_1_), channel_id=1, source_target_pairs={{0,1},{1,0},{2,3},{3,2},{4,5},{5,4},{6,7},{7,6},{8,9},{9,8},{10,11... | collective-permute-start | bytes 786440 | tf_op jit(solution)/shard_map/ppermute | solution.py:422
  18.4 6.4 %collective-permute-start.6 = (bf16[64,2048]{1,0:T(8,128)(2,1)S(1)}, bf16[64,2048]{1,0:T(8,128)(2,1)S(1)}, u32[]{:S(2)}, u32[]{:S(2)}) collective-permute-start(bf16[64,2048]{1,0:T(8,128)(2,1)S(1)} %shard_map.130.refs_5_.refs_6_.refs_7_), channel_id=1, source_target_pairs={{0,16},{16,0},{1,17},{17,1},{2,18},{18,2},{3,19},{19,3},{4,20},{20... | collective-permute-start | bytes 786440 | tf_op jit(solution)/shard_map/ppermute | solution.py:425
  19.9 6.4 %collective-permute-start.5 = (bf16[64,2048]{1,0:T(8,128)(2,1)S(1)}, bf16[64,2048]{1,0:T(8,128)(2,1)S(1)}, u32[]{:S(2)}, u32[]{:S(2)}) collective-permute-start(bf16[64,2048]{1,0:T(8,128)(2,1)S(1)} %shard_map.130.refs_5_.refs_6_.refs_7_), channel_id=1, source_target_pairs={{0,2},{1,3},{2,0},{3,1},{4,6},{5,7},{6,4},{7,5},{8,10},{9,11},{10,... | collective-permute-start | bytes 786440 | tf_op jit(solution)/shard_map/ppermute | solution.py:422
  21.4 4.9 %collective-permute-start.8 = (bf16[64,2048]{1,0:T(8,128)(2,1)S(1)}, bf16[64,2048]{1,0:T(8,128)(2,1)S(1)}, u32[]{:S(2)}, u32[]{:S(2)}) collective-permute-start(bf16[64,2048]{1,0:T(8,128)(2,1)S(1)} %collective-permute-done.2.refs_0_.refs_2_.refs_3_), channel_id=1, source_target_pairs={{0,1},{1,0},{2,3},{3,2},{4,5},{5,4},{6,7},{7,6},{8,9},{9,8},{10,11... | collective-permute-start | bytes 786440 | tf_op jit(solution)/shard_map/ppermute | solution.py:422
  21.4 4.9 %collective-permute-start.9 = (bf16[64,2048]{1,0:T(8,128)(2,1)S(1)}, bf16[64,2048]{1,0:T(8,128)(2,1)S(1)}, u32[]{:S(2)}, u32[]{:S(2)}) collective-permute-start(bf16[64,2048]{1,0:T(8,128)(2,1)S(1)} %collective-permute-done.1.value_ref.refs_4_.refs_1_.refs_5_), channel_id=1, source_target_pairs={{0,1},{1,0},{2,3},{3,2},{4,5},{5,4},{6,7},{7,6},{8,9},{9,8},{10,11... | collective-permute-start | bytes 786440 | tf_op jit(solution)/shard_map/ppermute | solution.py:422
  21.9 8.4 %collective-permute-start.11 = (bf16[64,2048]{1,0:T(8,128)(2,1)S(1)}, bf16[64,2048]{1,0:T(8,128)(2,1)S(1)}, u32[]{:S(2)}, u32[]{:S(2)}) collective-permute-start(bf16[64,2048]{1,0:T(8,128)(2,1)S(1)} %shard_map.130.refs_5_.refs_6_.refs_7_), channel_id=1, source_target_pairs={{0,1},{1,0},{2,3},{3,2},{4,5},{5,4},{6,7},{7,6},{8,9},{9,8},{10,11... | collective-permute-start | bytes 786440 | tf_op jit(solution)/shard_map/ppermute | solution.py:422
  24.8 5.5 %collective-permute-start.13 = (bf16[64,2048]{1,0:T(8,128)(2,1)S(1)}, bf16[64,2048]{1,0:T(8,128)(2,1)S(1)}, u32[]{:S(2)}, u32[]{:S(2)}) collective-permute-start(bf16[64,2048]{1,0:T(8,128)(2,1)S(1)} %collective-permute-done.6.refs_2_.refs_10_.refs_11_), channel_id=1, source_target_pairs={{0,1},{1,0},{2,3},{3,2},{4,5},{5,4},{6,7},{7,6},{8,9},{9,8},{10,11... | collective-permute-start | bytes 786440 | tf_op jit(solution)/shard_map/ppermute | solution.py:422
  26.3 4.1 %collective-permute-start.12 = (bf16[64,2048]{1,0:T(8,128)(2,1)S(1)}, bf16[64,2048]{1,0:T(8,128)(2,1)S(1)}, u32[]{:S(2)}, u32[]{:S(2)}) collective-permute-start(bf16[64,2048]{1,0:T(8,128)(2,1)S(1)} %collective-permute-done.5.refs_1_.refs_8_.value_ref.refs_9_), channel_id=1, source_target_pairs={{0,1},{1,0},{2,3},{3,2},{4,5},{5,4},{6,7},{7,6},{8,9},{9,8},{10,11... | collective-permute-start | bytes 786440 | tf_op jit(solution)/shard_map/ppermute | solution.py:422
  26.3 2.3 %copy-start = (bf16[2048,128]{1,0:T(8,128)(2,1)S(1)}, bf16[2048,128]{1,0:T(8,128)(2,1)}, u32[]{:S(2)}) copy-start(bf16[2048,128]{1,0:T(8,128)(2,1)} %refs_0_.1) | copy-start | bytes 1572868
  26.3 2.3 %copy-start.1 = (bf16[64,2048]{1,0:T(8,128)(2,1)S(1)}, bf16[64,2048]{1,0:T(8,128)(2,1)}, u32[]{:S(2)}) copy-start(bf16[64,2048]{1,0:T(8,128)(2,1)} %refs_3_.2) | copy-start | bytes 786436
  26.3 2.3 %copy-start.2 = (bf16[2048,32]{0,1:T(8,128)(2,1)S(1)}, bf16[2048,32]{0,1:T(8,128)(2,1)}, u32[]{:S(2)}) copy-start(bf16[2048,32]{0,1:T(8,128)(2,1)} %param.12) | copy-start | bytes 393220
  26.3 2.3 %copy-start.3 = (bf16[1,2048]{1,0:T(2,128)(2,1)S(1)}, bf16[1,2048]{1,0:T(2,128)(2,1)}, u32[]{:S(2)}) copy-start(bf16[1,2048]{1,0:T(2,128)(2,1)} %refs_2_.2) | copy-start | bytes 12292
  26.3 2.3 %copy-start.4 = (f32[4,64]{1,0:T(4,128)S(1)}, f32[4,64]{1,0:T(4,128)}, u32[]{:S(2)}) copy-start(f32[4,64]{1,0:T(4,128)} %refs_4_.1) | copy-start | bytes 3076
  26.4 10.1 %collective-permute-start.10 = (bf16[64,2048]{1,0:T(8,128)(2,1)S(1)}, bf16[64,2048]{1,0:T(8,128)(2,1)S(1)}, u32[]{:S(2)}, u32[]{:S(2)}) collective-permute-start(bf16[64,2048]{1,0:T(8,128)(2,1)S(1)} %shard_map.131), channel_id=1, source_target_pairs={{0,2},{1,3},{2,0},{3,1},{4,6},{5,7},{6,4},{7,5},{8,10},{9,11},{10,... | collective-permute-start | bytes 786440 | tf_op jit(solution)/shard_map/ppermute | solution.py:422
  27.9 8.5 %collective-permute-start.15 = (bf16[64,2048]{1,0:T(8,128)(2,1)S(1)}, bf16[64,2048]{1,0:T(8,128)(2,1)S(1)}, u32[]{:S(2)}, u32[]{:S(2)}) collective-permute-start(bf16[64,2048]{1,0:T(8,128)(2,1)S(1)} %shard_map.135), channel_id=1, source_target_pairs={{0,16},{16,0},{1,17},{17,1},{2,18},{18,2},{3,19},{19,3},{4,20},{20... | collective-permute-start | bytes 786440 | tf_op jit(solution)/shard_map/ppermute | solution.py:425
  36.4 2.5 %collective-permute-start.16 = (bf16[64,2048]{1,0:T(8,128)(2,1)S(1)}, bf16[64,2048]{1,0:T(8,128)(2,1)S(1)}, u32[]{:S(2)}, u32[]{:S(2)}) collective-permute-start(bf16[64,2048]{1,0:T(8,128)(2,1)S(1)} %collective-permute-done.15.refs_6_.refs_15_), channel_id=1, source_target_pairs={{0,1},{1,0},{2,3},{3,2},{4,5},{5,4},{6,7},{7,6},{8,9},{9,8},{10,11... | collective-permute-start | bytes 786440 | tf_op jit(solution)/shard_map/ppermute | solution.py:422
  36.5 2.5 %collective-permute-start.14 = (bf16[64,2048]{1,0:T(8,128)(2,1)S(1)}, bf16[64,2048]{1,0:T(8,128)(2,1)S(1)}, u32[]{:S(2)}, u32[]{:S(2)}) collective-permute-start(bf16[64,2048]{1,0:T(8,128)(2,1)S(1)} %shard_map.134), channel_id=1, source_target_pairs={{0,1},{1,0},{2,3},{3,2},{4,5},{5,4},{6,7},{7,6},{8,9},{9,8},{10,11... | collective-permute-start | bytes 786440 | tf_op jit(solution)/shard_map/ppermute | solution.py:422
  44.9 2.1 %collective-permute-start.17 = (bf16[144,2048]{1,0:T(8,128)(2,1)S(1)}, bf16[144,2048]{1,0:T(8,128)(2,1)S(1)}, u32[]{:S(2)}, u32[]{:S(2)}) collective-permute-start(bf16[144,2048]{1,0:T(8,128)(2,1)S(1)} %get-tuple-element.31), channel_id=1, source_target_pairs={{0,1},{1,0},{2,3},{3,2},{4,5},{5,4},{6,7},{7,6},{8,9},{9,8},{10,11... | collective-permute-start | bytes 1769480 | tf_op jit(solution)/shard_map/ppermute | solution.py:422
  47.1 8.4 %collective-permute-start.18 = (bf16[64,2048]{1,0:T(8,128)(2,1)S(1)}, bf16[64,2048]{1,0:T(8,128)(2,1)S(1)}, u32[]{:S(2)}, u32[]{:S(2)}) collective-permute-start(bf16[64,2048]{1,0:T(8,128)(2,1)S(1)} %get-tuple-element.44.refs_19_._), channel_id=1, source_target_pairs={{0,2},{1,3},{2,0},{3,1},{4,6},{5,7},{6,4},{7,5},{8,10},{9,11},{10,... | collective-permute-start | bytes 786440 | tf_op jit(solution)/shard_map/ppermute | solution.py:422
  47.8 6.1 %collective-permute-start.19 = (bf16[16,2048]{1,0:T(8,128)(2,1)S(1)}, bf16[16,2048]{1,0:T(8,128)(2,1)S(1)}, u32[]{:S(2)}, u32[]{:S(2)}) collective-permute-start(bf16[16,2048]{1,0:T(8,128)(2,1)S(1)} %shard_map.139.a_ref), channel_id=1, source_target_pairs={{0,8},{1,9},{2,10},{3,11},{4,12},{5,13},{6,14},{7,15},{8,0},{9,1},... | collective-permute-start | bytes 196616 | tf_op jit(solution)/shard_map/ppermute | solution.py:422
  53.9 6.2 %collective-permute-start.20 = (bf16[16,2048]{1,0:T(8,128)(2,1)S(1)}, bf16[16,2048]{1,0:T(8,128)(2,1)S(1)}, u32[]{:S(2)}, u32[]{:S(2)}) collective-permute-start(bf16[16,2048]{1,0:T(8,128)(2,1)S(1)} %shard_map.140.a_ref), channel_id=1, source_target_pairs={{0,4},{1,5},{2,6},{3,7},{4,0},{5,1},{6,2},{7,3},{8,12},{9,13},{10,... | collective-permute-start | bytes 196616 | tf_op jit(solution)/shard_map/ppermute | solution.py:422
  55.6 5.8 %collective-permute-start.22 = (bf16[16,2048]{1,0:T(8,128)(2,1)S(1)}, bf16[16,2048]{1,0:T(8,128)(2,1)S(1)}, u32[]{:S(2)}, u32[]{:S(2)}) collective-permute-start(bf16[16,2048]{1,0:T(8,128)(2,1)S(1)} %get-tuple-element.37), channel_id=1, source_target_pairs={{0,4},{1,5},{2,6},{3,7},{4,0},{5,1},{6,2},{7,3},{8,12},{9,13},{10,... | collective-permute-start | bytes 196616 | tf_op jit(solution)/shard_map/ppermute | solution.py:422
  56.1 7.1 %collective-permute-start.23 = (bf16[16,2048]{1,0:T(8,128)(2,1)S(1)}, bf16[16,2048]{1,0:T(8,128)(2,1)S(1)}, u32[]{:S(2)}, u32[]{:S(2)}) collective-permute-start(bf16[16,2048]{1,0:T(8,128)(2,1)S(1)} %get-tuple-element.38), channel_id=1, source_target_pairs={{0,8},{1,9},{2,10},{3,11},{4,12},{5,13},{6,14},{7,15},{8,0},{9,1},... | collective-permute-start | bytes 196616 | tf_op jit(solution)/shard_map/ppermute | solution.py:422
  58.7 6.1 %collective-permute-start.24 = (bf16[16,2048]{1,0:T(8,128)(2,1)S(1)}, bf16[16,2048]{1,0:T(8,128)(2,1)S(1)}, u32[]{:S(2)}, u32[]{:S(2)}) collective-permute-start(bf16[16,2048]{1,0:T(8,128)(2,1)S(1)} %get-tuple-element.39), channel_id=1, source_target_pairs={{0,12},{1,13},{2,14},{3,15},{4,8},{5,9},{6,10},{7,11},{8,4},{9,5},... | collective-permute-start | bytes 196616 | tf_op jit(solution)/shard_map/ppermute | solution.py:422
  60.1 4.7 %collective-permute-start.21 = (bf16[16,2048]{1,0:T(8,128)(2,1)S(1)}, bf16[16,2048]{1,0:T(8,128)(2,1)S(1)}, u32[]{:S(2)}, u32[]{:S(2)}) collective-permute-start(bf16[16,2048]{1,0:T(8,128)(2,1)S(1)} %shard_map.141.shared_ref), channel_id=1, source_target_pairs={{0,2},{1,3},{2,0},{3,1},{4,6},{5,7},{6,4},{7,5},{8,10},{9,11},{10,... | collective-permute-start | bytes 196616 | tf_op jit(solution)/shard_map/ppermute | solution.py:422

commit v9 on v8

--- a/solution.py
+++ b/solution.py
@@ -473,22 +473,26 @@
             lax.pad(d_out, low, [(own_rows, 0, 0), (0, 0, 0)]),
         )
         z_near, z_far = across(own, 4), across(own, 8)
-        chunk_a = pack([own, z_near])
-        chunk_b = pack([z_far, across(z_far, 4)])
-        direct = [[part, across(part, 2), along(part)] for part in (chunk_a, chunk_b)]
-        (_, a_x, a_c), (_, b_x, b_c) = direct
-        beside_a = [across(part, 1) for part in direct[0]]
-        wall, wallt, gall, taps = prepare(chunk_b)
-        a_d = across(after(a_c, a_x, b_x, b_c, *beside_a), 2)
-        b_d = along(after(b_x, a_x, a_c, b_c, *beside_a))
-        beside = [beside_a, [across(part, 1) for part in direct[1]]]
+        own_x, own_c = across(own, 2), along(own)
+        own_d = along(own_x)
+        last = across(z_far, 4)
+        pair = pack([z_near, z_far], own_d, own_c)
+        pair_c, pair_x = along(pair), across(pair, 2)
+        last_x, last_c = across(last, 2), along(last)
+        groups = (
+            ((0,), (own, own_x, own_c, own_d)),
+            ((1, 2), (pair, pair_x, pair_c)),
+            ((3,), (last, last_x, last_c)),
+        )
         early, coords = [], []
-        blocks = ((0, 1), (2, 3))
-        for g in range(2):
-            for place, part, other in zip(((0, 0), (0, 1), (1, 0)), direct[g], beside[g]):
-                early += [part, other]
-                coords += [(*place, 0, blocks[g]), (*place, 1, blocks[g])]
-        coords += [(1, 1, core, blocks[g]) for g in range(2) for core in range(2)]
+        for blocks, parts in groups:
+            for place, part in zip(((0, 0), (0, 1), (1, 0), (1, 1)), parts):
+                early += [part, across(part, 1)]
+                coords += [(*place, core, blocks) for core in range(2)]
+        wall, wallt, gall, taps = prepare(pair)
+        pair_d = across(after(pair_c, pair_x, *early[1:8:2]), 2)
+        last_d = along(after(last_x, pair_x, pair_c, *early[1:8:2]))
+        coords += [(1, 1, core, blocks) for blocks, _ in groups[1:] for core in range(2)]
         layout = (tp_size, own_rows, tuple(coords), len(early))
         late, pieces = None, None
     else:
@@ -510,7 +514,8 @@
         vmem=vmem,
     )
     if not ordered:
-        late = [a_d, across(after(a_d, projected[0]), 1), b_d, across(b_d, 1)]
+        last_other = across(after(last_d, projected[0]), 1)
+        late = [pair_d, across(pair_d, 1), last_d, last_other]
         pieces = early + late
     extra = 4 * STATE * length // width
     half = tp_size * own_rows // 2

time: 66.9 us -> 74.8 us (1.12)
  local copies, waits for them, and re-layouts: 0.02 us -> 2.9 us
  starting transfers between devices: 24.7 us -> 27.2 us
  Pallas kernels: 15.5 us -> 17.4 us
    unnamed x10, local copies, waits for them, and re-layouts: 0.02 us -> 2.9 us
    ppermute x22 -> x27, waiting for transfers between devices: 15.1 us -> 17.7 us  [across(): lax.ppermute(value, 'tp', [(i, i ^ flip_bits) for i in range(tp_size)])]
    ppermute x22 -> x27, starting transfers between devices: 21.1 us -> 23.6 us  [across(): lax.ppermute(value, 'tp', [(i, i ^ flip_bits) for i in range(tp_size)])]
    ppermute x3 -> x5, waiting for transfers between devices: 7.5 us -> 5.45 us  [along(): return lax.ppermute(value, 'ctx', [(0, 1), (1, 0)])]
    pallas_call x14 -> x13, Pallas kernels: 15.5 us -> 17.4 us  [call(): pl.pallas_call(kernel, out_shape=outs, in_specs=[spec(pltpu.SMEM)] * n_sm...]
    ppermute x3 -> x5, starting transfers between devices: 3.62 us -> 3.58 us  [along(): return lax.ppermute(value, 'ctx', [(0, 1), (1, 0)])]
  transfers between devices with their start and end apart: 25 -> 32, of which waited for: 10 -> 8; matrix products, arithmetic and copies ran while one was open for 0% -> 0% of each run, Pallas kernels for 12% -> 12%
where the time goes in v9:
time: 74.8 us; the launch traced here: 74.4 us
  starting transfers between devices  27.2 us (36%)
  waiting for transfers between devices  23.1 us (31%)
  Pallas kernels  17.4 us (23%)
  local copies, waits for them, and re-layouts  2.9 us (4%)
  between operations  2.76 us (4%)
  other arithmetic  1.1 us (1%)
    ppermute x27, starting transfers between devices, across(): lax.ppermute(value, 'tp', [(i, i ^ flip_bits) for i in range(tp_size)])  23.6 us
    ppermute x27, waiting for transfers between devices, across(): lax.ppermute(value, 'tp', [(i, i ^ flip_bits) for i in range(tp_size)])  17.7 us
    pallas_call x13, Pallas kernels, call(): pl.pallas_call(kernel, out_shape=outs, in_specs=[spec(pltpu.SMEM)] * n_sm...  17.4 us
    ppermute x5, waiting for transfers between devices, along(): return lax.ppermute(value, 'ctx', [(0, 1), (1, 0)])  5.45 us
    ppermute x5, starting transfers between devices, along(): return lax.ppermute(value, 'ctx', [(0, 1), (1, 0)])  3.58 us
    unnamed x10, local copies, waits for them, and re-layouts  2.9 us
  transfers between devices with their start and end apart: 32, of which 8 were waited for; matrix products, arithmetic and copies ran while one was open for 0% of the time, Pallas kernels for 12%

profile of v9, /device:TPU:0, one launch (start us, length us, event | category | flops | bytes accessed | tf_op | source)
XLA Modules:
  0.0 74.4 jit_solution(516907727699311174)
XLA Ops:
  0.7 0.9 %pad_maximum_fusion.refs_0_.refs_1_ = bf16[32,2048]{1,0:T(8,128)(2,1)S(1)} fusion(bf16[16,2048]{1,0:T(8,128)(2,1)} %param.19, bf16[16,2048]{1,0:T(8,128)(2,1)} %param.10), kind=kLoop, calls=%fused_computation.2 | loop fusion | flops 262144 | bytes 262144 | tf_op jit(solution)/shard_map/max | solution.py:471
  1.5 3.0 %collective-permute-start.2 = (bf16[32,2048]{1,0:T(8,128)(2,1)S(1)}, bf16[32,2048]{1,0:T(8,128)(2,1)S(1)}, u32[]{:S(2)}, u32[]{:S(2)}) collective-permute-start(bf16[32,2048]{1,0:T(8,128)(2,1)S(1)} %pad_maximum_fusion.refs_0_.refs_1_), channel_id=1, source_target_pairs={{0,2},{1,3},{2,0},{3,1},{4,6},{5,7},{6,4},{7,5},{8,10},{9,11},{10,... | collective-permute-start | bytes 393224 | tf_op jit(solution)/shard_map/ppermute | solution.py:422
  4.6 1.5 %collective-permute-start.4 = (bf16[32,2048]{1,0:T(8,128)(2,1)S(1)}, bf16[32,2048]{1,0:T(8,128)(2,1)S(1)}, u32[]{:S(2)}, u32[]{:S(2)}) collective-permute-start(bf16[32,2048]{1,0:T(8,128)(2,1)S(1)} %pad_maximum_fusion.refs_0_.refs_1_), channel_id=1, source_target_pairs={{0,16},{16,0},{1,17},{17,1},{2,18},{18,2},{3,19},{19,3},{4,20},{20... | collective-permute-start | bytes 393224 | tf_op jit(solution)/shard_map/ppermute | solution.py:425
  6.1 2.6 %collective-permute-start.1 = (bf16[32,2048]{1,0:T(8,128)(2,1)S(1)}, bf16[32,2048]{1,0:T(8,128)(2,1)S(1)}, u32[]{:S(2)}, u32[]{:S(2)}) collective-permute-start(bf16[32,2048]{1,0:T(8,128)(2,1)S(1)} %pad_maximum_fusion.refs_0_.refs_1_), channel_id=1, source_target_pairs={{0,8},{1,9},{2,10},{3,11},{4,12},{5,13},{6,14},{7,15},{8,0},{9,1},... | collective-permute-start | bytes 393224 | tf_op jit(solution)/shard_map/ppermute | solution.py:422
  8.7 1.6 %collective-permute-start = (bf16[32,2048]{1,0:T(8,128)(2,1)S(1)}, bf16[32,2048]{1,0:T(8,128)(2,1)S(1)}, u32[]{:S(2)}, u32[]{:S(2)}) collective-permute-start(bf16[32,2048]{1,0:T(8,128)(2,1)S(1)} %pad_maximum_fusion.refs_0_.refs_1_), channel_id=1, source_target_pairs={{0,4},{1,5},{2,6},{3,7},{4,0},{5,1},{6,2},{7,3},{8,12},{9,13},{10,... | collective-permute-start | bytes 393224 | tf_op jit(solution)/shard_map/ppermute | solution.py:422
  11.3 3.2 %collective-permute-done.1.refs_1_ = bf16[32,2048]{1,0:T(8,128)(2,1)S(1)} collective-permute-done((bf16[32,2048]{1,0:T(8,128)(2,1)S(1)}, bf16[32,2048]{1,0:T(8,128)(2,1)S(1)}, u32[]{:S(2)}, u32[]{:S(2)}) %collective-permute-start.1) | collective-permute-done | bytes 131104 | tf_op jit(solution)/shard_map/ppermute | solution.py:422
  14.5 0.6 collective-permute-start.13
  15.2 0.6 collective-permute-start.6
  15.8 0.5 collective-permute-start.5
  16.9 2.6 %collective-permute-done.13.refs_14_.refs_15_ = bf16[32,2048]{1,0:T(8,128)(2,1)S(1)} collective-permute-done((bf16[32,2048]{1,0:T(8,128)(2,1)S(1)}, bf16[32,2048]{1,0:T(8,128)(2,1)S(1)}, u32[]{:S(2)}, u32[]{:S(2)}) %collective-permute-start.13) | collective-permute-done | bytes 131104 | tf_op jit(solution)/shard_map/ppermute | solution.py:422
  20.0 0.5 collective-permute-start.14
  20.5 5.4 %collective-permute-done.21.refs_18_.refs_19_ = bf16[32,2048]{1,0:T(8,128)(2,1)S(1)} collective-permute-done((bf16[32,2048]{1,0:T(8,128)(2,1)S(1)}, bf16[32,2048]{1,0:T(8,128)(2,1)S(1)}, u32[]{:S(2)}, u32[]{:S(2)}) %collective-permute-start.21) | collective-permute-done | bytes 131104 | tf_op jit(solution)/shard_map/ppermute | solution.py:425
  25.9 1.6 %collective-permute-start.11 = (bf16[64,2048]{1,0:T(8,128)(2,1)S(1)}, bf16[64,2048]{1,0:T(8,128)(2,1)}, u32[]{:S(2)}, u32[]{:S(2)}) collective-permute-start(bf16[64,2048]{1,0:T(8,128)(2,1)S(1)} %shard_map.130), channel_id=1, source_target_pairs={{0,2},{1,3},{2,0},{3,1},{4,6},{5,7},{6,4},{7,5},{8,10},{9,11},{10,... | collective-permute-start | bytes 786440 | tf_op jit(solution)/shard_map/ppermute | solution.py:422
  28.6 1.3 %collective-permute-done.20.refs_17_.refs_18_ = bf16[32,2048]{1,0:T(8,128)(2,1)} collective-permute-done((bf16[32,2048]{1,0:T(8,128)(2,1)S(1)}, bf16[32,2048]{1,0:T(8,128)(2,1)}, u32[]{:S(2)}, u32[]{:S(2)}) %collective-permute-start.20) | collective-permute-done | bytes 131104 | tf_op jit(solution)/shard_map/ppermute | solution.py:422
  29.9 0.5 collective-permute-start.15
  30.5 4.4 %collective-permute-done.11.refs_4_.refs_21_ = bf16[64,2048]{1,0:T(8,128)(2,1)} collective-permute-done((bf16[64,2048]{1,0:T(8,128)(2,1)S(1)}, bf16[64,2048]{1,0:T(8,128)(2,1)}, u32[]{:S(2)}, u32[]{:S(2)}) %collective-permute-start.11) | collective-permute-done | bytes 262176 | tf_op jit(solution)/shard_map/ppermute | solution.py:422
  34.8 1.0 %copy-done = bf16[2048,128]{1,0:T(8,128)(2,1)S(1)} copy-done((bf16[2048,128]{1,0:T(8,128)(2,1)S(1)}, bf16[2048,128]{1,0:T(8,128)(2,1)}, u32[]{:S(2)}) %copy-start) | copy-done | bytes 524312
  35.9 0.9 %copy-done.1 = bf16[64,2048]{1,0:T(8,128)(2,1)S(1)} copy-done((bf16[64,2048]{1,0:T(8,128)(2,1)S(1)}, bf16[64,2048]{1,0:T(8,128)(2,1)}, u32[]{:S(2)}) %copy-start.1) | copy-done | bytes 262168
  36.8 0.9 %copy-done.2 = bf16[2048,32]{0,1:T(8,128)(2,1)S(1)} copy-done((bf16[2048,32]{0,1:T(8,128)(2,1)S(1)}, bf16[2048,32]{0,1:T(8,128)(2,1)}, u32[]{:S(2)}) %copy-start.2) | copy-done | bytes 131096
  37.7 1.7 %shard_map.132 = (bf16[2048,512]{1,0:T(8,128)(2,1)S(1)}, bf16[512,2048]{1,0:T(8,128)(2,1)S(1)}, bf16[2048,256]{1,0:T(8,128)(2,1)S(1)}, f32[4,128]{1,0:T(4,128)S(1)}) custom-call(s32[4]{0:T(128)S(1)} %pad_add_fusion.ids_ref.refs_0_, bf16[2048,128]{1,0:T(8,128)(2,1)S(1)} %copy-done, bf16[32,2048]{1,0:T(8,128)(2,1)S(1)} %bitcast.6, ...), custom_call_target="tpu_custom_call" | custom-call | flops 805306368 | bytes 5242880 | tf_op jit(solution)/shard_map/pallas_call | solution.py:395
  39.4 2.4 %shard_map.133 = (f32[416,512]{1,0:T(8,128)S(1)}, f32[416,256]{1,0:T(8,128)S(1)}) custom-call(bf16[32,2048]{1,0:T(8,128)(2,1)S(1)} %pad_maximum_fusion.refs_0_.refs_1_, bf16[32,2048]{1,0:T(8,128)(2,1)S(1)} %collective-permute-done.7.refs_1_.refs_2_, bf16[32,2048]{1,0:T(8,128)(2,1)S(1)} %collective-permute-done.2.refs_2_.refs_3_, ...), custom_call_target="tpu_custom_call" | custom-call | flops 1308622848 | bytes 3407872 | tf_op jit(solution)/shard_map/pallas_call | solution.py:395
  41.9 0.6 collective-permute-start.23
  44.4 6.4 %shard_map.135 = (bf16[144,2048]{1,0:T(8,128)(2,1)S(1)}, f32[144,2048]{1,0:T(8,128)S(1)}, bf16[512,512]{1,0:T(8,128)(2,1)S(1)}, bf16[512,256]{1,0:T(8,128)(2,1)S(1)}) custom-call(s32[4]{0:T(128)S(1)} %pad_add_fusion.ids_ref.refs_0_, f32[1]{0:T(128)S(6)} %copy.14.refs_1_, f32[1]{0:T(128)S(6)} %copy.15.refs_2_, f32[1]{0:T(128)S(6)} %copy.16.refs_3_, ...), custom_call_target="tpu_custom_call" | custom-call | flops 2147483648 | bytes 8388608 | tf_op jit(solution)/shard_map/pallas_call | solution.py:395
  50.9 2.0 %collective-permute-done.24.b_ref = bf16[144,2048]{1,0:T(8,128)(2,1)S(1)} collective-permute-done((bf16[144,2048]{1,0:T(8,128)(2,1)S(1)}, bf16[144,2048]{1,0:T(8,128)(2,1)S(1)}, u32[]{:S(2)}, u32[]{:S(2)}) %collective-permute-start.24) | collective-permute-done | bytes 589856 | tf_op jit(solution)/shard_map/ppermute | solution.py:422
  53.0 1.6 %collective-permute-start.25 = (bf16[64,2048]{1,0:T(8,128)(2,1)S(1)}, bf16[64,2048]{1,0:T(8,128)(2,1)S(1)}, u32[]{:S(2)}, u32[]{:S(2)}) collective-permute-start(bf16[64,2048]{1,0:T(8,128)(2,1)S(1)} %get-tuple-element.44.refs_27_._), channel_id=1, source_target_pairs={{0,2},{1,3},{2,0},{3,1},{4,6},{5,7},{6,4},{7,5},{8,10},{9,11},{10,... | collective-permute-start | bytes 786440 | tf_op jit(solution)/shard_map/ppermute | solution.py:422
  54.6 3.4 %collective-permute-start.26 = (bf16[16,2048]{1,0:T(8,128)(2,1)S(1)}, bf16[16,2048]{1,0:T(8,128)(2,1)S(1)}, u32[]{:S(2)}, u32[]{:S(2)}) collective-permute-start(bf16[16,2048]{1,0:T(8,128)(2,1)S(1)} %shard_map.138.a_ref), channel_id=1, source_target_pairs={{0,8},{1,9},{2,10},{3,11},{4,12},{5,13},{6,14},{7,15},{8,0},{9,1},... | collective-permute-start | bytes 196616 | tf_op jit(solution)/shard_map/ppermute | solution.py:422
  58.0 4.8 %shard_map.137 = (f32[2048,128]{1,0:T(8,128)}, f32[64,2048]{1,0:T(8,128)}, f32[8,128]{1,0:T(8,128)S(1)}, bf16[512,2048]{1,0:T(8,128)(2,1)S(1)}) custom-call(s32[4]{0:T(128)S(1)} %pad_add_fusion.ids_ref.refs_0_, bf16[32,2048]{1,0:T(8,128)(2,1)S(1)} %pad_maximum_fusion.refs_0_.refs_1_, bf16[32,2048]{1,0:T(8,128)(2,1)S(1)} %collective-permute-done.7.refs_1_.refs_2_, ...), custom_call_target="tpu_custom_call" | custom-call | flops 2147483648 | bytes 8388608 | tf_op jit(solution)/shard_map/pallas_call | solution.py:395
  63.3 1.8 %collective-permute-start.29 = (bf16[16,2048]{1,0:T(8,128)(2,1)S(1)}, bf16[16,2048]{1,0:T(8,128)(2,1)S(1)}, u32[]{:S(2)}, u32[]{:S(2)}) collective-permute-start(bf16[16,2048]{1,0:T(8,128)(2,1)S(1)} %get-tuple-element.37), channel_id=1, source_target_pairs={{0,4},{1,5},{2,6},{3,7},{4,0},{5,1},{6,2},{7,3},{8,12},{9,13},{10,... | collective-permute-start | bytes 196616 | tf_op jit(solution)/shard_map/ppermute | solution.py:422
  65.4 2.3 %collective-permute-start.31 = (bf16[16,2048]{1,0:T(8,128)(2,1)S(1)}, bf16[16,2048]{1,0:T(8,128)(2,1)S(1)}, u32[]{:S(2)}, u32[]{:S(2)}) collective-permute-start(bf16[16,2048]{1,0:T(8,128)(2,1)S(1)} %get-tuple-element.39), channel_id=1, source_target_pairs={{0,12},{1,13},{2,14},{3,15},{4,8},{5,9},{6,10},{7,11},{8,4},{9,5},... | collective-permute-start | bytes 196616 | tf_op jit(solution)/shard_map/ppermute | solution.py:422
  67.8 0.6 collective-permute-start.28
  68.4 4.1 %collective-permute-done.30.refs_1_ = bf16[16,2048]{1,0:T(8,128)(2,1)S(1)} collective-permute-done((bf16[16,2048]{1,0:T(8,128)(2,1)S(1)}, bf16[16,2048]{1,0:T(8,128)(2,1)S(1)}, u32[]{:S(2)}, u32[]{:S(2)}) %collective-permute-start.30) | collective-permute-done | bytes 65568 | tf_op jit(solution)/shard_map/ppermute | solution.py:422
  72.6 1.9 %shard_map.141 = (bf16[16,2048]{1,0:T(8,128)(2,1)}, f32[32,2048]{1,0:T(8,128)}) custom-call(f32[16,2048]{1,0:T(8,128)S(1)} %get-tuple-element.32._.own_ref, bf16[512,2048]{1,0:T(8,128)(2,1)S(1)} %get-tuple-element.35.h_ref, bf16[16,2048]{1,0:T(8,128)(2,1)S(1)} %shard_map.140.shared_ref, bf16[16,2048]{1,0:T(8,128)(2,1)S(1)} %collective-permute-done.28.other_ref, ...), custom_call_target="tpu_custom_call" | custom-call | flops 268435456 | bytes 4194304 | tf_op jit(solution)/shard_map/pallas_call | solution.py:395
  (58 shorter events, 4.3 us)
Async XLA Ops:
  1.5 8.7 %collective-permute-start.2 = (bf16[32,2048]{1,0:T(8,128)(2,1)S(1)}, bf16[32,2048]{1,0:T(8,128)(2,1)S(1)}, u32[]{:S(2)}, u32[]{:S(2)}) collective-permute-start(bf16[32,2048]{1,0:T(8,128)(2,1)S(1)} %pad_maximum_fusion.refs_0_.refs_1_), channel_id=1, source_target_pairs={{0,2},{1,3},{2,0},{3,1},{4,6},{5,7},{6,4},{7,5},{8,10},{9,11},{10,... | collective-permute-start | bytes 393224 | tf_op jit(solution)/shard_map/ppermute | solution.py:422
  4.6 6.2 %collective-permute-start.4 = (bf16[32,2048]{1,0:T(8,128)(2,1)S(1)}, bf16[32,2048]{1,0:T(8,128)(2,1)S(1)}, u32[]{:S(2)}, u32[]{:S(2)}) collective-permute-start(bf16[32,2048]{1,0:T(8,128)(2,1)S(1)} %pad_maximum_fusion.refs_0_.refs_1_), channel_id=1, source_target_pairs={{0,16},{16,0},{1,17},{17,1},{2,18},{18,2},{3,19},{19,3},{4,20},{20... | collective-permute-start | bytes 393224 | tf_op jit(solution)/shard_map/ppermute | solution.py:425
  6.1 8.4 %collective-permute-start.1 = (bf16[32,2048]{1,0:T(8,128)(2,1)S(1)}, bf16[32,2048]{1,0:T(8,128)(2,1)S(1)}, u32[]{:S(2)}, u32[]{:S(2)}) collective-permute-start(bf16[32,2048]{1,0:T(8,128)(2,1)S(1)} %pad_maximum_fusion.refs_0_.refs_1_), channel_id=1, source_target_pairs={{0,8},{1,9},{2,10},{3,11},{4,12},{5,13},{6,14},{7,15},{8,0},{9,1},... | collective-permute-start | bytes 393224 | tf_op jit(solution)/shard_map/ppermute | solution.py:422
  8.7 6.5 %collective-permute-start = (bf16[32,2048]{1,0:T(8,128)(2,1)S(1)}, bf16[32,2048]{1,0:T(8,128)(2,1)S(1)}, u32[]{:S(2)}, u32[]{:S(2)}) collective-permute-start(bf16[32,2048]{1,0:T(8,128)(2,1)S(1)} %pad_maximum_fusion.refs_0_.refs_1_), channel_id=1, source_target_pairs={{0,4},{1,5},{2,6},{3,7},{4,0},{5,1},{6,2},{7,3},{8,12},{9,13},{10,... | collective-permute-start | bytes 393224 | tf_op jit(solution)/shard_map/ppermute | solution.py:422
  10.2 5.0 %collective-permute-start.3 = (bf16[32,2048]{1,0:T(8,128)(2,1)S(1)}, bf16[32,2048]{1,0:T(8,128)(2,1)S(1)}, u32[]{:S(2)}, u32[]{:S(2)}) collective-permute-start(bf16[32,2048]{1,0:T(8,128)(2,1)S(1)} %collective-permute-done.2.refs_2_.refs_3_), channel_id=1, source_target_pairs={{0,16},{16,0},{1,17},{17,1},{2,18},{18,2},{3,19},{19,3},{4,20},{20... | collective-permute-start | bytes 393224 | tf_op jit(solution)/shard_map/ppermute | solution.py:425
  10.7 5.6 %collective-permute-start.7 = (bf16[32,2048]{1,0:T(8,128)(2,1)S(1)}, bf16[32,2048]{1,0:T(8,128)(2,1)S(1)}, u32[]{:S(2)}, u32[]{:S(2)}) collective-permute-start(bf16[32,2048]{1,0:T(8,128)(2,1)S(1)} %pad_maximum_fusion.refs_0_.refs_1_), channel_id=1, source_target_pairs={{0,1},{1,0},{2,3},{3,2},{4,5},{5,4},{6,7},{7,6},{8,9},{9,8},{10,11... | collective-permute-start | bytes 393224 | tf_op jit(solution)/shard_map/ppermute | solution.py:422
  10.8 5.6 %collective-permute-start.9 = (bf16[32,2048]{1,0:T(8,128)(2,1)S(1)}, bf16[32,2048]{1,0:T(8,128)(2,1)S(1)}, u32[]{:S(2)}, u32[]{:S(2)}) collective-permute-start(bf16[32,2048]{1,0:T(8,128)(2,1)S(1)} %collective-permute-done.4.refs_3_.refs_4_.refs_5_), channel_id=1, source_target_pairs={{0,1},{1,0},{2,3},{3,2},{4,5},{5,4},{6,7},{7,6},{8,9},{9,8},{10,11... | collective-permute-start | bytes 393224 | tf_op jit(solution)/shard_map/ppermute | solution.py:422
  14.5 5.0 %collective-permute-start.13 = (bf16[32,2048]{1,0:T(8,128)(2,1)S(1)}, bf16[32,2048]{1,0:T(8,128)(2,1)S(1)}, u32[]{:S(2)}, u32[]{:S(2)}) collective-permute-start(bf16[32,2048]{1,0:T(8,128)(2,1)S(1)} %collective-permute-done.1.refs_1_), channel_id=1, source_target_pairs={{0,4},{1,5},{2,6},{3,7},{4,0},{5,1},{6,2},{7,3},{8,12},{9,13},{10,... | collective-permute-start | bytes 393224 | tf_op jit(solution)/shard_map/ppermute | solution.py:422
  15.2 10.7 %collective-permute-start.6 = (bf16[64,2048]{1,0:T(8,128)(2,1)S(1)}, bf16[64,2048]{1,0:T(8,128)(2,1)S(1)}, u32[]{:S(2)}, u32[]{:S(2)}) collective-permute-start(bf16[64,2048]{1,0:T(8,128)(2,1)S(1)} %shard_map.129.refs_5_.refs_8_.refs_9_), channel_id=1, source_target_pairs={{0,2},{1,3},{2,0},{3,1},{4,6},{5,7},{6,4},{7,5},{8,10},{9,11},{10,... | collective-permute-start | bytes 786440 | tf_op jit(solution)/shard_map/ppermute | solution.py:422
  15.8 10.1 %collective-permute-start.5 = (bf16[64,2048]{1,0:T(8,128)(2,1)S(1)}, bf16[64,2048]{1,0:T(8,128)(2,1)S(1)}, u32[]{:S(2)}, u32[]{:S(2)}) collective-permute-start(bf16[64,2048]{1,0:T(8,128)(2,1)S(1)} %shard_map.129.refs_5_.refs_8_.refs_9_), channel_id=1, source_target_pairs={{0,16},{16,0},{1,17},{17,1},{2,18},{18,2},{3,19},{19,3},{4,20},{20... | collective-permute-start | bytes 786440 | tf_op jit(solution)/shard_map/ppermute | solution.py:425
  16.4 3.6 %collective-permute-start.8 = (bf16[32,2048]{1,0:T(8,128)(2,1)S(1)}, bf16[32,2048]{1,0:T(8,128)(2,1)S(1)}, u32[]{:S(2)}, u32[]{:S(2)}) collective-permute-start(bf16[32,2048]{1,0:T(8,128)(2,1)S(1)} %collective-permute-done.2.refs_2_.refs_3_), channel_id=1, source_target_pairs={{0,1},{1,0},{2,3},{3,2},{4,5},{5,4},{6,7},{7,6},{8,9},{9,8},{10,11... | collective-permute-start | bytes 393224 | tf_op jit(solution)/shard_map/ppermute | solution.py:422
  16.4 3.6 %collective-permute-start.10 = (bf16[32,2048]{1,0:T(8,128)(2,1)S(1)}, bf16[32,2048]{1,0:T(8,128)(2,1)S(1)}, u32[]{:S(2)}, u32[]{:S(2)}) collective-permute-start(bf16[32,2048]{1,0:T(8,128)(2,1)S(1)} %collective-permute-done.3.refs_2_.refs_6_.refs_7_), channel_id=1, source_target_pairs={{0,1},{1,0},{2,3},{3,2},{4,5},{5,4},{6,7},{7,6},{8,9},{9,8},{10,11... | collective-permute-start | bytes 393224 | tf_op jit(solution)/shard_map/ppermute | solution.py:422
  19.5 6.4 %collective-permute-start.21 = (bf16[32,2048]{1,0:T(8,128)(2,1)S(1)}, bf16[32,2048]{1,0:T(8,128)(2,1)S(1)}, u32[]{:S(2)}, u32[]{:S(2)}) collective-permute-start(bf16[32,2048]{1,0:T(8,128)(2,1)S(1)} %collective-permute-done.13.refs_14_.refs_15_), channel_id=1, source_target_pairs={{0,16},{16,0},{1,17},{17,1},{2,18},{18,2},{3,19},{19,3},{4,20},{20... | collective-permute-start | bytes 393224 | tf_op jit(solution)/shard_map/ppermute | solution.py:425
  20.0 7.7 %collective-permute-start.19 = (bf16[32,2048]{1,0:T(8,128)(2,1)S(1)}, bf16[32,2048]{1,0:T(8,128)(2,1)S(1)}, u32[]{:S(2)}, u32[]{:S(2)}) collective-permute-start(bf16[32,2048]{1,0:T(8,128)(2,1)S(1)} %collective-permute-done.13.refs_14_.refs_15_), channel_id=1, source_target_pairs={{0,1},{1,0},{2,3},{3,2},{4,5},{5,4},{6,7},{7,6},{8,9},{9,8},{10,11... | collective-permute-start | bytes 393224 | tf_op jit(solution)/shard_map/ppermute | solution.py:422
  20.0 8.0 %collective-permute-start.14 = (bf16[32,2048]{1,0:T(8,128)(2,1)S(1)}, bf16[32,2048]{1,0:T(8,128)(2,1)S(1)}, u32[]{:S(2)}, u32[]{:S(2)}) collective-permute-start(bf16[32,2048]{1,0:T(8,128)(2,1)S(1)} %collective-permute-done.13.refs_14_.refs_15_), channel_id=1, source_target_pairs={{0,2},{1,3},{2,0},{3,1},{4,6},{5,7},{6,4},{7,5},{8,10},{9,11},{10,... | collective-permute-start | bytes 393224 | tf_op jit(solution)/shard_map/ppermute | solution.py:422
  25.9 2.3 %collective-permute-start.22 = (bf16[32,2048]{1,0:T(8,128)(2,1)S(1)}, bf16[32,2048]{1,0:T(8,128)(2,1)S(1)}, u32[]{:S(2)}, u32[]{:S(2)}) collective-permute-start(bf16[32,2048]{1,0:T(8,128)(2,1)S(1)} %collective-permute-done.21.refs_18_.refs_19_), channel_id=1, source_target_pairs={{0,1},{1,0},{2,3},{3,2},{4,5},{5,4},{6,7},{7,6},{8,9},{9,8},{10,11... | collective-permute-start | bytes 393224 | tf_op jit(solution)/shard_map/ppermute | solution.py:422
  25.9 8.9 %collective-permute-start.11 = (bf16[64,2048]{1,0:T(8,128)(2,1)S(1)}, bf16[64,2048]{1,0:T(8,128)(2,1)}, u32[]{:S(2)}, u32[]{:S(2)}) collective-permute-start(bf16[64,2048]{1,0:T(8,128)(2,1)S(1)} %shard_map.130), channel_id=1, source_target_pairs={{0,2},{1,3},{2,0},{3,1},{4,6},{5,7},{6,4},{7,5},{8,10},{9,11},{10,... | collective-permute-start | bytes 786440 | tf_op jit(solution)/shard_map/ppermute | solution.py:422
  27.5 11.9 %collective-permute-start.16 = (bf16[64,2048]{1,0:T(8,128)(2,1)S(1)}, bf16[64,2048]{1,0:T(8,128)(2,1)S(1)}, u32[]{:S(2)}, u32[]{:S(2)}) collective-permute-start(bf16[64,2048]{1,0:T(8,128)(2,1)S(1)} %shard_map.129.refs_5_.refs_8_.refs_9_), channel_id=1, source_target_pairs={{0,1},{1,0},{2,3},{3,2},{4,5},{5,4},{6,7},{7,6},{8,9},{9,8},{10,11... | collective-permute-start | bytes 786440 | tf_op jit(solution)/shard_map/ppermute | solution.py:422
  27.7 11.7 %collective-permute-start.17 = (bf16[64,2048]{1,0:T(8,128)(2,1)S(1)}, bf16[64,2048]{1,0:T(8,128)(2,1)S(1)}, u32[]{:S(2)}, u32[]{:S(2)}) collective-permute-start(bf16[64,2048]{1,0:T(8,128)(2,1)S(1)} %collective-permute-done.6.refs_0_.refs_10_.refs_11_), channel_id=1, source_target_pairs={{0,1},{1,0},{2,3},{3,2},{4,5},{5,4},{6,7},{7,6},{8,9},{9,8},{10,11... | collective-permute-start | bytes 786440 | tf_op jit(solution)/shard_map/ppermute | solution.py:422
  28.0 11.4 %collective-permute-start.18 = (bf16[64,2048]{1,0:T(8,128)(2,1)S(1)}, bf16[64,2048]{1,0:T(8,128)(2,1)S(1)}, u32[]{:S(2)}, u32[]{:S(2)}) collective-permute-start(bf16[64,2048]{1,0:T(8,128)(2,1)S(1)} %collective-permute-done.5.value_ref.refs_1_.refs_12_.refs_13_), channel_id=1, source_target_pairs={{0,1},{1,0},{2,3},{3,2},{4,5},{5,4},{6,7},{7,6},{8,9},{9,8},{10,11... | collective-permute-start | bytes 786440 | tf_op jit(solution)/shard_map/ppermute | solution.py:422
  28.2 1.7 %collective-permute-start.20 = (bf16[32,2048]{1,0:T(8,128)(2,1)S(1)}, bf16[32,2048]{1,0:T(8,128)(2,1)}, u32[]{:S(2)}, u32[]{:S(2)}) collective-permute-start(bf16[32,2048]{1,0:T(8,128)(2,1)S(1)} %collective-permute-done.14.value_ref.refs_16_.refs_17_), channel_id=1, source_target_pairs={{0,1},{1,0},{2,3},{3,2},{4,5},{5,4},{6,7},{7,6},{8,9},{9,8},{10,11... | collective-permute-start | bytes 393224 | tf_op jit(solution)/shard_map/ppermute | solution.py:422
  29.9 11.9 %collective-permute-start.15 = (bf16[32,2048]{1,0:T(8,128)(2,1)S(1)}, bf16[32,2048]{1,0:T(8,128)(2,1)S(1)}, u32[]{:S(2)}, u32[]{:S(2)}) collective-permute-start(bf16[32,2048]{1,0:T(8,128)(2,1)S(1)} %shard_map.131), channel_id=1, source_target_pairs={{0,16},{16,0},{1,17},{17,1},{2,18},{18,2},{3,19},{19,3},{4,20},{20... | collective-permute-start | bytes 393224 | tf_op jit(solution)/shard_map/ppermute | solution.py:425
  34.8 9.6 %collective-permute-start.12 = (bf16[64,2048]{1,0:T(8,128)(2,1)}, bf16[64,2048]{1,0:T(8,128)(2,1)S(1)}, u32[]{:S(2)}, u32[]{:S(2)}) collective-permute-start(bf16[64,2048]{1,0:T(8,128)(2,1)} %collective-permute-done.11.refs_4_.refs_21_), channel_id=1, source_target_pairs={{0,1},{1,0},{2,3},{3,2},{4,5},{5,4},{6,7},{7,6},{8,9},{9,8},{10,11... | collective-permute-start | bytes 786440 | tf_op jit(solution)/shard_map/ppermute | solution.py:422
  41.9 2.5 %collective-permute-start.23 = (bf16[32,2048]{1,0:T(8,128)(2,1)S(1)}, bf16[32,2048]{1,0:T(8,128)(2,1)S(1)}, u32[]{:S(2)}, u32[]{:S(2)}) collective-permute-start(bf16[32,2048]{1,0:T(8,128)(2,1)S(1)} %shard_map.134), channel_id=1, source_target_pairs={{0,1},{1,0},{2,3},{3,2},{4,5},{5,4},{6,7},{7,6},{8,9},{9,8},{10,11... | collective-permute-start | bytes 393224 | tf_op jit(solution)/shard_map/ppermute | solution.py:422
  50.8 2.1 %collective-permute-start.24 = (bf16[144,2048]{1,0:T(8,128)(2,1)S(1)}, bf16[144,2048]{1,0:T(8,128)(2,1)S(1)}, u32[]{:S(2)}, u32[]{:S(2)}) collective-permute-start(bf16[144,2048]{1,0:T(8,128)(2,1)S(1)} %get-tuple-element.31), channel_id=1, source_target_pairs={{0,1},{1,0},{2,3},{3,2},{4,5},{5,4},{6,7},{7,6},{8,9},{9,8},{10,11... | collective-permute-start | bytes 1769480 | tf_op jit(solution)/shard_map/ppermute | solution.py:422
  53.0 10.3 %collective-permute-start.25 = (bf16[64,2048]{1,0:T(8,128)(2,1)S(1)}, bf16[64,2048]{1,0:T(8,128)(2,1)S(1)}, u32[]{:S(2)}, u32[]{:S(2)}) collective-permute-start(bf16[64,2048]{1,0:T(8,128)(2,1)S(1)} %get-tuple-element.44.refs_27_._), channel_id=1, source_target_pairs={{0,2},{1,3},{2,0},{3,1},{4,6},{5,7},{6,4},{7,5},{8,10},{9,11},{10,... | collective-permute-start | bytes 786440 | tf_op jit(solution)/shard_map/ppermute | solution.py:422
  54.6 8.3 %collective-permute-start.26 = (bf16[16,2048]{1,0:T(8,128)(2,1)S(1)}, bf16[16,2048]{1,0:T(8,128)(2,1)S(1)}, u32[]{:S(2)}, u32[]{:S(2)}) collective-permute-start(bf16[16,2048]{1,0:T(8,128)(2,1)S(1)} %shard_map.138.a_ref), channel_id=1, source_target_pairs={{0,8},{1,9},{2,10},{3,11},{4,12},{5,13},{6,14},{7,15},{8,0},{9,1},... | collective-permute-start | bytes 196616 | tf_op jit(solution)/shard_map/ppermute | solution.py:422
  62.9 4.9 %collective-permute-start.27 = (bf16[16,2048]{1,0:T(8,128)(2,1)S(1)}, bf16[16,2048]{1,0:T(8,128)(2,1)S(1)}, u32[]{:S(2)}, u32[]{:S(2)}) collective-permute-start(bf16[16,2048]{1,0:T(8,128)(2,1)S(1)} %shard_map.139.a_ref), channel_id=1, source_target_pairs={{0,4},{1,5},{2,6},{3,7},{4,0},{5,1},{6,2},{7,3},{8,12},{9,13},{10,... | collective-permute-start | bytes 196616 | tf_op jit(solution)/shard_map/ppermute | solution.py:422
  63.3 5.1 %collective-permute-start.29 = (bf16[16,2048]{1,0:T(8,128)(2,1)S(1)}, bf16[16,2048]{1,0:T(8,128)(2,1)S(1)}, u32[]{:S(2)}, u32[]{:S(2)}) collective-permute-start(bf16[16,2048]{1,0:T(8,128)(2,1)S(1)} %get-tuple-element.37), channel_id=1, source_target_pairs={{0,4},{1,5},{2,6},{3,7},{4,0},{5,1},{6,2},{7,3},{8,12},{9,13},{10,... | collective-permute-start | bytes 196616 | tf_op jit(solution)/shard_map/ppermute | solution.py:422
  65.1 7.4 %collective-permute-start.30 = (bf16[16,2048]{1,0:T(8,128)(2,1)S(1)}, bf16[16,2048]{1,0:T(8,128)(2,1)S(1)}, u32[]{:S(2)}, u32[]{:S(2)}) collective-permute-start(bf16[16,2048]{1,0:T(8,128)(2,1)S(1)} %get-tuple-element.38), channel_id=1, source_target_pairs={{0,8},{1,9},{2,10},{3,11},{4,12},{5,13},{6,14},{7,15},{8,0},{9,1},... | collective-permute-start | bytes 196616 | tf_op jit(solution)/shard_map/ppermute | solution.py:422
  65.4 7.1 %collective-permute-start.31 = (bf16[16,2048]{1,0:T(8,128)(2,1)S(1)}, bf16[16,2048]{1,0:T(8,128)(2,1)S(1)}, u32[]{:S(2)}, u32[]{:S(2)}) collective-permute-start(bf16[16,2048]{1,0:T(8,128)(2,1)S(1)} %get-tuple-element.39), channel_id=1, source_target_pairs={{0,12},{1,13},{2,14},{3,15},{4,8},{5,9},{6,10},{7,11},{8,4},{9,5},... | collective-permute-start | bytes 196616 | tf_op jit(solution)/shard_map/ppermute | solution.py:422
  67.8 4.7 %collective-permute-start.28 = (bf16[16,2048]{1,0:T(8,128)(2,1)S(1)}, bf16[16,2048]{1,0:T(8,128)(2,1)S(1)}, u32[]{:S(2)}, u32[]{:S(2)}) collective-permute-start(bf16[16,2048]{1,0:T(8,128)(2,1)S(1)} %shard_map.140.shared_ref), channel_id=1, source_target_pairs={{0,2},{1,3},{2,0},{3,1},{4,6},{5,7},{6,4},{7,5},{8,10},{9,11},{10,... | collective-permute-start | bytes 196616 | tf_op jit(solution)/shard_map/ppermute | solution.py:422
  (5 other events, 71.3 us)

commit v10 on v8

--- a/solution.py
+++ b/solution.py
@@ -203,16 +203,16 @@
     row_at = iota((length, LANES), 0)
 
     turned = [proj[:, 2 * LANES : 3 * LANES].astype(bf16)]
-    turned += split(proj[:, 3 * LANES :], 3) + split(grads[:, LANES:], 2)
+    turned += split(proj[:, 3 * LANES :], 2) + split(grads[:, LANES:], 2)
     turned = flip_rows(jnp.concatenate(turned, axis=1), flip)
-    turned = [turned[:, i * LANES : (i + 1) * LANES] for i in range(6)]
+    turned = [turned[:, i * LANES : (i + 1) * LANES] for i in range(5)]
     strands = (
         (
             proj[:, :LANES].astype(bf16).astype(f32),
             proj[:, LANES : 2 * LANES],
             grads[:, :LANES],
         ),
-        (turned[0], turned[1] + turned[2] + turned[3], turned[4] + turned[5]),
+        (turned[0], turned[1] + turned[2], turned[3] + turned[4]),
     )
 
     def gates(xz, rest, grad_g):
@@ -234,8 +234,8 @@
     def enter_chunk(c, gate, state):
         rows = slice(c * BLOCK, (c + 1) * BLOCK)
         dt, b_all, c_all, w_all = gate[3][rows], gate[5][rows], gate[6][rows], gate[7][rows]
-        log_keep = dot(tri, jnp.concatenate(split(dt * rate, 3), axis=1))
-        log_keep = log_keep[:, :LANES] + log_keep[:, LANES : 2 * LANES] + log_keep[:, 2 * LANES :]
+        log_keep = dot(tri, jnp.concatenate(split(dt * rate, 2), axis=1))
+        log_keep = log_keep[:, :LANES] + log_keep[:, LANES:]
         across = jnp.transpose(log_keep)[0:1, :]
         gap = jnp.concatenate([log_keep] * (BLOCK // LANES), axis=1) - across
         decay = jnp.exp(jnp.where(causal, gap, -jnp.inf))
@@ -367,15 +367,18 @@
         ref[...] = value.astype(ref.dtype)
 
 
-def last_kernel(scaling, own_ref, h_ref, shared_ref, other_ref, *refs):
-    got_refs, (dhid_ref, dwbct_ref) = refs[:-2], refs[-2:]
+def sum_kernel(own_ref, *refs):
+    total = own_ref[...]
+    for got in refs[:-2]:
+        total += got[...].astype(f32)
+    refs[-1][...] = total.astype(bf16)
+
+
+def shared_kernel(scaling, h_ref, shared_ref, other_ref, dwbct_ref, mark_ref):
+    mark_ref[...] = jnp.zeros_like(mark_ref)
     flip = mirror(BLOCK)
     length, width = h_ref.shape
     groups = width // length
-    total = own_ref[...]
-    for got in got_refs:
-        total += got[...].astype(f32)
-    dhid_ref[...] = total.astype(bf16)
     shared = (shared_ref[...].astype(f32) + other_ref[...].astype(f32)).astype(bf16)
     shared = jnp.concatenate(
         [shared[:, i * length : (i + 1) * length] for i in range(groups)], axis=0
@@ -383,7 +386,7 @@
     fwd = shared[: 2 * STATE]
     rev = turn_columns(shared[2 * STATE :], flip).astype(bf16)
     pairs = dot(jnp.concatenate([fwd, rev], axis=0), h_ref[...])
-    turned = exact(split(pairs[2 * STATE :], 3), lambda part: turn_columns(part, flip))
+    turned = exact(split(pairs[2 * STATE :], 2), lambda part: turn_columns(part, flip))
     dwbct_ref[...] = (pairs[: 2 * STATE] + turned) * scaling
 
 
@@ -577,20 +580,30 @@
         4 * quarter * width,
         10 * quarter * width,
     )
+    got = [across(piece, 4 * (j + 1)) for j, piece in enumerate(send)]
     shared = add_shared(own_given, given, sent)
     step = nz // 2
     while step:
-        shared = add_shared(shared, across(shared, 4 * step), mark if step > 1 else own)
+        shared = add_shared(shared, across(shared, 4 * step), mark if step > 1 else got[0])
         step //= 2
-    got = [across(piece, 4 * (j + 1)) for j, piece in enumerate(send)]
-    d_hidden, d_w_bc = call(
-        functools.partial(last_kernel, scaling),
-        [own, in_order, shared, across(shared, 2), *got],
+    d_w_bc, mark = call(
+        functools.partial(shared_kernel, scaling),
+        [in_order, shared, across(shared, 2)],
         0,
-        (shape((own_rows, width), bf16), shape((2 * STATE, width), f32)),
+        (shape((2 * STATE, width), f32), shape((8, LANES), f32)),
         [],
         2 * length * width * LANES,
         4 * length * width,
+    )
+    d_hidden = call(
+        sum_kernel,
+        [own, *got, mark],
+        0,
+        shape((own_rows, width), bf16),
+        [],
+        4 * own_rows * width,
+        12 * own_rows * width,
+        1,
     )
     return (d_hidden, d_w_in, d_w_out, d_w_bc.T)
 

time: 66.9 us -> 69.4 us (1.037)
  waiting for transfers between devices: 22.6 us -> 25.7 us
  starting transfers between devices: 24.7 us -> 23.8 us
    ppermute x22, waiting for transfers between devices: 15.1 us -> 18.2 us  [across(): lax.ppermute(value, 'tp', [(i, i ^ flip_bits) for i in range(tp_size)])]
    ppermute x22, starting transfers between devices: 21.1 us -> 20.2 us  [across(): lax.ppermute(value, 'tp', [(i, i ^ flip_bits) for i in range(tp_size)])]
    pallas_call x14 -> x15, Pallas kernels: 15.5 us -> 15.9 us  [call(): pl.pallas_call(kernel, out_shape=outs, in_specs=[spec(pltpu.SMEM)] * n_sm...]
  transfers between devices with their start and end apart: 25 -> 25, of which waited for: 10 -> 12; matrix products, arithmetic and copies ran while one was open for 0% -> 0% of each run, Pallas kernels for 12% -> 14%
where the time goes in v10:
time: 69.4 us; the launch traced here: 69.2 us
  waiting for transfers between devices  25.7 us (37%)
  starting transfers between devices  23.8 us (34%)
  Pallas kernels  15.9 us (23%)
  between operations  2.76 us (4%)
  other arithmetic  1.09 us (2%)
    ppermute x22, starting transfers between devices, across(): lax.ppermute(value, 'tp', [(i, i ^ flip_bits) for i in range(tp_size)])  20.2 us
    ppermute x22, waiting for transfers between devices, across(): lax.ppermute(value, 'tp', [(i, i ^ flip_bits) for i in range(tp_size)])  18.2 us
    pallas_call x15, Pallas kernels, call(): pl.pallas_call(kernel, out_shape=outs, in_specs=[spec(pltpu.SMEM)] * n_sm...  15.9 us
    ppermute x3, waiting for transfers between devices, along(): return lax.ppermute(value, 'ctx', [(0, 1), (1, 0)])  7.5 us
    ppermute x3, starting transfers between devices, along(): return lax.ppermute(value, 'ctx', [(0, 1), (1, 0)])  3.62 us
  transfers between devices with their start and end apart: 25, of which 12 were waited for; matrix products, arithmetic and copies ran while one was open for 0% of the time, Pallas kernels for 14%

profile of v10, /device:TPU:0, one launch (start us, length us, event | category | flops | bytes accessed | tf_op | source)
XLA Modules:
  0.0 69.2 jit_solution(4750546138426260843)
XLA Ops:
  0.6 0.9 %pad_maximum_fusion.refs_0_ = bf16[32,2048]{1,0:T(8,128)(2,1)S(1)} fusion(bf16[16,2048]{1,0:T(8,128)(2,1)} %param.19, bf16[16,2048]{1,0:T(8,128)(2,1)} %param.10), kind=kLoop, calls=%fused_computation.2 | loop fusion | flops 262144 | bytes 262144 | tf_op jit(solution)/shard_map/max | solution.py:474
  1.5 3.1 %collective-permute-start = (bf16[32,2048]{1,0:T(8,128)(2,1)S(1)}, bf16[32,2048]{1,0:T(8,128)(2,1)S(1)}, u32[]{:S(2)}, u32[]{:S(2)}) collective-permute-start(bf16[32,2048]{1,0:T(8,128)(2,1)S(1)} %pad_maximum_fusion.refs_0_), channel_id=1, source_target_pairs={{0,4},{1,5},{2,6},{3,7},{4,0},{5,1},{6,2},{7,3},{8,12},{9,13},{10,... | collective-permute-start | bytes 393224 | tf_op jit(solution)/shard_map/ppermute | solution.py:425
  4.6 2.6 %collective-permute-start.3 = (bf16[32,2048]{1,0:T(8,128)(2,1)S(1)}, bf16[32,2048]{1,0:T(8,128)(2,1)S(1)}, u32[]{:S(2)}, u32[]{:S(2)}) collective-permute-start(bf16[32,2048]{1,0:T(8,128)(2,1)S(1)} %pad_maximum_fusion.refs_0_), channel_id=1, source_target_pairs={{0,8},{1,9},{2,10},{3,11},{4,12},{5,13},{6,14},{7,15},{8,0},{9,1},... | collective-permute-start | bytes 393224 | tf_op jit(solution)/shard_map/ppermute | solution.py:425
  7.2 2.8 %collective-permute-done.refs_1_ = bf16[32,2048]{1,0:T(8,128)(2,1)S(1)} collective-permute-done((bf16[32,2048]{1,0:T(8,128)(2,1)S(1)}, bf16[32,2048]{1,0:T(8,128)(2,1)S(1)}, u32[]{:S(2)}, u32[]{:S(2)}) %collective-permute-start) | collective-permute-done | bytes 131104 | tf_op jit(solution)/shard_map/ppermute | solution.py:425
  10.0 1.9 %collective-permute-start.2 = (bf16[64,2048]{1,0:T(8,128)(2,1)S(1)}, bf16[64,2048]{1,0:T(8,128)(2,1)S(1)}, u32[]{:S(2)}, u32[]{:S(2)}) collective-permute-start(bf16[64,2048]{1,0:T(8,128)(2,1)S(1)} %shard_map.129.refs_0_.refs_1_), channel_id=1, source_target_pairs={{0,2},{1,3},{2,0},{3,1},{4,6},{5,7},{6,4},{7,5},{8,10},{9,11},{10,... | collective-permute-start | bytes 786440 | tf_op jit(solution)/shard_map/ppermute | solution.py:425
  11.9 1.5 %collective-permute-start.1 = (bf16[64,2048]{1,0:T(8,128)(2,1)S(1)}, bf16[64,2048]{1,0:T(8,128)(2,1)S(1)}, u32[]{:S(2)}, u32[]{:S(2)}) collective-permute-start(bf16[64,2048]{1,0:T(8,128)(2,1)S(1)} %shard_map.129.refs_0_.refs_1_), channel_id=1, source_target_pairs={{0,16},{16,0},{1,17},{17,1},{2,18},{18,2},{3,19},{19,3},{4,20},{20... | collective-permute-start | bytes 786440 | tf_op jit(solution)/shard_map/ppermute | solution.py:428
  13.8 4.6 %collective-permute-done.4.refs_1_ = bf16[32,2048]{1,0:T(8,128)(2,1)S(1)} collective-permute-done((bf16[32,2048]{1,0:T(8,128)(2,1)S(1)}, bf16[32,2048]{1,0:T(8,128)(2,1)S(1)}, u32[]{:S(2)}, u32[]{:S(2)}) %collective-permute-start.4) | collective-permute-done | bytes 131104 | tf_op jit(solution)/shard_map/ppermute | solution.py:425
  18.4 1.5 %collective-permute-start.6 = (bf16[64,2048]{1,0:T(8,128)(2,1)S(1)}, bf16[64,2048]{1,0:T(8,128)(2,1)S(1)}, u32[]{:S(2)}, u32[]{:S(2)}) collective-permute-start(bf16[64,2048]{1,0:T(8,128)(2,1)S(1)} %shard_map.130.refs_5_.refs_6_.refs_7_), channel_id=1, source_target_pairs={{0,16},{16,0},{1,17},{17,1},{2,18},{18,2},{3,19},{19,3},{4,20},{20... | collective-permute-start | bytes 786440 | tf_op jit(solution)/shard_map/ppermute | solution.py:428
  19.9 1.5 %collective-permute-start.5 = (bf16[64,2048]{1,0:T(8,128)(2,1)S(1)}, bf16[64,2048]{1,0:T(8,128)(2,1)S(1)}, u32[]{:S(2)}, u32[]{:S(2)}) collective-permute-start(bf16[64,2048]{1,0:T(8,128)(2,1)S(1)} %shard_map.130.refs_5_.refs_6_.refs_7_), channel_id=1, source_target_pairs={{0,2},{1,3},{2,0},{3,1},{4,6},{5,7},{6,4},{7,5},{8,10},{9,11},{10,... | collective-permute-start | bytes 786440 | tf_op jit(solution)/shard_map/ppermute | solution.py:425
  22.0 2.8 %collective-permute-done.6.refs_2_.refs_10_.refs_11_ = bf16[64,2048]{1,0:T(8,128)(2,1)S(1)} collective-permute-done((bf16[64,2048]{1,0:T(8,128)(2,1)S(1)}, bf16[64,2048]{1,0:T(8,128)(2,1)S(1)}, u32[]{:S(2)}, u32[]{:S(2)}) %collective-permute-start.6) | collective-permute-done | bytes 262176 | tf_op jit(solution)/shard_map/ppermute | solution.py:428
  24.8 1.5 %collective-permute-done.5.refs_1_.refs_8_.value_ref.refs_9_ = bf16[64,2048]{1,0:T(8,128)(2,1)S(1)} collective-permute-done((bf16[64,2048]{1,0:T(8,128)(2,1)S(1)}, bf16[64,2048]{1,0:T(8,128)(2,1)S(1)}, u32[]{:S(2)}, u32[]{:S(2)}) %collective-permute-start.5) | collective-permute-done | bytes 262176 | tf_op jit(solution)/shard_map/ppermute | solution.py:425
  26.4 1.6 %collective-permute-start.10 = (bf16[64,2048]{1,0:T(8,128)(2,1)S(1)}, bf16[64,2048]{1,0:T(8,128)(2,1)S(1)}, u32[]{:S(2)}, u32[]{:S(2)}) collective-permute-start(bf16[64,2048]{1,0:T(8,128)(2,1)S(1)} %shard_map.131), channel_id=1, source_target_pairs={{0,2},{1,3},{2,0},{3,1},{4,6},{5,7},{6,4},{7,5},{8,10},{9,11},{10,... | collective-permute-start | bytes 786440 | tf_op jit(solution)/shard_map/ppermute | solution.py:425
  27.9 0.6 collective-permute-start.15
  28.6 1.7 %shard_map.132 = (bf16[2048,512]{1,0:T(8,128)(2,1)S(1)}, bf16[512,2048]{1,0:T(8,128)(2,1)S(1)}, bf16[2048,256]{1,0:T(8,128)(2,1)S(1)}, f32[4,128]{1,0:T(4,128)S(1)}) custom-call(s32[4]{0:T(128)S(1)} %pad_add_fusion.ids_ref.refs_0_, bf16[2048,128]{1,0:T(8,128)(2,1)S(1)} %copy-done, bf16[32,2048]{1,0:T(8,128)(2,1)S(1)} %bitcast.6, ...), custom_call_target="tpu_custom_call" | custom-call | flops 805306368 | bytes 5242880 | tf_op jit(solution)/shard_map/pallas_call | solution.py:398
  30.3 1.4 %shard_map.133 = (f32[384,512]{1,0:T(8,128)S(1)}, f32[384,256]{1,0:T(8,128)S(1)}) custom-call(bf16[64,2048]{1,0:T(8,128)(2,1)S(1)} %shard_map.129.refs_0_.refs_1_, bf16[64,2048]{1,0:T(8,128)(2,1)S(1)} %collective-permute-done.7.refs_3_.refs_1_.refs_2_, bf16[64,2048]{1,0:T(8,128)(2,1)S(1)} %collective-permute-done.2.refs_0_.refs_2_.refs_3_, ...), custom_call_target="tpu_custom_call" | custom-call | flops 1207959552 | bytes 3145728 | tf_op jit(solution)/shard_map/pallas_call | solution.py:398
  31.8 4.7 %collective-permute-done.15.refs_6_.refs_15_ = bf16[64,2048]{1,0:T(8,128)(2,1)S(1)} collective-permute-done((bf16[64,2048]{1,0:T(8,128)(2,1)S(1)}, bf16[64,2048]{1,0:T(8,128)(2,1)S(1)}, u32[]{:S(2)}, u32[]{:S(2)}) %collective-permute-start.15) | collective-permute-done | bytes 262176 | tf_op jit(solution)/shard_map/ppermute | solution.py:428
  39.0 5.8 %shard_map.136 = (bf16[144,2048]{1,0:T(8,128)(2,1)S(1)}, f32[144,2048]{1,0:T(8,128)S(1)}, bf16[512,512]{1,0:T(8,128)(2,1)S(1)}, bf16[512,256]{1,0:T(8,128)(2,1)S(1)}) custom-call(s32[4]{0:T(128)S(1)} %pad_add_fusion.ids_ref.refs_0_, f32[1]{0:T(128)S(6)} %copy.14.refs_1_, f32[1]{0:T(128)S(6)} %copy.15.refs_2_, f32[1]{0:T(128)S(6)} %copy.16.refs_3_, ...), custom_call_target="tpu_custom_call" | custom-call | flops 2147483648 | bytes 8388608 | tf_op jit(solution)/shard_map/pallas_call | solution.py:398
  44.9 2.0 %collective-permute-done.17.b_ref = bf16[144,2048]{1,0:T(8,128)(2,1)S(1)} collective-permute-done((bf16[144,2048]{1,0:T(8,128)(2,1)S(1)}, bf16[144,2048]{1,0:T(8,128)(2,1)S(1)}, u32[]{:S(2)}, u32[]{:S(2)}) %collective-permute-start.17) | collective-permute-done | bytes 589856 | tf_op jit(solution)/shard_map/ppermute | solution.py:425
  47.0 0.6 collective-permute-start.18
  47.7 1.1 %collective-permute-start.22 = (bf16[16,2048]{1,0:T(8,128)(2,1)S(1)}, bf16[16,2048]{1,0:T(8,128)(2,1)S(1)}, u32[]{:S(2)}, u32[]{:S(2)}) collective-permute-start(bf16[16,2048]{1,0:T(8,128)(2,1)S(1)} %shard_map.139.a_ref), channel_id=1, source_target_pairs={{0,8},{1,9},{2,10},{3,11},{4,12},{5,13},{6,14},{7,15},{8,0},{9,1},... | collective-permute-start | bytes 196616 | tf_op jit(solution)/shard_map/ppermute | solution.py:425
  48.7 4.4 %shard_map.138 = (f32[2048,128]{1,0:T(8,128)}, f32[64,2048]{1,0:T(8,128)}, f32[8,128]{1,0:T(8,128)S(1)}, bf16[512,2048]{1,0:T(8,128)(2,1)S(1)}) custom-call(s32[4]{0:T(128)S(1)} %pad_add_fusion.ids_ref.refs_0_, bf16[64,2048]{1,0:T(8,128)(2,1)S(1)} %shard_map.129.refs_0_.refs_1_, bf16[64,2048]{1,0:T(8,128)(2,1)S(1)} %collective-permute-done.7.refs_3_.refs_1_.refs_2_, ...), custom_call_target="tpu_custom_call" | custom-call | flops 2147483648 | bytes 8388608 | tf_op jit(solution)/shard_map/pallas_call | solution.py:398
  53.1 0.7 collective-permute-done.22.b_ref
  53.8 1.4 %collective-permute-start.23 = (bf16[16,2048]{1,0:T(8,128)(2,1)S(1)}, bf16[16,2048]{1,0:T(8,128)(2,1)S(1)}, u32[]{:S(2)}, u32[]{:S(2)}) collective-permute-start(bf16[16,2048]{1,0:T(8,128)(2,1)S(1)} %shard_map.140.a_ref), channel_id=1, source_target_pairs={{0,4},{1,5},{2,6},{3,7},{4,0},{5,1},{6,2},{7,3},{8,12},{9,13},{10,... | collective-permute-start | bytes 196616 | tf_op jit(solution)/shard_map/ppermute | solution.py:425
  56.0 2.7 %collective-permute-done.23.b_ref = bf16[16,2048]{1,0:T(8,128)(2,1)S(1)} collective-permute-done((bf16[16,2048]{1,0:T(8,128)(2,1)S(1)}, bf16[16,2048]{1,0:T(8,128)(2,1)S(1)}, u32[]{:S(2)}, u32[]{:S(2)}) %collective-permute-start.23) | collective-permute-done | bytes 65568 | tf_op jit(solution)/shard_map/ppermute | solution.py:425
  58.7 1.1 %collective-permute-done.19._.refs_0_ = bf16[16,2048]{1,0:T(8,128)(2,1)S(1)} collective-permute-done((bf16[16,2048]{1,0:T(8,128)(2,1)S(1)}, bf16[16,2048]{1,0:T(8,128)(2,1)S(1)}, u32[]{:S(2)}, u32[]{:S(2)}) %collective-permute-start.19) | collective-permute-done | bytes 65568 | tf_op jit(solution)/shard_map/ppermute | solution.py:425
  59.9 1.3 %collective-permute-start.24 = (bf16[16,2048]{1,0:T(8,128)(2,1)S(1)}, bf16[16,2048]{1,0:T(8,128)(2,1)S(1)}, u32[]{:S(2)}, u32[]{:S(2)}) collective-permute-start(bf16[16,2048]{1,0:T(8,128)(2,1)S(1)} %shard_map.141.shared_ref), channel_id=1, source_target_pairs={{0,2},{1,3},{2,0},{3,1},{4,6},{5,7},{6,4},{7,5},{8,10},{9,11},{10,... | collective-permute-start | bytes 196616 | tf_op jit(solution)/shard_map/ppermute | solution.py:425
  61.2 1.2 %collective-permute-start.20 = (bf16[16,2048]{1,0:T(8,128)(2,1)S(1)}, bf16[16,2048]{1,0:T(8,128)(2,1)S(1)}, u32[]{:S(2)}, u32[]{:S(2)}) collective-permute-start(bf16[16,2048]{1,0:T(8,128)(2,1)S(1)} %get-tuple-element.34), channel_id=1, source_target_pairs={{0,8},{1,9},{2,10},{3,11},{4,12},{5,13},{6,14},{7,15},{8,0},{9,1},... | collective-permute-start | bytes 196616 | tf_op jit(solution)/shard_map/ppermute | solution.py:425
  62.4 1.8 %collective-permute-start.21 = (bf16[16,2048]{1,0:T(8,128)(2,1)S(1)}, bf16[16,2048]{1,0:T(8,128)(2,1)S(1)}, u32[]{:S(2)}, u32[]{:S(2)}) collective-permute-start(bf16[16,2048]{1,0:T(8,128)(2,1)S(1)} %get-tuple-element.35), channel_id=1, source_target_pairs={{0,12},{1,13},{2,14},{3,15},{4,8},{5,9},{6,10},{7,11},{8,4},{9,5},... | collective-permute-start | bytes 196616 | tf_op jit(solution)/shard_map/ppermute | solution.py:425
  64.2 1.7 %shard_map.142 = (f32[32,2048]{1,0:T(8,128)}, f32[8,128]{1,0:T(8,128)S(1)}) custom-call(bf16[512,2048]{1,0:T(8,128)(2,1)S(1)} %get-tuple-element.38.h_ref, bf16[16,2048]{1,0:T(8,128)(2,1)S(1)} %shard_map.141.shared_ref, bf16[16,2048]{1,0:T(8,128)(2,1)S(1)} %collective-permute-done.24.other_ref), custom_call_target="tpu_custom_call" | custom-call | flops 268435456 | bytes 4194304 | tf_op jit(solution)/shard_map/pallas_call | solution.py:398
  65.9 1.6 %collective-permute-done.20.refs_1_ = bf16[16,2048]{1,0:T(8,128)(2,1)S(1)} collective-permute-done((bf16[16,2048]{1,0:T(8,128)(2,1)S(1)}, bf16[16,2048]{1,0:T(8,128)(2,1)S(1)}, u32[]{:S(2)}, u32[]{:S(2)}) %collective-permute-start.20) | collective-permute-done | bytes 65568 | tf_op jit(solution)/shard_map/ppermute | solution.py:425
  67.5 1.1 %collective-permute-done.21.refs_2_ = bf16[16,2048]{1,0:T(8,128)(2,1)S(1)} collective-permute-done((bf16[16,2048]{1,0:T(8,128)(2,1)S(1)}, bf16[16,2048]{1,0:T(8,128)(2,1)S(1)}, u32[]{:S(2)}, u32[]{:S(2)}) %collective-permute-start.21) | collective-permute-done | bytes 65568 | tf_op jit(solution)/shard_map/ppermute | solution.py:425
  68.6 0.7 shard_map.143
  (46 shorter events, 2.8 us)
Async XLA Ops:
  1.5 8.4 %collective-permute-start = (bf16[32,2048]{1,0:T(8,128)(2,1)S(1)}, bf16[32,2048]{1,0:T(8,128)(2,1)S(1)}, u32[]{:S(2)}, u32[]{:S(2)}) collective-permute-start(bf16[32,2048]{1,0:T(8,128)(2,1)S(1)} %pad_maximum_fusion.refs_0_), channel_id=1, source_target_pairs={{0,4},{1,5},{2,6},{3,7},{4,0},{5,1},{6,2},{7,3},{8,12},{9,13},{10,... | collective-permute-start | bytes 393224 | tf_op jit(solution)/shard_map/ppermute | solution.py:425
  4.6 8.8 %collective-permute-start.3 = (bf16[32,2048]{1,0:T(8,128)(2,1)S(1)}, bf16[32,2048]{1,0:T(8,128)(2,1)S(1)}, u32[]{:S(2)}, u32[]{:S(2)}) collective-permute-start(bf16[32,2048]{1,0:T(8,128)(2,1)S(1)} %pad_maximum_fusion.refs_0_), channel_id=1, source_target_pairs={{0,8},{1,9},{2,10},{3,11},{4,12},{5,13},{6,14},{7,15},{8,0},{9,1},... | collective-permute-start | bytes 393224 | tf_op jit(solution)/shard_map/ppermute | solution.py:425
  10.0 11.4 %collective-permute-start.2 = (bf16[64,2048]{1,0:T(8,128)(2,1)S(1)}, bf16[64,2048]{1,0:T(8,128)(2,1)S(1)}, u32[]{:S(2)}, u32[]{:S(2)}) collective-permute-start(bf16[64,2048]{1,0:T(8,128)(2,1)S(1)} %shard_map.129.refs_0_.refs_1_), channel_id=1, source_target_pairs={{0,2},{1,3},{2,0},{3,1},{4,6},{5,7},{6,4},{7,5},{8,10},{9,11},{10,... | collective-permute-start | bytes 786440 | tf_op jit(solution)/shard_map/ppermute | solution.py:425
  11.9 9.5 %collective-permute-start.1 = (bf16[64,2048]{1,0:T(8,128)(2,1)S(1)}, bf16[64,2048]{1,0:T(8,128)(2,1)S(1)}, u32[]{:S(2)}, u32[]{:S(2)}) collective-permute-start(bf16[64,2048]{1,0:T(8,128)(2,1)S(1)} %shard_map.129.refs_0_.refs_1_), channel_id=1, source_target_pairs={{0,16},{16,0},{1,17},{17,1},{2,18},{18,2},{3,19},{19,3},{4,20},{20... | collective-permute-start | bytes 786440 | tf_op jit(solution)/shard_map/ppermute | solution.py:428
  13.4 5.0 %collective-permute-start.4 = (bf16[32,2048]{1,0:T(8,128)(2,1)S(1)}, bf16[32,2048]{1,0:T(8,128)(2,1)S(1)}, u32[]{:S(2)}, u32[]{:S(2)}) collective-permute-start(bf16[32,2048]{1,0:T(8,128)(2,1)S(1)} %collective-permute-done.3.refs_0_), channel_id=1, source_target_pairs={{0,4},{1,5},{2,6},{3,7},{4,0},{5,1},{6,2},{7,3},{8,12},{9,13},{10,... | collective-permute-start | bytes 393224 | tf_op jit(solution)/shard_map/ppermute | solution.py:425
  13.8 8.1 %collective-permute-start.7 = (bf16[64,2048]{1,0:T(8,128)(2,1)S(1)}, bf16[64,2048]{1,0:T(8,128)(2,1)S(1)}, u32[]{:S(2)}, u32[]{:S(2)}) collective-permute-start(bf16[64,2048]{1,0:T(8,128)(2,1)S(1)} %shard_map.129.refs_0_.refs_1_), channel_id=1, source_target_pairs={{0,1},{1,0},{2,3},{3,2},{4,5},{5,4},{6,7},{7,6},{8,9},{9,8},{10,11... | collective-permute-start | bytes 786440 | tf_op jit(solution)/shard_map/ppermute | solution.py:425
  18.4 6.4 %collective-permute-start.6 = (bf16[64,2048]{1,0:T(8,128)(2,1)S(1)}, bf16[64,2048]{1,0:T(8,128)(2,1)S(1)}, u32[]{:S(2)}, u32[]{:S(2)}) collective-permute-start(bf16[64,2048]{1,0:T(8,128)(2,1)S(1)} %shard_map.130.refs_5_.refs_6_.refs_7_), channel_id=1, source_target_pairs={{0,16},{16,0},{1,17},{17,1},{2,18},{18,2},{3,19},{19,3},{4,20},{20... | collective-permute-start | bytes 786440 | tf_op jit(solution)/shard_map/ppermute | solution.py:428
  19.9 6.4 %collective-permute-start.5 = (bf16[64,2048]{1,0:T(8,128)(2,1)S(1)}, bf16[64,2048]{1,0:T(8,128)(2,1)S(1)}, u32[]{:S(2)}, u32[]{:S(2)}) collective-permute-start(bf16[64,2048]{1,0:T(8,128)(2,1)S(1)} %shard_map.130.refs_5_.refs_6_.refs_7_), channel_id=1, source_target_pairs={{0,2},{1,3},{2,0},{3,1},{4,6},{5,7},{6,4},{7,5},{8,10},{9,11},{10,... | collective-permute-start | bytes 786440 | tf_op jit(solution)/shard_map/ppermute | solution.py:425
  21.4 4.9 %collective-permute-start.8 = (bf16[64,2048]{1,0:T(8,128)(2,1)S(1)}, bf16[64,2048]{1,0:T(8,128)(2,1)S(1)}, u32[]{:S(2)}, u32[]{:S(2)}) collective-permute-start(bf16[64,2048]{1,0:T(8,128)(2,1)S(1)} %collective-permute-done.2.refs_0_.refs_2_.refs_3_), channel_id=1, source_target_pairs={{0,1},{1,0},{2,3},{3,2},{4,5},{5,4},{6,7},{7,6},{8,9},{9,8},{10,11... | collective-permute-start | bytes 786440 | tf_op jit(solution)/shard_map/ppermute | solution.py:425
  21.4 4.9 %collective-permute-start.9 = (bf16[64,2048]{1,0:T(8,128)(2,1)S(1)}, bf16[64,2048]{1,0:T(8,128)(2,1)S(1)}, u32[]{:S(2)}, u32[]{:S(2)}) collective-permute-start(bf16[64,2048]{1,0:T(8,128)(2,1)S(1)} %collective-permute-done.1.value_ref.refs_4_.refs_1_.refs_5_), channel_id=1, source_target_pairs={{0,1},{1,0},{2,3},{3,2},{4,5},{5,4},{6,7},{7,6},{8,9},{9,8},{10,11... | collective-permute-start | bytes 786440 | tf_op jit(solution)/shard_map/ppermute | solution.py:425
  21.9 8.4 %collective-permute-start.11 = (bf16[64,2048]{1,0:T(8,128)(2,1)S(1)}, bf16[64,2048]{1,0:T(8,128)(2,1)S(1)}, u32[]{:S(2)}, u32[]{:S(2)}) collective-permute-start(bf16[64,2048]{1,0:T(8,128)(2,1)S(1)} %shard_map.130.refs_5_.refs_6_.refs_7_), channel_id=1, source_target_pairs={{0,1},{1,0},{2,3},{3,2},{4,5},{5,4},{6,7},{7,6},{8,9},{9,8},{10,11... | collective-permute-start | bytes 786440 | tf_op jit(solution)/shard_map/ppermute | solution.py:425
  24.8 5.5 %collective-permute-start.13 = (bf16[64,2048]{1,0:T(8,128)(2,1)S(1)}, bf16[64,2048]{1,0:T(8,128)(2,1)S(1)}, u32[]{:S(2)}, u32[]{:S(2)}) collective-permute-start(bf16[64,2048]{1,0:T(8,128)(2,1)S(1)} %collective-permute-done.6.refs_2_.refs_10_.refs_11_), channel_id=1, source_target_pairs={{0,1},{1,0},{2,3},{3,2},{4,5},{5,4},{6,7},{7,6},{8,9},{9,8},{10,11... | collective-permute-start | bytes 786440 | tf_op jit(solution)/shard_map/ppermute | solution.py:425
  26.3 4.1 %collective-permute-start.12 = (bf16[64,2048]{1,0:T(8,128)(2,1)S(1)}, bf16[64,2048]{1,0:T(8,128)(2,1)S(1)}, u32[]{:S(2)}, u32[]{:S(2)}) collective-permute-start(bf16[64,2048]{1,0:T(8,128)(2,1)S(1)} %collective-permute-done.5.refs_1_.refs_8_.value_ref.refs_9_), channel_id=1, source_target_pairs={{0,1},{1,0},{2,3},{3,2},{4,5},{5,4},{6,7},{7,6},{8,9},{9,8},{10,11... | collective-permute-start | bytes 786440 | tf_op jit(solution)/shard_map/ppermute | solution.py:425
  26.3 2.3 %copy-start = (bf16[2048,128]{1,0:T(8,128)(2,1)S(1)}, bf16[2048,128]{1,0:T(8,128)(2,1)}, u32[]{:S(2)}) copy-start(bf16[2048,128]{1,0:T(8,128)(2,1)} %refs_0_.1) | copy-start | bytes 1572868
  26.3 2.3 %copy-start.1 = (bf16[64,2048]{1,0:T(8,128)(2,1)S(1)}, bf16[64,2048]{1,0:T(8,128)(2,1)}, u32[]{:S(2)}) copy-start(bf16[64,2048]{1,0:T(8,128)(2,1)} %refs_3_.2) | copy-start | bytes 786436
  26.3 2.3 %copy-start.2 = (bf16[2048,32]{0,1:T(8,128)(2,1)S(1)}, bf16[2048,32]{0,1:T(8,128)(2,1)}, u32[]{:S(2)}) copy-start(bf16[2048,32]{0,1:T(8,128)(2,1)} %param.12) | copy-start | bytes 393220
  26.3 2.3 %copy-start.3 = (bf16[1,2048]{1,0:T(2,128)(2,1)S(1)}, bf16[1,2048]{1,0:T(2,128)(2,1)}, u32[]{:S(2)}) copy-start(bf16[1,2048]{1,0:T(2,128)(2,1)} %refs_2_.2) | copy-start | bytes 12292
  26.3 2.3 %copy-start.4 = (f32[4,64]{1,0:T(4,128)S(1)}, f32[4,64]{1,0:T(4,128)}, u32[]{:S(2)}) copy-start(f32[4,64]{1,0:T(4,128)} %refs_4_.1) | copy-start | bytes 3076
  26.4 10.1 %collective-permute-start.10 = (bf16[64,2048]{1,0:T(8,128)(2,1)S(1)}, bf16[64,2048]{1,0:T(8,128)(2,1)S(1)}, u32[]{:S(2)}, u32[]{:S(2)}) collective-permute-start(bf16[64,2048]{1,0:T(8,128)(2,1)S(1)} %shard_map.131), channel_id=1, source_target_pairs={{0,2},{1,3},{2,0},{3,1},{4,6},{5,7},{6,4},{7,5},{8,10},{9,11},{10,... | collective-permute-start | bytes 786440 | tf_op jit(solution)/shard_map/ppermute | solution.py:425
  27.9 8.5 %collective-permute-start.15 = (bf16[64,2048]{1,0:T(8,128)(2,1)S(1)}, bf16[64,2048]{1,0:T(8,128)(2,1)S(1)}, u32[]{:S(2)}, u32[]{:S(2)}) collective-permute-start(bf16[64,2048]{1,0:T(8,128)(2,1)S(1)} %shard_map.135), channel_id=1, source_target_pairs={{0,16},{16,0},{1,17},{17,1},{2,18},{18,2},{3,19},{19,3},{4,20},{20... | collective-permute-start | bytes 786440 | tf_op jit(solution)/shard_map/ppermute | solution.py:428
  36.4 2.5 %collective-permute-start.16 = (bf16[64,2048]{1,0:T(8,128)(2,1)S(1)}, bf16[64,2048]{1,0:T(8,128)(2,1)S(1)}, u32[]{:S(2)}, u32[]{:S(2)}) collective-permute-start(bf16[64,2048]{1,0:T(8,128)(2,1)S(1)} %collective-permute-done.15.refs_6_.refs_15_), channel_id=1, source_target_pairs={{0,1},{1,0},{2,3},{3,2},{4,5},{5,4},{6,7},{7,6},{8,9},{9,8},{10,11... | collective-permute-start | bytes 786440 | tf_op jit(solution)/shard_map/ppermute | solution.py:425
  36.5 2.5 %collective-permute-start.14 = (bf16[64,2048]{1,0:T(8,128)(2,1)S(1)}, bf16[64,2048]{1,0:T(8,128)(2,1)S(1)}, u32[]{:S(2)}, u32[]{:S(2)}) collective-permute-start(bf16[64,2048]{1,0:T(8,128)(2,1)S(1)} %shard_map.134), channel_id=1, source_target_pairs={{0,1},{1,0},{2,3},{3,2},{4,5},{5,4},{6,7},{7,6},{8,9},{9,8},{10,11... | collective-permute-start | bytes 786440 | tf_op jit(solution)/shard_map/ppermute | solution.py:425
  44.8 2.1 %collective-permute-start.17 = (bf16[144,2048]{1,0:T(8,128)(2,1)S(1)}, bf16[144,2048]{1,0:T(8,128)(2,1)S(1)}, u32[]{:S(2)}, u32[]{:S(2)}) collective-permute-start(bf16[144,2048]{1,0:T(8,128)(2,1)S(1)} %get-tuple-element.31), channel_id=1, source_target_pairs={{0,1},{1,0},{2,3},{3,2},{4,5},{5,4},{6,7},{7,6},{8,9},{9,8},{10,11... | collective-permute-start | bytes 1769480 | tf_op jit(solution)/shard_map/ppermute | solution.py:425
  47.0 8.4 %collective-permute-start.18 = (bf16[64,2048]{1,0:T(8,128)(2,1)S(1)}, bf16[64,2048]{1,0:T(8,128)(2,1)S(1)}, u32[]{:S(2)}, u32[]{:S(2)}) collective-permute-start(bf16[64,2048]{1,0:T(8,128)(2,1)S(1)} %get-tuple-element.44.refs_19_._), channel_id=1, source_target_pairs={{0,2},{1,3},{2,0},{3,1},{4,6},{5,7},{6,4},{7,5},{8,10},{9,11},{10,... | collective-permute-start | bytes 786440 | tf_op jit(solution)/shard_map/ppermute | solution.py:425
  47.7 6.1 %collective-permute-start.22 = (bf16[16,2048]{1,0:T(8,128)(2,1)S(1)}, bf16[16,2048]{1,0:T(8,128)(2,1)S(1)}, u32[]{:S(2)}, u32[]{:S(2)}) collective-permute-start(bf16[16,2048]{1,0:T(8,128)(2,1)S(1)} %shard_map.139.a_ref), channel_id=1, source_target_pairs={{0,8},{1,9},{2,10},{3,11},{4,12},{5,13},{6,14},{7,15},{8,0},{9,1},... | collective-permute-start | bytes 196616 | tf_op jit(solution)/shard_map/ppermute | solution.py:425
  53.8 5.0 %collective-permute-start.23 = (bf16[16,2048]{1,0:T(8,128)(2,1)S(1)}, bf16[16,2048]{1,0:T(8,128)(2,1)S(1)}, u32[]{:S(2)}, u32[]{:S(2)}) collective-permute-start(bf16[16,2048]{1,0:T(8,128)(2,1)S(1)} %shard_map.140.a_ref), channel_id=1, source_target_pairs={{0,4},{1,5},{2,6},{3,7},{4,0},{5,1},{6,2},{7,3},{8,12},{9,13},{10,... | collective-permute-start | bytes 196616 | tf_op jit(solution)/shard_map/ppermute | solution.py:425
  55.5 4.3 %collective-permute-start.19 = (bf16[16,2048]{1,0:T(8,128)(2,1)S(1)}, bf16[16,2048]{1,0:T(8,128)(2,1)S(1)}, u32[]{:S(2)}, u32[]{:S(2)}) collective-permute-start(bf16[16,2048]{1,0:T(8,128)(2,1)S(1)} %get-tuple-element.33), channel_id=1, source_target_pairs={{0,4},{1,5},{2,6},{3,7},{4,0},{5,1},{6,2},{7,3},{8,12},{9,13},{10,... | collective-permute-start | bytes 196616 | tf_op jit(solution)/shard_map/ppermute | solution.py:425
  59.9 4.3 %collective-permute-start.24 = (bf16[16,2048]{1,0:T(8,128)(2,1)S(1)}, bf16[16,2048]{1,0:T(8,128)(2,1)S(1)}, u32[]{:S(2)}, u32[]{:S(2)}) collective-permute-start(bf16[16,2048]{1,0:T(8,128)(2,1)S(1)} %shard_map.141.shared_ref), channel_id=1, source_target_pairs={{0,2},{1,3},{2,0},{3,1},{4,6},{5,7},{6,4},{7,5},{8,10},{9,11},{10,... | collective-permute-start | bytes 196616 | tf_op jit(solution)/shard_map/ppermute | solution.py:425
  61.2 6.3 %collective-permute-start.20 = (bf16[16,2048]{1,0:T(8,128)(2,1)S(1)}, bf16[16,2048]{1,0:T(8,128)(2,1)S(1)}, u32[]{:S(2)}, u32[]{:S(2)}) collective-permute-start(bf16[16,2048]{1,0:T(8,128)(2,1)S(1)} %get-tuple-element.34), channel_id=1, source_target_pairs={{0,8},{1,9},{2,10},{3,11},{4,12},{5,13},{6,14},{7,15},{8,0},{9,1},... | collective-permute-start | bytes 196616 | tf_op jit(solution)/shard_map/ppermute | solution.py:425
  62.4 6.2 %collective-permute-start.21 = (bf16[16,2048]{1,0:T(8,128)(2,1)S(1)}, bf16[16,2048]{1,0:T(8,128)(2,1)S(1)}, u32[]{:S(2)}, u32[]{:S(2)}) collective-permute-start(bf16[16,2048]{1,0:T(8,128)(2,1)S(1)} %get-tuple-element.35), channel_id=1, source_target_pairs={{0,12},{1,13},{2,14},{3,15},{4,8},{5,9},{6,10},{7,11},{8,4},{9,5},... | collective-permute-start | bytes 196616 | tf_op jit(solution)/shard_map/ppermute | solution.py:425

commit v11 on v8

--- a/solution.py
+++ b/solution.py
@@ -203,16 +203,16 @@
     row_at = iota((length, LANES), 0)
 
     turned = [proj[:, 2 * LANES : 3 * LANES].astype(bf16)]
-    turned += split(proj[:, 3 * LANES :], 3) + split(grads[:, LANES:], 2)
+    turned += split(proj[:, 3 * LANES :], 2) + split(grads[:, LANES:], 2)
     turned = flip_rows(jnp.concatenate(turned, axis=1), flip)
-    turned = [turned[:, i * LANES : (i + 1) * LANES] for i in range(6)]
+    turned = [turned[:, i * LANES : (i + 1) * LANES] for i in range(5)]
     strands = (
         (
             proj[:, :LANES].astype(bf16).astype(f32),
             proj[:, LANES : 2 * LANES],
             grads[:, :LANES],
         ),
-        (turned[0], turned[1] + turned[2] + turned[3], turned[4] + turned[5]),
+        (turned[0], turned[1] + turned[2], turned[3] + turned[4]),
     )
 
     def gates(xz, rest, grad_g):
@@ -234,8 +234,8 @@
     def enter_chunk(c, gate, state):
         rows = slice(c * BLOCK, (c + 1) * BLOCK)
         dt, b_all, c_all, w_all = gate[3][rows], gate[5][rows], gate[6][rows], gate[7][rows]
-        log_keep = dot(tri, jnp.concatenate(split(dt * rate, 3), axis=1))
-        log_keep = log_keep[:, :LANES] + log_keep[:, LANES : 2 * LANES] + log_keep[:, 2 * LANES :]
+        log_keep = dot(tri, jnp.concatenate(split(dt * rate, 2), axis=1))
+        log_keep = log_keep[:, :LANES] + log_keep[:, LANES:]
         across = jnp.transpose(log_keep)[0:1, :]
         gap = jnp.concatenate([log_keep] * (BLOCK // LANES), axis=1) - across
         decay = jnp.exp(jnp.where(causal, gap, -jnp.inf))
@@ -383,7 +383,7 @@
     fwd = shared[: 2 * STATE]
     rev = turn_columns(shared[2 * STATE :], flip).astype(bf16)
     pairs = dot(jnp.concatenate([fwd, rev], axis=0), h_ref[...])
-    turned = exact(split(pairs[2 * STATE :], 3), lambda part: turn_columns(part, flip))
+    turned = exact(split(pairs[2 * STATE :], 2), lambda part: turn_columns(part, flip))
     dwbct_ref[...] = (pairs[: 2 * STATE] + turned) * scaling
 
 
@@ -510,7 +510,9 @@
         vmem=vmem,
     )
     if not ordered:
-        late = [a_d, across(after(a_d, projected[0]), 1), b_d, across(b_d, 1)]
+        a_other = across(after(a_d, projected[0]), 1)
+        b_other = across(after(b_d, projected[0]), 1)
+        late = [a_d, a_other, b_d, b_other]
         pieces = early + late
     extra = 4 * STATE * length // width
     half = tp_size * own_rows // 2

time: 66.9 us -> 66.5 us (level)
    ppermute x22, waiting for transfers between devices: 15.1 us -> 18.6 us  [across(): lax.ppermute(value, 'tp', [(i, i ^ flip_bits) for i in range(tp_size)])]
    ppermute x3, waiting for transfers between devices: 7.5 us -> 4.03 us  [along(): return lax.ppermute(value, 'ctx', [(0, 1), (1, 0)])]
    pallas_call x14 -> x15, Pallas kernels: 15.5 us -> 15.2 us  [call(): pl.pallas_call(kernel, out_shape=outs, in_specs=[spec(pltpu.SMEM)] * n_sm...]
  transfers between devices with their start and end apart: 25 -> 25, of which waited for: 10 -> 11; matrix products, arithmetic and copies ran while one was open for 0% -> 0% of each run, Pallas kernels for 12% -> 12%
where the time goes in v11:
time: 66.5 us; the launch traced here: 66.3 us
  starting transfers between devices  24.6 us (37%)
  waiting for transfers between devices  22.6 us (34%)
  Pallas kernels  15.2 us (23%)
  between operations  2.77 us (4%)
  other arithmetic  1.09 us (2%)
    ppermute x22, starting transfers between devices, across(): lax.ppermute(value, 'tp', [(i, i ^ flip_bits) for i in range(tp_size)])  21 us
    ppermute x22, waiting for transfers between devices, across(): lax.ppermute(value, 'tp', [(i, i ^ flip_bits) for i in range(tp_size)])  18.6 us
    pallas_call x15, Pallas kernels, call(): pl.pallas_call(kernel, out_shape=outs, in_specs=[spec(pltpu.SMEM)] * n_sm...  15.2 us
    ppermute x3, waiting for transfers between devices, along(): return lax.ppermute(value, 'ctx', [(0, 1), (1, 0)])  4.03 us
    ppermute x3, starting transfers between devices, along(): return lax.ppermute(value, 'ctx', [(0, 1), (1, 0)])  3.62 us
  transfers between devices with their start and end apart: 25, of which 11 were waited for; matrix products, arithmetic and copies ran while one was open for 0% of the time, Pallas kernels for 12%

profile of v11, /device:TPU:0, one launch (start us, length us, event | category | flops | bytes accessed | tf_op | source)
XLA Modules:
  0.0 66.3 jit_solution(2369040990904560879)
XLA Ops:
  0.6 0.9 %pad_maximum_fusion.refs_0_ = bf16[32,2048]{1,0:T(8,128)(2,1)S(1)} fusion(bf16[16,2048]{1,0:T(8,128)(2,1)} %param.19, bf16[16,2048]{1,0:T(8,128)(2,1)} %param.10), kind=kLoop, calls=%fused_computation.2 | loop fusion | flops 262144 | bytes 262144 | tf_op jit(solution)/shard_map/max | solution.py:471
  1.5 3.1 %collective-permute-start = (bf16[32,2048]{1,0:T(8,128)(2,1)S(1)}, bf16[32,2048]{1,0:T(8,128)(2,1)S(1)}, u32[]{:S(2)}, u32[]{:S(2)}) collective-permute-start(bf16[32,2048]{1,0:T(8,128)(2,1)S(1)} %pad_maximum_fusion.refs_0_), channel_id=1, source_target_pairs={{0,4},{1,5},{2,6},{3,7},{4,0},{5,1},{6,2},{7,3},{8,12},{9,13},{10,... | collective-permute-start | bytes 393224 | tf_op jit(solution)/shard_map/ppermute | solution.py:422
  4.6 2.6 %collective-permute-start.3 = (bf16[32,2048]{1,0:T(8,128)(2,1)S(1)}, bf16[32,2048]{1,0:T(8,128)(2,1)S(1)}, u32[]{:S(2)}, u32[]{:S(2)}) collective-permute-start(bf16[32,2048]{1,0:T(8,128)(2,1)S(1)} %pad_maximum_fusion.refs_0_), channel_id=1, source_target_pairs={{0,8},{1,9},{2,10},{3,11},{4,12},{5,13},{6,14},{7,15},{8,0},{9,1},... | collective-permute-start | bytes 393224 | tf_op jit(solution)/shard_map/ppermute | solution.py:422
  7.2 2.8 %collective-permute-done.refs_1_ = bf16[32,2048]{1,0:T(8,128)(2,1)S(1)} collective-permute-done((bf16[32,2048]{1,0:T(8,128)(2,1)S(1)}, bf16[32,2048]{1,0:T(8,128)(2,1)S(1)}, u32[]{:S(2)}, u32[]{:S(2)}) %collective-permute-start) | collective-permute-done | bytes 131104 | tf_op jit(solution)/shard_map/ppermute | solution.py:422
  10.0 1.9 %collective-permute-start.2 = (bf16[64,2048]{1,0:T(8,128)(2,1)S(1)}, bf16[64,2048]{1,0:T(8,128)(2,1)S(1)}, u32[]{:S(2)}, u32[]{:S(2)}) collective-permute-start(bf16[64,2048]{1,0:T(8,128)(2,1)S(1)} %shard_map.129.refs_0_.refs_1_), channel_id=1, source_target_pairs={{0,2},{1,3},{2,0},{3,1},{4,6},{5,7},{6,4},{7,5},{8,10},{9,11},{10,... | collective-permute-start | bytes 786440 | tf_op jit(solution)/shard_map/ppermute | solution.py:422
  11.9 1.5 %collective-permute-start.1 = (bf16[64,2048]{1,0:T(8,128)(2,1)S(1)}, bf16[64,2048]{1,0:T(8,128)(2,1)S(1)}, u32[]{:S(2)}, u32[]{:S(2)}) collective-permute-start(bf16[64,2048]{1,0:T(8,128)(2,1)S(1)} %shard_map.129.refs_0_.refs_1_), channel_id=1, source_target_pairs={{0,16},{16,0},{1,17},{17,1},{2,18},{18,2},{3,19},{19,3},{4,20},{20... | collective-permute-start | bytes 786440 | tf_op jit(solution)/shard_map/ppermute | solution.py:425
  13.8 4.6 %collective-permute-done.4.refs_1_ = bf16[32,2048]{1,0:T(8,128)(2,1)S(1)} collective-permute-done((bf16[32,2048]{1,0:T(8,128)(2,1)S(1)}, bf16[32,2048]{1,0:T(8,128)(2,1)S(1)}, u32[]{:S(2)}, u32[]{:S(2)}) %collective-permute-start.4) | collective-permute-done | bytes 131104 | tf_op jit(solution)/shard_map/ppermute | solution.py:422
  18.4 1.5 %collective-permute-start.6 = (bf16[64,2048]{1,0:T(8,128)(2,1)S(1)}, bf16[64,2048]{1,0:T(8,128)(2,1)S(1)}, u32[]{:S(2)}, u32[]{:S(2)}) collective-permute-start(bf16[64,2048]{1,0:T(8,128)(2,1)S(1)} %shard_map.130.refs_5_.refs_6_.refs_7_), channel_id=1, source_target_pairs={{0,16},{16,0},{1,17},{17,1},{2,18},{18,2},{3,19},{19,3},{4,20},{20... | collective-permute-start | bytes 786440 | tf_op jit(solution)/shard_map/ppermute | solution.py:425
  19.9 1.5 %collective-permute-start.5 = (bf16[64,2048]{1,0:T(8,128)(2,1)S(1)}, bf16[64,2048]{1,0:T(8,128)(2,1)S(1)}, u32[]{:S(2)}, u32[]{:S(2)}) collective-permute-start(bf16[64,2048]{1,0:T(8,128)(2,1)S(1)} %shard_map.130.refs_5_.refs_6_.refs_7_), channel_id=1, source_target_pairs={{0,2},{1,3},{2,0},{3,1},{4,6},{5,7},{6,4},{7,5},{8,10},{9,11},{10,... | collective-permute-start | bytes 786440 | tf_op jit(solution)/shard_map/ppermute | solution.py:422
  22.0 2.8 %collective-permute-done.6.refs_2_.refs_10_.refs_11_ = bf16[64,2048]{1,0:T(8,128)(2,1)S(1)} collective-permute-done((bf16[64,2048]{1,0:T(8,128)(2,1)S(1)}, bf16[64,2048]{1,0:T(8,128)(2,1)S(1)}, u32[]{:S(2)}, u32[]{:S(2)}) %collective-permute-start.6) | collective-permute-done | bytes 262176 | tf_op jit(solution)/shard_map/ppermute | solution.py:425
  24.8 1.5 %collective-permute-done.5.refs_1_.refs_8_.value_ref.refs_9_ = bf16[64,2048]{1,0:T(8,128)(2,1)S(1)} collective-permute-done((bf16[64,2048]{1,0:T(8,128)(2,1)S(1)}, bf16[64,2048]{1,0:T(8,128)(2,1)S(1)}, u32[]{:S(2)}, u32[]{:S(2)}) %collective-permute-start.5) | collective-permute-done | bytes 262176 | tf_op jit(solution)/shard_map/ppermute | solution.py:422
  26.4 1.6 %collective-permute-start.10 = (bf16[64,2048]{1,0:T(8,128)(2,1)S(1)}, bf16[64,2048]{1,0:T(8,128)(2,1)S(1)}, u32[]{:S(2)}, u32[]{:S(2)}) collective-permute-start(bf16[64,2048]{1,0:T(8,128)(2,1)S(1)} %shard_map.131), channel_id=1, source_target_pairs={{0,2},{1,3},{2,0},{3,1},{4,6},{5,7},{6,4},{7,5},{8,10},{9,11},{10,... | collective-permute-start | bytes 786440 | tf_op jit(solution)/shard_map/ppermute | solution.py:422
  27.9 0.6 collective-permute-start.15
  28.6 1.7 %shard_map.132 = (bf16[2048,512]{1,0:T(8,128)(2,1)S(1)}, bf16[512,2048]{1,0:T(8,128)(2,1)S(1)}, bf16[2048,256]{1,0:T(8,128)(2,1)S(1)}, f32[4,128]{1,0:T(4,128)S(1)}) custom-call(s32[4]{0:T(128)S(1)} %pad_add_fusion.ids_ref.refs_0_, bf16[2048,128]{1,0:T(8,128)(2,1)S(1)} %copy-done, bf16[32,2048]{1,0:T(8,128)(2,1)S(1)} %bitcast.6, ...), custom_call_target="tpu_custom_call" | custom-call | flops 805306368 | bytes 5242880 | tf_op jit(solution)/shard_map/pallas_call | solution.py:395
  30.3 1.4 %shard_map.133 = (f32[384,512]{1,0:T(8,128)S(1)}, f32[384,256]{1,0:T(8,128)S(1)}) custom-call(bf16[64,2048]{1,0:T(8,128)(2,1)S(1)} %shard_map.129.refs_0_.refs_1_, bf16[64,2048]{1,0:T(8,128)(2,1)S(1)} %collective-permute-done.7.refs_3_.refs_1_.refs_2_, bf16[64,2048]{1,0:T(8,128)(2,1)S(1)} %collective-permute-done.2.refs_0_.refs_2_.refs_3_, ...), custom_call_target="tpu_custom_call" | custom-call | flops 1207959552 | bytes 3145728 | tf_op jit(solution)/shard_map/pallas_call | solution.py:395
  31.8 3.4 %collective-permute-done.10.value_ref.refs_4_.refs_13_ = bf16[64,2048]{1,0:T(8,128)(2,1)S(1)} collective-permute-done((bf16[64,2048]{1,0:T(8,128)(2,1)S(1)}, bf16[64,2048]{1,0:T(8,128)(2,1)S(1)}, u32[]{:S(2)}, u32[]{:S(2)}) %collective-permute-start.10) | collective-permute-done | bytes 262176 | tf_op jit(solution)/shard_map/ppermute | solution.py:422
  35.2 1.2 %collective-permute-done.15.value_ref.refs_6_.refs_15_ = bf16[64,2048]{1,0:T(8,128)(2,1)S(1)} collective-permute-done((bf16[64,2048]{1,0:T(8,128)(2,1)S(1)}, bf16[64,2048]{1,0:T(8,128)(2,1)S(1)}, u32[]{:S(2)}, u32[]{:S(2)}) %collective-permute-start.15) | collective-permute-done | bytes 262176 | tf_op jit(solution)/shard_map/ppermute | solution.py:425
  38.5 5.8 %shard_map.137 = (bf16[144,2048]{1,0:T(8,128)(2,1)S(1)}, f32[144,2048]{1,0:T(8,128)S(1)}, bf16[512,512]{1,0:T(8,128)(2,1)S(1)}, bf16[512,256]{1,0:T(8,128)(2,1)S(1)}) custom-call(s32[4]{0:T(128)S(1)} %pad_add_fusion.ids_ref.refs_0_, f32[1]{0:T(128)S(6)} %copy.14.refs_1_, f32[1]{0:T(128)S(6)} %copy.15.refs_2_, f32[1]{0:T(128)S(6)} %copy.16.refs_3_, ...), custom_call_target="tpu_custom_call" | custom-call | flops 2147483648 | bytes 8388608 | tf_op jit(solution)/shard_map/pallas_call | solution.py:395
  44.3 0.6 collective-permute-start.17
  44.9 1.6 %collective-permute-done.17.b_ref = bf16[144,2048]{1,0:T(8,128)(2,1)S(1)} collective-permute-done((bf16[144,2048]{1,0:T(8,128)(2,1)S(1)}, bf16[144,2048]{1,0:T(8,128)(2,1)S(1)}, u32[]{:S(2)}, u32[]{:S(2)}) %collective-permute-start.17) | collective-permute-done | bytes 589856 | tf_op jit(solution)/shard_map/ppermute | solution.py:422
  46.6 0.7 %collective-permute-start.18 = (bf16[64,2048]{1,0:T(8,128)(2,1)S(1)}, bf16[64,2048]{1,0:T(8,128)(2,1)S(1)}, u32[]{:S(2)}, u32[]{:S(2)}) collective-permute-start(bf16[64,2048]{1,0:T(8,128)(2,1)S(1)} %get-tuple-element.44.refs_19_._), channel_id=1, source_target_pairs={{0,2},{1,3},{2,0},{3,1},{4,6},{5,7},{6,4},{7,5},{8,10},{9,11},{10,... | collective-permute-start | bytes 786440 | tf_op jit(solution)/shard_map/ppermute | solution.py:422
  47.4 1.1 %collective-permute-start.19 = (bf16[16,2048]{1,0:T(8,128)(2,1)S(1)}, bf16[16,2048]{1,0:T(8,128)(2,1)S(1)}, u32[]{:S(2)}, u32[]{:S(2)}) collective-permute-start(bf16[16,2048]{1,0:T(8,128)(2,1)S(1)} %shard_map.140.a_ref), channel_id=1, source_target_pairs={{0,8},{1,9},{2,10},{3,11},{4,12},{5,13},{6,14},{7,15},{8,0},{9,1},... | collective-permute-start | bytes 196616 | tf_op jit(solution)/shard_map/ppermute | solution.py:422
  48.5 4.4 %shard_map.139 = (f32[2048,128]{1,0:T(8,128)}, f32[64,2048]{1,0:T(8,128)}, f32[8,128]{1,0:T(8,128)S(1)}, bf16[512,2048]{1,0:T(8,128)(2,1)S(1)}) custom-call(s32[4]{0:T(128)S(1)} %pad_add_fusion.ids_ref.refs_0_, bf16[64,2048]{1,0:T(8,128)(2,1)S(1)} %shard_map.129.refs_0_.refs_1_, bf16[64,2048]{1,0:T(8,128)(2,1)S(1)} %collective-permute-done.7.refs_3_.refs_1_.refs_2_, ...), custom_call_target="tpu_custom_call" | custom-call | flops 2147483648 | bytes 8388608 | tf_op jit(solution)/shard_map/pallas_call | solution.py:395
  52.8 0.8 %collective-permute-done.19.b_ref = bf16[16,2048]{1,0:T(8,128)(2,1)S(1)} collective-permute-done((bf16[16,2048]{1,0:T(8,128)(2,1)S(1)}, bf16[16,2048]{1,0:T(8,128)(2,1)S(1)}, u32[]{:S(2)}, u32[]{:S(2)}) %collective-permute-start.19) | collective-permute-done | bytes 65568 | tf_op jit(solution)/shard_map/ppermute | solution.py:422
  53.6 1.3 %collective-permute-start.20 = (bf16[16,2048]{1,0:T(8,128)(2,1)S(1)}, bf16[16,2048]{1,0:T(8,128)(2,1)S(1)}, u32[]{:S(2)}, u32[]{:S(2)}) collective-permute-start(bf16[16,2048]{1,0:T(8,128)(2,1)S(1)} %shard_map.141.a_ref), channel_id=1, source_target_pairs={{0,4},{1,5},{2,6},{3,7},{4,0},{5,1},{6,2},{7,3},{8,12},{9,13},{10,... | collective-permute-start | bytes 196616 | tf_op jit(solution)/shard_map/ppermute | solution.py:422
  55.3 0.5 collective-permute-start.22
  55.8 2.6 %collective-permute-start.23 = (bf16[16,2048]{1,0:T(8,128)(2,1)S(1)}, bf16[16,2048]{1,0:T(8,128)(2,1)S(1)}, u32[]{:S(2)}, u32[]{:S(2)}) collective-permute-start(bf16[16,2048]{1,0:T(8,128)(2,1)S(1)} %get-tuple-element.38), channel_id=1, source_target_pairs={{0,8},{1,9},{2,10},{3,11},{4,12},{5,13},{6,14},{7,15},{8,0},{9,1},... | collective-permute-start | bytes 196616 | tf_op jit(solution)/shard_map/ppermute | solution.py:422
  58.4 1.4 %collective-permute-start.24 = (bf16[16,2048]{1,0:T(8,128)(2,1)S(1)}, bf16[16,2048]{1,0:T(8,128)(2,1)S(1)}, u32[]{:S(2)}, u32[]{:S(2)}) collective-permute-start(bf16[16,2048]{1,0:T(8,128)(2,1)S(1)} %get-tuple-element.39), channel_id=1, source_target_pairs={{0,12},{1,13},{2,14},{3,15},{4,8},{5,9},{6,10},{7,11},{8,4},{9,5},... | collective-permute-start | bytes 196616 | tf_op jit(solution)/shard_map/ppermute | solution.py:422
  59.8 1.1 %collective-permute-start.21 = (bf16[16,2048]{1,0:T(8,128)(2,1)S(1)}, bf16[16,2048]{1,0:T(8,128)(2,1)S(1)}, u32[]{:S(2)}, u32[]{:S(2)}) collective-permute-start(bf16[16,2048]{1,0:T(8,128)(2,1)S(1)} %shard_map.142.shared_ref), channel_id=1, source_target_pairs={{0,2},{1,3},{2,0},{3,1},{4,6},{5,7},{6,4},{7,5},{8,10},{9,11},{10,... | collective-permute-start | bytes 196616 | tf_op jit(solution)/shard_map/ppermute | solution.py:422
  60.9 2.3 %collective-permute-done.23.refs_1_ = bf16[16,2048]{1,0:T(8,128)(2,1)S(1)} collective-permute-done((bf16[16,2048]{1,0:T(8,128)(2,1)S(1)}, bf16[16,2048]{1,0:T(8,128)(2,1)S(1)}, u32[]{:S(2)}, u32[]{:S(2)}) %collective-permute-start.23) | collective-permute-done | bytes 65568 | tf_op jit(solution)/shard_map/ppermute | solution.py:422
  63.2 1.4 %collective-permute-done.24.refs_2_ = bf16[16,2048]{1,0:T(8,128)(2,1)S(1)} collective-permute-done((bf16[16,2048]{1,0:T(8,128)(2,1)S(1)}, bf16[16,2048]{1,0:T(8,128)(2,1)S(1)}, u32[]{:S(2)}, u32[]{:S(2)}) %collective-permute-start.24) | collective-permute-done | bytes 65568 | tf_op jit(solution)/shard_map/ppermute | solution.py:422
  64.6 1.7 %shard_map.143 = (bf16[16,2048]{1,0:T(8,128)(2,1)}, f32[32,2048]{1,0:T(8,128)}) custom-call(f32[16,2048]{1,0:T(8,128)S(1)} %get-tuple-element.32._.own_ref, bf16[512,2048]{1,0:T(8,128)(2,1)S(1)} %get-tuple-element.35.h_ref, bf16[16,2048]{1,0:T(8,128)(2,1)S(1)} %shard_map.142.shared_ref, bf16[16,2048]{1,0:T(8,128)(2,1)S(1)} %collective-permute-done.21.other_ref, ...), custom_call_target="tpu_custom_call" | custom-call | flops 268435456 | bytes 4194304 | tf_op jit(solution)/shard_map/pallas_call | solution.py:395
  (46 shorter events, 2.0 us)
Async XLA Ops:
  1.5 8.4 %collective-permute-start = (bf16[32,2048]{1,0:T(8,128)(2,1)S(1)}, bf16[32,2048]{1,0:T(8,128)(2,1)S(1)}, u32[]{:S(2)}, u32[]{:S(2)}) collective-permute-start(bf16[32,2048]{1,0:T(8,128)(2,1)S(1)} %pad_maximum_fusion.refs_0_), channel_id=1, source_target_pairs={{0,4},{1,5},{2,6},{3,7},{4,0},{5,1},{6,2},{7,3},{8,12},{9,13},{10,... | collective-permute-start | bytes 393224 | tf_op jit(solution)/shard_map/ppermute | solution.py:422
  4.6 8.8 %collective-permute-start.3 = (bf16[32,2048]{1,0:T(8,128)(2,1)S(1)}, bf16[32,2048]{1,0:T(8,128)(2,1)S(1)}, u32[]{:S(2)}, u32[]{:S(2)}) collective-permute-start(bf16[32,2048]{1,0:T(8,128)(2,1)S(1)} %pad_maximum_fusion.refs_0_), channel_id=1, source_target_pairs={{0,8},{1,9},{2,10},{3,11},{4,12},{5,13},{6,14},{7,15},{8,0},{9,1},... | collective-permute-start | bytes 393224 | tf_op jit(solution)/shard_map/ppermute | solution.py:422
  10.0 11.4 %collective-permute-start.2 = (bf16[64,2048]{1,0:T(8,128)(2,1)S(1)}, bf16[64,2048]{1,0:T(8,128)(2,1)S(1)}, u32[]{:S(2)}, u32[]{:S(2)}) collective-permute-start(bf16[64,2048]{1,0:T(8,128)(2,1)S(1)} %shard_map.129.refs_0_.refs_1_), channel_id=1, source_target_pairs={{0,2},{1,3},{2,0},{3,1},{4,6},{5,7},{6,4},{7,5},{8,10},{9,11},{10,... | collective-permute-start | bytes 786440 | tf_op jit(solution)/shard_map/ppermute | solution.py:422
  11.9 9.5 %collective-permute-start.1 = (bf16[64,2048]{1,0:T(8,128)(2,1)S(1)}, bf16[64,2048]{1,0:T(8,128)(2,1)S(1)}, u32[]{:S(2)}, u32[]{:S(2)}) collective-permute-start(bf16[64,2048]{1,0:T(8,128)(2,1)S(1)} %shard_map.129.refs_0_.refs_1_), channel_id=1, source_target_pairs={{0,16},{16,0},{1,17},{17,1},{2,18},{18,2},{3,19},{19,3},{4,20},{20... | collective-permute-start | bytes 786440 | tf_op jit(solution)/shard_map/ppermute | solution.py:425
  13.4 5.0 %collective-permute-start.4 = (bf16[32,2048]{1,0:T(8,128)(2,1)S(1)}, bf16[32,2048]{1,0:T(8,128)(2,1)S(1)}, u32[]{:S(2)}, u32[]{:S(2)}) collective-permute-start(bf16[32,2048]{1,0:T(8,128)(2,1)S(1)} %collective-permute-done.3.refs_0_), channel_id=1, source_target_pairs={{0,4},{1,5},{2,6},{3,7},{4,0},{5,1},{6,2},{7,3},{8,12},{9,13},{10,... | collective-permute-start | bytes 393224 | tf_op jit(solution)/shard_map/ppermute | solution.py:422
  13.8 8.1 %collective-permute-start.7 = (bf16[64,2048]{1,0:T(8,128)(2,1)S(1)}, bf16[64,2048]{1,0:T(8,128)(2,1)S(1)}, u32[]{:S(2)}, u32[]{:S(2)}) collective-permute-start(bf16[64,2048]{1,0:T(8,128)(2,1)S(1)} %shard_map.129.refs_0_.refs_1_), channel_id=1, source_target_pairs={{0,1},{1,0},{2,3},{3,2},{4,5},{5,4},{6,7},{7,6},{8,9},{9,8},{10,11... | collective-permute-start | bytes 786440 | tf_op jit(solution)/shard_map/ppermute | solution.py:422
  18.4 6.4 %collective-permute-start.6 = (bf16[64,2048]{1,0:T(8,128)(2,1)S(1)}, bf16[64,2048]{1,0:T(8,128)(2,1)S(1)}, u32[]{:S(2)}, u32[]{:S(2)}) collective-permute-start(bf16[64,2048]{1,0:T(8,128)(2,1)S(1)} %shard_map.130.refs_5_.refs_6_.refs_7_), channel_id=1, source_target_pairs={{0,16},{16,0},{1,17},{17,1},{2,18},{18,2},{3,19},{19,3},{4,20},{20... | collective-permute-start | bytes 786440 | tf_op jit(solution)/shard_map/ppermute | solution.py:425
  19.9 6.4 %collective-permute-start.5 = (bf16[64,2048]{1,0:T(8,128)(2,1)S(1)}, bf16[64,2048]{1,0:T(8,128)(2,1)S(1)}, u32[]{:S(2)}, u32[]{:S(2)}) collective-permute-start(bf16[64,2048]{1,0:T(8,128)(2,1)S(1)} %shard_map.130.refs_5_.refs_6_.refs_7_), channel_id=1, source_target_pairs={{0,2},{1,3},{2,0},{3,1},{4,6},{5,7},{6,4},{7,5},{8,10},{9,11},{10,... | collective-permute-start | bytes 786440 | tf_op jit(solution)/shard_map/ppermute | solution.py:422
  21.4 4.9 %collective-permute-start.8 = (bf16[64,2048]{1,0:T(8,128)(2,1)S(1)}, bf16[64,2048]{1,0:T(8,128)(2,1)S(1)}, u32[]{:S(2)}, u32[]{:S(2)}) collective-permute-start(bf16[64,2048]{1,0:T(8,128)(2,1)S(1)} %collective-permute-done.2.refs_0_.refs_2_.refs_3_), channel_id=1, source_target_pairs={{0,1},{1,0},{2,3},{3,2},{4,5},{5,4},{6,7},{7,6},{8,9},{9,8},{10,11... | collective-permute-start | bytes 786440 | tf_op jit(solution)/shard_map/ppermute | solution.py:422
  21.4 4.9 %collective-permute-start.9 = (bf16[64,2048]{1,0:T(8,128)(2,1)S(1)}, bf16[64,2048]{1,0:T(8,128)(2,1)S(1)}, u32[]{:S(2)}, u32[]{:S(2)}) collective-permute-start(bf16[64,2048]{1,0:T(8,128)(2,1)S(1)} %collective-permute-done.1.value_ref.refs_4_.refs_1_.refs_5_), channel_id=1, source_target_pairs={{0,1},{1,0},{2,3},{3,2},{4,5},{5,4},{6,7},{7,6},{8,9},{9,8},{10,11... | collective-permute-start | bytes 786440 | tf_op jit(solution)/shard_map/ppermute | solution.py:422
  21.9 8.4 %collective-permute-start.11 = (bf16[64,2048]{1,0:T(8,128)(2,1)S(1)}, bf16[64,2048]{1,0:T(8,128)(2,1)S(1)}, u32[]{:S(2)}, u32[]{:S(2)}) collective-permute-start(bf16[64,2048]{1,0:T(8,128)(2,1)S(1)} %shard_map.130.refs_5_.refs_6_.refs_7_), channel_id=1, source_target_pairs={{0,1},{1,0},{2,3},{3,2},{4,5},{5,4},{6,7},{7,6},{8,9},{9,8},{10,11... | collective-permute-start | bytes 786440 | tf_op jit(solution)/shard_map/ppermute | solution.py:422
  24.8 5.5 %collective-permute-start.13 = (bf16[64,2048]{1,0:T(8,128)(2,1)S(1)}, bf16[64,2048]{1,0:T(8,128)(2,1)S(1)}, u32[]{:S(2)}, u32[]{:S(2)}) collective-permute-start(bf16[64,2048]{1,0:T(8,128)(2,1)S(1)} %collective-permute-done.6.refs_2_.refs_10_.refs_11_), channel_id=1, source_target_pairs={{0,1},{1,0},{2,3},{3,2},{4,5},{5,4},{6,7},{7,6},{8,9},{9,8},{10,11... | collective-permute-start | bytes 786440 | tf_op jit(solution)/shard_map/ppermute | solution.py:422
  26.3 4.1 %collective-permute-start.12 = (bf16[64,2048]{1,0:T(8,128)(2,1)S(1)}, bf16[64,2048]{1,0:T(8,128)(2,1)S(1)}, u32[]{:S(2)}, u32[]{:S(2)}) collective-permute-start(bf16[64,2048]{1,0:T(8,128)(2,1)S(1)} %collective-permute-done.5.refs_1_.refs_8_.value_ref.refs_9_), channel_id=1, source_target_pairs={{0,1},{1,0},{2,3},{3,2},{4,5},{5,4},{6,7},{7,6},{8,9},{9,8},{10,11... | collective-permute-start | bytes 786440 | tf_op jit(solution)/shard_map/ppermute | solution.py:422
  26.3 2.3 %copy-start = (bf16[2048,128]{1,0:T(8,128)(2,1)S(1)}, bf16[2048,128]{1,0:T(8,128)(2,1)}, u32[]{:S(2)}) copy-start(bf16[2048,128]{1,0:T(8,128)(2,1)} %refs_0_.1) | copy-start | bytes 1572868
  26.3 2.3 %copy-start.1 = (bf16[64,2048]{1,0:T(8,128)(2,1)S(1)}, bf16[64,2048]{1,0:T(8,128)(2,1)}, u32[]{:S(2)}) copy-start(bf16[64,2048]{1,0:T(8,128)(2,1)} %refs_3_.2) | copy-start | bytes 786436
  26.3 2.3 %copy-start.2 = (bf16[2048,32]{0,1:T(8,128)(2,1)S(1)}, bf16[2048,32]{0,1:T(8,128)(2,1)}, u32[]{:S(2)}) copy-start(bf16[2048,32]{0,1:T(8,128)(2,1)} %param.12) | copy-start | bytes 393220
  26.3 2.3 %copy-start.3 = (bf16[1,2048]{1,0:T(2,128)(2,1)S(1)}, bf16[1,2048]{1,0:T(2,128)(2,1)}, u32[]{:S(2)}) copy-start(bf16[1,2048]{1,0:T(2,128)(2,1)} %refs_2_.2) | copy-start | bytes 12292
  26.3 2.3 %copy-start.4 = (f32[4,64]{1,0:T(4,128)S(1)}, f32[4,64]{1,0:T(4,128)}, u32[]{:S(2)}) copy-start(f32[4,64]{1,0:T(4,128)} %refs_4_.1) | copy-start | bytes 3076
  26.4 8.8 %collective-permute-start.10 = (bf16[64,2048]{1,0:T(8,128)(2,1)S(1)}, bf16[64,2048]{1,0:T(8,128)(2,1)S(1)}, u32[]{:S(2)}, u32[]{:S(2)}) collective-permute-start(bf16[64,2048]{1,0:T(8,128)(2,1)S(1)} %shard_map.131), channel_id=1, source_target_pairs={{0,2},{1,3},{2,0},{3,1},{4,6},{5,7},{6,4},{7,5},{8,10},{9,11},{10,... | collective-permute-start | bytes 786440 | tf_op jit(solution)/shard_map/ppermute | solution.py:422
  27.9 8.5 %collective-permute-start.15 = (bf16[64,2048]{1,0:T(8,128)(2,1)S(1)}, bf16[64,2048]{1,0:T(8,128)(2,1)S(1)}, u32[]{:S(2)}, u32[]{:S(2)}) collective-permute-start(bf16[64,2048]{1,0:T(8,128)(2,1)S(1)} %shard_map.135), channel_id=1, source_target_pairs={{0,16},{16,0},{1,17},{17,1},{2,18},{18,2},{3,19},{19,3},{4,20},{20... | collective-permute-start | bytes 786440 | tf_op jit(solution)/shard_map/ppermute | solution.py:425
  35.1 3.3 %collective-permute-start.14 = (bf16[64,2048]{1,0:T(8,128)(2,1)S(1)}, bf16[64,2048]{1,0:T(8,128)(2,1)S(1)}, u32[]{:S(2)}, u32[]{:S(2)}) collective-permute-start(bf16[64,2048]{1,0:T(8,128)(2,1)S(1)} %shard_map.134), channel_id=1, source_target_pairs={{0,1},{1,0},{2,3},{3,2},{4,5},{5,4},{6,7},{7,6},{8,9},{9,8},{10,11... | collective-permute-start | bytes 786440 | tf_op jit(solution)/shard_map/ppermute | solution.py:422
  36.4 2.0 %collective-permute-start.16 = (bf16[64,2048]{1,0:T(8,128)(2,1)S(1)}, bf16[64,2048]{1,0:T(8,128)(2,1)S(1)}, u32[]{:S(2)}, u32[]{:S(2)}) collective-permute-start(bf16[64,2048]{1,0:T(8,128)(2,1)S(1)} %shard_map.136), channel_id=1, source_target_pairs={{0,1},{1,0},{2,3},{3,2},{4,5},{5,4},{6,7},{7,6},{8,9},{9,8},{10,11... | collective-permute-start | bytes 786440 | tf_op jit(solution)/shard_map/ppermute | solution.py:422
  44.3 2.2 %collective-permute-start.17 = (bf16[144,2048]{1,0:T(8,128)(2,1)S(1)}, bf16[144,2048]{1,0:T(8,128)(2,1)S(1)}, u32[]{:S(2)}, u32[]{:S(2)}) collective-permute-start(bf16[144,2048]{1,0:T(8,128)(2,1)S(1)} %get-tuple-element.31), channel_id=1, source_target_pairs={{0,1},{1,0},{2,3},{3,2},{4,5},{5,4},{6,7},{7,6},{8,9},{9,8},{10,11... | collective-permute-start | bytes 1769480 | tf_op jit(solution)/shard_map/ppermute | solution.py:422
  46.6 8.7 %collective-permute-start.18 = (bf16[64,2048]{1,0:T(8,128)(2,1)S(1)}, bf16[64,2048]{1,0:T(8,128)(2,1)S(1)}, u32[]{:S(2)}, u32[]{:S(2)}) collective-permute-start(bf16[64,2048]{1,0:T(8,128)(2,1)S(1)} %get-tuple-element.44.refs_19_._), channel_id=1, source_target_pairs={{0,2},{1,3},{2,0},{3,1},{4,6},{5,7},{6,4},{7,5},{8,10},{9,11},{10,... | collective-permute-start | bytes 786440 | tf_op jit(solution)/shard_map/ppermute | solution.py:422
  47.4 6.2 %collective-permute-start.19 = (bf16[16,2048]{1,0:T(8,128)(2,1)S(1)}, bf16[16,2048]{1,0:T(8,128)(2,1)S(1)}, u32[]{:S(2)}, u32[]{:S(2)}) collective-permute-start(bf16[16,2048]{1,0:T(8,128)(2,1)S(1)} %shard_map.140.a_ref), channel_id=1, source_target_pairs={{0,8},{1,9},{2,10},{3,11},{4,12},{5,13},{6,14},{7,15},{8,0},{9,1},... | collective-permute-start | bytes 196616 | tf_op jit(solution)/shard_map/ppermute | solution.py:422
  53.6 6.2 %collective-permute-start.20 = (bf16[16,2048]{1,0:T(8,128)(2,1)S(1)}, bf16[16,2048]{1,0:T(8,128)(2,1)S(1)}, u32[]{:S(2)}, u32[]{:S(2)}) collective-permute-start(bf16[16,2048]{1,0:T(8,128)(2,1)S(1)} %shard_map.141.a_ref), channel_id=1, source_target_pairs={{0,4},{1,5},{2,6},{3,7},{4,0},{5,1},{6,2},{7,3},{8,12},{9,13},{10,... | collective-permute-start | bytes 196616 | tf_op jit(solution)/shard_map/ppermute | solution.py:422
  55.3 5.6 %collective-permute-start.22 = (bf16[16,2048]{1,0:T(8,128)(2,1)S(1)}, bf16[16,2048]{1,0:T(8,128)(2,1)S(1)}, u32[]{:S(2)}, u32[]{:S(2)}) collective-permute-start(bf16[16,2048]{1,0:T(8,128)(2,1)S(1)} %get-tuple-element.37), channel_id=1, source_target_pairs={{0,4},{1,5},{2,6},{3,7},{4,0},{5,1},{6,2},{7,3},{8,12},{9,13},{10,... | collective-permute-start | bytes 196616 | tf_op jit(solution)/shard_map/ppermute | solution.py:422
  55.8 7.4 %collective-permute-start.23 = (bf16[16,2048]{1,0:T(8,128)(2,1)S(1)}, bf16[16,2048]{1,0:T(8,128)(2,1)S(1)}, u32[]{:S(2)}, u32[]{:S(2)}) collective-permute-start(bf16[16,2048]{1,0:T(8,128)(2,1)S(1)} %get-tuple-element.38), channel_id=1, source_target_pairs={{0,8},{1,9},{2,10},{3,11},{4,12},{5,13},{6,14},{7,15},{8,0},{9,1},... | collective-permute-start | bytes 196616 | tf_op jit(solution)/shard_map/ppermute | solution.py:422
  58.4 6.2 %collective-permute-start.24 = (bf16[16,2048]{1,0:T(8,128)(2,1)S(1)}, bf16[16,2048]{1,0:T(8,128)(2,1)S(1)}, u32[]{:S(2)}, u32[]{:S(2)}) collective-permute-start(bf16[16,2048]{1,0:T(8,128)(2,1)S(1)} %get-tuple-element.39), channel_id=1, source_target_pairs={{0,12},{1,13},{2,14},{3,15},{4,8},{5,9},{6,10},{7,11},{8,4},{9,5},... | collective-permute-start | bytes 196616 | tf_op jit(solution)/shard_map/ppermute | solution.py:422
  59.8 4.8 %collective-permute-start.21 = (bf16[16,2048]{1,0:T(8,128)(2,1)S(1)}, bf16[16,2048]{1,0:T(8,128)(2,1)S(1)}, u32[]{:S(2)}, u32[]{:S(2)}) collective-permute-start(bf16[16,2048]{1,0:T(8,128)(2,1)S(1)} %shard_map.142.shared_ref), channel_id=1, source_target_pairs={{0,2},{1,3},{2,0},{3,1},{4,6},{5,7},{6,4},{7,5},{8,10},{9,11},{10,... | collective-permute-start | bytes 196616 | tf_op jit(solution)/shard_map/ppermute | solution.py:422
